TPU v7x, 512 devices: a whole 4x8x8 slice. The times are simulated.
512 devices in a mesh: sec: 2 (over z_hi), gx: 32 (over x, y), gy: 8 (over z_lo, core).
Axes of the slice: x: 4, y: 8, z: 8 (z_hi: 2, z_lo: 4; z = z_hi * 4 + z_lo), core: 2. Of those that a mesh axis runs over, the one named last changes fastest.
Arguments:
- section_state: float32 [2, 8, 512, 2048], P('sec', None, 'gx', 'gy'), may hold values from -6 to 6
- prev_import: float32 [2, 8, 512, 2048], P('sec', None, 'gx', 'gy'), may hold values from -6 to 6
- land_mask: int32 [2, 512, 2048], P('sec', 'gx', 'gy'), may hold values 0 or 1
- state_mix: float32 [2, 8, 8], P('sec'), may hold values from -1.5 to 1.5
- import_mix: float32 [2, 8, 8], P('sec'), may hold values from -1.5 to 1.5
- damping: float32 [2, 8], P('sec'), may hold values from 0.015 to 0.3
- wave_speed: float32 [2, 2], P('sec'), may hold values from 0.95 to 1
- remap_owner: int32 [2, 512, 32, 2], P('sec', 'gx', 'gy'), may hold values from 0 to 31, as said below
- remap_slot: int32 [2, 512, 32, 2], P('sec', 'gx', 'gy'), may hold values from 0 to 63
- remap_weight: bfloat16 [2, 512, 32, 64, 128], P('sec', 'gx', 'gy'), may hold values from 0 to 1, as said below
Outputs:
- final_state: float32 [2, 8, 512, 2048], P('sec', None, 'gx', 'gy')
- final_import: float32 [2, 8, 512, 2048], P('sec', None, 'gx', 'gy')
Inputs may be any that keep to these rules, and one draw needn't show every extreme that they name: `remap_owner`: the source tile lies in the same gy column of the other section and within 2 tiles of the destination block's own gx tile index. `remap_weight`: every destination cell has a positive weight on some cell of each of its source blocks.
All inputs are finite; a program needn't handle non-finite values. No bound on the sum of `land_mask` on one device may be relied on, other than what follows from the above.
Results may differ from a plain program's by a relative error of at most 0.0018.
Values may be sent and summed in bfloat16 or wider, within the bound.
No kernel may reach another device: no remote copies, remote signals or barrier semaphores. Data moves between devices by JAX's collectives and lax.ppermute only.
A program may use at most 64 MiB of HBM per device.

v0:
```python
import jax
import jax.numpy as jnp
from jax import lax
from jax.sharding import PartitionSpec as P

SUBSTEPS = 16
ITERS = 2


DIFFUSION = 0.1
COUPLING = 0.2


def swapped(block, axis, distance):
    count = lax.axis_size(axis)
    route = []
    for low in range(count):
        high = low | 1 << distance
        if high != low and high < count:
            route += [(low, high), (high, low)]
    return lax.ppermute(block, axis, route)


def passed_along(shard, axis, by):
    length = lax.axis_size(axis)
    pairs = [(i, i + by) for i in range(length) if 0 <= i + by < length]
    return lax.ppermute(shard, axis, pairs)


def with_halo(cells, sides, width):
    for axis, dim in sides:
        count = lax.axis_size(axis)
        ends = count - 1
        head = lax.slice_in_dim(cells, 0, width, axis=dim)
        tail = lax.slice_in_dim(cells, cells.shape[dim] - width, cells.shape[dim], axis=dim)
        cells = jnp.concatenate(
            [
                lax.ppermute(tail, axis, [(i, (i + 1) % count) for i in range(ends)]),
                cells,
                lax.ppermute(head, axis, [((i + 1) % count, i) for i in range(ends)]),
            ],
            axis=dim,
        )
    return cells


def trimmed(field, amount):
    return field[..., amount : field.shape[-2] - amount, amount : field.shape[-1] - amount]


def diff_x(field):
    return 0.5 * (field[..., 2:, 1:-1] - field[..., :-2, 1:-1])


def diff_y(field):
    return 0.5 * (field[..., 1:-1, 2:] - field[..., 1:-1, :-2])


def advance(extended, forcing, inside, damping_rates, wave_terms):
    height = extended[0:1]
    east_flow = extended[1:2]
    north_flow = extended[2:3]
    tracers = extended[3:]
    new_height = (
        (1.0 - damping_rates[0]) * trimmed(height, 1)
        - wave_terms[0] * (diff_x(east_flow) + diff_y(north_flow))
        + trimmed(forcing[0:1], 1)
    ) * trimmed(inside, 1)
    new_east = (
        (1.0 - damping_rates[1]) * trimmed(east_flow, 2)
        - wave_terms[1] * diff_x(new_height)
        + trimmed(forcing[1:2], 2)
    ) * trimmed(inside, 2)
    new_north = (
        (1.0 - damping_rates[2]) * trimmed(north_flow, 2)
        - wave_terms[1] * diff_y(new_height)
        + trimmed(forcing[2:3], 2)
    ) * trimmed(inside, 2)
    laplacian = (
        tracers[..., 2:, 1:-1]
        + tracers[..., :-2, 1:-1]
        + tracers[..., 1:-1, 2:]
        + tracers[..., 1:-1, :-2]
        - 4.0 * trimmed(tracers, 1)
    )
    new_tracers = (
        (1.0 - damping_rates[3:, None, None]) * trimmed(tracers, 1)
        + DIFFUSION * laplacian
        + trimmed(forcing[3:], 1)
    )
    new_tracers = trimmed(new_tracers, 1) * trimmed(inside, 2)
    return jnp.concatenate([trimmed(new_height, 1), new_east, new_north, new_tracers], axis=0)


def local(
    section_state,
    prev_import,
    land_mask,
    state_mix,
    import_mix,
    damping,
    wave_speed,
    remap_owner,
    remap_slot,
    remap_weight,
):
    fields = section_state[0]
    received = prev_import[0]
    wet_cells = land_mask[0].astype(jnp.float32)
    channels = fields.shape[0]
    tile_rows = fields.shape[1]
    tile_cols = fields.shape[2]
    blocks_tile = tile_rows * (tile_cols // 64)
    gx_index = lax.axis_index("gx")
    gx_count = lax.axis_size("gx")
    gy_index = lax.axis_index("gy")
    gy_count = lax.axis_size("gy")
    relative = remap_owner[0] - gx_index
    block_index = ((relative + 2) * blocks_tile + remap_slot[0]).reshape(-1)
    weights = remap_weight[0].reshape(blocks_tile, 64, -1)
    weight_total = jnp.sum(weights, axis=-1, dtype=jnp.float32).reshape(tile_rows, tile_cols)
    damping_rates = damping[0]
    wave_terms = wave_speed[0]
    group = 1
    width = 2 * group
    rows_global = gx_index * tile_rows + jnp.arange(tile_rows + 2 * width, dtype=jnp.int32) - width
    cols_global = gy_index * tile_cols + jnp.arange(tile_cols + 2 * width, dtype=jnp.int32) - width
    valid_rows = ((rows_global >= 0) & (rows_global < gx_count * tile_rows)).astype(jnp.float32)
    valid_cols = ((cols_global >= 0) & (cols_global < gy_count * tile_cols)).astype(jnp.float32)
    inside = valid_rows[:, None] * valid_cols[None, :]
    for interval in range(ITERS):
        mixture = jnp.einsum("ck,kxy->cxy", state_mix[0], fields, precision=lax.Precision.HIGHEST)
        mixture = mixture + jnp.einsum(
            "ck,kxy->cxy", import_mix[0], received, precision=lax.Precision.HIGHEST
        )
        wind_speed = jnp.sqrt(1.0 + fields[1] * fields[1] + fields[2] * fields[2])
        export_field = (wet_cells * wind_speed * mixture).astype(jnp.bfloat16)
        opposite = swapped(export_field, "sec", 0)
        nearby = [
            passed_along(opposite, "gx", offset) if offset != 0 else opposite
            for offset in (2, 1, 0, -1, -2)
        ]
        source = jnp.concatenate(nearby, axis=1)
        picked = jnp.take(source.reshape(channels, 5 * blocks_tile, 64), block_index, axis=1)
        picked = picked.reshape(channels, blocks_tile, -1)
        weighted = jnp.einsum("rcj,frj->frc", weights, picked, preferred_element_type=jnp.float32)
        received = weighted.reshape(channels, tile_rows, tile_cols) / weight_total
        forcing = COUPLING * wet_cells * received
        forcing_wide = with_halo(forcing, (("gx", 1), ("gy", 2)), width)

        def one_turn(counter, current):
            extended = with_halo(current, (("gx", 1), ("gy", 2)), width)
            extended = advance(
                extended, trimmed(forcing_wide, 0), trimmed(inside, 0), damping_rates, wave_terms
            )
            return extended

        fields = lax.fori_loop(0, SUBSTEPS // group, one_turn, fields)
    return (fields[None], received[None])


def solution(mesh):
    in_specs = (
        P("sec", None, "gx", "gy"),
        P("sec", None, "gx", "gy"),
        P("sec", "gx", "gy"),
        P("sec", None, None),
        P("sec", None, None),
        P("sec", None),
        P("sec", None),
        P("sec", "gx", "gy", None),
        P("sec", "gx", "gy", None),
        P("sec", "gx", "gy", None, None),
    )
    out_specs = (P("sec", None, "gx", "gy"), P("sec", None, "gx", "gy"))
    return jax.shard_map(local, mesh=mesh, in_specs=in_specs, out_specs=out_specs, check_vma=False)
```

profile of v0, /device:TPU:6, one launch (start us, length us, event | category | flops | bytes accessed | tf_op | source)
XLA Modules:
  0.0 718.0 jit_solution(1241718520021347334)
XLA Ops:
  4.4 10.9 %collective-permute-start.8 = (bf16[8,16,256]{2,0,1:T(8,128)(2,1)S(1)}, bf16[8,16,256]{2,0,1:T(8,128)(2,1)S(1)}, u32[]{:S(2)}, u32[]{:S(2)}) collective-permute-start(bf16[8,16,256]{2,0,1:T(8,128)(2,1)S(1)} %fusion.39), channel_id=1, source_target_pairs={{0,256},{256,0},{1,257},{257,1},{2,258},{258,2},{3,259},{259,3},{4... | collective-permute-start | bytes 196616 | tf_op jit(solution)/shard_map/ppermute | solution.py:21
  18.4 4.5 collective-permute-start.9
  22.9 4.3 collective-permute-start.12
  33.1 5.9 collective-permute-done.10
  43.9 6.0 collective-permute-start.14
  58.3 302.7 %while.26 = (s32[]{:T(128)}, f32[8,16,256]{2,1,0:T(8,128)S(1)}, f32[]{:T(128)}, f32[]{:T(128)}, f32[8,20,260]{2,1,0:T(8,128)S(1)}, /*index=5*/f32[20,260]{1,0:T(...) while((s32[]{:T(128)}, f32[8,16,256]{2,1,0:T(8,128)S(1)}, f32[]{:T(128)}, ...), condition=%wide.region_2.4_spmd, body=%wide.region_1.0_spmd.sunk | while | flops 860647 | bytes 3113053 | solution.py:158
  58.3 6.3 collective-permute-start
  66.6 5.8 collective-permute-done.1
  90.1 5.4 collective-permute-start.3
  99.5 3.9 collective-permute-start.1
  108.7 5.6 collective-permute-start.3
  127.5 5.6 collective-permute-start.3
  146.4 5.6 collective-permute-start.3
  165.2 5.6 collective-permute-start.3
  184.0 5.6 collective-permute-start.3
  202.8 5.6 collective-permute-start.3
  221.6 5.6 collective-permute-start.3
  240.4 5.6 collective-permute-start.3
  259.3 5.6 collective-permute-start.3
  278.1 5.6 collective-permute-start.3
  296.9 5.6 collective-permute-start.3
  315.7 5.6 collective-permute-start.3
  334.5 5.6 collective-permute-start.3
  353.3 5.6 collective-permute-start.3
  361.7 7.7 %collective-permute-start.17 = (bf16[8,16,256]{2,0,1:T(8,128)(2,1)S(1)}, bf16[8,16,256]{2,0,1:T(8,128)(2,1)S(1)}, u32[]{:S(2)}, u32[]{:S(2)}) collective-permute-start(bf16[8,16,256]{2,0,1:T(8,128)(2,1)S(1)} %fusion.40), channel_id=1, source_target_pairs={{0,256},{256,0},{1,257},{257,1},{2,258},{258,2},{3,259},{259,3},{4... | collective-permute-start | bytes 196616 | tf_op jit(solution)/shard_map/ppermute | solution.py:21
  373.7 6.9 collective-permute-start.21
  382.6 3.9 collective-permute-start.19
  386.5 4.3 collective-permute-done.19
  395.6 6.0 collective-permute-start.23
  407.6 7.1 collective-permute-done.25
  414.9 302.4 %while.27 = (s32[]{:T(128)}, f32[8,16,256]{2,1,0:T(8,128)S(1)}, f32[]{:T(128)}, f32[]{:T(128)}, f32[8,20,260]{2,1,0:T(8,128)S(1)}, /*index=5*/f32[20,260]{1,0:T(...) while((s32[]{:T(128)}, f32[8,16,256]{2,1,0:T(8,128)S(1)}, f32[]{:T(128)}, ...), condition=%wide.region_4.6_spmd, body=%wide.region_3.5_spmd.sunk | while | flops 860647 | bytes 3113053 | solution.py:158
  415.0 6.3 collective-permute-start.4
  423.2 5.8 collective-permute-done.5
  430.5 4.3 collective-permute-start.7
  465.0 5.6 collective-permute-start.7
  483.8 5.6 collective-permute-start.7
  502.6 5.6 collective-permute-start.7
  521.5 5.6 collective-permute-start.7
  540.3 5.6 collective-permute-start.7
  559.1 5.6 collective-permute-start.7
  577.9 5.6 collective-permute-start.7
  596.7 5.6 collective-permute-start.7
  615.5 5.6 collective-permute-start.7
  634.4 5.6 collective-permute-start.7
  653.2 5.6 collective-permute-start.7
  672.0 5.6 collective-permute-start.7
  690.8 5.6 collective-permute-start.7
  709.6 5.6 collective-permute-start.7
  (742 shorter events, 446.4 us)
Async XLA Ops:
  4.4 14.0 %collective-permute-start.8 = (bf16[8,16,256]{2,0,1:T(8,128)(2,1)S(1)}, bf16[8,16,256]{2,0,1:T(8,128)(2,1)S(1)}, u32[]{:S(2)}, u32[]{:S(2)}) collective-permute-start(bf16[8,16,256]{2,0,1:T(8,128)(2,1)S(1)} %fusion.39), channel_id=1, source_target_pairs={{0,256},{256,0},{1,257},{257,1},{2,258},{258,2},{3,259},{259,3},{4... | collective-permute-start | bytes 196616 | tf_op jit(solution)/shard_map/ppermute | solution.py:21
  18.4 14.7 %collective-permute-start.9 = (bf16[8,16,256]{2,0,1:T(8,128)(2,1)S(1)}, bf16[8,16,256]{2,0,1:T(8,128)(2,1)S(1)}, u32[]{:S(2)}, u32[]{:S(2)}) collective-permute-start(bf16[8,16,256]{2,0,1:T(8,128)(2,1)S(1)} %collective-permute-done.8), channel_id=1, source_target_pairs={{0,16},{8,24},{16,32},{24,40},{32,48},{40,56},{48,64},{56,72},{64,... | collective-permute-start | bytes 196616 | tf_op jit(solution)/shard_map/ppermute | solution.py:27
  22.9 16.2 %collective-permute-start.12 = (bf16[8,16,256]{2,0,1:T(8,128)(2,1)S(1)}, bf16[8,16,256]{2,0,1:T(8,128)(2,1)S(1)}, u32[]{:S(2)}, u32[]{:S(2)}) collective-permute-start(bf16[8,16,256]{2,0,1:T(8,128)(2,1)S(1)} %collective-permute-done.8), channel_id=1, source_target_pairs={{16,0},{24,8},{32,16},{40,24},{48,32},{56,40},{64,48},{72,56},{80,... | collective-permute-start | bytes 196616 | tf_op jit(solution)/shard_map/ppermute | solution.py:27
  27.2 11.8 %collective-permute-start.11 = (bf16[8,16,256]{2,0,1:T(8,128)(2,1)S(1)}, bf16[8,16,256]{2,0,1:T(8,128)(2,1)S(1)}, u32[]{:S(2)}, u32[]{:S(2)}) collective-permute-start(bf16[8,16,256]{2,0,1:T(8,128)(2,1)S(1)} %collective-permute-done.8), channel_id=1, source_target_pairs={{8,0},{16,8},{24,16},{32,24},{40,32},{48,40},{56,48},{64,56},{72,6... | collective-permute-start | bytes 196616 | tf_op jit(solution)/shard_map/ppermute | solution.py:27
  30.8 8.3 %collective-permute-start.10 = (bf16[8,16,256]{2,0,1:T(8,128)(2,1)S(1)}, bf16[8,16,256]{2,0,1:T(8,128)(2,1)S(1)}, u32[]{:S(2)}, u32[]{:S(2)}) collective-permute-start(bf16[8,16,256]{2,0,1:T(8,128)(2,1)S(1)} %collective-permute-done.8), channel_id=1, source_target_pairs={{0,8},{8,16},{16,24},{24,32},{32,40},{40,48},{48,56},{56,64},{64,7... | collective-permute-start | bytes 196616 | tf_op jit(solution)/shard_map/ppermute | solution.py:27
  41.9 8.6 %collective-permute-start.13 = (f32[8,2,256]{2,1,0:T(2,128)S(1)}, f32[8,2,256]{2,1,0:T(2,128)S(1)}, u32[]{:S(2)}, u32[]{:S(2)}) collective-permute-start(f32[8,2,256]{2,1,0:T(2,128)S(1)} %get-tuple-element.311), channel_id=1, source_target_pairs={{0,8},{8,16},{16,24},{24,32},{32,40},{40,48},{48,56},{56,64},{64,7... | collective-permute-start | bytes 49160 | tf_op jit(solution)/shard_map/ppermute | solution.py:38
  43.9 7.5 %collective-permute-start.14 = (f32[8,2,256]{2,1,0:T(2,128)S(1)}, f32[8,2,256]{2,1,0:T(2,128)S(1)}, u32[]{:S(2)}, u32[]{:S(2)}) collective-permute-start(f32[8,2,256]{2,1,0:T(2,128)S(1)} %get-tuple-element.312), channel_id=1, source_target_pairs={{8,0},{16,8},{24,16},{32,24},{40,32},{48,40},{56,48},{64,56},{72,6... | collective-permute-start | bytes 49160 | tf_op jit(solution)/shard_map/ppermute | solution.py:40
  58.3 8.3 %collective-permute-start = (f32[8,2,256]{2,1,0:T(2,128)S(1)}, f32[8,2,256]{2,1,0:T(2,128)S(1)}, u32[]{:S(2)}, u32[]{:S(2)}) collective-permute-start(f32[8,2,256]{2,1,0:T(2,128)S(1)} %get-tuple-element.456), channel_id=1, source_target_pairs={{8,0},{16,8},{24,16},{32,24},{40,32},{48,40},{56,48},{64,56},{72,6... | collective-permute-start | bytes 49160 | tf_op jit(solution)/shard_map/while/body/eval_jaxpr/ppermute | solution.py:40
  64.6 7.7 %collective-permute-start.1 = (f32[8,2,256]{2,1,0:T(2,128)S(1)}, f32[8,2,256]{2,1,0:T(2,128)S(1)}, u32[]{:S(2)}, u32[]{:S(2)}) collective-permute-start(f32[8,2,256]{2,1,0:T(2,128)S(1)} %get-tuple-element.457), channel_id=1, source_target_pairs={{0,8},{8,16},{16,24},{24,32},{32,40},{40,48},{48,56},{56,64},{64,7... | collective-permute-start | bytes 49160 | tf_op jit(solution)/shard_map/while/body/eval_jaxpr/ppermute | solution.py:38
  81.0 7.7 %collective-permute-start.1 = (f32[8,2,256]{2,1,0:T(2,128)S(1)}, f32[8,2,256]{2,1,0:T(2,128)S(1)}, u32[]{:S(2)}, u32[]{:S(2)}) collective-permute-start(f32[8,2,256]{2,1,0:T(2,128)S(1)} %get-tuple-element.457), channel_id=1, source_target_pairs={{0,8},{8,16},{16,24},{24,32},{32,40},{40,48},{48,56},{56,64},{64,7... | collective-permute-start | bytes 49160 | tf_op jit(solution)/shard_map/while/body/eval_jaxpr/ppermute | solution.py:38
  99.5 7.7 %collective-permute-start.1 = (f32[8,2,256]{2,1,0:T(2,128)S(1)}, f32[8,2,256]{2,1,0:T(2,128)S(1)}, u32[]{:S(2)}, u32[]{:S(2)}) collective-permute-start(f32[8,2,256]{2,1,0:T(2,128)S(1)} %get-tuple-element.457), channel_id=1, source_target_pairs={{0,8},{8,16},{16,24},{24,32},{32,40},{40,48},{48,56},{56,64},{64,7... | collective-permute-start | bytes 49160 | tf_op jit(solution)/shard_map/while/body/eval_jaxpr/ppermute | solution.py:38
  118.4 7.7 %collective-permute-start.1 = (f32[8,2,256]{2,1,0:T(2,128)S(1)}, f32[8,2,256]{2,1,0:T(2,128)S(1)}, u32[]{:S(2)}, u32[]{:S(2)}) collective-permute-start(f32[8,2,256]{2,1,0:T(2,128)S(1)} %get-tuple-element.457), channel_id=1, source_target_pairs={{0,8},{8,16},{16,24},{24,32},{32,40},{40,48},{48,56},{56,64},{64,7... | collective-permute-start | bytes 49160 | tf_op jit(solution)/shard_map/while/body/eval_jaxpr/ppermute | solution.py:38
  137.2 7.7 %collective-permute-start.1 = (f32[8,2,256]{2,1,0:T(2,128)S(1)}, f32[8,2,256]{2,1,0:T(2,128)S(1)}, u32[]{:S(2)}, u32[]{:S(2)}) collective-permute-start(f32[8,2,256]{2,1,0:T(2,128)S(1)} %get-tuple-element.457), channel_id=1, source_target_pairs={{0,8},{8,16},{16,24},{24,32},{32,40},{40,48},{48,56},{56,64},{64,7... | collective-permute-start | bytes 49160 | tf_op jit(solution)/shard_map/while/body/eval_jaxpr/ppermute | solution.py:38
  156.0 7.7 %collective-permute-start.1 = (f32[8,2,256]{2,1,0:T(2,128)S(1)}, f32[8,2,256]{2,1,0:T(2,128)S(1)}, u32[]{:S(2)}, u32[]{:S(2)}) collective-permute-start(f32[8,2,256]{2,1,0:T(2,128)S(1)} %get-tuple-element.457), channel_id=1, source_target_pairs={{0,8},{8,16},{16,24},{24,32},{32,40},{40,48},{48,56},{56,64},{64,7... | collective-permute-start | bytes 49160 | tf_op jit(solution)/shard_map/while/body/eval_jaxpr/ppermute | solution.py:38
  174.8 7.7 %collective-permute-start.1 = (f32[8,2,256]{2,1,0:T(2,128)S(1)}, f32[8,2,256]{2,1,0:T(2,128)S(1)}, u32[]{:S(2)}, u32[]{:S(2)}) collective-permute-start(f32[8,2,256]{2,1,0:T(2,128)S(1)} %get-tuple-element.457), channel_id=1, source_target_pairs={{0,8},{8,16},{16,24},{24,32},{32,40},{40,48},{48,56},{56,64},{64,7... | collective-permute-start | bytes 49160 | tf_op jit(solution)/shard_map/while/body/eval_jaxpr/ppermute | solution.py:38
  193.6 7.7 %collective-permute-start.1 = (f32[8,2,256]{2,1,0:T(2,128)S(1)}, f32[8,2,256]{2,1,0:T(2,128)S(1)}, u32[]{:S(2)}, u32[]{:S(2)}) collective-permute-start(f32[8,2,256]{2,1,0:T(2,128)S(1)} %get-tuple-element.457), channel_id=1, source_target_pairs={{0,8},{8,16},{16,24},{24,32},{32,40},{40,48},{48,56},{56,64},{64,7... | collective-permute-start | bytes 49160 | tf_op jit(solution)/shard_map/while/body/eval_jaxpr/ppermute | solution.py:38
  212.5 7.7 %collective-permute-start.1 = (f32[8,2,256]{2,1,0:T(2,128)S(1)}, f32[8,2,256]{2,1,0:T(2,128)S(1)}, u32[]{:S(2)}, u32[]{:S(2)}) collective-permute-start(f32[8,2,256]{2,1,0:T(2,128)S(1)} %get-tuple-element.457), channel_id=1, source_target_pairs={{0,8},{8,16},{16,24},{24,32},{32,40},{40,48},{48,56},{56,64},{64,7... | collective-permute-start | bytes 49160 | tf_op jit(solution)/shard_map/while/body/eval_jaxpr/ppermute | solution.py:38
  231.3 7.7 %collective-permute-start.1 = (f32[8,2,256]{2,1,0:T(2,128)S(1)}, f32[8,2,256]{2,1,0:T(2,128)S(1)}, u32[]{:S(2)}, u32[]{:S(2)}) collective-permute-start(f32[8,2,256]{2,1,0:T(2,128)S(1)} %get-tuple-element.457), channel_id=1, source_target_pairs={{0,8},{8,16},{16,24},{24,32},{32,40},{40,48},{48,56},{56,64},{64,7... | collective-permute-start | bytes 49160 | tf_op jit(solution)/shard_map/while/body/eval_jaxpr/ppermute | solution.py:38
  250.1 7.7 %collective-permute-start.1 = (f32[8,2,256]{2,1,0:T(2,128)S(1)}, f32[8,2,256]{2,1,0:T(2,128)S(1)}, u32[]{:S(2)}, u32[]{:S(2)}) collective-permute-start(f32[8,2,256]{2,1,0:T(2,128)S(1)} %get-tuple-element.457), channel_id=1, source_target_pairs={{0,8},{8,16},{16,24},{24,32},{32,40},{40,48},{48,56},{56,64},{64,7... | collective-permute-start | bytes 49160 | tf_op jit(solution)/shard_map/while/body/eval_jaxpr/ppermute | solution.py:38
  268.9 7.7 %collective-permute-start.1 = (f32[8,2,256]{2,1,0:T(2,128)S(1)}, f32[8,2,256]{2,1,0:T(2,128)S(1)}, u32[]{:S(2)}, u32[]{:S(2)}) collective-permute-start(f32[8,2,256]{2,1,0:T(2,128)S(1)} %get-tuple-element.457), channel_id=1, source_target_pairs={{0,8},{8,16},{16,24},{24,32},{32,40},{40,48},{48,56},{56,64},{64,7... | collective-permute-start | bytes 49160 | tf_op jit(solution)/shard_map/while/body/eval_jaxpr/ppermute | solution.py:38
  287.7 7.7 %collective-permute-start.1 = (f32[8,2,256]{2,1,0:T(2,128)S(1)}, f32[8,2,256]{2,1,0:T(2,128)S(1)}, u32[]{:S(2)}, u32[]{:S(2)}) collective-permute-start(f32[8,2,256]{2,1,0:T(2,128)S(1)} %get-tuple-element.457), channel_id=1, source_target_pairs={{0,8},{8,16},{16,24},{24,32},{32,40},{40,48},{48,56},{56,64},{64,7... | collective-permute-start | bytes 49160 | tf_op jit(solution)/shard_map/while/body/eval_jaxpr/ppermute | solution.py:38
  306.5 7.7 %collective-permute-start.1 = (f32[8,2,256]{2,1,0:T(2,128)S(1)}, f32[8,2,256]{2,1,0:T(2,128)S(1)}, u32[]{:S(2)}, u32[]{:S(2)}) collective-permute-start(f32[8,2,256]{2,1,0:T(2,128)S(1)} %get-tuple-element.457), channel_id=1, source_target_pairs={{0,8},{8,16},{16,24},{24,32},{32,40},{40,48},{48,56},{56,64},{64,7... | collective-permute-start | bytes 49160 | tf_op jit(solution)/shard_map/while/body/eval_jaxpr/ppermute | solution.py:38
  325.4 7.7 %collective-permute-start.1 = (f32[8,2,256]{2,1,0:T(2,128)S(1)}, f32[8,2,256]{2,1,0:T(2,128)S(1)}, u32[]{:S(2)}, u32[]{:S(2)}) collective-permute-start(f32[8,2,256]{2,1,0:T(2,128)S(1)} %get-tuple-element.457), channel_id=1, source_target_pairs={{0,8},{8,16},{16,24},{24,32},{32,40},{40,48},{48,56},{56,64},{64,7... | collective-permute-start | bytes 49160 | tf_op jit(solution)/shard_map/while/body/eval_jaxpr/ppermute | solution.py:38
  344.2 7.7 %collective-permute-start.1 = (f32[8,2,256]{2,1,0:T(2,128)S(1)}, f32[8,2,256]{2,1,0:T(2,128)S(1)}, u32[]{:S(2)}, u32[]{:S(2)}) collective-permute-start(f32[8,2,256]{2,1,0:T(2,128)S(1)} %get-tuple-element.457), channel_id=1, source_target_pairs={{0,8},{8,16},{16,24},{24,32},{32,40},{40,48},{48,56},{56,64},{64,7... | collective-permute-start | bytes 49160 | tf_op jit(solution)/shard_map/while/body/eval_jaxpr/ppermute | solution.py:38
  361.7 10.1 %collective-permute-start.17 = (bf16[8,16,256]{2,0,1:T(8,128)(2,1)S(1)}, bf16[8,16,256]{2,0,1:T(8,128)(2,1)S(1)}, u32[]{:S(2)}, u32[]{:S(2)}) collective-permute-start(bf16[8,16,256]{2,0,1:T(8,128)(2,1)S(1)} %fusion.40), channel_id=1, source_target_pairs={{0,256},{256,0},{1,257},{257,1},{2,258},{258,2},{3,259},{259,3},{4... | collective-permute-start | bytes 196616 | tf_op jit(solution)/shard_map/ppermute | solution.py:21
  371.8 14.7 %collective-permute-start.18 = (bf16[8,16,256]{2,0,1:T(8,128)(2,1)S(1)}, bf16[8,16,256]{2,0,1:T(8,128)(2,1)S(1)}, u32[]{:S(2)}, u32[]{:S(2)}) collective-permute-start(bf16[8,16,256]{2,0,1:T(8,128)(2,1)S(1)} %collective-permute-done.17), channel_id=1, source_target_pairs={{0,16},{8,24},{16,32},{24,40},{32,48},{40,56},{48,64},{56,72},{64,... | collective-permute-start | bytes 196616 | tf_op jit(solution)/shard_map/ppermute | solution.py:27
  373.7 17.2 %collective-permute-start.21 = (bf16[8,16,256]{2,0,1:T(8,128)(2,1)S(1)}, bf16[8,16,256]{2,0,1:T(8,128)(2,1)S(1)}, u32[]{:S(2)}, u32[]{:S(2)}) collective-permute-start(bf16[8,16,256]{2,0,1:T(8,128)(2,1)S(1)} %collective-permute-done.17), channel_id=1, source_target_pairs={{16,0},{24,8},{32,16},{40,24},{48,32},{56,40},{64,48},{72,56},{80,... | collective-permute-start | bytes 196616 | tf_op jit(solution)/shard_map/ppermute | solution.py:27
  380.7 10.2 %collective-permute-start.20 = (bf16[8,16,256]{2,0,1:T(8,128)(2,1)S(1)}, bf16[8,16,256]{2,0,1:T(8,128)(2,1)S(1)}, u32[]{:S(2)}, u32[]{:S(2)}) collective-permute-start(bf16[8,16,256]{2,0,1:T(8,128)(2,1)S(1)} %collective-permute-done.17), channel_id=1, source_target_pairs={{8,0},{16,8},{24,16},{32,24},{40,32},{48,40},{56,48},{64,56},{72,6... | collective-permute-start | bytes 196616 | tf_op jit(solution)/shard_map/ppermute | solution.py:27
  382.6 8.3 %collective-permute-start.19 = (bf16[8,16,256]{2,0,1:T(8,128)(2,1)S(1)}, bf16[8,16,256]{2,0,1:T(8,128)(2,1)S(1)}, u32[]{:S(2)}, u32[]{:S(2)}) collective-permute-start(bf16[8,16,256]{2,0,1:T(8,128)(2,1)S(1)} %collective-permute-done.17), channel_id=1, source_target_pairs={{0,8},{8,16},{16,24},{24,32},{32,40},{40,48},{48,56},{56,64},{64,7... | collective-permute-start | bytes 196616 | tf_op jit(solution)/shard_map/ppermute | solution.py:27
  393.7 8.1 %collective-permute-start.22 = (f32[8,2,256]{2,1,0:T(2,128)S(1)}, f32[8,2,256]{2,1,0:T(2,128)S(1)}, u32[]{:S(2)}, u32[]{:S(2)}) collective-permute-start(f32[8,2,256]{2,1,0:T(2,128)S(1)} %get-tuple-element.309), channel_id=1, source_target_pairs={{0,8},{8,16},{16,24},{24,32},{32,40},{40,48},{48,56},{56,64},{64,7... | collective-permute-start | bytes 49160 | tf_op jit(solution)/shard_map/ppermute | solution.py:38
  405.6 9.1 %collective-permute-start.25 = (f32[8,20,2]{2,1,0:T(8,128)S(1)}, f32[8,20,2]{2,1,0:T(8,128)S(1)}, u32[]{:S(2)}, u32[]{:S(2)}) collective-permute-start(f32[8,20,2]{2,1,0:T(8,128)S(1)} %get-tuple-element.306), channel_id=1, source_target_pairs={{1,0},{2,1},{3,2},{4,3},{5,4},{6,5},{7,6},{9,8},{10,9},{11,10},{12... | collective-permute-start | bytes 3848 | tf_op jit(solution)/shard_map/ppermute | solution.py:40
  415.0 8.3 %collective-permute-start.4 = (f32[8,2,256]{2,1,0:T(2,128)S(1)}, f32[8,2,256]{2,1,0:T(2,128)S(1)}, u32[]{:S(2)}, u32[]{:S(2)}) collective-permute-start(f32[8,2,256]{2,1,0:T(2,128)S(1)} %get-tuple-element.477), channel_id=1, source_target_pairs={{8,0},{16,8},{24,16},{32,24},{40,32},{48,40},{56,48},{64,56},{72,6... | collective-permute-start | bytes 49160 | tf_op jit(solution)/shard_map/while/body/eval_jaxpr/ppermute | solution.py:40
  421.3 7.7 %collective-permute-start.5 = (f32[8,2,256]{2,1,0:T(2,128)S(1)}, f32[8,2,256]{2,1,0:T(2,128)S(1)}, u32[]{:S(2)}, u32[]{:S(2)}) collective-permute-start(f32[8,2,256]{2,1,0:T(2,128)S(1)} %get-tuple-element.478), channel_id=1, source_target_pairs={{0,8},{8,16},{16,24},{24,32},{32,40},{40,48},{48,56},{56,64},{64,7... | collective-permute-start | bytes 49160 | tf_op jit(solution)/shard_map/while/body/eval_jaxpr/ppermute | solution.py:38
  438.8 7.7 %collective-permute-start.5 = (f32[8,2,256]{2,1,0:T(2,128)S(1)}, f32[8,2,256]{2,1,0:T(2,128)S(1)}, u32[]{:S(2)}, u32[]{:S(2)}) collective-permute-start(f32[8,2,256]{2,1,0:T(2,128)S(1)} %get-tuple-element.478), channel_id=1, source_target_pairs={{0,8},{8,16},{16,24},{24,32},{32,40},{40,48},{48,56},{56,64},{64,7... | collective-permute-start | bytes 49160 | tf_op jit(solution)/shard_map/while/body/eval_jaxpr/ppermute | solution.py:38
  455.8 7.7 %collective-permute-start.5 = (f32[8,2,256]{2,1,0:T(2,128)S(1)}, f32[8,2,256]{2,1,0:T(2,128)S(1)}, u32[]{:S(2)}, u32[]{:S(2)}) collective-permute-start(f32[8,2,256]{2,1,0:T(2,128)S(1)} %get-tuple-element.478), channel_id=1, source_target_pairs={{0,8},{8,16},{16,24},{24,32},{32,40},{40,48},{48,56},{56,64},{64,7... | collective-permute-start | bytes 49160 | tf_op jit(solution)/shard_map/while/body/eval_jaxpr/ppermute | solution.py:38
  474.7 7.7 %collective-permute-start.5 = (f32[8,2,256]{2,1,0:T(2,128)S(1)}, f32[8,2,256]{2,1,0:T(2,128)S(1)}, u32[]{:S(2)}, u32[]{:S(2)}) collective-permute-start(f32[8,2,256]{2,1,0:T(2,128)S(1)} %get-tuple-element.478), channel_id=1, source_target_pairs={{0,8},{8,16},{16,24},{24,32},{32,40},{40,48},{48,56},{56,64},{64,7... | collective-permute-start | bytes 49160 | tf_op jit(solution)/shard_map/while/body/eval_jaxpr/ppermute | solution.py:38
  493.5 7.7 %collective-permute-start.5 = (f32[8,2,256]{2,1,0:T(2,128)S(1)}, f32[8,2,256]{2,1,0:T(2,128)S(1)}, u32[]{:S(2)}, u32[]{:S(2)}) collective-permute-start(f32[8,2,256]{2,1,0:T(2,128)S(1)} %get-tuple-element.478), channel_id=1, source_target_pairs={{0,8},{8,16},{16,24},{24,32},{32,40},{40,48},{48,56},{56,64},{64,7... | collective-permute-start | bytes 49160 | tf_op jit(solution)/shard_map/while/body/eval_jaxpr/ppermute | solution.py:38
  512.3 7.7 %collective-permute-start.5 = (f32[8,2,256]{2,1,0:T(2,128)S(1)}, f32[8,2,256]{2,1,0:T(2,128)S(1)}, u32[]{:S(2)}, u32[]{:S(2)}) collective-permute-start(f32[8,2,256]{2,1,0:T(2,128)S(1)} %get-tuple-element.478), channel_id=1, source_target_pairs={{0,8},{8,16},{16,24},{24,32},{32,40},{40,48},{48,56},{56,64},{64,7... | collective-permute-start | bytes 49160 | tf_op jit(solution)/shard_map/while/body/eval_jaxpr/ppermute | solution.py:38
  531.1 7.7 %collective-permute-start.5 = (f32[8,2,256]{2,1,0:T(2,128)S(1)}, f32[8,2,256]{2,1,0:T(2,128)S(1)}, u32[]{:S(2)}, u32[]{:S(2)}) collective-permute-start(f32[8,2,256]{2,1,0:T(2,128)S(1)} %get-tuple-element.478), channel_id=1, source_target_pairs={{0,8},{8,16},{16,24},{24,32},{32,40},{40,48},{48,56},{56,64},{64,7... | collective-permute-start | bytes 49160 | tf_op jit(solution)/shard_map/while/body/eval_jaxpr/ppermute | solution.py:38
  549.9 7.7 %collective-permute-start.5 = (f32[8,2,256]{2,1,0:T(2,128)S(1)}, f32[8,2,256]{2,1,0:T(2,128)S(1)}, u32[]{:S(2)}, u32[]{:S(2)}) collective-permute-start(f32[8,2,256]{2,1,0:T(2,128)S(1)} %get-tuple-element.478), channel_id=1, source_target_pairs={{0,8},{8,16},{16,24},{24,32},{32,40},{40,48},{48,56},{56,64},{64,7... | collective-permute-start | bytes 49160 | tf_op jit(solution)/shard_map/while/body/eval_jaxpr/ppermute | solution.py:38
  568.7 7.7 %collective-permute-start.5 = (f32[8,2,256]{2,1,0:T(2,128)S(1)}, f32[8,2,256]{2,1,0:T(2,128)S(1)}, u32[]{:S(2)}, u32[]{:S(2)}) collective-permute-start(f32[8,2,256]{2,1,0:T(2,128)S(1)} %get-tuple-element.478), channel_id=1, source_target_pairs={{0,8},{8,16},{16,24},{24,32},{32,40},{40,48},{48,56},{56,64},{64,7... | collective-permute-start | bytes 49160 | tf_op jit(solution)/shard_map/while/body/eval_jaxpr/ppermute | solution.py:38
  587.6 7.7 %collective-permute-start.5 = (f32[8,2,256]{2,1,0:T(2,128)S(1)}, f32[8,2,256]{2,1,0:T(2,128)S(1)}, u32[]{:S(2)}, u32[]{:S(2)}) collective-permute-start(f32[8,2,256]{2,1,0:T(2,128)S(1)} %get-tuple-element.478), channel_id=1, source_target_pairs={{0,8},{8,16},{16,24},{24,32},{32,40},{40,48},{48,56},{56,64},{64,7... | collective-permute-start | bytes 49160 | tf_op jit(solution)/shard_map/while/body/eval_jaxpr/ppermute | solution.py:38
  606.4 7.7 %collective-permute-start.5 = (f32[8,2,256]{2,1,0:T(2,128)S(1)}, f32[8,2,256]{2,1,0:T(2,128)S(1)}, u32[]{:S(2)}, u32[]{:S(2)}) collective-permute-start(f32[8,2,256]{2,1,0:T(2,128)S(1)} %get-tuple-element.478), channel_id=1, source_target_pairs={{0,8},{8,16},{16,24},{24,32},{32,40},{40,48},{48,56},{56,64},{64,7... | collective-permute-start | bytes 49160 | tf_op jit(solution)/shard_map/while/body/eval_jaxpr/ppermute | solution.py:38
  625.2 7.7 %collective-permute-start.5 = (f32[8,2,256]{2,1,0:T(2,128)S(1)}, f32[8,2,256]{2,1,0:T(2,128)S(1)}, u32[]{:S(2)}, u32[]{:S(2)}) collective-permute-start(f32[8,2,256]{2,1,0:T(2,128)S(1)} %get-tuple-element.478), channel_id=1, source_target_pairs={{0,8},{8,16},{16,24},{24,32},{32,40},{40,48},{48,56},{56,64},{64,7... | collective-permute-start | bytes 49160 | tf_op jit(solution)/shard_map/while/body/eval_jaxpr/ppermute | solution.py:38
  644.0 7.7 %collective-permute-start.5 = (f32[8,2,256]{2,1,0:T(2,128)S(1)}, f32[8,2,256]{2,1,0:T(2,128)S(1)}, u32[]{:S(2)}, u32[]{:S(2)}) collective-permute-start(f32[8,2,256]{2,1,0:T(2,128)S(1)} %get-tuple-element.478), channel_id=1, source_target_pairs={{0,8},{8,16},{16,24},{24,32},{32,40},{40,48},{48,56},{56,64},{64,7... | collective-permute-start | bytes 49160 | tf_op jit(solution)/shard_map/while/body/eval_jaxpr/ppermute | solution.py:38
  662.8 7.7 %collective-permute-start.5 = (f32[8,2,256]{2,1,0:T(2,128)S(1)}, f32[8,2,256]{2,1,0:T(2,128)S(1)}, u32[]{:S(2)}, u32[]{:S(2)}) collective-permute-start(f32[8,2,256]{2,1,0:T(2,128)S(1)} %get-tuple-element.478), channel_id=1, source_target_pairs={{0,8},{8,16},{16,24},{24,32},{32,40},{40,48},{48,56},{56,64},{64,7... | collective-permute-start | bytes 49160 | tf_op jit(solution)/shard_map/while/body/eval_jaxpr/ppermute | solution.py:38
  681.6 7.7 %collective-permute-start.5 = (f32[8,2,256]{2,1,0:T(2,128)S(1)}, f32[8,2,256]{2,1,0:T(2,128)S(1)}, u32[]{:S(2)}, u32[]{:S(2)}) collective-permute-start(f32[8,2,256]{2,1,0:T(2,128)S(1)} %get-tuple-element.478), channel_id=1, source_target_pairs={{0,8},{8,16},{16,24},{24,32},{32,40},{40,48},{48,56},{56,64},{64,7... | collective-permute-start | bytes 49160 | tf_op jit(solution)/shard_map/while/body/eval_jaxpr/ppermute | solution.py:38
  700.5 7.7 %collective-permute-start.5 = (f32[8,2,256]{2,1,0:T(2,128)S(1)}, f32[8,2,256]{2,1,0:T(2,128)S(1)}, u32[]{:S(2)}, u32[]{:S(2)}) collective-permute-start(f32[8,2,256]{2,1,0:T(2,128)S(1)} %get-tuple-element.478), channel_id=1, source_target_pairs={{0,8},{8,16},{16,24},{24,32},{32,40},{40,48},{48,56},{56,64},{64,7... | collective-permute-start | bytes 49160 | tf_op jit(solution)/shard_map/while/body/eval_jaxpr/ppermute | solution.py:38
  (106 other events, 1576.4 us)
where the time goes:
time: 727 us; the launch traced here: 718 us
  starting transfers between devices  477 us (66%)
  waiting for transfers between devices  170 us (23%)
  other arithmetic  41.7 us (6%)
  local copies, waits for them, and re-layouts  16.6 us (2%)
    ppermute x68, starting transfers between devices, with_halo(): lax.ppermute(tail, axis, [(i, (i + 1) % count) for i in range(ends)])  303 us
    ppermute x68, waiting for transfers between devices, with_halo(): lax.ppermute(tail, axis, [(i, (i + 1) % count) for i in range(ends)])  147 us
    ppermute x68, starting transfers between devices, with_halo(): lax.ppermute(head, axis, [((i + 1) % count, i) for i in range(ends)])  127 us
    ppermute x8, starting transfers between devices, passed_along(): return lax.ppermute(shard, axis, pairs)  29.4 us
    ppermute x2, starting transfers between devices, swapped(): return lax.ppermute(block, axis, route)  18.6 us
  transfers between devices with their start and end apart: 146, of which 71 were waited for; matrix products, arithmetic and copies ran while one was open for 2% of the time, Pallas kernels for 0%

commit v1 on v0

v1 whole, which is shorter than its diff:
```python
import jax
import jax.numpy as jnp
from jax import lax
from jax.experimental import pallas as pl
from jax.experimental.pallas import tpu as pltpu
from jax.sharding import PartitionSpec as P

SUBSTEPS = 16
ITERS = 2
DIFFUSION = 0.1
COUPLING = 0.2

FIELDS = 8
ROWS = 16
COLS = 256
LANES = 128
HALO = 2 * SUBSTEPS
WIDE = 3 * LANES
STEPS_PER_PHASE = 4

TRACER_MAIN = 0
STRIPS = 20
STRIP_PLANES = 5
WAVE_MAIN = 30
PLANES = 42
FAR_FROM = 23

SMEM = pl.BlockSpec(memory_space=pltpu.SMEM)
VMEM = pl.BlockSpec(memory_space=pltpu.VMEM)
PARAMS = pltpu.CompilerParams(vmem_limit_bytes=32 * 1024 * 1024)

f32 = jnp.float32


def write_export(fields, received, wet, smix_ref, imix_ref, turned, out_ref):
    speed = jnp.sqrt(1.0 + fields[1] * fields[1] + fields[2] * fields[2])
    scale = wet * speed
    for c in range(FIELDS):
        total = smix_ref[c, 0] * fields[0]
        for k in range(1, FIELDS):
            total = total + smix_ref[c, k] * fields[k]
        other = imix_ref[c, 0] * received[0]
        for k in range(1, FIELDS):
            other = other + imix_ref[c, k] * received[k]
        value = scale * (total + other)
        for half in range(2):
            turned[half, pl.ds(c, ROWS, stride=FIELDS), :] = value[:, half * LANES : (half + 1) * LANES]
    for half in range(2):
        out_ref[:, half * LANES : (half + 1) * LANES] = turned[half].astype(jnp.bfloat16)


def export_kernel(smix_ref, imix_ref, fields_ref, received_ref, land_ref, out_ref, turned):
    fields = [fields_ref[c] for c in range(FIELDS)]
    received = [received_ref[c] for c in range(FIELDS)]
    write_export(fields, received, land_ref[...].astype(f32), smix_ref, imix_ref, turned, out_ref)


def export(fields, received, land, smix, imix):
    return pl.pallas_call(
        export_kernel,
        out_shape=jax.ShapeDtypeStruct((ROWS * FIELDS, COLS), jnp.bfloat16),
        in_specs=[SMEM, SMEM, VMEM, VMEM, VMEM],
        out_specs=VMEM,
        scratch_shapes=[pltpu.VMEM((2, ROWS * FIELDS, LANES), f32)],
        compiler_params=PARAMS,
        name="export",
    )(smix, imix, fields, received, land)


def packed(planes, lane, first):
    out = jnp.zeros((ROWS, LANES), f32)
    for j, plane in enumerate(planes):
        shift = (32 * j) if first else (32 * j + 32) % LANES
        moved = pltpu.roll(plane, shift, 1) if shift else plane
        out = jnp.where((lane >= 32 * j) & (lane < 32 * j + 32), moved, out)
    return out


def remap_kernel(
    index_ref, near_ref, far_ref, left_ref, right_ref, weight_ref, fields_ref, land_ref,
    payload_ref, low_ref, high_ref, import_ref, table, turned,
):
    windows = [
        (near_ref, 0), (left_ref, 0), (near_ref, ROWS * FIELDS), (right_ref, 0), (far_ref, 0),
    ]
    half_count = 5 * ROWS * 2
    for w, (ref, start) in enumerate(windows):
        for pair in range(ROWS // 2):
            chunk = ref[start + pair * 16 : start + pair * 16 + 16, :].astype(f32)
            for sub in range(2):
                for half in range(2):
                    part = chunk[sub * 8 : sub * 8 + 8, half * LANES : (half + 1) * LANES]
                    at = (w * ROWS + pair * 2 + sub) * 2 + half
                    table[at] = part
                    table[half_count + at] = pltpu.roll(part, 64, 1)
    lane8 = lax.broadcasted_iota(jnp.int32, (8, LANES), 1)
    low_half = lane8 < 64
    ones = jnp.ones((8, LANES), f32)
    for x in range(ROWS):
        pieces = []
        for seg in range(4):
            at = (x * 4 + seg) * 2
            pieces.append(jnp.where(low_half, table[index_ref[at]], table[index_ref[at + 1]]))
        picked = jnp.concatenate(pieces + [ones], axis=0).astype(jnp.bfloat16)
        product = lax.dot_general(
            picked, weight_ref[x], (((1,), (1,)), ((), ())), preferred_element_type=f32
        )
        for half in range(2):
            cols = product[:, half * LANES : (half + 1) * LANES]
            summed = jnp.where(low_half, cols[16 * half : 16 * half + 8], cols[16 * half + 8 : 16 * half + 16])
            turned[half, x * 8 : x * 8 + 8, :] = summed / cols[32:40]
    lane = lax.broadcasted_iota(jnp.int32, (ROWS, LANES), 1)
    wet = land_ref[...].astype(f32)
    state = []
    forcing = []
    for c in range(FIELDS):
        state.append([fields_ref[c, :, h * LANES : (h + 1) * LANES] for h in range(2)])
        parts = []
        for half in range(2):
            value = turned[half, pl.ds(c, ROWS, stride=FIELDS), :]
            import_ref[c, :, half * LANES : (half + 1) * LANES] = value
            parts.append(COUPLING * wet[:, half * LANES : (half + 1) * LANES] * value)
        forcing.append(parts)
    waves = state[:3] + forcing[:3]
    tracers = state[3:] + forcing[3:]
    for i, pair in enumerate(tracers):
        for half in range(2):
            payload_ref[TRACER_MAIN + 2 * i + half] = pair[half]
    for i, pair in enumerate(waves):
        for half in range(2):
            payload_ref[WAVE_MAIN + 2 * i + half] = pair[half]
    for p in range(2 * STRIP_PLANES):
        payload_ref[STRIPS + p] = jnp.zeros((ROWS, LANES), f32)
    groups = [tracers[0:4], tracers[4:8], tracers[8:10], waves[0:4], waves[4:6]]
    for p, group in enumerate(groups):
        low_ref[p] = packed([pair[0] for pair in group], lane, True)
        high_ref[p] = packed([pair[1] for pair in group], lane, False)


def remap(index, near, far, left, right, weight, fields, land):
    return pl.pallas_call(
        remap_kernel,
        out_shape=(
            jax.ShapeDtypeStruct((PLANES, ROWS, LANES), f32),
            jax.ShapeDtypeStruct((STRIP_PLANES, ROWS, LANES), f32),
            jax.ShapeDtypeStruct((STRIP_PLANES, ROWS, LANES), f32),
            jax.ShapeDtypeStruct((FIELDS, ROWS, COLS), f32),
        ),
        in_specs=[SMEM] + [VMEM] * 7,
        out_specs=(VMEM,) * 4,
        scratch_shapes=[
            pltpu.VMEM((2 * 5 * ROWS * 2, FIELDS, LANES), f32),
            pltpu.VMEM((2, ROWS * FIELDS, LANES), f32),
        ],
        compiler_params=PARAMS,
        name="remap",
    )(index, near, far, left, right, weight, fields, land)


def up(value):
    return pltpu.roll(value, value.shape[0] - 1, 0)


def down(value):
    return pltpu.roll(value, 1, 0)


def east(value):
    return pltpu.roll(value, WIDE - 1, 1)


def west(value):
    return pltpu.roll(value, 1, 1)


def substep_kernel(last, place_ref, damping_ref, wave_ref, smix_ref, imix_ref, *refs):
    tiles = refs[:5]
    if last:
        state_ref, *scratch = refs[5:]
    else:
        received_ref, land_ref, state_ref, export_ref, *scratch = refs[5:]
    waves, wave_forcing, tracers, tracer_forcing, coef, turned = scratch
    lane = lax.broadcasted_iota(jnp.int32, (ROWS, LANES), 1)

    def strip(ref, base, group, j):
        left = ref[STRIPS - base + group]
        right = ref[STRIPS - base + STRIP_PLANES + group]
        if j:
            right = pltpu.roll(right, LANES - 32 * j, 1)
        if j != 3:
            left = pltpu.roll(left, 96 - 32 * j, 1)
        return jnp.where(lane < 32, right, jnp.where(lane >= 96, left, 0.0))

    for t, ref in enumerate(tiles):
        base = FAR_FROM if t in (0, 4) else 0
        for i in range(6):
            dest = waves if i < 3 else wave_forcing
            rows = slice(t * ROWS, (t + 1) * ROWS)
            for half in range(2):
                dest[i % 3, rows, half * LANES : (half + 1) * LANES] = ref[WAVE_MAIN - base + 2 * i + half]
            dest[i % 3, rows, 2 * LANES :] = strip(ref, base, 3 + i // 4, i % 4)
        if t in (0, 4):
            continue
        for i in range(10):
            dest = tracers if i < 5 else tracer_forcing
            rows = slice((t - 1) * ROWS, t * ROWS)
            for half in range(2):
                dest[i % 5, rows, half * LANES : (half + 1) * LANES] = ref[TRACER_MAIN + 2 * i + half]
            dest[i % 5, rows, 2 * LANES :] = strip(ref, base, i // 4, i % 4)

    height = 5 * ROWS
    row = lax.broadcasted_iota(jnp.int32, (height, WIDE), 0) + (place_ref[0] * ROWS - HALO)
    col = lax.broadcasted_iota(jnp.int32, (height, WIDE), 1)
    col = jnp.where(col >= WIDE - HALO, col - WIDE, col) + place_ref[1] * COLS
    ok = (row >= 0) & (row < place_ref[2]) & (col >= 0) & (col < place_ref[3])
    inside = jnp.where(ok, 1.0, 0.0)
    coef[0] = inside * (0.5 * wave_ref[0])
    coef[1] = inside * (0.5 * wave_ref[1])
    coef[2] = inside * DIFFUSION

    keep = [1.0 - damping_ref[c] for c in range(FIELDS)]
    for phase in range(SUBSTEPS // STEPS_PER_PHASE):
        reach = (SUBSTEPS - phase * STEPS_PER_PHASE) * 2
        rows = slice(HALO - reach, HALO + ROWS + reach)
        spread = 16 if phase < 2 else 8
        trows = slice(ROWS - spread, 2 * ROWS + spread)
        crows = slice(HALO - spread, HALO + ROWS + spread)

        def one_step(_, carry, rows=rows, trows=trows, crows=crows):
            h = waves[0, rows]
            u = waves[1, rows]
            v = waves[2, rows]
            spread_u = up(u) - down(u)
            spread_v = east(v) - west(v)
            h = keep[0] * h - coef[0, rows] * (spread_u + spread_v) + wave_forcing[0, rows]
            waves[0, rows] = h
            waves[1, rows] = keep[1] * u - coef[1, rows] * (up(h) - down(h)) + wave_forcing[1, rows]
            waves[2, rows] = keep[2] * v - coef[1, rows] * (east(h) - west(h)) + wave_forcing[2, rows]
            for c in range(5):
                a = tracers[c, trows]
                around = (up(a) + down(a)) + (east(a) + west(a))
                tracers[c, trows] = (
                    (keep[3 + c] - 4.0 * DIFFUSION) * a + coef[2, crows] * around + tracer_forcing[c, trows]
                )
            return carry

        lax.fori_loop(0, STEPS_PER_PHASE, one_step, 0)

    final = [waves[c, HALO : HALO + ROWS, :COLS] for c in range(3)]
    final += [tracers[c, ROWS : 2 * ROWS, :COLS] for c in range(5)]
    for c in range(FIELDS):
        state_ref[c] = final[c]
    if not last:
        received = [received_ref[c] for c in range(FIELDS)]
        write_export(final, received, land_ref[...].astype(f32), smix_ref, imix_ref, turned, export_ref)


def substeps(last, place, damping, wave, smix, imix, tiles, received, land):
    state = jax.ShapeDtypeStruct((FIELDS, ROWS, COLS), f32)
    exported = jax.ShapeDtypeStruct((ROWS * FIELDS, COLS), jnp.bfloat16)
    extra = () if last else (received, land)
    return pl.pallas_call(
        lambda *refs: substep_kernel(last, *refs),
        out_shape=state if last else (state, exported),
        in_specs=[SMEM] * 5 + [VMEM] * (5 + len(extra)),
        out_specs=VMEM if last else (VMEM, VMEM),
        scratch_shapes=[
            pltpu.VMEM((3, 5 * ROWS, WIDE), f32),
            pltpu.VMEM((3, 5 * ROWS, WIDE), f32),
            pltpu.VMEM((5, 3 * ROWS, WIDE), f32),
            pltpu.VMEM((5, 3 * ROWS, WIDE), f32),
            pltpu.VMEM((3, 5 * ROWS, WIDE), f32),
            pltpu.VMEM((2, ROWS * FIELDS, LANES), f32),
        ],
        compiler_params=PARAMS,
        name="substeps_last" if last else "substeps",
    )(place, damping, wave, smix, imix, *tiles, *extra)


def ring(block, axis, by):
    count = lax.axis_size(axis)
    return lax.ppermute(block, axis, [(i, (i + by) % count) for i in range(count)])


def line(block, axis, by):
    count = lax.axis_size(axis)
    return lax.ppermute(block, axis, [(i, i + by) for i in range(count) if 0 <= i + by < count])


def crossed(block, by):
    count = lax.axis_size("gx")
    route = [
        (s * count + g, (1 - s) * count + (g + by) % count) for s in range(2) for g in range(count)
    ]
    return lax.ppermute(block, ("sec", "gx"), route)


def local(
    section_state, prev_import, land_mask, state_mix, import_mix, damping, wave_speed,
    remap_owner, remap_slot, remap_weight,
):
    fields = section_state[0]
    land = land_mask[0]
    smix = state_mix[0]
    imix = import_mix[0]
    damping = damping[0]
    wave = wave_speed[0]
    gx = lax.axis_index("gx")
    gy = lax.axis_index("gy")
    place = jnp.stack(
        [gx, gy, lax.axis_size("gx") * ROWS, lax.axis_size("gy") * COLS]
    ).astype(jnp.int32)
    owner = remap_owner[0].reshape(-1)
    slot = remap_slot[0].reshape(-1)
    entry = ((owner - gx + 2) * ROWS + slot // 4) * 2 + (slot % 4) // 2
    second = lax.iota(jnp.int32, owner.shape[0]) % 2
    index = entry + ((slot % 2) ^ second) * (5 * ROWS * 2)
    weight = remap_weight[0].reshape(ROWS, COLS, 128)

    exported = export(fields, prev_import[0], land, smix, imix)
    for interval in range(ITERS):
        last = interval == ITERS - 1
        left = crossed(exported, 1)
        right = crossed(exported, -1)
        near = ring(jnp.concatenate([left, right], axis=0), "gx", 1)
        far = ring(right, "gx", -1)
        payload, low, high, received = remap(index, near, far, left, right, weight, fields, land)
        from_right = line(low, "gy", -1)
        from_left = line(high, "gy", 1)
        payload = lax.dynamic_update_slice(
            payload, jnp.concatenate([from_left, from_right], axis=0), (STRIPS, 0, 0)
        )
        outer = payload[FAR_FROM:]
        tiles = (
            line(outer, "gx", 2),
            line(payload, "gx", 1),
            payload,
            line(payload, "gx", -1),
            line(outer, "gx", -2),
        )
        result = substeps(last, place, damping, wave, smix, imix, tiles, received, land)
        if last:
            fields = result
        else:
            fields, exported = result
    return (fields[None], received[None])


def solution(mesh):
    in_specs = (
        P("sec", None, "gx", "gy"),
        P("sec", None, "gx", "gy"),
        P("sec", "gx", "gy"),
        P("sec", None, None),
        P("sec", None, None),
        P("sec", None),
        P("sec", None),
        P("sec", "gx", "gy", None),
        P("sec", "gx", "gy", None),
        P("sec", "gx", "gy", None, None),
    )
    out_specs = (P("sec", None, "gx", "gy"), P("sec", None, "gx", "gy"))
    return jax.shard_map(local, mesh=mesh, in_specs=in_specs, out_specs=out_specs, check_vma=False)
```

time: 727 us -> 157 us (0.22)
  the two profiles are of different devices: /device:TPU:6 before, /device:TPU:79 now
where the time goes in v1:
time: 157 us; the launch traced here: 156 us
  starting transfers between devices  90 us (57%)
  waiting for transfers between devices  40.1 us (26%)
  Pallas kernels  19.3 us (12%)
  local copies, waits for them, and re-layouts  5.53 us (4%)
    ppermute x12, starting transfers between devices, line(): lax.ppermute(block, axis, [(i, i + by) for i in range(count) if 0 <= i +...  53.2 us
    ppermute x12, waiting for transfers between devices, line(): lax.ppermute(block, axis, [(i, i + by) for i in range(count) if 0 <= i +...  28.7 us
    ppermute x4, starting transfers between devices, crossed(): return lax.ppermute(block, ('sec', 'gx'), route)  22.8 us
    pallas_call x2, Pallas kernels, substeps(): pl.pallas_call(lambda *refs: substep_kernel(last, *refs), out_shape=state...  15.3 us
    ppermute x4, starting transfers between devices, ring(): lax.ppermute(block, axis, [(i, (i + by) % count) for i in range(count)])  14.1 us
    ppermute x4, waiting for transfers between devices, crossed(): return lax.ppermute(block, ('sec', 'gx'), route)  8.17 us
    unnamed x27, local copies, waits for them, and re-layouts  5.11 us
    ppermute x4, waiting for transfers between devices, ring(): lax.ppermute(block, axis, [(i, (i + by) % count) for i in range(count)])  3.23 us
  transfers between devices with their start and end apart: 20, of which 11 were waited for; matrix products, arithmetic and copies ran while one was open for 0% of the time, Pallas kernels for 0%

profile of v1, /device:TPU:79, one launch (start us, length us, event | category | flops | bytes accessed | tf_op | source)
XLA Modules:
  0.0 156.1 jit_solution(18305770329957220738)
XLA Ops:
  0.7 0.7 copy-done.8
  1.3 0.0 copy-done.7
  1.3 0.9 copy-done.2
  2.2 0.7 copy-done.4
  3.0 0.9 copy-done.6
  3.9 0.8 export.1
  4.7 9.6 %collective-permute-start.1 = (bf16[128,256]{1,0:T(8,128)(2,1)S(1)}, bf16[128,256]{1,0:T(8,128)(2,1)S(1)}, u32[]{:S(2)}, u32[]{:S(2)}) collective-permute-start(bf16[128,256]{1,0:T(8,128)(2,1)S(1)} %export.1), channel_id=1, source_target_pairs={{0,504},{8,256},{16,264},{24,272},{32,280},{40,288},{48,296},{56,3... | collective-permute-start | bytes 196616 | tf_op jit(solution)/shard_map/ppermute | solution.py:295
  14.3 3.0 %collective-permute-start = (bf16[128,256]{1,0:T(8,128)(2,1)S(1)}, bf16[128,256]{1,0:T(8,128)(2,1)S(1)}, u32[]{:S(2)}, u32[]{:S(2)}) collective-permute-start(bf16[128,256]{1,0:T(8,128)(2,1)S(1)} %export.1), channel_id=1, source_target_pairs={{0,264},{8,272},{16,280},{24,288},{32,296},{40,304},{48,312},{56,3... | collective-permute-start | bytes 196616 | tf_op jit(solution)/shard_map/ppermute | solution.py:295
  17.4 0.1 copy.14
  17.5 0.1 mul.20
  17.7 0.5 copy-done.11
  18.2 0.1 copy.15
  18.3 0.1 reshape_squeeze.7
  18.5 6.2 %collective-permute-done.left_ref = bf16[128,256]{1,0:T(8,128)(2,1)S(1)} collective-permute-done((bf16[128,256]{1,0:T(8,128)(2,1)S(1)}, bf16[128,256]{1,0:T(8,128)(2,1)S(1)}, u32[]{:S(2)}, u32[]{:S(2)}) %collective-permute-start) | collective-permute-done | bytes 65568 | tf_op jit(solution)/shard_map/ppermute | solution.py:295
  24.7 2.7 %collective-permute-start.2 = (bf16[256,256]{1,0:T(8,128)(2,1)S(1)}, bf16[256,256]{1,0:T(8,128)(2,1)S(1)}, u32[]{:S(2)}, u32[]{:S(2)}) collective-permute-start(bf16[256,256]{1,0:T(8,128)(2,1)S(1)} %pad_maximum_fusion), channel_id=1, source_target_pairs={{0,8},{8,16},{16,24},{24,32},{32,40},{40,48},{48,56},{56,64},{64,7... | collective-permute-start | bytes 393224 | tf_op jit(solution)/shard_map/ppermute | solution.py:282
  27.4 6.2 %collective-permute-start.3 = (bf16[128,256]{1,0:T(8,128)(2,1)S(1)}, bf16[128,256]{1,0:T(8,128)(2,1)S(1)}, u32[]{:S(2)}, u32[]{:S(2)}) collective-permute-start(bf16[128,256]{1,0:T(8,128)(2,1)S(1)} %collective-permute-done.1.right_ref), channel_id=1, source_target_pairs={{0,248},{8,0},{16,8},{24,16},{32,24},{40,32},{48,40},{56,48},{64,5... | collective-permute-start | bytes 196616 | tf_op jit(solution)/shard_map/ppermute | solution.py:282
  33.6 1.3 collective-permute-done.3.far_ref
  34.9 1.2 copy-done
  36.1 1.3 remap.2
  37.4 6.6 %collective-permute-start.4 = (f32[5,16,128]{2,1,0:T(8,128)S(1)}, f32[5,16,128]{2,1,0:T(8,128)S(1)}, u32[]{:S(2)}, u32[]{:S(2)}) collective-permute-start(f32[5,16,128]{2,1,0:T(8,128)S(1)} %get-tuple-element.13), channel_id=1, source_target_pairs={{0,1},{1,2},{2,3},{3,4},{4,5},{5,6},{6,7},{8,9},{9,10},{10,11},{11... | collective-permute-start | bytes 122888 | tf_op jit(solution)/shard_map/ppermute | solution.py:287
  44.0 1.9 %collective-permute-start.5 = (f32[5,16,128]{2,1,0:T(8,128)S(1)}, f32[5,16,128]{2,1,0:T(8,128)S(1)}, u32[]{:S(2)}, u32[]{:S(2)}) collective-permute-start(f32[5,16,128]{2,1,0:T(8,128)S(1)} %get-tuple-element.14), channel_id=1, source_target_pairs={{1,0},{2,1},{3,2},{4,3},{5,4},{6,5},{7,6},{9,8},{10,9},{11,10},{12... | collective-permute-start | bytes 122888 | tf_op jit(solution)/shard_map/ppermute | solution.py:287
  46.0 3.4 %collective-permute-done.5 = f32[5,16,128]{2,1,0:T(8,128)S(1)} collective-permute-done((f32[5,16,128]{2,1,0:T(8,128)S(1)}, f32[5,16,128]{2,1,0:T(8,128)S(1)}, u32[]{:S(2)}, u32[]{:S(2)}) %collective-permute-start.5) | collective-permute-done | bytes 40992 | tf_op jit(solution)/shard_map/ppermute | solution.py:287
  49.4 5.9 %collective-permute-start.8 = (f32[42,16,128]{2,1,0:T(8,128)S(1)}, f32[42,16,128]{2,1,0:T(8,128)S(1)}, u32[]{:S(2)}, u32[]{:S(2)}) collective-permute-start(f32[42,16,128]{2,1,0:T(8,128)S(1)} %maximum_dynamic-update-slice_fusion.refs_7_), channel_id=1, source_target_pairs={{8,0},{16,8},{24,16},{32,24},{40,32},{48,40},{56,48},{64,56},{72,6... | collective-permute-start | bytes 1032200 | tf_op jit(solution)/shard_map/ppermute | solution.py:287
  55.3 1.9 %collective-permute-start.7 = (f32[42,16,128]{2,1,0:T(8,128)S(1)}, f32[42,16,128]{2,1,0:T(8,128)S(1)}, u32[]{:S(2)}, u32[]{:S(2)}) collective-permute-start(f32[42,16,128]{2,1,0:T(8,128)S(1)} %maximum_dynamic-update-slice_fusion.refs_7_), channel_id=1, source_target_pairs={{0,8},{8,16},{16,24},{24,32},{32,40},{40,48},{48,56},{56,64},{64,7... | collective-permute-start | bytes 1032200 | tf_op jit(solution)/shard_map/ppermute | solution.py:287
  57.2 9.4 %collective-permute-start.9 = (f32[19,16,128]{2,1,0:T(8,128)S(1)}, f32[19,16,128]{2,1,0:T(8,128)S(1)}, u32[]{:S(2)}, u32[]{:S(2)}) collective-permute-start(f32[19,16,128]{2,1,0:T(8,128)S(1)} %slice.8), channel_id=1, source_target_pairs={{16,0},{24,8},{32,16},{40,24},{48,32},{56,40},{64,48},{72,56},{80,... | collective-permute-start | bytes 466952 | tf_op jit(solution)/shard_map/ppermute | solution.py:287
  66.6 1.9 %collective-permute-start.6 = (f32[19,16,128]{2,1,0:T(8,128)S(1)}, f32[19,16,128]{2,1,0:T(8,128)S(1)}, u32[]{:S(2)}, u32[]{:S(2)}) collective-permute-start(f32[19,16,128]{2,1,0:T(8,128)S(1)} %slice.8), channel_id=1, source_target_pairs={{0,16},{8,24},{16,32},{24,40},{32,48},{40,56},{48,64},{56,72},{64,... | collective-permute-start | bytes 466952 | tf_op jit(solution)/shard_map/ppermute | solution.py:287
  68.5 0.1 pad_add_fusion.refs_0_
  68.6 3.4 %collective-permute-done.9.refs_9_ = f32[19,16,128]{2,1,0:T(8,128)S(1)} collective-permute-done((f32[19,16,128]{2,1,0:T(8,128)S(1)}, f32[19,16,128]{2,1,0:T(8,128)S(1)}, u32[]{:S(2)}, u32[]{:S(2)}) %collective-permute-start.9) | collective-permute-done | bytes 155680 | tf_op jit(solution)/shard_map/ppermute | solution.py:287
  72.0 7.8 %collective-permute-done.6.refs_5_ = f32[19,16,128]{2,1,0:T(8,128)S(1)} collective-permute-done((f32[19,16,128]{2,1,0:T(8,128)S(1)}, f32[19,16,128]{2,1,0:T(8,128)S(1)}, u32[]{:S(2)}, u32[]{:S(2)}) %collective-permute-start.6) | collective-permute-done | bytes 155680 | tf_op jit(solution)/shard_map/ppermute | solution.py:287
  79.8 7.4 %substeps.1 = (f32[8,16,256]{2,1,0:T(8,128)S(1)}, bf16[128,256]{1,0:T(8,128)(2,1)S(1)}) custom-call(s32[4]{0:T(128)S(1)} %pad_add_fusion.refs_0_, f32[8]{0:T(128)S(1)} %bitcast.27, f32[2]{0:T(128)S(1)} %bitcast.29, f32[8,8]{1,0:T(8,128)S(1)} %bitcast.22, f32[8,8]{1,0:T(8,128)S(1)} %bitcast.25, f32[19,16,128]{2,1,0:T(8,128)S(1)} %collective-permute-done.6.refs_5_, ...), custom_call_target="tpu_custom_call" | custom-call | tf_op jit(solution)/shard_map/substeps/pallas_call | solution.py:262
  87.2 1.9 %collective-permute-start.11 = (bf16[128,256]{1,0:T(8,128)(2,1)S(1)}, bf16[128,256]{1,0:T(8,128)(2,1)S(1)}, u32[]{:S(2)}, u32[]{:S(2)}) collective-permute-start(bf16[128,256]{1,0:T(8,128)(2,1)S(1)} %get-tuple-element.16), channel_id=1, source_target_pairs={{0,504},{8,256},{16,264},{24,272},{32,280},{40,288},{48,296},{56,3... | collective-permute-start | bytes 196616 | tf_op jit(solution)/shard_map/ppermute | solution.py:295
  89.2 8.2 %collective-permute-start.10 = (bf16[128,256]{1,0:T(8,128)(2,1)S(1)}, bf16[128,256]{1,0:T(8,128)(2,1)S(1)}, u32[]{:S(2)}, u32[]{:S(2)}) collective-permute-start(bf16[128,256]{1,0:T(8,128)(2,1)S(1)} %get-tuple-element.16), channel_id=1, source_target_pairs={{0,264},{8,272},{16,280},{24,288},{32,296},{40,304},{48,312},{56,3... | collective-permute-start | bytes 196616 | tf_op jit(solution)/shard_map/ppermute | solution.py:295
  97.3 0.3 collective-permute-done.11.right_ref
  97.6 1.7 %collective-permute-done.10.left_ref = bf16[128,256]{1,0:T(8,128)(2,1)S(1)} collective-permute-done((bf16[128,256]{1,0:T(8,128)(2,1)S(1)}, bf16[128,256]{1,0:T(8,128)(2,1)S(1)}, u32[]{:S(2)}, u32[]{:S(2)}) %collective-permute-start.10) | collective-permute-done | bytes 65568 | tf_op jit(solution)/shard_map/ppermute | solution.py:295
  99.3 1.9 %collective-permute-start.12 = (bf16[256,256]{1,0:T(8,128)(2,1)S(1)}, bf16[256,256]{1,0:T(8,128)(2,1)S(1)}, u32[]{:S(2)}, u32[]{:S(2)}) collective-permute-start(bf16[256,256]{1,0:T(8,128)(2,1)S(1)} %pad_maximum_fusion.1), channel_id=1, source_target_pairs={{0,8},{8,16},{16,24},{24,32},{32,40},{40,48},{48,56},{56,64},{64,7... | collective-permute-start | bytes 393224 | tf_op jit(solution)/shard_map/ppermute | solution.py:282
  101.2 3.4 %collective-permute-start.13 = (bf16[128,256]{1,0:T(8,128)(2,1)S(1)}, bf16[128,256]{1,0:T(8,128)(2,1)S(1)}, u32[]{:S(2)}, u32[]{:S(2)}) collective-permute-start(bf16[128,256]{1,0:T(8,128)(2,1)S(1)} %collective-permute-done.11.right_ref), channel_id=1, source_target_pairs={{0,248},{8,0},{16,8},{24,16},{32,24},{40,32},{48,40},{56,48},{64,5... | collective-permute-start | bytes 196616 | tf_op jit(solution)/shard_map/ppermute | solution.py:282
  104.6 1.9 %collective-permute-done.13.far_ref = bf16[128,256]{1,0:T(8,128)(2,1)S(1)} collective-permute-done((bf16[128,256]{1,0:T(8,128)(2,1)S(1)}, bf16[128,256]{1,0:T(8,128)(2,1)S(1)}, u32[]{:S(2)}, u32[]{:S(2)}) %collective-permute-start.13) | collective-permute-done | bytes 65568 | tf_op jit(solution)/shard_map/ppermute | solution.py:282
  106.6 1.8 %remap.3 = (f32[42,16,128]{2,1,0:T(8,128)S(1)}, f32[5,16,128]{2,1,0:T(8,128)S(1)}, f32[5,16,128]{2,1,0:T(8,128)S(1)}, f32[8,16,256]{2,1,0:T(8,128)}) custom-call(s32[128]{0:T(128)S(1)} %multiply_add_fusion.index_ref, bf16[256,256]{1,0:T(8,128)(2,1)S(1)} %collective-permute-done.12.near_ref, bf16[128,256]{1,0:T(8,128)(2,1)S(1)} %collective-permute-done.13.far_ref, ...), custom_call_target="tpu_custom_call" | custom-call | tf_op jit(solution)/shard_map/remap/pallas_call | solution.py:141
  108.4 5.9 %collective-permute-start.14 = (f32[5,16,128]{2,1,0:T(8,128)S(1)}, f32[5,16,128]{2,1,0:T(8,128)S(1)}, u32[]{:S(2)}, u32[]{:S(2)}) collective-permute-start(f32[5,16,128]{2,1,0:T(8,128)S(1)} %get-tuple-element.19), channel_id=1, source_target_pairs={{0,1},{1,2},{2,3},{3,4},{4,5},{5,6},{6,7},{8,9},{9,10},{10,11},{11... | collective-permute-start | bytes 122888 | tf_op jit(solution)/shard_map/ppermute | solution.py:287
  114.3 1.9 %collective-permute-start.15 = (f32[5,16,128]{2,1,0:T(8,128)S(1)}, f32[5,16,128]{2,1,0:T(8,128)S(1)}, u32[]{:S(2)}, u32[]{:S(2)}) collective-permute-start(f32[5,16,128]{2,1,0:T(8,128)S(1)} %get-tuple-element.20), channel_id=1, source_target_pairs={{1,0},{2,1},{3,2},{4,3},{5,4},{6,5},{7,6},{9,8},{10,9},{11,10},{12... | collective-permute-start | bytes 122888 | tf_op jit(solution)/shard_map/ppermute | solution.py:287
  116.2 3.4 %collective-permute-done.15 = f32[5,16,128]{2,1,0:T(8,128)S(1)} collective-permute-done((f32[5,16,128]{2,1,0:T(8,128)S(1)}, f32[5,16,128]{2,1,0:T(8,128)S(1)}, u32[]{:S(2)}, u32[]{:S(2)}) %collective-permute-start.15) | collective-permute-done | bytes 40992 | tf_op jit(solution)/shard_map/ppermute | solution.py:287
  119.6 4.5 %collective-permute-start.18 = (f32[42,16,128]{2,1,0:T(8,128)S(1)}, f32[42,16,128]{2,1,0:T(8,128)S(1)}, u32[]{:S(2)}, u32[]{:S(2)}) collective-permute-start(f32[42,16,128]{2,1,0:T(8,128)S(1)} %maximum_dynamic-update-slice_fusion.1.refs_7_), channel_id=1, source_target_pairs={{8,0},{16,8},{24,16},{32,24},{40,32},{48,40},{56,48},{64,56},{72,6... | collective-permute-start | bytes 1032200 | tf_op jit(solution)/shard_map/ppermute | solution.py:287
  124.1 1.9 %collective-permute-start.17 = (f32[42,16,128]{2,1,0:T(8,128)S(1)}, f32[42,16,128]{2,1,0:T(8,128)S(1)}, u32[]{:S(2)}, u32[]{:S(2)}) collective-permute-start(f32[42,16,128]{2,1,0:T(8,128)S(1)} %maximum_dynamic-update-slice_fusion.1.refs_7_), channel_id=1, source_target_pairs={{0,8},{8,16},{16,24},{24,32},{32,40},{40,48},{48,56},{56,64},{64,7... | collective-permute-start | bytes 1032200 | tf_op jit(solution)/shard_map/ppermute | solution.py:287
  126.1 9.4 %collective-permute-start.19 = (f32[19,16,128]{2,1,0:T(8,128)S(1)}, f32[19,16,128]{2,1,0:T(8,128)S(1)}, u32[]{:S(2)}, u32[]{:S(2)}) collective-permute-start(f32[19,16,128]{2,1,0:T(8,128)S(1)} %slice.9), channel_id=1, source_target_pairs={{16,0},{24,8},{32,16},{40,24},{48,32},{56,40},{64,48},{72,56},{80,... | collective-permute-start | bytes 466952 | tf_op jit(solution)/shard_map/ppermute | solution.py:287
  135.4 1.9 %collective-permute-start.16 = (f32[19,16,128]{2,1,0:T(8,128)S(1)}, f32[19,16,128]{2,1,0:T(8,128)S(1)}, u32[]{:S(2)}, u32[]{:S(2)}) collective-permute-start(f32[19,16,128]{2,1,0:T(8,128)S(1)} %slice.9), channel_id=1, source_target_pairs={{0,16},{8,24},{16,32},{24,40},{32,48},{40,56},{48,64},{56,72},{64,... | collective-permute-start | bytes 466952 | tf_op jit(solution)/shard_map/ppermute | solution.py:287
  137.4 3.1 %collective-permute-done.19.refs_9_ = f32[19,16,128]{2,1,0:T(8,128)S(1)} collective-permute-done((f32[19,16,128]{2,1,0:T(8,128)S(1)}, f32[19,16,128]{2,1,0:T(8,128)S(1)}, u32[]{:S(2)}, u32[]{:S(2)}) %collective-permute-start.19) | collective-permute-done | bytes 155680 | tf_op jit(solution)/shard_map/ppermute | solution.py:287
  140.5 7.7 %collective-permute-done.16.refs_5_ = f32[19,16,128]{2,1,0:T(8,128)S(1)} collective-permute-done((f32[19,16,128]{2,1,0:T(8,128)S(1)}, f32[19,16,128]{2,1,0:T(8,128)S(1)}, u32[]{:S(2)}, u32[]{:S(2)}) %collective-permute-start.16) | collective-permute-done | bytes 155680 | tf_op jit(solution)/shard_map/ppermute | solution.py:287
  148.2 7.9 %substeps_last.1 = f32[8,16,256]{2,1,0:T(8,128)} custom-call(s32[4]{0:T(128)S(1)} %pad_add_fusion.refs_0_, f32[8]{0:T(128)S(1)} %bitcast.28, f32[2]{0:T(128)S(1)} %bitcast.30, f32[8,8]{1,0:T(8,128)S(1)} %bitcast.23, f32[8,8]{1,0:T(8,128)S(1)} %bitcast.26, f32[19,16,128]{2,1,0:T(8,128)S(1)} %collective-permute-done.16.refs_5_, ...), custom_call_target="tpu_custom_call" | custom-call | tf_op jit(solution)/shard_map/substeps_last/pallas_call | solution.py:262
  (36 shorter events, 0.2 us)
Async XLA Ops:
  0.6 0.7 copy-start.8
  0.6 0.7 copy-start.7
  1.3 0.9 copy-start.2
  2.2 0.7 copy-start.4
  3.0 0.9 copy-start.6
  4.7 12.7 %copy-start.12 = (s32[1,16,4,2]{1,3,2,0:T(2,128)S(1)}, s32[1,16,4,2]{1,3,2,0:T(2,128)}, u32[]{:S(2)}) copy-start(s32[1,16,4,2]{1,3,2,0:T(2,128)} %param.17) | copy-start | bytes 1540
  4.7 13.8 %collective-permute-start.1 = (bf16[128,256]{1,0:T(8,128)(2,1)S(1)}, bf16[128,256]{1,0:T(8,128)(2,1)S(1)}, u32[]{:S(2)}, u32[]{:S(2)}) collective-permute-start(bf16[128,256]{1,0:T(8,128)(2,1)S(1)} %export.1), channel_id=1, source_target_pairs={{0,504},{8,256},{16,264},{24,272},{32,280},{40,288},{48,296},{56,3... | collective-permute-start | bytes 196616 | tf_op jit(solution)/shard_map/ppermute | solution.py:295
  14.3 10.4 %collective-permute-start = (bf16[128,256]{1,0:T(8,128)(2,1)S(1)}, bf16[128,256]{1,0:T(8,128)(2,1)S(1)}, u32[]{:S(2)}, u32[]{:S(2)}) collective-permute-start(bf16[128,256]{1,0:T(8,128)(2,1)S(1)} %export.1), channel_id=1, source_target_pairs={{0,264},{8,272},{16,280},{24,288},{32,296},{40,304},{48,312},{56,3... | collective-permute-start | bytes 196616 | tf_op jit(solution)/shard_map/ppermute | solution.py:295
  17.5 0.7 copy-start.11
  18.5 16.4 %copy-start.3 = (f32[1,8,16,256]{3,2,1,0:T(8,128)S(1)}, f32[1,8,16,256]{3,2,1,0:T(8,128)}, u32[]{:S(2)}) copy-start(f32[1,8,16,256]{3,2,1,0:T(8,128)} %param.10) | copy-start | bytes 393220
  18.5 16.4 %copy-start.5 = (s32[1,16,256]{2,1,0:T(8,128)S(1)}, s32[1,16,256]{2,1,0:T(8,128)}, u32[]{:S(2)}) copy-start(s32[1,16,256]{2,1,0:T(8,128)} %param.12) | copy-start | bytes 49156
  24.7 10.2 %collective-permute-start.2 = (bf16[256,256]{1,0:T(8,128)(2,1)S(1)}, bf16[256,256]{1,0:T(8,128)(2,1)S(1)}, u32[]{:S(2)}, u32[]{:S(2)}) collective-permute-start(bf16[256,256]{1,0:T(8,128)(2,1)S(1)} %pad_maximum_fusion), channel_id=1, source_target_pairs={{0,8},{8,16},{16,24},{24,32},{32,40},{40,48},{48,56},{56,64},{64,7... | collective-permute-start | bytes 393224 | tf_op jit(solution)/shard_map/ppermute | solution.py:282
  27.4 7.5 %collective-permute-start.3 = (bf16[128,256]{1,0:T(8,128)(2,1)S(1)}, bf16[128,256]{1,0:T(8,128)(2,1)S(1)}, u32[]{:S(2)}, u32[]{:S(2)}) collective-permute-start(bf16[128,256]{1,0:T(8,128)(2,1)S(1)} %collective-permute-done.1.right_ref), channel_id=1, source_target_pairs={{0,248},{8,0},{16,8},{24,16},{32,24},{40,32},{48,40},{56,48},{64,5... | collective-permute-start | bytes 196616 | tf_op jit(solution)/shard_map/ppermute | solution.py:282
  34.9 1.2 copy-start
  37.4 8.6 %collective-permute-start.4 = (f32[5,16,128]{2,1,0:T(8,128)S(1)}, f32[5,16,128]{2,1,0:T(8,128)S(1)}, u32[]{:S(2)}, u32[]{:S(2)}) collective-permute-start(f32[5,16,128]{2,1,0:T(8,128)S(1)} %get-tuple-element.13), channel_id=1, source_target_pairs={{0,1},{1,2},{2,3},{3,4},{4,5},{5,6},{6,7},{8,9},{9,10},{10,11},{11... | collective-permute-start | bytes 122888 | tf_op jit(solution)/shard_map/ppermute | solution.py:287
  44.0 5.3 %collective-permute-start.5 = (f32[5,16,128]{2,1,0:T(8,128)S(1)}, f32[5,16,128]{2,1,0:T(8,128)S(1)}, u32[]{:S(2)}, u32[]{:S(2)}) collective-permute-start(f32[5,16,128]{2,1,0:T(8,128)S(1)} %get-tuple-element.14), channel_id=1, source_target_pairs={{1,0},{2,1},{3,2},{4,3},{5,4},{6,5},{7,6},{9,8},{10,9},{11,10},{12... | collective-permute-start | bytes 122888 | tf_op jit(solution)/shard_map/ppermute | solution.py:287
  49.4 30.4 %copy-start.9 = (f32[1,8]{1,0:T(1,128)S(1)}, f32[1,8]{1,0:T(1,128)}, u32[]{:S(2)}) copy-start(f32[1,8]{1,0:T(1,128)} %param.15) | copy-start | bytes 100
  49.4 30.4 %copy-start.10 = (f32[1,2]{1,0:T(1,128)S(1)}, f32[1,2]{1,0:T(1,128)}, u32[]{:S(2)}) copy-start(f32[1,2]{1,0:T(1,128)} %param.16) | copy-start | bytes 28
  49.4 57.2 %copy-start.1 = (bf16[1,16,4,64,128]{4,3,2,1,0:T(8,128)(2,1)S(1)}, bf16[1,16,4,64,128]{4,3,2,1,0:T(8,128)(2,1)}, u32[]{:S(2)}) copy-start(bf16[1,16,4,64,128]{4,3,2,1,0:T(8,128)(2,1)} %param.19) | copy-start | bytes 3145732
  49.4 30.4 %collective-permute-start.8 = (f32[42,16,128]{2,1,0:T(8,128)S(1)}, f32[42,16,128]{2,1,0:T(8,128)S(1)}, u32[]{:S(2)}, u32[]{:S(2)}) collective-permute-start(f32[42,16,128]{2,1,0:T(8,128)S(1)} %maximum_dynamic-update-slice_fusion.refs_7_), channel_id=1, source_target_pairs={{8,0},{16,8},{24,16},{32,24},{40,32},{48,40},{56,48},{64,56},{72,6... | collective-permute-start | bytes 1032200 | tf_op jit(solution)/shard_map/ppermute | solution.py:287
  55.3 24.5 %collective-permute-start.7 = (f32[42,16,128]{2,1,0:T(8,128)S(1)}, f32[42,16,128]{2,1,0:T(8,128)S(1)}, u32[]{:S(2)}, u32[]{:S(2)}) collective-permute-start(f32[42,16,128]{2,1,0:T(8,128)S(1)} %maximum_dynamic-update-slice_fusion.refs_7_), channel_id=1, source_target_pairs={{0,8},{8,16},{16,24},{24,32},{32,40},{40,48},{48,56},{56,64},{64,7... | collective-permute-start | bytes 1032200 | tf_op jit(solution)/shard_map/ppermute | solution.py:287
  57.2 14.8 %collective-permute-start.9 = (f32[19,16,128]{2,1,0:T(8,128)S(1)}, f32[19,16,128]{2,1,0:T(8,128)S(1)}, u32[]{:S(2)}, u32[]{:S(2)}) collective-permute-start(f32[19,16,128]{2,1,0:T(8,128)S(1)} %slice.8), channel_id=1, source_target_pairs={{16,0},{24,8},{32,16},{40,24},{48,32},{56,40},{64,48},{72,56},{80,... | collective-permute-start | bytes 466952 | tf_op jit(solution)/shard_map/ppermute | solution.py:287
  66.6 13.2 %collective-permute-start.6 = (f32[19,16,128]{2,1,0:T(8,128)S(1)}, f32[19,16,128]{2,1,0:T(8,128)S(1)}, u32[]{:S(2)}, u32[]{:S(2)}) collective-permute-start(f32[19,16,128]{2,1,0:T(8,128)S(1)} %slice.8), channel_id=1, source_target_pairs={{0,16},{8,24},{16,32},{24,40},{32,48},{40,56},{48,64},{56,72},{64,... | collective-permute-start | bytes 466952 | tf_op jit(solution)/shard_map/ppermute | solution.py:287
  87.2 10.4 %collective-permute-start.11 = (bf16[128,256]{1,0:T(8,128)(2,1)S(1)}, bf16[128,256]{1,0:T(8,128)(2,1)S(1)}, u32[]{:S(2)}, u32[]{:S(2)}) collective-permute-start(bf16[128,256]{1,0:T(8,128)(2,1)S(1)} %get-tuple-element.16), channel_id=1, source_target_pairs={{0,504},{8,256},{16,264},{24,272},{32,280},{40,288},{48,296},{56,3... | collective-permute-start | bytes 196616 | tf_op jit(solution)/shard_map/ppermute | solution.py:295
  89.2 10.1 %collective-permute-start.10 = (bf16[128,256]{1,0:T(8,128)(2,1)S(1)}, bf16[128,256]{1,0:T(8,128)(2,1)S(1)}, u32[]{:S(2)}, u32[]{:S(2)}) collective-permute-start(bf16[128,256]{1,0:T(8,128)(2,1)S(1)} %get-tuple-element.16), channel_id=1, source_target_pairs={{0,264},{8,272},{16,280},{24,288},{32,296},{40,304},{48,312},{56,3... | collective-permute-start | bytes 196616 | tf_op jit(solution)/shard_map/ppermute | solution.py:295
  99.3 7.2 %collective-permute-start.12 = (bf16[256,256]{1,0:T(8,128)(2,1)S(1)}, bf16[256,256]{1,0:T(8,128)(2,1)S(1)}, u32[]{:S(2)}, u32[]{:S(2)}) collective-permute-start(bf16[256,256]{1,0:T(8,128)(2,1)S(1)} %pad_maximum_fusion.1), channel_id=1, source_target_pairs={{0,8},{8,16},{16,24},{24,32},{32,40},{40,48},{48,56},{56,64},{64,7... | collective-permute-start | bytes 393224 | tf_op jit(solution)/shard_map/ppermute | solution.py:282
  101.2 5.3 %collective-permute-start.13 = (bf16[128,256]{1,0:T(8,128)(2,1)S(1)}, bf16[128,256]{1,0:T(8,128)(2,1)S(1)}, u32[]{:S(2)}, u32[]{:S(2)}) collective-permute-start(bf16[128,256]{1,0:T(8,128)(2,1)S(1)} %collective-permute-done.11.right_ref), channel_id=1, source_target_pairs={{0,248},{8,0},{16,8},{24,16},{32,24},{40,32},{48,40},{56,48},{64,5... | collective-permute-start | bytes 196616 | tf_op jit(solution)/shard_map/ppermute | solution.py:282
  108.4 7.8 %collective-permute-start.14 = (f32[5,16,128]{2,1,0:T(8,128)S(1)}, f32[5,16,128]{2,1,0:T(8,128)S(1)}, u32[]{:S(2)}, u32[]{:S(2)}) collective-permute-start(f32[5,16,128]{2,1,0:T(8,128)S(1)} %get-tuple-element.19), channel_id=1, source_target_pairs={{0,1},{1,2},{2,3},{3,4},{4,5},{5,6},{6,7},{8,9},{9,10},{10,11},{11... | collective-permute-start | bytes 122888 | tf_op jit(solution)/shard_map/ppermute | solution.py:287
  114.3 5.3 %collective-permute-start.15 = (f32[5,16,128]{2,1,0:T(8,128)S(1)}, f32[5,16,128]{2,1,0:T(8,128)S(1)}, u32[]{:S(2)}, u32[]{:S(2)}) collective-permute-start(f32[5,16,128]{2,1,0:T(8,128)S(1)} %get-tuple-element.20), channel_id=1, source_target_pairs={{1,0},{2,1},{3,2},{4,3},{5,4},{6,5},{7,6},{9,8},{10,9},{11,10},{12... | collective-permute-start | bytes 122888 | tf_op jit(solution)/shard_map/ppermute | solution.py:287
  119.6 28.5 %collective-permute-start.18 = (f32[42,16,128]{2,1,0:T(8,128)S(1)}, f32[42,16,128]{2,1,0:T(8,128)S(1)}, u32[]{:S(2)}, u32[]{:S(2)}) collective-permute-start(f32[42,16,128]{2,1,0:T(8,128)S(1)} %maximum_dynamic-update-slice_fusion.1.refs_7_), channel_id=1, source_target_pairs={{8,0},{16,8},{24,16},{32,24},{40,32},{48,40},{56,48},{64,56},{72,6... | collective-permute-start | bytes 1032200 | tf_op jit(solution)/shard_map/ppermute | solution.py:287
  124.1 24.0 %collective-permute-start.17 = (f32[42,16,128]{2,1,0:T(8,128)S(1)}, f32[42,16,128]{2,1,0:T(8,128)S(1)}, u32[]{:S(2)}, u32[]{:S(2)}) collective-permute-start(f32[42,16,128]{2,1,0:T(8,128)S(1)} %maximum_dynamic-update-slice_fusion.1.refs_7_), channel_id=1, source_target_pairs={{0,8},{8,16},{16,24},{24,32},{32,40},{40,48},{48,56},{56,64},{64,7... | collective-permute-start | bytes 1032200 | tf_op jit(solution)/shard_map/ppermute | solution.py:287
  126.1 14.4 %collective-permute-start.19 = (f32[19,16,128]{2,1,0:T(8,128)S(1)}, f32[19,16,128]{2,1,0:T(8,128)S(1)}, u32[]{:S(2)}, u32[]{:S(2)}) collective-permute-start(f32[19,16,128]{2,1,0:T(8,128)S(1)} %slice.9), channel_id=1, source_target_pairs={{16,0},{24,8},{32,16},{40,24},{48,32},{56,40},{64,48},{72,56},{80,... | collective-permute-start | bytes 466952 | tf_op jit(solution)/shard_map/ppermute | solution.py:287
  135.4 12.7 %collective-permute-start.16 = (f32[19,16,128]{2,1,0:T(8,128)S(1)}, f32[19,16,128]{2,1,0:T(8,128)S(1)}, u32[]{:S(2)}, u32[]{:S(2)}) collective-permute-start(f32[19,16,128]{2,1,0:T(8,128)S(1)} %slice.9), channel_id=1, source_target_pairs={{0,16},{8,24},{16,32},{24,40},{32,48},{40,56},{48,64},{56,72},{64,... | collective-permute-start | bytes 466952 | tf_op jit(solution)/shard_map/ppermute | solution.py:287

commit v2 on v1

v2 whole, which is shorter than its diff:
```python
import jax
import jax.numpy as jnp
from jax import lax
from jax.experimental import pallas as pl
from jax.experimental.pallas import tpu as pltpu
from jax.sharding import PartitionSpec as P

SUBSTEPS = 16
ITERS = 2
DIFFUSION = 0.1
COUPLING = 0.2

FIELDS = 8
WAVES = 3
TRACERS = 5
ROWS = 16
COLS = 256
LANES = 128
TURNED = ROWS * FIELDS
STRIP = 32
STEPS_PER_PHASE = 4

F_TRACER = 0
F_STRIP_T = 10
F_STRIP_W = 12
F_WAVE = 14
F_PLANES = 20
F_FAR = 12
X_TRACER = 0
X_TRACER_LOW = 12
X_WAVE = 24
X_WAVE_LOW = 32
X_EXPORT = 40
X_PLANES = 56
X_FAR = 24

PAD = 8
SMEM = pl.BlockSpec(memory_space=pltpu.SMEM)
VMEM = pl.BlockSpec(memory_space=pltpu.VMEM)
HBM = pl.BlockSpec(memory_space=pl.ANY)

f32 = jnp.float32
bf16 = jnp.bfloat16


def params(mib=24):
    return pltpu.CompilerParams(vmem_limit_bytes=mib * 1024 * 1024)


def shaped(shape, dtype=f32):
    return jax.ShapeDtypeStruct(shape, dtype)


def half_of(value, half):
    return value[:, half * LANES : (half + 1) * LANES]


def write_export(fields, received, wet, smix_ref, imix_ref, turned, out_ref):
    scale = wet * jnp.sqrt(1.0 + fields[1] * fields[1] + fields[2] * fields[2])
    for c in range(FIELDS):
        total = smix_ref[c, 0] * fields[0]
        for k in range(1, FIELDS):
            total = total + smix_ref[c, k] * fields[k]
        other = imix_ref[c, 0] * received[0]
        for k in range(1, FIELDS):
            other = other + imix_ref[c, k] * received[k]
        value = scale * (total + other)
        for half in range(2):
            turned[half, pl.ds(c, ROWS, stride=FIELDS), :] = half_of(value, half)
    for half in range(2):
        out_ref[:, half * LANES : (half + 1) * LANES] = turned[half].astype(bf16)


def write_strips(fields, low_ref, high_ref):
    lane = lax.broadcasted_iota(jnp.int32, (ROWS, LANES), 1)
    groups = [fields[3:7], [fields[7]] + fields[0:3]]
    for p, group in enumerate(groups):
        first = group[0][0]
        last = pltpu.roll(group[0][1], STRIP, 1)
        for j in range(1, 4):
            here = lane >= STRIP * j
            first = jnp.where(here, pltpu.roll(group[j][0], STRIP * j, 1), first)
            moved = group[j][1] if j == 3 else pltpu.roll(group[j][1], STRIP * (j + 1), 1)
            last = jnp.where(here, moved, last)
        low_ref[p] = first
        high_ref[p] = last


def export_kernel(
    smix_ref, imix_ref, fields_ref, received_ref, land_ref, out_ref, low_ref, high_ref,
    turned, fields_buf, received_buf, land_buf, sems,
):
    copies = [
        pltpu.make_async_copy(fields_ref, fields_buf, sems.at[0]),
        pltpu.make_async_copy(received_ref, received_buf, sems.at[1]),
        pltpu.make_async_copy(land_ref, land_buf, sems.at[2]),
    ]
    for copy in copies:
        copy.start()
    for copy in copies:
        copy.wait()
    fields = [fields_buf[c] for c in range(FIELDS)]
    received = [received_buf[c] for c in range(FIELDS)]
    write_export(fields, received, land_buf[...].astype(f32), smix_ref, imix_ref, turned, out_ref)
    write_strips([[half_of(v, 0), half_of(v, 1)] for v in fields], low_ref, high_ref)


def export(fields, received, land, smix, imix):
    strips = shaped((2, ROWS, LANES))
    return pl.pallas_call(
        export_kernel,
        out_shape=(shaped((TURNED, COLS), bf16), strips, strips),
        in_specs=[SMEM, SMEM, HBM, HBM, HBM],
        out_specs=(VMEM,) * 3,
        scratch_shapes=[
            pltpu.VMEM((2, TURNED, LANES), f32),
            pltpu.VMEM((FIELDS, ROWS, COLS), f32),
            pltpu.VMEM((FIELDS, ROWS, COLS), f32),
            pltpu.VMEM((ROWS, COLS), jnp.int32),
            pltpu.SemaphoreType.DMA((3,)),
        ],
        compiler_params=params(56),
        name="export",
    )(smix, imix, fields, received, land)


def pack_kernel(opposite_ref, fields_ref, left_ref, right_ref, near_ref, far_ref):
    def put(at, low_at, value):
        high = value.astype(bf16)
        low = (value - high.astype(f32)).astype(bf16)
        for index, part in ((at, high), (low_at, low)):
            near_ref[index] = part
            if index >= X_FAR:
                far_ref[index - X_FAR] = part

    for i in range(TRACERS):
        for half in range(2):
            plane = 2 * i + half
            value = fields_ref[WAVES + i, :, half * LANES : (half + 1) * LANES]
            put(X_TRACER + plane, X_TRACER_LOW + plane, value)
    put(X_TRACER + 10, X_TRACER_LOW + 10, left_ref[0])
    put(X_TRACER + 11, X_TRACER_LOW + 11, right_ref[0])
    put(X_WAVE, X_WAVE_LOW, left_ref[1])
    put(X_WAVE + 1, X_WAVE_LOW + 1, right_ref[1])
    for i in range(WAVES):
        for half in range(2):
            plane = 2 + 2 * i + half
            value = fields_ref[i, :, half * LANES : (half + 1) * LANES]
            put(X_WAVE + plane, X_WAVE_LOW + plane, value)
    for half in range(2):
        for i in range(TURNED // 16):
            part = opposite_ref[16 * i : 16 * i + 16, half * LANES : (half + 1) * LANES]
            near_ref[X_EXPORT + half * 8 + i] = part
            far_ref[X_EXPORT - X_FAR + half * 8 + i] = part


def pack(opposite, fields, left, right):
    return pl.pallas_call(
        pack_kernel,
        out_shape=(shaped((X_PLANES, ROWS, LANES), bf16), shaped((X_PLANES - X_FAR, ROWS, LANES), bf16)),
        in_specs=[VMEM] * 4,
        out_specs=(VMEM,) * 2,
        compiler_params=params(),
        name="pack",
    )(opposite, fields, left, right)


def remap_kernel(
    index_ref, far_before_ref, before_ref, opposite_ref, after_ref, far_after_ref, weight_ref, land_ref,
    payload_ref, low_ref, high_ref, import_ref, table, turned,
):
    half_count = 5 * ROWS * 2
    windows = [far_before_ref, before_ref, opposite_ref, after_ref, far_after_ref]
    for w, ref in enumerate(windows):
        for half in range(2):
            for i in range(TURNED // 16):
                if w == 2:
                    chunk = ref[16 * i : 16 * i + 16, half * LANES : (half + 1) * LANES]
                else:
                    chunk = ref[X_EXPORT - (X_FAR if w in (0, 4) else 0) + half * 8 + i]
                chunk = chunk.astype(f32)
                for sub in range(2):
                    part = chunk[sub * 8 : sub * 8 + 8]
                    at = (w * ROWS + i * 2 + sub) * 2 + half
                    table[at] = part
                    table[half_count + at] = pltpu.roll(part, 64, 1)
    lane8 = lax.broadcasted_iota(jnp.int32, (8, LANES), 1)
    low_half = lane8 < 64
    ones = jnp.ones((8, LANES), f32)
    for x in range(ROWS):
        pieces = []
        for seg in range(4):
            at = (x * 4 + seg) * 2
            pieces.append(jnp.where(low_half, table[index_ref[at]], table[index_ref[at + 1]]))
        picked = jnp.concatenate(pieces + [ones], axis=0).astype(bf16)
        product = lax.dot_general(
            picked, weight_ref[x], (((1,), (1,)), ((), ())), preferred_element_type=f32
        )
        for half in range(2):
            cols = half_of(product, half)
            summed = jnp.where(low_half, cols[16 * half : 16 * half + 8], cols[16 * half + 8 : 16 * half + 16])
            turned[half, x * 8 : x * 8 + 8, :] = summed / cols[32:40]
    wet = land_ref[...].astype(f32)
    forcing = []
    for c in range(FIELDS):
        parts = []
        for half in range(2):
            value = turned[half, pl.ds(c, ROWS, stride=FIELDS), :]
            import_ref[c, :, half * LANES : (half + 1) * LANES] = value
            part = COUPLING * half_of(wet, half) * value
            parts.append(part)
            if c < WAVES:
                payload_ref[F_WAVE + 2 * c + half] = part
            else:
                payload_ref[F_TRACER + 2 * (c - WAVES) + half] = part
        forcing.append(parts)
    for p in range(F_STRIP_T, F_WAVE):
        payload_ref[p] = jnp.zeros((ROWS, LANES), f32)
    write_strips(forcing, low_ref, high_ref)


def remap(index, windows, weight, land):
    strips = shaped((2, ROWS, LANES))
    return pl.pallas_call(
        remap_kernel,
        out_shape=(shaped((F_PLANES, ROWS, LANES)), strips, strips, shaped((FIELDS, ROWS, COLS))),
        in_specs=[SMEM] + [VMEM] * 7,
        out_specs=(VMEM,) * 4,
        scratch_shapes=[
            pltpu.VMEM((2 * 5 * ROWS * 2, FIELDS, LANES), f32),
            pltpu.VMEM((2, TURNED, LANES), f32),
        ],
        compiler_params=params(),
        name="remap",
    )(index, *windows, weight, land)


def sides(left, right, j):
    lane = lax.broadcasted_iota(jnp.int32, (ROWS, LANES), 1)
    if j:
        right = pltpu.roll(right, LANES - STRIP * j, 1)
    if j != 3:
        left = pltpu.roll(left, 96 - STRIP * j, 1)
    return jnp.where(lane < STRIP, right, jnp.where(lane >= 96, left, 0.0))


def place_field(dest, rows, parts):
    for j, part in enumerate(parts):
        dest[j, rows, :] = part


def joined(ref, at, low_at):
    return ref[at].astype(f32) + ref[low_at].astype(f32)


def inside_tile(place_ref, first_row, count, j):
    shape = (count, LANES)
    row = lax.broadcasted_iota(jnp.int32, shape, 0) + (place_ref[0] * ROWS + first_row)
    col = lax.broadcasted_iota(jnp.int32, shape, 1) + j * LANES
    if j == 2:
        col = jnp.where(col >= 3 * LANES - STRIP, col - 3 * LANES, col)
    col = col + place_ref[1] * COLS
    ok = (row >= 0) & (row < place_ref[2]) & (col >= 0) & (col < place_ref[3])
    return jnp.where(ok, 1.0, 0.0)


def westward(parts, lane):
    moved = [pltpu.roll(part, 1, 1) for part in parts]
    return [jnp.where(lane == 0, moved[j - 1], moved[j]) for j in range(3)]


def eastward(parts, lane):
    moved = [pltpu.roll(part, LANES - 1, 1) for part in parts]
    return [jnp.where(lane == LANES - 1, moved[(j + 1) % 3], moved[j]) for j in range(3)]


def tracer_kernel(
    place_ref, damping_ref, forcing_before_ref, forcing_ref, forcing_after_ref, state_before_ref,
    fields_ref, left_ref, right_ref, state_after_ref, out_ref, state, forcing, coef,
):
    for t, ref in enumerate((forcing_before_ref, forcing_ref, forcing_after_ref)):
        rows = slice(t * ROWS, (t + 1) * ROWS)
        for i in range(TRACERS):
            strip = F_STRIP_T if i < 4 else F_STRIP_W
            beside = sides(ref[strip], ref[strip + 1], i % 4)
            place_field(forcing.at[i], rows, [ref[F_TRACER + 2 * i], ref[F_TRACER + 2 * i + 1], beside])
    for t, ref in enumerate((state_before_ref, None, state_after_ref)):
        rows = slice(PAD + t * ROWS, PAD + (t + 1) * ROWS)
        for i in range(TRACERS):
            if ref is None:
                p = 0 if i < 4 else 1
                parts = [half_of(fields_ref[WAVES + i], 0), half_of(fields_ref[WAVES + i], 1)]
                parts.append(sides(left_ref[p], right_ref[p], i % 4))
            else:
                at, low = X_TRACER + 2 * i, X_TRACER_LOW + 2 * i
                parts = [joined(ref, at, low), joined(ref, at + 1, low + 1)]
                at, low = (X_TRACER + 10, X_TRACER_LOW + 10) if i < 4 else (X_WAVE, X_WAVE_LOW)
                parts.append(sides(joined(ref, at, low), joined(ref, at + 1, low + 1), i % 4))
            place_field(state.at[0, i], rows, parts)
    height = 3 * ROWS
    for k in range(2):
        for i in range(TRACERS):
            for j in range(3):
                state[k, i, j, 0:PAD, :] = jnp.zeros((PAD, LANES), f32)
                state[k, i, j, PAD + height : height + 2 * PAD, :] = jnp.zeros((PAD, LANES), f32)
    for j in range(3):
        coef[j] = inside_tile(place_ref, -ROWS, height, j) * DIFFUSION

    lane = lax.broadcasted_iota(jnp.int32, (8, LANES), 1)
    keep = [(1.0 - damping_ref[WAVES + c]) - 4.0 * DIFFUSION for c in range(TRACERS)]

    def step(source, dest, first, count):
        for t in range(first, first + count):
            at = PAD + 8 * t
            here = slice(8 * t, 8 * t + 8)
            for c in range(TRACERS):
                mid = [state[source, c, j, at : at + 8, :] for j in range(3)]
                west = westward(mid, lane)
                east = eastward(mid, lane)
                for j in range(3):
                    above = state[source, c, j, at + 1 : at + 9, :]
                    below = state[source, c, j, at - 1 : at + 7, :]
                    around = (above + below) + (east[j] + west[j])
                    state[dest, c, j, at : at + 8, :] = (
                        keep[c] * mid[j] + forcing[c, j, here, :]
                    ) + coef[j, here, :] * around

    def pair_of_steps(first, count):
        def run(_, carry):
            step(0, 1, first, count)
            step(1, 0, first, count)
            return carry
        return run

    lax.fori_loop(0, SUBSTEPS // 4, pair_of_steps(0, 6), 0)
    lax.fori_loop(0, SUBSTEPS // 4, pair_of_steps(1, 4), 0)
    for i in range(TRACERS):
        for half in range(2):
            out_ref[i, :, half * LANES : (half + 1) * LANES] = state[0, i, half, PAD + ROWS : PAD + 2 * ROWS, :]


def tracer_steps(place, damping, forcings, before, fields, left, right, after):
    return pl.pallas_call(
        tracer_kernel,
        out_shape=shaped((TRACERS, ROWS, COLS)),
        in_specs=[SMEM] * 2 + [VMEM] * 8,
        out_specs=VMEM,
        scratch_shapes=[
            pltpu.VMEM((2, TRACERS, 3, 3 * ROWS + 2 * PAD, LANES), f32),
            pltpu.VMEM((TRACERS, 3, 3 * ROWS, LANES), f32),
            pltpu.VMEM((3, 3 * ROWS, LANES), f32),
        ],
        compiler_params=params(),
        cost_estimate=pl.CostEstimate(flops=10_000_000, bytes_accessed=4_000_000, transcendentals=0),
        name="tracer_steps",
    )(place, damping, *forcings, before, fields, left, right, after)


def wave_kernel(last, place_ref, damping_ref, wave_ref, smix_ref, imix_ref, *refs):
    forcing_refs = refs[:5]
    state_refs = list(refs[5:7]) + [None] + list(refs[7:9])
    fields_ref, left_ref, right_ref, tracers_ref = refs[9:13]
    if last:
        out_ref, state, forcing, coef, turned = refs[13:]
    else:
        received_ref, land_ref, out_ref, export_ref, low_ref, high_ref, state, forcing, coef, turned = refs[13:]
    height = 5 * ROWS
    for t, ref in enumerate(forcing_refs):
        rows = slice(t * ROWS, (t + 1) * ROWS)
        base = F_FAR if t in (0, 4) else 0
        left, right = ref[F_STRIP_W - base], ref[F_STRIP_W - base + 1]
        for i in range(WAVES):
            at = F_WAVE - base + 2 * i
            place_field(forcing.at[i], rows, [ref[at], ref[at + 1], sides(left, right, i + 1)])
    for t, ref in enumerate(state_refs):
        rows = slice(PAD + t * ROWS, PAD + (t + 1) * ROWS)
        base = X_FAR if t in (0, 4) else 0
        if ref is None:
            left, right = left_ref[1], right_ref[1]
        else:
            at, low = X_WAVE - base, X_WAVE_LOW - base
            left, right = joined(ref, at, low), joined(ref, at + 1, low + 1)
        for i in range(WAVES):
            if ref is None:
                parts = [half_of(fields_ref[i], 0), half_of(fields_ref[i], 1)]
            else:
                shift = 2 + 2 * i
                parts = [joined(ref, at + shift, low + shift), joined(ref, at + shift + 1, low + shift + 1)]
            place_field(state.at[i], rows, parts + [sides(left, right, i + 1)])
    for i in range(WAVES):
        for j in range(3):
            state[i, j, 0:PAD, :] = jnp.zeros((PAD, LANES), f32)
            state[i, j, PAD + height : height + 2 * PAD, :] = jnp.zeros((PAD, LANES), f32)
    for j in range(3):
        inside = inside_tile(place_ref, -2 * ROWS, height, j)
        coef[0, j] = inside * (0.5 * wave_ref[0])
        coef[1, j] = inside * (0.5 * wave_ref[1])

    lane = lax.broadcasted_iota(jnp.int32, (8, LANES), 1)
    keep = [1.0 - damping_ref[c] for c in range(WAVES)]

    def step(first, end):
        for t in range(first, end):
            at = PAD + 8 * t
            here = slice(8 * t, 8 * t + 8)
            v = [state[2, j, at : at + 8, :] for j in range(3)]
            west = westward(v, lane)
            east = eastward(v, lane)
            for j in range(3):
                spread = (state[1, j, at + 1 : at + 9, :] - state[1, j, at - 1 : at + 7, :]) + (east[j] - west[j])
                state[0, j, at : at + 8, :] = (
                    keep[0] * state[0, j, at : at + 8, :] + forcing[0, j, here, :]
                ) - coef[0, j, here, :] * spread
        for t in range(first, end):
            at = PAD + 8 * t
            here = slice(8 * t, 8 * t + 8)
            h = [state[0, j, at : at + 8, :] for j in range(3)]
            west = westward(h, lane)
            east = eastward(h, lane)
            for j in range(3):
                slope = state[0, j, at + 1 : at + 9, :] - state[0, j, at - 1 : at + 7, :]
                factor = coef[1, j, here, :]
                state[1, j, at : at + 8, :] = (
                    keep[1] * state[1, j, at : at + 8, :] + forcing[1, j, here, :]
                ) - factor * slope
                state[2, j, at : at + 8, :] = (
                    keep[2] * state[2, j, at : at + 8, :] + forcing[2, j, here, :]
                ) - factor * (east[j] - west[j])

    def steps(first, end):
        def run(_, carry):
            step(first, end)
            return carry
        return run

    for phase in range(SUBSTEPS // STEPS_PER_PHASE):
        lax.fori_loop(0, STEPS_PER_PHASE, steps(phase, 10 - phase), 0)

    own = slice(PAD + 2 * ROWS, PAD + 3 * ROWS)
    halves = [[state[i, half, own, :] for half in range(2)] for i in range(WAVES)]
    for i in range(TRACERS):
        halves.append([half_of(tracers_ref[i], half) for half in range(2)])
    for i in range(FIELDS):
        for half in range(2):
            out_ref[i, :, half * LANES : (half + 1) * LANES] = halves[i][half]
    if not last:
        fields = [jnp.concatenate(pair, axis=1) for pair in halves]
        received = [received_ref[c] for c in range(FIELDS)]
        write_export(fields, received, land_ref[...].astype(f32), smix_ref, imix_ref, turned, export_ref)
        write_strips(halves, low_ref, high_ref)


def wave_steps(last, place, damping, wave, smix, imix, operands):
    state = shaped((FIELDS, ROWS, COLS))
    strips = shaped((2, ROWS, LANES))
    return pl.pallas_call(
        lambda *refs: wave_kernel(last, *refs),
        out_shape=state if last else (state, shaped((TURNED, COLS), bf16), strips, strips),
        in_specs=[SMEM] * 5 + [VMEM] * len(operands),
        out_specs=VMEM if last else (VMEM,) * 4,
        scratch_shapes=[
            pltpu.VMEM((WAVES, 3, 5 * ROWS + 2 * PAD, LANES), f32),
            pltpu.VMEM((WAVES, 3, 5 * ROWS, LANES), f32),
            pltpu.VMEM((2, 3, 5 * ROWS, LANES), f32),
            pltpu.VMEM((2, TURNED, LANES), f32),
        ],
        compiler_params=params(),
        name="wave_steps_last" if last else "wave_steps",
    )(place, damping, wave, smix, imix, *operands)


def line(block, axis, by):
    count = lax.axis_size(axis)
    return lax.ppermute(block, axis, [(i, i + by) for i in range(count) if 0 <= i + by < count])


def local(
    section_state, prev_import, land_mask, state_mix, import_mix, damping, wave_speed,
    remap_owner, remap_slot, remap_weight,
):
    fields = section_state[0]
    land = land_mask[0]
    smix = state_mix[0]
    imix = import_mix[0]
    damping = damping[0]
    wave = wave_speed[0]
    gx = lax.axis_index("gx")
    gy = lax.axis_index("gy")
    place = jnp.stack(
        [gx, gy, lax.axis_size("gx") * ROWS, lax.axis_size("gy") * COLS]
    ).astype(jnp.int32)
    owner = remap_owner[0].reshape(-1)
    slot = remap_slot[0].reshape(-1)
    entry = ((owner - gx + 2) * ROWS + slot // 4) * 2 + (slot % 4) // 2
    second = lax.iota(jnp.int32, owner.shape[0]) % 2
    index = entry + ((slot % 2) ^ second) * (5 * ROWS * 2)
    weight = remap_weight[0].reshape(ROWS, COLS, 128)

    exported, low, high = export(fields, prev_import[0], land, smix, imix)
    for interval in range(ITERS):
        last = interval == ITERS - 1
        opposite = lax.ppermute(exported, "sec", [(0, 1), (1, 0)])
        left = line(high, "gy", 1)
        right = line(low, "gy", -1)
        near, far = pack(opposite, fields, left, right)
        before = line(near, "gx", 1)
        after = line(near, "gx", -1)
        far_before = line(far, "gx", 2)
        far_after = line(far, "gx", -2)
        forcing, low, high, received = remap(
            index, (far_before, before, opposite, after, far_after), weight, land
        )
        from_left = line(high, "gy", 1)
        from_right = line(low, "gy", -1)
        strips = jnp.stack([from_left, from_right], axis=1).reshape(4, ROWS, LANES)
        forcing = lax.dynamic_update_slice(forcing, strips, (F_STRIP_T, 0, 0))
        outer = forcing[F_FAR:]
        forcing_before = line(forcing, "gx", 1)
        forcing_after = line(forcing, "gx", -1)
        forcing_far_before = line(outer, "gx", 2)
        forcing_far_after = line(outer, "gx", -2)
        tracers = tracer_steps(
            place, damping, (forcing_before, forcing, forcing_after), before, fields, left, right, after
        )
        operands = (forcing_far_before, forcing_before, forcing, forcing_after, forcing_far_after)
        operands += (far_before, before, after, far_after, fields, left, right, tracers)
        if last:
            fields = wave_steps(last, place, damping, wave, smix, imix, operands)
        else:
            operands += (received, land)
            fields, exported, low, high = wave_steps(last, place, damping, wave, smix, imix, operands)
    return (fields[None], received[None])


def solution(mesh):
    in_specs = (
        P("sec", None, "gx", "gy"),
        P("sec", None, "gx", "gy"),
        P("sec", "gx", "gy"),
        P("sec", None, None),
        P("sec", None, None),
        P("sec", None),
        P("sec", None),
        P("sec", "gx", "gy", None),
        P("sec", "gx", "gy", None),
        P("sec", "gx", "gy", None, None),
    )
    out_specs = (P("sec", None, "gx", "gy"), P("sec", None, "gx", "gy"))
    return jax.shard_map(local, mesh=mesh, in_specs=in_specs, out_specs=out_specs, check_vma=False)
```

time: 157 us -> 149 us (0.949)
  the two profiles are of different devices: /device:TPU:79 before, /device:TPU:11 now
where the time goes in v2:
time: 149 us; the launch traced here: 148 us
  starting transfers between devices  85.9 us (58%)
  waiting for transfers between devices  35.5 us (24%)
  Pallas kernels  22.6 us (15%)
  local copies, waits for them, and re-layouts  2.98 us (2%)
    ppermute x24, starting transfers between devices, line(): lax.ppermute(block, axis, [(i, i + by) for i in range(count) if 0 <= i +...  73.4 us
    ppermute x24, waiting for transfers between devices, line(): lax.ppermute(block, axis, [(i, i + by) for i in range(count) if 0 <= i +...  35.5 us
    ppermute x2, starting transfers between devices, local(): opposite = lax.ppermute(exported, 'sec', [(0, 1), (1, 0)])  12.6 us
    pallas_call x2, Pallas kernels, wave_steps(): pl.pallas_call(lambda *refs: wave_kernel(last, *refs), out_shape=state if...  9.11 us
    pallas_call x2, Pallas kernels, tracer_steps(): pl.pallas_call(tracer_kernel, out_shape=shaped((TRACERS, ROWS, COLS)), in...  7.59 us
    pallas_call x2, Pallas kernels, remap(): pl.pallas_call(remap_kernel, out_shape=(shaped((F_PLANES, ROWS, LANES)),...  3.1 us
  transfers between devices with their start and end apart: 26, of which 10 were waited for; matrix products, arithmetic and copies ran while one was open for 0% of the time, Pallas kernels for 5%

profile of v2, /device:TPU:11, one launch (start us, length us, event | category | flops | bytes accessed | tf_op | source)
XLA Modules:
  0.0 148.2 jit_solution(6946020457808359579)
XLA Ops:
  0.6 2.8 %export.1 = (bf16[128,256]{1,0:T(8,128)(2,1)}, f32[2,16,128]{2,1,0:T(8,128)}, f32[2,16,128]{2,1,0:T(8,128)}) custom-call(f32[8,8]{1,0:T(8,128)} %bitcast.28, f32[8,8]{1,0:T(8,128)} %bitcast.31, f32[8,16,256]{2,1,0:T(8,128)} %bitcast.20, f32[8,16,256]{2,1,0:T(8,128)} %bitcast.40, s32[16,256]{1,0:T(8,128)} %bitcast.24), custom_call_target="tpu_custom_call" | custom-call | tf_op jit(solution)/shard_map/export/pallas_call | solution.py:110
  3.4 10.6 %collective-permute-start = (bf16[128,256]{1,0:T(8,128)(2,1)}, bf16[128,256]{1,0:T(8,128)(2,1)S(1)}, u32[]{:S(2)}, u32[]{:S(2)}) collective-permute-start(bf16[128,256]{1,0:T(8,128)(2,1)} %get-tuple-element.21), channel_id=1, source_target_pairs={{0,256},{256,0},{1,257},{257,1},{2,258},{258,2},{3,259},{259,3},{4... | collective-permute-start | bytes 196616 | tf_op jit(solution)/shard_map/ppermute | solution.py:502
  14.1 3.9 %collective-permute-start.1 = (f32[2,16,128]{2,1,0:T(8,128)}, f32[2,16,128]{2,1,0:T(8,128)S(1)}, u32[]{:S(2)}, u32[]{:S(2)}) collective-permute-start(f32[2,16,128]{2,1,0:T(8,128)} %get-tuple-element.22), channel_id=1, source_target_pairs={{0,1},{1,2},{2,3},{3,4},{4,5},{5,6},{6,7},{8,9},{9,10},{10,11},{11... | collective-permute-start | bytes 49160 | tf_op jit(solution)/shard_map/ppermute | solution.py:474
  18.0 1.9 %collective-permute-start.2 = (f32[2,16,128]{2,1,0:T(8,128)}, f32[2,16,128]{2,1,0:T(8,128)S(1)}, u32[]{:S(2)}, u32[]{:S(2)}) collective-permute-start(f32[2,16,128]{2,1,0:T(8,128)} %get-tuple-element.23), channel_id=1, source_target_pairs={{1,0},{2,1},{3,2},{4,3},{5,4},{6,5},{7,6},{9,8},{10,9},{11,10},{12... | collective-permute-start | bytes 49160 | tf_op jit(solution)/shard_map/ppermute | solution.py:474
  19.9 3.3 %collective-permute-done.2.right_ref.refs_16_ = f32[2,16,128]{2,1,0:T(8,128)S(1)} collective-permute-done((f32[2,16,128]{2,1,0:T(8,128)}, f32[2,16,128]{2,1,0:T(8,128)S(1)}, u32[]{:S(2)}, u32[]{:S(2)}) %collective-permute-start.2) | collective-permute-done | bytes 16416 | tf_op jit(solution)/shard_map/ppermute | solution.py:474
  23.3 2.1 %collective-permute-start.5 = (bf16[56,16,128]{2,1,0:T(8,128)(2,1)S(1)}, bf16[56,16,128]{2,1,0:T(8,128)(2,1)S(1)}, u32[]{:S(2)}, u32[]{:S(2)}) collective-permute-start(bf16[56,16,128]{2,1,0:T(8,128)(2,1)S(1)} %get-tuple-element.25), channel_id=1, source_target_pairs={{8,0},{16,8},{24,16},{32,24},{40,32},{48,40},{56,48},{64,56},{72,6... | collective-permute-start | bytes 688136 | tf_op jit(solution)/shard_map/ppermute | solution.py:474
  25.4 3.2 %collective-permute-start.4 = (bf16[56,16,128]{2,1,0:T(8,128)(2,1)S(1)}, bf16[56,16,128]{2,1,0:T(8,128)(2,1)S(1)}, u32[]{:S(2)}, u32[]{:S(2)}) collective-permute-start(bf16[56,16,128]{2,1,0:T(8,128)(2,1)S(1)} %get-tuple-element.25), channel_id=1, source_target_pairs={{0,8},{8,16},{16,24},{24,32},{32,40},{40,48},{48,56},{56,64},{64,7... | collective-permute-start | bytes 688136 | tf_op jit(solution)/shard_map/ppermute | solution.py:474
  28.8 0.1 mul.20
  28.9 0.5 copy-done.8
  29.6 0.1 reshape_squeeze.7
  29.7 7.1 %collective-permute-start.6 = (bf16[32,16,128]{2,1,0:T(8,128)(2,1)S(1)}, bf16[32,16,128]{2,1,0:T(8,128)(2,1)S(1)}, u32[]{:S(2)}, u32[]{:S(2)}) collective-permute-start(bf16[32,16,128]{2,1,0:T(8,128)(2,1)S(1)} %get-tuple-element.24), channel_id=1, source_target_pairs={{16,0},{24,8},{32,16},{40,24},{48,32},{56,40},{64,48},{72,56},{80,... | collective-permute-start | bytes 393224 | tf_op jit(solution)/shard_map/ppermute | solution.py:474
  36.8 1.9 %collective-permute-start.3 = (bf16[32,16,128]{2,1,0:T(8,128)(2,1)S(1)}, bf16[32,16,128]{2,1,0:T(8,128)(2,1)S(1)}, u32[]{:S(2)}, u32[]{:S(2)}) collective-permute-start(bf16[32,16,128]{2,1,0:T(8,128)(2,1)S(1)} %get-tuple-element.24), channel_id=1, source_target_pairs={{0,16},{8,24},{16,32},{24,40},{32,48},{40,56},{48,64},{56,72},{64,... | collective-permute-start | bytes 393224 | tf_op jit(solution)/shard_map/ppermute | solution.py:474
  38.7 2.0 %collective-permute-done.6.far_after_ref.refs_13_ = bf16[32,16,128]{2,1,0:T(8,128)(2,1)S(1)} collective-permute-done((bf16[32,16,128]{2,1,0:T(8,128)(2,1)S(1)}, bf16[32,16,128]{2,1,0:T(8,128)(2,1)S(1)}, u32[]{:S(2)}, u32[]{:S(2)}) %collective-permute-start.6) | collective-permute-done | bytes 131104 | tf_op jit(solution)/shard_map/ppermute | solution.py:474
  40.7 7.2 %collective-permute-done.3.far_before_ref.refs_10_ = bf16[32,16,128]{2,1,0:T(8,128)(2,1)S(1)} collective-permute-done((bf16[32,16,128]{2,1,0:T(8,128)(2,1)S(1)}, bf16[32,16,128]{2,1,0:T(8,128)(2,1)S(1)}, u32[]{:S(2)}, u32[]{:S(2)}) %collective-permute-start.3) | collective-permute-done | bytes 131104 | tf_op jit(solution)/shard_map/ppermute | solution.py:474
  48.0 1.2 copy-done
  49.2 1.3 remap.2
  50.5 4.1 %collective-permute-start.7 = (f32[2,16,128]{2,1,0:T(8,128)S(1)}, f32[2,16,128]{2,1,0:T(8,128)S(1)}, u32[]{:S(2)}, u32[]{:S(2)}) collective-permute-start(f32[2,16,128]{2,1,0:T(8,128)S(1)} %get-tuple-element.27), channel_id=1, source_target_pairs={{0,1},{1,2},{2,3},{3,4},{4,5},{5,6},{6,7},{8,9},{9,10},{10,11},{11... | collective-permute-start | bytes 49160 | tf_op jit(solution)/shard_map/ppermute | solution.py:474
  54.6 1.9 %collective-permute-start.8 = (f32[2,16,128]{2,1,0:T(8,128)S(1)}, f32[2,16,128]{2,1,0:T(8,128)S(1)}, u32[]{:S(2)}, u32[]{:S(2)}) collective-permute-start(f32[2,16,128]{2,1,0:T(8,128)S(1)} %get-tuple-element.28), channel_id=1, source_target_pairs={{1,0},{2,1},{3,2},{4,3},{5,4},{6,5},{7,6},{9,8},{10,9},{11,10},{12... | collective-permute-start | bytes 49160 | tf_op jit(solution)/shard_map/ppermute | solution.py:474
  56.5 3.1 %collective-permute-done.8 = f32[2,16,128]{2,1,0:T(8,128)S(1)} collective-permute-done((f32[2,16,128]{2,1,0:T(8,128)S(1)}, f32[2,16,128]{2,1,0:T(8,128)S(1)}, u32[]{:S(2)}, u32[]{:S(2)}) %collective-permute-start.8) | collective-permute-done | bytes 16416 | tf_op jit(solution)/shard_map/ppermute | solution.py:474
  59.7 1.9 %collective-permute-start.11 = (f32[20,16,128]{2,1,0:T(8,128)S(1)}, f32[20,16,128]{2,1,0:T(8,128)S(1)}, u32[]{:S(2)}, u32[]{:S(2)}) collective-permute-start(f32[20,16,128]{2,1,0:T(8,128)S(1)} %constant_dynamic-update-slice_fusion.1.forcing_ref.refs_7_), channel_id=1, source_target_pairs={{8,0},{16,8},{24,16},{32,24},{40,32},{48,40},{56,48},{64,56},{72,6... | collective-permute-start | bytes 491528 | tf_op jit(solution)/shard_map/ppermute | solution.py:474
  61.6 3.4 %collective-permute-start.10 = (f32[20,16,128]{2,1,0:T(8,128)S(1)}, f32[20,16,128]{2,1,0:T(8,128)S(1)}, u32[]{:S(2)}, u32[]{:S(2)}) collective-permute-start(f32[20,16,128]{2,1,0:T(8,128)S(1)} %constant_dynamic-update-slice_fusion.1.forcing_ref.refs_7_), channel_id=1, source_target_pairs={{0,8},{8,16},{16,24},{24,32},{32,40},{40,48},{48,56},{56,64},{64,7... | collective-permute-start | bytes 491528 | tf_op jit(solution)/shard_map/ppermute | solution.py:474
  65.0 3.5 %collective-permute-start.12 = (f32[8,16,128]{2,1,0:T(8,128)S(1)}, f32[8,16,128]{2,1,0:T(8,128)S(1)}, u32[]{:S(2)}, u32[]{:S(2)}) collective-permute-start(f32[8,16,128]{2,1,0:T(8,128)S(1)} %slice.8), channel_id=1, source_target_pairs={{16,0},{24,8},{32,16},{40,24},{48,32},{56,40},{64,48},{72,56},{80,... | collective-permute-start | bytes 196616 | tf_op jit(solution)/shard_map/ppermute | solution.py:474
  68.5 2.7 %collective-permute-start.9 = (f32[8,16,128]{2,1,0:T(8,128)S(1)}, f32[8,16,128]{2,1,0:T(8,128)S(1)}, u32[]{:S(2)}, u32[]{:S(2)}) collective-permute-start(f32[8,16,128]{2,1,0:T(8,128)S(1)} %slice.8), channel_id=1, source_target_pairs={{0,16},{8,24},{16,32},{24,40},{32,48},{40,56},{48,64},{56,72},{64,... | collective-permute-start | bytes 196616 | tf_op jit(solution)/shard_map/ppermute | solution.py:474
  71.3 0.6 copy-done.6
  71.9 3.8 %tracer_steps.2.refs_17_ = f32[5,16,256]{2,1,0:T(8,128)S(1)} custom-call(s32[4]{0:T(128)S(1)} %pad_add_fusion.place_ref.refs_0_, f32[8]{0:T(128)S(1)} %bitcast.34, f32[20,16,128]{2,1,0:T(8,128)S(1)} %collective-permute-done.10.forcing_before_ref.refs_6_, f32[20,16,128]{2,1,0:T(8,128)S(1)} %constant_dynamic-update-slice_fusion.1.forcing_ref.refs_7_, ...), custom_call_target="tpu_custom_call" | custom-call | flops 10000000 | bytes 4000000 | tf_op jit(solution)/shard_map/tracer_steps/pallas_call | solution.py:343
  75.7 1.5 collective-permute-done.9.refs_5_
  77.2 4.3 %wave_steps.1 = (f32[8,16,256]{2,1,0:T(8,128)S(1)}, bf16[128,256]{1,0:T(8,128)(2,1)S(1)}, f32[2,16,128]{2,1,0:T(8,128)S(1)}, f32[2,16,128]{2,1,0:T(8,128)S(1)}) custom-call(s32[4]{0:T(128)S(1)} %pad_add_fusion.place_ref.refs_0_, f32[8]{0:T(128)S(1)} %bitcast.35, f32[2]{0:T(128)S(1)} %bitcast.38, f32[8,8]{1,0:T(8,128)S(1)} %bitcast.29, f32[8,8]{1,0:T(8,128)S(1)} %bitcast.32, ...), custom_call_target="tpu_custom_call" | custom-call | tf_op jit(solution)/shard_map/wave_steps/pallas_call | solution.py:456
  81.5 1.9 %collective-permute-start.13 = (bf16[128,256]{1,0:T(8,128)(2,1)S(1)}, bf16[128,256]{1,0:T(8,128)(2,1)S(1)}, u32[]{:S(2)}, u32[]{:S(2)}) collective-permute-start(bf16[128,256]{1,0:T(8,128)(2,1)S(1)} %get-tuple-element.30), channel_id=1, source_target_pairs={{0,256},{256,0},{1,257},{257,1},{2,258},{258,2},{3,259},{259,3},{4... | collective-permute-start | bytes 196616 | tf_op jit(solution)/shard_map/ppermute | solution.py:502
  83.5 4.5 %collective-permute-start.14 = (f32[2,16,128]{2,1,0:T(8,128)S(1)}, f32[2,16,128]{2,1,0:T(8,128)S(1)}, u32[]{:S(2)}, u32[]{:S(2)}) collective-permute-start(f32[2,16,128]{2,1,0:T(8,128)S(1)} %get-tuple-element.32), channel_id=1, source_target_pairs={{0,1},{1,2},{2,3},{3,4},{4,5},{5,6},{6,7},{8,9},{9,10},{10,11},{11... | collective-permute-start | bytes 49160 | tf_op jit(solution)/shard_map/ppermute | solution.py:474
  88.0 1.9 %collective-permute-start.15 = (f32[2,16,128]{2,1,0:T(8,128)S(1)}, f32[2,16,128]{2,1,0:T(8,128)S(1)}, u32[]{:S(2)}, u32[]{:S(2)}) collective-permute-start(f32[2,16,128]{2,1,0:T(8,128)S(1)} %get-tuple-element.33), channel_id=1, source_target_pairs={{1,0},{2,1},{3,2},{4,3},{5,4},{6,5},{7,6},{9,8},{10,9},{11,10},{12... | collective-permute-start | bytes 49160 | tf_op jit(solution)/shard_map/ppermute | solution.py:474
  89.9 3.1 %collective-permute-done.15.right_ref.refs_16_ = f32[2,16,128]{2,1,0:T(8,128)S(1)} collective-permute-done((f32[2,16,128]{2,1,0:T(8,128)S(1)}, f32[2,16,128]{2,1,0:T(8,128)S(1)}, u32[]{:S(2)}, u32[]{:S(2)}) %collective-permute-start.15) | collective-permute-done | bytes 16416 | tf_op jit(solution)/shard_map/ppermute | solution.py:474
  93.1 1.9 %collective-permute-start.18 = (bf16[56,16,128]{2,1,0:T(8,128)(2,1)S(1)}, bf16[56,16,128]{2,1,0:T(8,128)(2,1)S(1)}, u32[]{:S(2)}, u32[]{:S(2)}) collective-permute-start(bf16[56,16,128]{2,1,0:T(8,128)(2,1)S(1)} %get-tuple-element.35), channel_id=1, source_target_pairs={{8,0},{16,8},{24,16},{32,24},{40,32},{48,40},{56,48},{64,56},{72,6... | collective-permute-start | bytes 688136 | tf_op jit(solution)/shard_map/ppermute | solution.py:474
  95.0 3.4 %collective-permute-start.17 = (bf16[56,16,128]{2,1,0:T(8,128)(2,1)S(1)}, bf16[56,16,128]{2,1,0:T(8,128)(2,1)S(1)}, u32[]{:S(2)}, u32[]{:S(2)}) collective-permute-start(bf16[56,16,128]{2,1,0:T(8,128)(2,1)S(1)} %get-tuple-element.35), channel_id=1, source_target_pairs={{0,8},{8,16},{16,24},{24,32},{32,40},{40,48},{48,56},{56,64},{64,7... | collective-permute-start | bytes 688136 | tf_op jit(solution)/shard_map/ppermute | solution.py:474
  98.4 4.6 %collective-permute-start.19 = (bf16[32,16,128]{2,1,0:T(8,128)(2,1)S(1)}, bf16[32,16,128]{2,1,0:T(8,128)(2,1)S(1)}, u32[]{:S(2)}, u32[]{:S(2)}) collective-permute-start(bf16[32,16,128]{2,1,0:T(8,128)(2,1)S(1)} %get-tuple-element.34), channel_id=1, source_target_pairs={{16,0},{24,8},{32,16},{40,24},{48,32},{56,40},{64,48},{72,56},{80,... | collective-permute-start | bytes 393224 | tf_op jit(solution)/shard_map/ppermute | solution.py:474
  103.1 1.9 %collective-permute-start.16 = (bf16[32,16,128]{2,1,0:T(8,128)(2,1)S(1)}, bf16[32,16,128]{2,1,0:T(8,128)(2,1)S(1)}, u32[]{:S(2)}, u32[]{:S(2)}) collective-permute-start(bf16[32,16,128]{2,1,0:T(8,128)(2,1)S(1)} %get-tuple-element.34), channel_id=1, source_target_pairs={{0,16},{8,24},{16,32},{24,40},{32,48},{40,56},{48,64},{56,72},{64,... | collective-permute-start | bytes 393224 | tf_op jit(solution)/shard_map/ppermute | solution.py:474
  105.0 3.1 %collective-permute-done.19.far_after_ref.refs_13_ = bf16[32,16,128]{2,1,0:T(8,128)(2,1)S(1)} collective-permute-done((bf16[32,16,128]{2,1,0:T(8,128)(2,1)S(1)}, bf16[32,16,128]{2,1,0:T(8,128)(2,1)S(1)}, u32[]{:S(2)}, u32[]{:S(2)}) %collective-permute-start.19) | collective-permute-done | bytes 131104 | tf_op jit(solution)/shard_map/ppermute | solution.py:474
  108.1 7.5 %collective-permute-done.16.far_before_ref.refs_10_ = bf16[32,16,128]{2,1,0:T(8,128)(2,1)S(1)} collective-permute-done((bf16[32,16,128]{2,1,0:T(8,128)(2,1)S(1)}, bf16[32,16,128]{2,1,0:T(8,128)(2,1)S(1)}, u32[]{:S(2)}, u32[]{:S(2)}) %collective-permute-start.16) | collective-permute-done | bytes 131104 | tf_op jit(solution)/shard_map/ppermute | solution.py:474
  115.6 1.8 %remap.3 = (f32[20,16,128]{2,1,0:T(8,128)S(1)}, f32[2,16,128]{2,1,0:T(8,128)S(1)}, f32[2,16,128]{2,1,0:T(8,128)S(1)}, f32[8,16,256]{2,1,0:T(8,128)}) custom-call(s32[128]{0:T(128)S(1)} %multiply_add_fusion.index_ref, bf16[32,16,128]{2,1,0:T(8,128)(2,1)S(1)} %collective-permute-done.16.far_before_ref.refs_10_, ...), custom_call_target="tpu_custom_call" | custom-call | tf_op jit(solution)/shard_map/remap/pallas_call | solution.py:224
  117.4 4.1 %collective-permute-start.20 = (f32[2,16,128]{2,1,0:T(8,128)S(1)}, f32[2,16,128]{2,1,0:T(8,128)S(1)}, u32[]{:S(2)}, u32[]{:S(2)}) collective-permute-start(f32[2,16,128]{2,1,0:T(8,128)S(1)} %get-tuple-element.37), channel_id=1, source_target_pairs={{0,1},{1,2},{2,3},{3,4},{4,5},{5,6},{6,7},{8,9},{9,10},{10,11},{11... | collective-permute-start | bytes 49160 | tf_op jit(solution)/shard_map/ppermute | solution.py:474
  121.5 1.9 %collective-permute-start.21 = (f32[2,16,128]{2,1,0:T(8,128)S(1)}, f32[2,16,128]{2,1,0:T(8,128)S(1)}, u32[]{:S(2)}, u32[]{:S(2)}) collective-permute-start(f32[2,16,128]{2,1,0:T(8,128)S(1)} %get-tuple-element.38), channel_id=1, source_target_pairs={{1,0},{2,1},{3,2},{4,3},{5,4},{6,5},{7,6},{9,8},{10,9},{11,10},{12... | collective-permute-start | bytes 49160 | tf_op jit(solution)/shard_map/ppermute | solution.py:474
  123.5 3.1 %collective-permute-done.21 = f32[2,16,128]{2,1,0:T(8,128)S(1)} collective-permute-done((f32[2,16,128]{2,1,0:T(8,128)S(1)}, f32[2,16,128]{2,1,0:T(8,128)S(1)}, u32[]{:S(2)}, u32[]{:S(2)}) %collective-permute-start.21) | collective-permute-done | bytes 16416 | tf_op jit(solution)/shard_map/ppermute | solution.py:474
  126.6 1.9 %collective-permute-start.24 = (f32[20,16,128]{2,1,0:T(8,128)S(1)}, f32[20,16,128]{2,1,0:T(8,128)S(1)}, u32[]{:S(2)}, u32[]{:S(2)}) collective-permute-start(f32[20,16,128]{2,1,0:T(8,128)S(1)} %constant_dynamic-update-slice_fusion.forcing_ref.refs_7_), channel_id=1, source_target_pairs={{8,0},{16,8},{24,16},{32,24},{40,32},{48,40},{56,48},{64,56},{72,6... | collective-permute-start | bytes 491528 | tf_op jit(solution)/shard_map/ppermute | solution.py:474
  128.5 3.4 %collective-permute-start.23 = (f32[20,16,128]{2,1,0:T(8,128)S(1)}, f32[20,16,128]{2,1,0:T(8,128)S(1)}, u32[]{:S(2)}, u32[]{:S(2)}) collective-permute-start(f32[20,16,128]{2,1,0:T(8,128)S(1)} %constant_dynamic-update-slice_fusion.forcing_ref.refs_7_), channel_id=1, source_target_pairs={{0,8},{8,16},{16,24},{24,32},{32,40},{40,48},{48,56},{56,64},{64,7... | collective-permute-start | bytes 491528 | tf_op jit(solution)/shard_map/ppermute | solution.py:474
  131.9 3.3 %collective-permute-start.25 = (f32[8,16,128]{2,1,0:T(8,128)S(1)}, f32[8,16,128]{2,1,0:T(8,128)S(1)}, u32[]{:S(2)}, u32[]{:S(2)}) collective-permute-start(f32[8,16,128]{2,1,0:T(8,128)S(1)} %slice.9), channel_id=1, source_target_pairs={{16,0},{24,8},{32,16},{40,24},{48,32},{56,40},{64,48},{72,56},{80,... | collective-permute-start | bytes 196616 | tf_op jit(solution)/shard_map/ppermute | solution.py:474
  135.2 2.9 %collective-permute-start.22 = (f32[8,16,128]{2,1,0:T(8,128)S(1)}, f32[8,16,128]{2,1,0:T(8,128)S(1)}, u32[]{:S(2)}, u32[]{:S(2)}) collective-permute-start(f32[8,16,128]{2,1,0:T(8,128)S(1)} %slice.9), channel_id=1, source_target_pairs={{0,16},{8,24},{16,32},{24,40},{32,48},{40,56},{48,64},{56,72},{64,... | collective-permute-start | bytes 196616 | tf_op jit(solution)/shard_map/ppermute | solution.py:474
  138.1 3.8 %tracer_steps.3.refs_17_ = f32[5,16,256]{2,1,0:T(8,128)S(1)} custom-call(s32[4]{0:T(128)S(1)} %pad_add_fusion.place_ref.refs_0_, f32[8]{0:T(128)S(1)} %bitcast.36, f32[20,16,128]{2,1,0:T(8,128)S(1)} %collective-permute-done.23.forcing_before_ref.refs_6_, f32[20,16,128]{2,1,0:T(8,128)S(1)} %constant_dynamic-update-slice_fusion.forcing_ref.refs_7_, ...), custom_call_target="tpu_custom_call" | custom-call | flops 10000000 | bytes 4000000 | tf_op jit(solution)/shard_map/tracer_steps/pallas_call | solution.py:343
  142.0 1.5 collective-permute-done.22.refs_5_
  143.4 4.8 %wave_steps_last.1 = f32[8,16,256]{2,1,0:T(8,128)} custom-call(s32[4]{0:T(128)S(1)} %pad_add_fusion.place_ref.refs_0_, f32[8]{0:T(128)S(1)} %bitcast.37, f32[2]{0:T(128)S(1)} %bitcast.39, f32[8,8]{1,0:T(8,128)S(1)} %bitcast.30, f32[8,8]{1,0:T(8,128)S(1)} %bitcast.33, f32[8,16,128]{2,1,0:T(8,128)S(1)} %collective-permute-done.22.refs_5_, ...), custom_call_target="tpu_custom_call" | custom-call | tf_op jit(solution)/shard_map/wave_steps_last/pallas_call | solution.py:456
  (48 shorter events, 0.5 us)
Async XLA Ops:
  0.6 22.6 %copy-start.2 = (f32[1,8,16,256]{3,2,1,0:T(8,128)S(1)}, f32[1,8,16,256]{3,2,1,0:T(8,128)}, u32[]{:S(2)}) copy-start(f32[1,8,16,256]{3,2,1,0:T(8,128)} %param.10) | copy-start | bytes 393220
  3.4 19.9 %collective-permute-start = (bf16[128,256]{1,0:T(8,128)(2,1)}, bf16[128,256]{1,0:T(8,128)(2,1)S(1)}, u32[]{:S(2)}, u32[]{:S(2)}) collective-permute-start(bf16[128,256]{1,0:T(8,128)(2,1)} %get-tuple-element.21), channel_id=1, source_target_pairs={{0,256},{256,0},{1,257},{257,1},{2,258},{258,2},{3,259},{259,3},{4... | collective-permute-start | bytes 196616 | tf_op jit(solution)/shard_map/ppermute | solution.py:502
  14.1 5.9 %collective-permute-start.1 = (f32[2,16,128]{2,1,0:T(8,128)}, f32[2,16,128]{2,1,0:T(8,128)S(1)}, u32[]{:S(2)}, u32[]{:S(2)}) collective-permute-start(f32[2,16,128]{2,1,0:T(8,128)} %get-tuple-element.22), channel_id=1, source_target_pairs={{0,1},{1,2},{2,3},{3,4},{4,5},{5,6},{6,7},{8,9},{9,10},{10,11},{11... | collective-permute-start | bytes 49160 | tf_op jit(solution)/shard_map/ppermute | solution.py:474
  18.0 5.3 %collective-permute-start.2 = (f32[2,16,128]{2,1,0:T(8,128)}, f32[2,16,128]{2,1,0:T(8,128)S(1)}, u32[]{:S(2)}, u32[]{:S(2)}) collective-permute-start(f32[2,16,128]{2,1,0:T(8,128)} %get-tuple-element.23), channel_id=1, source_target_pairs={{1,0},{2,1},{3,2},{4,3},{5,4},{6,5},{7,6},{9,8},{10,9},{11,10},{12... | collective-permute-start | bytes 49160 | tf_op jit(solution)/shard_map/ppermute | solution.py:474
  23.3 5.4 %copy-start.9 = (s32[1,16,4,2]{1,3,2,0:T(2,128)S(1)}, s32[1,16,4,2]{1,3,2,0:T(2,128)}, u32[]{:S(2)}) copy-start(s32[1,16,4,2]{1,3,2,0:T(2,128)} %param.17) | copy-start | bytes 1540
  23.3 24.6 %collective-permute-start.5 = (bf16[56,16,128]{2,1,0:T(8,128)(2,1)S(1)}, bf16[56,16,128]{2,1,0:T(8,128)(2,1)S(1)}, u32[]{:S(2)}, u32[]{:S(2)}) collective-permute-start(bf16[56,16,128]{2,1,0:T(8,128)(2,1)S(1)} %get-tuple-element.25), channel_id=1, source_target_pairs={{8,0},{16,8},{24,16},{32,24},{40,32},{48,40},{56,48},{64,56},{72,6... | collective-permute-start | bytes 688136 | tf_op jit(solution)/shard_map/ppermute | solution.py:474
  25.4 22.5 %collective-permute-start.4 = (bf16[56,16,128]{2,1,0:T(8,128)(2,1)S(1)}, bf16[56,16,128]{2,1,0:T(8,128)(2,1)S(1)}, u32[]{:S(2)}, u32[]{:S(2)}) collective-permute-start(bf16[56,16,128]{2,1,0:T(8,128)(2,1)S(1)} %get-tuple-element.25), channel_id=1, source_target_pairs={{0,8},{8,16},{16,24},{24,32},{32,40},{40,48},{48,56},{56,64},{64,7... | collective-permute-start | bytes 688136 | tf_op jit(solution)/shard_map/ppermute | solution.py:474
  28.8 0.7 copy-start.8
  29.6 18.4 %copy-start.3 = (s32[1,16,256]{2,1,0:T(8,128)S(1)}, s32[1,16,256]{2,1,0:T(8,128)}, u32[]{:S(2)}) copy-start(s32[1,16,256]{2,1,0:T(8,128)} %param.12) | copy-start | bytes 49156
  29.7 11.0 %collective-permute-start.6 = (bf16[32,16,128]{2,1,0:T(8,128)(2,1)S(1)}, bf16[32,16,128]{2,1,0:T(8,128)(2,1)S(1)}, u32[]{:S(2)}, u32[]{:S(2)}) collective-permute-start(bf16[32,16,128]{2,1,0:T(8,128)(2,1)S(1)} %get-tuple-element.24), channel_id=1, source_target_pairs={{16,0},{24,8},{32,16},{40,24},{48,32},{56,40},{64,48},{72,56},{80,... | collective-permute-start | bytes 393224 | tf_op jit(solution)/shard_map/ppermute | solution.py:474
  36.8 11.2 %collective-permute-start.3 = (bf16[32,16,128]{2,1,0:T(8,128)(2,1)S(1)}, bf16[32,16,128]{2,1,0:T(8,128)(2,1)S(1)}, u32[]{:S(2)}, u32[]{:S(2)}) collective-permute-start(bf16[32,16,128]{2,1,0:T(8,128)(2,1)S(1)} %get-tuple-element.24), channel_id=1, source_target_pairs={{0,16},{8,24},{16,32},{24,40},{32,48},{40,56},{48,64},{56,72},{64,... | collective-permute-start | bytes 393224 | tf_op jit(solution)/shard_map/ppermute | solution.py:474
  48.0 1.2 copy-start
  50.5 6.1 %collective-permute-start.7 = (f32[2,16,128]{2,1,0:T(8,128)S(1)}, f32[2,16,128]{2,1,0:T(8,128)S(1)}, u32[]{:S(2)}, u32[]{:S(2)}) collective-permute-start(f32[2,16,128]{2,1,0:T(8,128)S(1)} %get-tuple-element.27), channel_id=1, source_target_pairs={{0,1},{1,2},{2,3},{3,4},{4,5},{5,6},{6,7},{8,9},{9,10},{10,11},{11... | collective-permute-start | bytes 49160 | tf_op jit(solution)/shard_map/ppermute | solution.py:474
  54.6 5.1 %collective-permute-start.8 = (f32[2,16,128]{2,1,0:T(8,128)S(1)}, f32[2,16,128]{2,1,0:T(8,128)S(1)}, u32[]{:S(2)}, u32[]{:S(2)}) collective-permute-start(f32[2,16,128]{2,1,0:T(8,128)S(1)} %get-tuple-element.28), channel_id=1, source_target_pairs={{1,0},{2,1},{3,2},{4,3},{5,4},{6,5},{7,6},{9,8},{10,9},{11,10},{12... | collective-permute-start | bytes 49160 | tf_op jit(solution)/shard_map/ppermute | solution.py:474
  59.7 11.6 %collective-permute-start.11 = (f32[20,16,128]{2,1,0:T(8,128)S(1)}, f32[20,16,128]{2,1,0:T(8,128)S(1)}, u32[]{:S(2)}, u32[]{:S(2)}) collective-permute-start(f32[20,16,128]{2,1,0:T(8,128)S(1)} %constant_dynamic-update-slice_fusion.1.forcing_ref.refs_7_), channel_id=1, source_target_pairs={{8,0},{16,8},{24,16},{32,24},{40,32},{48,40},{56,48},{64,56},{72,6... | collective-permute-start | bytes 491528 | tf_op jit(solution)/shard_map/ppermute | solution.py:474
  61.6 9.7 %collective-permute-start.10 = (f32[20,16,128]{2,1,0:T(8,128)S(1)}, f32[20,16,128]{2,1,0:T(8,128)S(1)}, u32[]{:S(2)}, u32[]{:S(2)}) collective-permute-start(f32[20,16,128]{2,1,0:T(8,128)S(1)} %constant_dynamic-update-slice_fusion.1.forcing_ref.refs_7_), channel_id=1, source_target_pairs={{0,8},{8,16},{16,24},{24,32},{32,40},{40,48},{48,56},{56,64},{64,7... | collective-permute-start | bytes 491528 | tf_op jit(solution)/shard_map/ppermute | solution.py:474
  65.0 10.8 %collective-permute-start.12 = (f32[8,16,128]{2,1,0:T(8,128)S(1)}, f32[8,16,128]{2,1,0:T(8,128)S(1)}, u32[]{:S(2)}, u32[]{:S(2)}) collective-permute-start(f32[8,16,128]{2,1,0:T(8,128)S(1)} %slice.8), channel_id=1, source_target_pairs={{16,0},{24,8},{32,16},{40,24},{48,32},{56,40},{64,48},{72,56},{80,... | collective-permute-start | bytes 196616 | tf_op jit(solution)/shard_map/ppermute | solution.py:474
  68.5 8.7 %collective-permute-start.9 = (f32[8,16,128]{2,1,0:T(8,128)S(1)}, f32[8,16,128]{2,1,0:T(8,128)S(1)}, u32[]{:S(2)}, u32[]{:S(2)}) collective-permute-start(f32[8,16,128]{2,1,0:T(8,128)S(1)} %slice.8), channel_id=1, source_target_pairs={{0,16},{8,24},{16,32},{24,40},{32,48},{40,56},{48,64},{56,72},{64,... | collective-permute-start | bytes 196616 | tf_op jit(solution)/shard_map/ppermute | solution.py:474
  71.2 0.7 copy-start.6
  71.9 5.3 %copy-start.4 = (f32[1,8,8]{2,1,0:T(8,128)S(1)}, f32[1,8,8]{2,1,0:T(8,128)}, u32[]{:S(2)}) copy-start(f32[1,8,8]{2,1,0:T(8,128)} %param.13) | copy-start | bytes 772
  71.9 5.3 %copy-start.5 = (f32[1,8,8]{2,1,0:T(8,128)S(1)}, f32[1,8,8]{2,1,0:T(8,128)}, u32[]{:S(2)}) copy-start(f32[1,8,8]{2,1,0:T(8,128)} %param.14) | copy-start | bytes 772
  71.9 5.3 %copy-start.7 = (f32[1,2]{1,0:T(1,128)S(1)}, f32[1,2]{1,0:T(1,128)}, u32[]{:S(2)}) copy-start(f32[1,2]{1,0:T(1,128)} %param.16) | copy-start | bytes 28
  75.7 39.9 %copy-start.1 = (bf16[1,16,4,64,128]{4,3,2,1,0:T(8,128)(2,1)S(1)}, bf16[1,16,4,64,128]{4,3,2,1,0:T(8,128)(2,1)}, u32[]{:S(2)}) copy-start(bf16[1,16,4,64,128]{4,3,2,1,0:T(8,128)(2,1)} %param.19) | copy-start | bytes 3145732
  81.5 11.5 %collective-permute-start.13 = (bf16[128,256]{1,0:T(8,128)(2,1)S(1)}, bf16[128,256]{1,0:T(8,128)(2,1)S(1)}, u32[]{:S(2)}, u32[]{:S(2)}) collective-permute-start(bf16[128,256]{1,0:T(8,128)(2,1)S(1)} %get-tuple-element.30), channel_id=1, source_target_pairs={{0,256},{256,0},{1,257},{257,1},{2,258},{258,2},{3,259},{259,3},{4... | collective-permute-start | bytes 196616 | tf_op jit(solution)/shard_map/ppermute | solution.py:502
  83.5 6.5 %collective-permute-start.14 = (f32[2,16,128]{2,1,0:T(8,128)S(1)}, f32[2,16,128]{2,1,0:T(8,128)S(1)}, u32[]{:S(2)}, u32[]{:S(2)}) collective-permute-start(f32[2,16,128]{2,1,0:T(8,128)S(1)} %get-tuple-element.32), channel_id=1, source_target_pairs={{0,1},{1,2},{2,3},{3,4},{4,5},{5,6},{6,7},{8,9},{9,10},{10,11},{11... | collective-permute-start | bytes 49160 | tf_op jit(solution)/shard_map/ppermute | solution.py:474
  88.0 5.1 %collective-permute-start.15 = (f32[2,16,128]{2,1,0:T(8,128)S(1)}, f32[2,16,128]{2,1,0:T(8,128)S(1)}, u32[]{:S(2)}, u32[]{:S(2)}) collective-permute-start(f32[2,16,128]{2,1,0:T(8,128)S(1)} %get-tuple-element.33), channel_id=1, source_target_pairs={{1,0},{2,1},{3,2},{4,3},{5,4},{6,5},{7,6},{9,8},{10,9},{11,10},{12... | collective-permute-start | bytes 49160 | tf_op jit(solution)/shard_map/ppermute | solution.py:474
  93.1 22.5 %collective-permute-start.18 = (bf16[56,16,128]{2,1,0:T(8,128)(2,1)S(1)}, bf16[56,16,128]{2,1,0:T(8,128)(2,1)S(1)}, u32[]{:S(2)}, u32[]{:S(2)}) collective-permute-start(bf16[56,16,128]{2,1,0:T(8,128)(2,1)S(1)} %get-tuple-element.35), channel_id=1, source_target_pairs={{8,0},{16,8},{24,16},{32,24},{40,32},{48,40},{56,48},{64,56},{72,6... | collective-permute-start | bytes 688136 | tf_op jit(solution)/shard_map/ppermute | solution.py:474
  95.0 20.6 %collective-permute-start.17 = (bf16[56,16,128]{2,1,0:T(8,128)(2,1)S(1)}, bf16[56,16,128]{2,1,0:T(8,128)(2,1)S(1)}, u32[]{:S(2)}, u32[]{:S(2)}) collective-permute-start(bf16[56,16,128]{2,1,0:T(8,128)(2,1)S(1)} %get-tuple-element.35), channel_id=1, source_target_pairs={{0,8},{8,16},{16,24},{24,32},{32,40},{40,48},{48,56},{56,64},{64,7... | collective-permute-start | bytes 688136 | tf_op jit(solution)/shard_map/ppermute | solution.py:474
  98.4 9.7 %collective-permute-start.19 = (bf16[32,16,128]{2,1,0:T(8,128)(2,1)S(1)}, bf16[32,16,128]{2,1,0:T(8,128)(2,1)S(1)}, u32[]{:S(2)}, u32[]{:S(2)}) collective-permute-start(bf16[32,16,128]{2,1,0:T(8,128)(2,1)S(1)} %get-tuple-element.34), channel_id=1, source_target_pairs={{16,0},{24,8},{32,16},{40,24},{48,32},{56,40},{64,48},{72,56},{80,... | collective-permute-start | bytes 393224 | tf_op jit(solution)/shard_map/ppermute | solution.py:474
  103.1 12.5 %collective-permute-start.16 = (bf16[32,16,128]{2,1,0:T(8,128)(2,1)S(1)}, bf16[32,16,128]{2,1,0:T(8,128)(2,1)S(1)}, u32[]{:S(2)}, u32[]{:S(2)}) collective-permute-start(bf16[32,16,128]{2,1,0:T(8,128)(2,1)S(1)} %get-tuple-element.34), channel_id=1, source_target_pairs={{0,16},{8,24},{16,32},{24,40},{32,48},{40,56},{48,64},{56,72},{64,... | collective-permute-start | bytes 393224 | tf_op jit(solution)/shard_map/ppermute | solution.py:474
  117.4 6.0 %collective-permute-start.20 = (f32[2,16,128]{2,1,0:T(8,128)S(1)}, f32[2,16,128]{2,1,0:T(8,128)S(1)}, u32[]{:S(2)}, u32[]{:S(2)}) collective-permute-start(f32[2,16,128]{2,1,0:T(8,128)S(1)} %get-tuple-element.37), channel_id=1, source_target_pairs={{0,1},{1,2},{2,3},{3,4},{4,5},{5,6},{6,7},{8,9},{9,10},{10,11},{11... | collective-permute-start | bytes 49160 | tf_op jit(solution)/shard_map/ppermute | solution.py:474
  121.5 5.1 %collective-permute-start.21 = (f32[2,16,128]{2,1,0:T(8,128)S(1)}, f32[2,16,128]{2,1,0:T(8,128)S(1)}, u32[]{:S(2)}, u32[]{:S(2)}) collective-permute-start(f32[2,16,128]{2,1,0:T(8,128)S(1)} %get-tuple-element.38), channel_id=1, source_target_pairs={{1,0},{2,1},{3,2},{4,3},{5,4},{6,5},{7,6},{9,8},{10,9},{11,10},{12... | collective-permute-start | bytes 49160 | tf_op jit(solution)/shard_map/ppermute | solution.py:474
  126.6 11.5 %collective-permute-start.24 = (f32[20,16,128]{2,1,0:T(8,128)S(1)}, f32[20,16,128]{2,1,0:T(8,128)S(1)}, u32[]{:S(2)}, u32[]{:S(2)}) collective-permute-start(f32[20,16,128]{2,1,0:T(8,128)S(1)} %constant_dynamic-update-slice_fusion.forcing_ref.refs_7_), channel_id=1, source_target_pairs={{8,0},{16,8},{24,16},{32,24},{40,32},{48,40},{56,48},{64,56},{72,6... | collective-permute-start | bytes 491528 | tf_op jit(solution)/shard_map/ppermute | solution.py:474
  128.5 9.6 %collective-permute-start.23 = (f32[20,16,128]{2,1,0:T(8,128)S(1)}, f32[20,16,128]{2,1,0:T(8,128)S(1)}, u32[]{:S(2)}, u32[]{:S(2)}) collective-permute-start(f32[20,16,128]{2,1,0:T(8,128)S(1)} %constant_dynamic-update-slice_fusion.forcing_ref.refs_7_), channel_id=1, source_target_pairs={{0,8},{8,16},{16,24},{24,32},{32,40},{40,48},{48,56},{56,64},{64,7... | collective-permute-start | bytes 491528 | tf_op jit(solution)/shard_map/ppermute | solution.py:474
  131.9 10.0 %collective-permute-start.25 = (f32[8,16,128]{2,1,0:T(8,128)S(1)}, f32[8,16,128]{2,1,0:T(8,128)S(1)}, u32[]{:S(2)}, u32[]{:S(2)}) collective-permute-start(f32[8,16,128]{2,1,0:T(8,128)S(1)} %slice.9), channel_id=1, source_target_pairs={{16,0},{24,8},{32,16},{40,24},{48,32},{56,40},{64,48},{72,56},{80,... | collective-permute-start | bytes 196616 | tf_op jit(solution)/shard_map/ppermute | solution.py:474
  135.2 8.2 %collective-permute-start.22 = (f32[8,16,128]{2,1,0:T(8,128)S(1)}, f32[8,16,128]{2,1,0:T(8,128)S(1)}, u32[]{:S(2)}, u32[]{:S(2)}) collective-permute-start(f32[8,16,128]{2,1,0:T(8,128)S(1)} %slice.9), channel_id=1, source_target_pairs={{0,16},{8,24},{16,32},{24,40},{32,48},{40,56},{48,64},{56,72},{64,... | collective-permute-start | bytes 196616 | tf_op jit(solution)/shard_map/ppermute | solution.py:474

commit v3 on v2

v3 whole, which is shorter than its diff:
```python
import jax
import jax.numpy as jnp
from jax import lax
from jax.experimental import pallas as pl
from jax.experimental.pallas import tpu as pltpu
from jax.sharding import PartitionSpec as P

SUBSTEPS = 16
ITERS = 2
DIFFUSION = 0.1
COUPLING = 0.2

FIELDS = 8
WAVES = 3
TRACERS = 5
ROWS = 16
COLS = 256
LANES = 128
TURNED = ROWS * FIELDS
STRIP = 32
STEPS_PER_PHASE = 4

T_PLANES = 12
W_PLANES = 8
A_WAVE = T_PLANES
A_EXPORT = A_WAVE + 2 * W_PLANES
A_PLANES = A_EXPORT + 16
B_WAVE = T_PLANES
B_BEHIND = B_WAVE + 2 * W_PLANES
B_PLANES = B_BEHIND + 2 * W_PLANES

PAD = 8
WAVE_SPEED = 8
ROW0, COL0, ROW_END, COL_END = 10, 11, 12, 13
SMEM = pl.BlockSpec(memory_space=pltpu.SMEM)
VMEM = pl.BlockSpec(memory_space=pltpu.VMEM)
HBM = pl.BlockSpec(memory_space=pl.ANY)

f32 = jnp.float32
bf16 = jnp.bfloat16


def params(mib=24):
    return pltpu.CompilerParams(vmem_limit_bytes=mib * 1024 * 1024)


def shaped(shape, dtype=f32):
    return jax.ShapeDtypeStruct(shape, dtype)


def half_of(value, half):
    return value[:, half * LANES : (half + 1) * LANES]


def write_export(fields, received, wet, smix_ref, imix_ref, turned, out_ref):
    scale = wet * jnp.sqrt(1.0 + fields[1] * fields[1] + fields[2] * fields[2])
    for c in range(FIELDS):
        total = smix_ref[c, 0] * fields[0]
        for k in range(1, FIELDS):
            total = total + smix_ref[c, k] * fields[k]
        other = imix_ref[c, 0] * received[0]
        for k in range(1, FIELDS):
            other = other + imix_ref[c, k] * received[k]
        value = scale * (total + other)
        for half in range(2):
            turned[half, pl.ds(c, ROWS, stride=FIELDS), :] = half_of(value, half)
    for half in range(2):
        out_ref[:, half * LANES : (half + 1) * LANES] = turned[half].astype(bf16)


def write_strips(fields, low_ref, high_ref):
    lane = lax.broadcasted_iota(jnp.int32, (ROWS, LANES), 1)
    groups = [fields[3:7], [fields[7]] + fields[0:3]]
    for p, group in enumerate(groups):
        first = group[0][0]
        last = pltpu.roll(group[0][1], STRIP, 1)
        for j in range(1, 4):
            here = lane >= STRIP * j
            first = jnp.where(here, pltpu.roll(group[j][0], STRIP * j, 1), first)
            moved = group[j][1] if j == 3 else pltpu.roll(group[j][1], STRIP * (j + 1), 1)
            last = jnp.where(here, moved, last)
        low_ref[p] = first
        high_ref[p] = last


def export_kernel(
    smix_ref, imix_ref, fields_ref, received_ref, land_ref,
    out_ref, low_ref, high_ref, fields_out, land_out, turned, received_buf, sems,
):
    copies = [
        pltpu.make_async_copy(fields_ref, fields_out, sems.at[0]),
        pltpu.make_async_copy(received_ref, received_buf, sems.at[1]),
        pltpu.make_async_copy(land_ref, land_out, sems.at[2]),
    ]
    for copy in copies:
        copy.start()
    for copy in copies:
        copy.wait()
    fields = [fields_out[c] for c in range(FIELDS)]
    received = [received_buf[c] for c in range(FIELDS)]
    write_export(fields, received, land_out[...].astype(f32), smix_ref, imix_ref, turned, out_ref)
    write_strips([[half_of(v, 0), half_of(v, 1)] for v in fields], low_ref, high_ref)


def export(fields, received, land, smix, imix):
    strips = shaped((2, ROWS, LANES))
    return pl.pallas_call(
        export_kernel,
        out_shape=(
            shaped((TURNED, COLS), bf16), strips, strips, shaped((FIELDS, ROWS, COLS)), shaped((ROWS, COLS), jnp.int32),
        ),
        in_specs=[SMEM, SMEM, HBM, HBM, HBM],
        out_specs=(VMEM,) * 5,
        scratch_shapes=[
            pltpu.VMEM((2, TURNED, LANES), f32),
            pltpu.VMEM((FIELDS, ROWS, COLS), f32),
            pltpu.SemaphoreType.DMA((3,)),
        ],
        compiler_params=params(56),
        name="export",
    )(smix, imix, fields, received, land)


def stage_kernel(weight_ref, out_ref, sem):
    copy = pltpu.make_async_copy(weight_ref, out_ref, sem)
    copy.start()
    copy.wait()


def stage(weight):
    return pl.pallas_call(
        stage_kernel,
        out_shape=shaped(weight.shape, weight.dtype),
        in_specs=[HBM],
        out_specs=VMEM,
        scratch_shapes=[pltpu.SemaphoreType.DMA],
        compiler_params=params(56),
        cost_estimate=pl.CostEstimate(flops=0, bytes_accessed=4_000_000, transcendentals=0),
        name="stage_weights",
    )(weight)


def split_to(ref, at, low_at, value):
    high = value.astype(bf16)
    ref[at] = high
    ref[low_at] = (value - high.astype(f32)).astype(bf16)


def write_halo(ref, base, fields, left, right):
    for i in range(TRACERS):
        for half in range(2):
            ref[2 * i + half] = fields(WAVES + i, half).astype(bf16)
    ref[10] = left[0].astype(bf16)
    ref[11] = right[0].astype(bf16)
    split_to(ref, base, base + W_PLANES, left[1])
    split_to(ref, base + 1, base + 1 + W_PLANES, right[1])
    for i in range(WAVES):
        for half in range(2):
            at = base + 2 + 2 * i + half
            split_to(ref, at, at + W_PLANES, fields(i, half))


def pack_kernel(opposite_ref, fields_ref, left_ref, right_ref, index_ref, config_ref, weight_ref, near_ref, far_ref):
    del index_ref, config_ref, weight_ref
    write_halo(
        near_ref, A_WAVE, lambda i, half: fields_ref[i, :, half * LANES : (half + 1) * LANES], left_ref, right_ref
    )
    for half in range(2):
        for i in range(TURNED // 16):
            part = opposite_ref[16 * i : 16 * i + 16, half * LANES : (half + 1) * LANES]
            near_ref[A_EXPORT + half * 8 + i] = part
            far_ref[half * 8 + i] = part


def pack(opposite, fields, left, right, index, config, weight):
    return pl.pallas_call(
        pack_kernel,
        out_shape=(shaped((A_PLANES, ROWS, LANES), bf16), shaped((16, ROWS, LANES), bf16)),
        in_specs=[VMEM] * 4 + [HBM] * 3,
        out_specs=(VMEM,) * 2,
        compiler_params=params(),
        name="pack",
    )(opposite, fields, left, right, index, config, weight)


def pack_forcing_kernel(
    forcing_ref, left_ref, right_ref, before_ref, after_ref, forward_ref, backward_ref, far_ref,
):
    for ref, behind in ((forward_ref, before_ref), (backward_ref, after_ref)):
        write_halo(
            ref, B_WAVE, lambda i, half: forcing_ref[i, :, half * LANES : (half + 1) * LANES], left_ref, right_ref
        )
        for p in range(2 * W_PLANES):
            ref[B_BEHIND + p] = behind[A_WAVE + p]
    for p in range(2 * W_PLANES):
        far_ref[p] = forward_ref[B_WAVE + p]


def pack_forcing(forcing, left, right, before, after):
    payload = shaped((B_PLANES, ROWS, LANES), bf16)
    return pl.pallas_call(
        pack_forcing_kernel,
        out_shape=(payload, payload, shaped((2 * W_PLANES, ROWS, LANES), bf16)),
        in_specs=[VMEM] * 5,
        out_specs=(VMEM,) * 3,
        compiler_params=params(),
        name="pack_forcing",
    )(forcing, left, right, before, after)


def remap_kernel(
    index_ref, far_before_ref, before_ref, opposite_ref, after_ref, far_after_ref, weight_ref, land_ref,
    forcing_ref, low_ref, high_ref, import_ref, table, turned,
):
    half_count = 5 * ROWS * 2
    windows = [far_before_ref, before_ref, opposite_ref, after_ref, far_after_ref]
    for w, ref in enumerate(windows):
        for half in range(2):
            for i in range(TURNED // 16):
                if w == 2:
                    chunk = ref[16 * i : 16 * i + 16, half * LANES : (half + 1) * LANES]
                else:
                    chunk = ref[(0 if w in (0, 4) else A_EXPORT) + half * 8 + i]
                chunk = chunk.astype(f32)
                for sub in range(2):
                    part = chunk[sub * 8 : sub * 8 + 8]
                    at = (w * ROWS + i * 2 + sub) * 2 + half
                    table[at] = part
                    table[half_count + at] = pltpu.roll(part, 64, 1)
    lane8 = lax.broadcasted_iota(jnp.int32, (8, LANES), 1)
    low_half = lane8 < 64
    ones = jnp.ones((8, LANES), f32)
    for x in range(ROWS):
        pieces = []
        for seg in range(4):
            at = (x * 4 + seg) * 2
            pieces.append(jnp.where(low_half, table[index_ref[at]], table[index_ref[at + 1]]))
        picked = jnp.concatenate(pieces + [ones], axis=0).astype(bf16)
        product = lax.dot_general(
            picked, weight_ref[x], (((1,), (1,)), ((), ())), preferred_element_type=f32
        )
        for half in range(2):
            cols = half_of(product, half)
            summed = jnp.where(low_half, cols[16 * half : 16 * half + 8], cols[16 * half + 8 : 16 * half + 16])
            turned[half, x * 8 : x * 8 + 8, :] = summed / cols[32:40]
    wet = land_ref[...].astype(f32)
    forcing = []
    for c in range(FIELDS):
        parts = []
        for half in range(2):
            value = turned[half, pl.ds(c, ROWS, stride=FIELDS), :]
            import_ref[c, :, half * LANES : (half + 1) * LANES] = value
            part = COUPLING * half_of(wet, half) * value
            forcing_ref[c, :, half * LANES : (half + 1) * LANES] = part
            parts.append(part)
        forcing.append(parts)
    write_strips(forcing, low_ref, high_ref)


def remap(index, windows, weight, land):
    strips = shaped((2, ROWS, LANES))
    return pl.pallas_call(
        remap_kernel,
        out_shape=(shaped((FIELDS, ROWS, COLS)), strips, strips, shaped((FIELDS, ROWS, COLS))),
        in_specs=[SMEM] + [VMEM] * 7,
        out_specs=(VMEM,) * 4,
        scratch_shapes=[
            pltpu.VMEM((2 * 5 * ROWS * 2, FIELDS, LANES), f32),
            pltpu.VMEM((2, TURNED, LANES), f32),
        ],
        compiler_params=params(),
        name="remap",
    )(index, *windows, weight, land)


def sides(left, right, j):
    lane = lax.broadcasted_iota(jnp.int32, (ROWS, LANES), 1)
    if j:
        right = pltpu.roll(right, LANES - STRIP * j, 1)
    if j != 3:
        left = pltpu.roll(left, 96 - STRIP * j, 1)
    return jnp.where(lane < STRIP, right, jnp.where(lane >= 96, left, 0.0))


def place_field(dest, rows, parts):
    for j, part in enumerate(parts):
        dest[j, rows, :] = part


def joined(ref, at, low_at):
    return ref[at].astype(f32) + ref[low_at].astype(f32)


def inside_tile(config_ref, first_row, count, j, shift=0):
    shape = (count, LANES)
    row = lax.broadcasted_iota(jnp.int32, shape, 0).astype(f32) + (config_ref[ROW0] + first_row)
    col = lax.broadcasted_iota(jnp.int32, shape, 1) + j * LANES
    if j == 2:
        col = jnp.where(col >= 3 * LANES - STRIP, col - 3 * LANES, col)
    col = (col + shift).astype(f32) + config_ref[COL0]
    ok = (row >= 0.0) & (row < config_ref[ROW_END]) & (col >= 0.0) & (col < config_ref[COL_END])
    return jnp.where(ok, 1.0, 0.0)


def westward(parts, lane, by=1):
    moved = [pltpu.roll(part, by, 1) for part in parts]
    return [jnp.where(lane < by, moved[j - 1], moved[j]) for j in range(3)]


def eastward(parts, lane, by=1):
    moved = [pltpu.roll(part, LANES - by, 1) for part in parts]
    return [jnp.where(lane >= LANES - by, moved[(j + 1) % 3], moved[j]) for j in range(3)]


def own_parts(fields_ref, left_ref, right_ref, i):
    p, j = (0, i - WAVES) if WAVES <= i < FIELDS - 1 else (1, (i + 1) % FIELDS)
    return [
        fields_ref[i, :, :LANES], fields_ref[i, :, LANES:], sides(left_ref[p], right_ref[p], j),
    ]


def tracer_parts(ref, wave_base, i):
    parts = [ref[2 * i].astype(f32), ref[2 * i + 1].astype(f32)]
    at = 10 if i < 4 else wave_base
    return parts + [sides(ref[at].astype(f32), ref[at + 1].astype(f32), i % 4)]


def wave_parts(ref, base, i):
    planes = [base + 2 + 2 * i, base + 3 + 2 * i, base, base + 1]
    first, second, left, right = [joined(ref, p, p + W_PLANES) for p in planes]
    return [first, second, sides(left, right, i + 1)]


def tracer_kernel(
    config_ref, forcing_before_ref, forcing_ref, forcing_left_ref, forcing_right_ref, forcing_after_ref,
    state_before_ref, fields_ref, left_ref, right_ref, state_after_ref, out_ref, state, forcing, coef,
):
    own_forcing = (forcing_ref, forcing_left_ref, forcing_right_ref)
    own_state = (fields_ref, left_ref, right_ref)
    for t, ref in enumerate((forcing_before_ref, None, forcing_after_ref)):
        rows = slice(t * ROWS, (t + 1) * ROWS)
        for i in range(TRACERS):
            parts = own_parts(*own_forcing, WAVES + i) if ref is None else tracer_parts(ref, B_WAVE, i)
            place_field(forcing.at[i], rows, parts)
    for t, ref in enumerate((state_before_ref, None, state_after_ref)):
        rows = slice(PAD + t * ROWS, PAD + (t + 1) * ROWS)
        for i in range(TRACERS):
            parts = own_parts(*own_state, WAVES + i) if ref is None else tracer_parts(ref, A_WAVE, i)
            place_field(state.at[0, i], rows, parts)
    height = 3 * ROWS
    for k in range(2):
        for i in range(TRACERS):
            for j in range(3):
                state[k, i, j, 0:PAD, :] = jnp.zeros((PAD, LANES), f32)
                state[k, i, j, PAD + height : height + 2 * PAD, :] = jnp.zeros((PAD, LANES), f32)
    for j in range(3):
        coef[j] = inside_tile(config_ref, -ROWS, height, j) * DIFFUSION

    lane = lax.broadcasted_iota(jnp.int32, (8, LANES), 1)
    keep = [(1.0 - config_ref[WAVES + c]) - 4.0 * DIFFUSION for c in range(TRACERS)]

    def step(source, dest, first, count):
        for t in range(first, first + count):
            at = PAD + 8 * t
            here = slice(8 * t, 8 * t + 8)
            for c in range(TRACERS):
                mid = [state[source, c, j, at : at + 8, :] for j in range(3)]
                west = westward(mid, lane)
                east = eastward(mid, lane)
                for j in range(3):
                    above = state[source, c, j, at + 1 : at + 9, :]
                    below = state[source, c, j, at - 1 : at + 7, :]
                    around = (above + below) + (east[j] + west[j])
                    state[dest, c, j, at : at + 8, :] = (
                        keep[c] * mid[j] + forcing[c, j, here, :]
                    ) + coef[j, here, :] * around

    def pair_of_steps(first, count):
        def run(_, carry):
            step(0, 1, first, count)
            step(1, 0, first, count)
            return carry
        return run

    lax.fori_loop(0, SUBSTEPS // 4, pair_of_steps(0, 6), 0)
    lax.fori_loop(0, SUBSTEPS // 4, pair_of_steps(1, 4), 0)
    for i in range(TRACERS):
        for half in range(2):
            out_ref[i, :, half * LANES : (half + 1) * LANES] = state[0, i, half, PAD + ROWS : PAD + 2 * ROWS, :]


def tracer_steps(config, operands):
    return pl.pallas_call(
        tracer_kernel,
        out_shape=shaped((TRACERS, ROWS, COLS)),
        in_specs=[SMEM] + [VMEM] * len(operands),
        out_specs=VMEM,
        scratch_shapes=[
            pltpu.VMEM((2, TRACERS, 3, 3 * ROWS + 2 * PAD, LANES), f32),
            pltpu.VMEM((TRACERS, 3, 3 * ROWS, LANES), f32),
            pltpu.VMEM((3, 3 * ROWS, LANES), f32),
        ],
        compiler_params=params(),
        cost_estimate=pl.CostEstimate(flops=10_000_000, bytes_accessed=4_000_000, transcendentals=0),
        name="tracer_steps",
    )(config, *operands)


def wave_kernel(last, config_ref, *refs):
    if not last:
        smix_ref, imix_ref, *refs = refs
    (far_before, near_before, forcing_ref, forcing_left_ref, forcing_right_ref, near_after, far_after,
     state_before, fields_ref, left_ref, right_ref, state_after, tracers_ref, *refs) = refs
    if last:
        out_ref, state, forcing, coef = refs
    else:
        received_ref, land_ref, out_ref, export_ref, low_ref, high_ref, state, forcing, coef, turned = refs
    height = 5 * ROWS
    tiles = height // 8

    for i in range(WAVES):
        forcing_tiles = [
            wave_parts(far_before, 0, i), wave_parts(near_before, B_WAVE, i),
            own_parts(forcing_ref, forcing_left_ref, forcing_right_ref, i),
            wave_parts(near_after, B_WAVE, i), wave_parts(far_after, 0, i),
        ]
        state_tiles = [
            wave_parts(near_before, B_BEHIND, i), wave_parts(state_before, A_WAVE, i),
            own_parts(fields_ref, left_ref, right_ref, i),
            wave_parts(state_after, A_WAVE, i), wave_parts(near_after, B_BEHIND, i),
        ]
        for t in range(5):
            rows = slice(PAD + t * ROWS, PAD + (t + 1) * ROWS)
            place_field(forcing.at[i], rows, forcing_tiles[t])
            place_field(state.at[i], rows, state_tiles[t])
        for j in range(3):
            for ref in (state, forcing):
                ref[i, j, 0:PAD, :] = jnp.zeros((PAD, LANES), f32)
                ref[i, j, PAD + height : height + 2 * PAD, :] = jnp.zeros((PAD, LANES), f32)
    half_a = 0.5 * config_ref[WAVE_SPEED]
    half_b = 0.5 * config_ref[WAVE_SPEED + 1]
    first_row = -2.0 * ROWS
    for j in range(3):
        coef[0, j] = inside_tile(config_ref, first_row, height, j) * half_a
        coef[1, j] = inside_tile(config_ref, first_row + 1.0, height, j) * half_b
        coef[2, j] = inside_tile(config_ref, first_row - 1.0, height, j) * half_b
        coef[3, j] = inside_tile(config_ref, first_row, height, j, 1) * half_b
        coef[4, j] = inside_tile(config_ref, first_row, height, j, -1) * half_b

    lane = lax.broadcasted_iota(jnp.int32, (8, LANES), 1)
    keep = [1.0 - config_ref[c] for c in range(WAVES)]

    def load(ref, i, t, by=0):
        at = PAD + 8 * t + by
        return [ref[i, j, at : at + 8, :] for j in range(3)]

    def along(ref, i, t):
        ahead, behind = load(ref, i, t, 1), load(ref, i, t, -1)
        return [ahead[j] - behind[j] for j in range(3)]

    def across(parts):
        ahead, behind = eastward(parts, lane), westward(parts, lane)
        return [ahead[j] - behind[j] for j in range(3)]

    h = [load(state, 0, t) for t in range(tiles)]
    du = [along(state, 1, t) for t in range(tiles)]
    dv = [across(load(state, 2, t)) for t in range(tiles)]
    for t in range(tiles):
        at = PAD + 8 * t
        push_u, push_v = along(forcing, 1, t), across(load(forcing, 2, t))
        for j in range(3):
            coef[5, j, 8 * t : 8 * t + 8, :] = push_u[j]
            coef[6, j, 8 * t : 8 * t + 8, :] = push_v[j]
    own = (4, 5)
    sum_u = {t: [jnp.zeros((8, LANES), f32)] * 2 for t in (3, 4, 5, 6)}
    sum_v = {t: [jnp.zeros((8, LANES), f32)] * 3 for t in own}
    for step in range(SUBSTEPS):
        first = step // STEPS_PER_PHASE
        final = step == SUBSTEPS - 1
        span = range(first, tiles - first)
        for t in span:
            here = slice(8 * t, 8 * t + 8)
            push = load(forcing, 0, t)
            for j in range(3):
                h[t][j] = (keep[0] * h[t][j] + push[j]) - coef[0, j, here, :] * (du[t][j] + dv[t][j])
                if not final:
                    state[0, j, PAD + 8 * t : PAD + 8 * t + 8, :] = h[t][j]
        for t in sum_u:
            sum_u[t] = [keep[1] * sum_u[t][j] + h[t][j] for j in range(2)]
        for t in own:
            sum_v[t] = [keep[2] * sum_v[t][j] + h[t][j] for j in range(3)]
        if final:
            break
        for t in span:
            here = slice(8 * t, 8 * t + 8)
            east, west = eastward(h[t], lane, 2), westward(h[t], lane, 2)
            up, down = load(state, 0, t, 2), load(state, 0, t, -2)
            for j in range(3):
                mid = h[t][j]
                du[t][j] = (keep[1] * du[t][j] + coef[5, j, here, :]) - (
                    coef[1, j, here, :] * (up[j] - mid) - coef[2, j, here, :] * (mid - down[j])
                )
                dv[t][j] = (keep[2] * dv[t][j] + coef[6, j, here, :]) - (
                    coef[3, j, here, :] * (east[j] - mid) - coef[4, j, here, :] * (mid - west[j])
                )

    def decays(c):
        power, total = c, 1.0 + 0.0 * c
        for _ in range(SUBSTEPS - 1):
            total = total + power
            power = power * c
        return power, total

    for t in sum_u:
        for j in range(2):
            state[0, j, PAD + 8 * t : PAD + 8 * t + 8, :] = sum_u[t][j]
    power_u, total_u = decays(keep[1])
    power_v, total_v = decays(keep[2])
    for j in range(2):
        inside = inside_tile(config_ref, 0.0, ROWS, j) * half_b
        for t in own:
            at = PAD + 8 * t
            rows = slice(8 * (t - 4), 8 * (t - 4) + 8)
            factor = inside[rows]
            slope_u = state[0, j, at + 1 : at + 9, :] - state[0, j, at - 1 : at + 7, :]
            slope_v = across(sum_v[t])[j]
            new_u = power_u * state[1, j, at : at + 8, :] + total_u * forcing[1, j, at : at + 8, :] - factor * slope_u
            new_v = power_v * state[2, j, at : at + 8, :] + total_v * forcing[2, j, at : at + 8, :] - factor * slope_v
            cols = slice(j * LANES, (j + 1) * LANES)
            out_ref[0, rows, cols] = h[t][j]
            out_ref[1, rows, cols] = new_u
            out_ref[2, rows, cols] = new_v
    for i in range(TRACERS):
        out_ref[WAVES + i] = tracers_ref[i]
    if not last:
        fields = [out_ref[c] for c in range(FIELDS)]
        received = [received_ref[c] for c in range(FIELDS)]
        write_export(fields, received, land_ref[...].astype(f32), smix_ref, imix_ref, turned, export_ref)
        write_strips([[half_of(v, 0), half_of(v, 1)] for v in fields], low_ref, high_ref)


def wave_steps(last, config, mixes, operands):
    state = shaped((FIELDS, ROWS, COLS))
    strips = shaped((2, ROWS, LANES))
    scratch = [
        pltpu.VMEM((WAVES, 3, 5 * ROWS + 2 * PAD, LANES), f32),
        pltpu.VMEM((WAVES, 3, 5 * ROWS + 2 * PAD, LANES), f32),
        pltpu.VMEM((7, 3, 5 * ROWS, LANES), f32),
    ]
    if not last:
        scratch.append(pltpu.VMEM((2, TURNED, LANES), f32))
    return pl.pallas_call(
        lambda *refs: wave_kernel(last, *refs),
        out_shape=state if last else (state, shaped((TURNED, COLS), bf16), strips, strips),
        in_specs=[SMEM] * (1 + len(mixes)) + [VMEM] * len(operands),
        out_specs=VMEM if last else (VMEM,) * 4,
        scratch_shapes=scratch,
        compiler_params=params(),
        name="wave_steps_last" if last else "wave_steps",
    )(config, *mixes, *operands)


def line(block, axis, by):
    count = lax.axis_size(axis)
    return lax.ppermute(block, axis, [(i, i + by) for i in range(count) if 0 <= i + by < count])


def local(
    section_state, prev_import, land_mask, state_mix, import_mix, damping, wave_speed,
    remap_owner, remap_slot, remap_weight,
):
    smix = state_mix[0]
    imix = import_mix[0]
    gx = lax.axis_index("gx")
    gy = lax.axis_index("gy")
    place = jnp.stack([gx * ROWS, gy * COLS, lax.axis_size("gx") * ROWS, lax.axis_size("gy") * COLS])
    config = jnp.concatenate([damping[0], wave_speed[0], place.astype(f32)])
    owner = remap_owner[0].reshape(-1)
    slot = remap_slot[0].reshape(-1)
    entry = ((owner - gx + 2) * ROWS + slot // 4) * 2 + (slot % 4) // 2
    second = lax.iota(jnp.int32, owner.shape[0]) % 2
    index = entry + ((slot % 2) ^ second) * (5 * ROWS * 2)

    exported, low, high, fields, land = export(section_state[0], prev_import[0], land_mask[0], smix, imix)
    weight = stage(remap_weight[0].reshape(ROWS, COLS, 128))
    for interval in range(ITERS):
        last = interval == ITERS - 1
        opposite = lax.ppermute(exported, "sec", [(0, 1), (1, 0)])
        left = line(high, "gy", 1)
        right = line(low, "gy", -1)
        near, far = pack(opposite, fields, left, right, index, config, weight)
        before = line(near, "gx", 1)
        after = line(near, "gx", -1)
        far_before = line(far, "gx", 2)
        far_after = line(far, "gx", -2)
        forcing, low, high, received = remap(
            index, (far_before, before, opposite, after, far_after), weight, land
        )
        forcing_left = line(high, "gy", 1)
        forcing_right = line(low, "gy", -1)
        forward, backward, outer = pack_forcing(forcing, forcing_left, forcing_right, before, after)
        near_before = line(forward, "gx", 1)
        near_after = line(backward, "gx", -1)
        outer_before = line(outer, "gx", 2)
        outer_after = line(outer, "gx", -2)
        own = (forcing, forcing_left, forcing_right)
        state = (before, fields, left, right, after)
        tracers = tracer_steps(config, (near_before, *own, near_after, *state))
        operands = (outer_before, near_before, *own, near_after, outer_after, *state, tracers)
        if last:
            fields = wave_steps(last, config, (), operands)
        else:
            operands += (received, land)
            fields, exported, low, high = wave_steps(last, config, (smix, imix), operands)
    return (fields[None], received[None])


def solution(mesh):
    in_specs = (
        P("sec", None, "gx", "gy"),
        P("sec", None, "gx", "gy"),
        P("sec", "gx", "gy"),
        P("sec", None, None),
        P("sec", None, None),
        P("sec", None),
        P("sec", None),
        P("sec", "gx", "gy", None),
        P("sec", "gx", "gy", None),
        P("sec", "gx", "gy", None, None),
    )
    out_specs = (P("sec", None, "gx", "gy"), P("sec", None, "gx", "gy"))
    return jax.shard_map(local, mesh=mesh, in_specs=in_specs, out_specs=out_specs, check_vma=False)
```

time: 149 us -> 143 us (0.960)
  the two profiles are of different devices: /device:TPU:11 before, /device:TPU:6 now
where the time goes in v3:
time: 143 us; the launch traced here: 142 us
  starting transfers between devices  87.1 us (61%)
  waiting for transfers between devices  28.7 us (20%)
  Pallas kernels  21.2 us (15%)
  local copies, waits for them, and re-layouts  3.64 us (3%)
    ppermute x24, starting transfers between devices, line(): lax.ppermute(block, axis, [(i, i + by) for i in range(count) if 0 <= i +...  70.4 us
    ppermute x24, waiting for transfers between devices, line(): lax.ppermute(block, axis, [(i, i + by) for i in range(count) if 0 <= i +...  28.7 us
    ppermute x2, starting transfers between devices, local(): opposite = lax.ppermute(exported, 'sec', [(0, 1), (1, 0)])  16.7 us
    pallas_call x2, Pallas kernels, tracer_steps(): pl.pallas_call(tracer_kernel, out_shape=shaped((TRACERS, ROWS, COLS)), in...  7.54 us
    pallas_call x2, Pallas kernels, wave_steps(): pl.pallas_call(lambda *refs: wave_kernel(last, *refs), out_shape=state if...  5.54 us
    unnamed x21, local copies, waits for them, and re-layouts  3.24 us
    pallas_call x2, Pallas kernels, remap(): pl.pallas_call(remap_kernel, out_shape=(shaped((FIELDS, ROWS, COLS)), str...  3.11 us
  transfers between devices with their start and end apart: 26, of which 9 were waited for; matrix products, arithmetic and copies ran while one was open for 0% of the time, Pallas kernels for 7%

profile of v3, /device:TPU:6, one launch (start us, length us, event | category | flops | bytes accessed | tf_op | source)
XLA Modules:
  0.0 141.9 jit_solution(625773811158196829)
XLA Ops:
  0.6 2.6 %export.1 = (bf16[128,256]{1,0:T(8,128)(2,1)}, f32[2,16,128]{2,1,0:T(8,128)}, f32[2,16,128]{2,1,0:T(8,128)}, f32[8,16,256]{2,1,0:T(8,128)}, s32[16,256]{1,0:T(8,128)}) custom-call(f32[8,8]{1,0:T(8,128)} %bitcast.12, f32[8,8]{1,0:T(8,128)} %bitcast.14, f32[8,16,256]{2,1,0:T(8,128)} %bitcast.18, f32[8,16,256]{2,1,0:T(8,128)} %bitcast.19, s32[16,256]{1,0:T(8,128)} %bitcast.20), custom_call_target="tpu_custom_call" | custom-call | tf_op jit(solution)/shard_map/export/pallas_call | solution.py:107
  3.3 1.7 %collective-permute-start.1 = (f32[2,16,128]{2,1,0:T(8,128)}, f32[2,16,128]{2,1,0:T(8,128)S(1)}, u32[]{:S(2)}, u32[]{:S(2)}) collective-permute-start(f32[2,16,128]{2,1,0:T(8,128)} %get-tuple-element.31), channel_id=1, source_target_pairs={{0,1},{1,2},{2,3},{3,4},{4,5},{5,6},{6,7},{8,9},{9,10},{10,11},{11... | collective-permute-start | bytes 49160 | tf_op jit(solution)/shard_map/ppermute | solution.py:565
  5.0 1.3 collective-permute-start.2
  6.3 10.9 %collective-permute-start = (bf16[128,256]{1,0:T(8,128)(2,1)}, bf16[128,256]{1,0:T(8,128)(2,1)S(1)}, u32[]{:S(2)}, u32[]{:S(2)}) collective-permute-start(bf16[128,256]{1,0:T(8,128)(2,1)} %get-tuple-element.29), channel_id=1, source_target_pairs={{0,256},{256,0},{1,257},{257,1},{2,258},{258,2},{3,259},{259,3},{4... | collective-permute-start | bytes 196616 | tf_op jit(solution)/shard_map/ppermute | solution.py:588
  17.2 0.7 copy-done.7
  18.2 0.5 copy-done.6
  18.8 0.1 reshape_squeeze.7
  19.1 0.7 copy-done.8
  19.8 2.3 %stage_weights.1.weight_ref = bf16[16,256,128]{2,1,0:T(8,128)(2,1)} custom-call(bf16[16,256,128]{2,1,0:T(8,128)(2,1)} %bitcast.16), custom_call_target="tpu_custom_call" | custom-call | bytes 4000000 | tf_op jit(solution)/shard_map/stage_weights/pallas_call | solution.py:131
  22.2 1.2 copy-done
  23.4 5.8 %collective-permute-start.5 = (bf16[44,16,128]{2,1,0:T(8,128)(2,1)S(1)}, bf16[44,16,128]{2,1,0:T(8,128)(2,1)S(1)}, u32[]{:S(2)}, u32[]{:S(2)}) collective-permute-start(bf16[44,16,128]{2,1,0:T(8,128)(2,1)S(1)} %get-tuple-element.34), channel_id=1, source_target_pairs={{8,0},{16,8},{24,16},{32,24},{40,32},{48,40},{56,48},{64,56},{72,6... | collective-permute-start | bytes 540680 | tf_op jit(solution)/shard_map/ppermute | solution.py:565
  29.2 1.9 %collective-permute-start.4 = (bf16[44,16,128]{2,1,0:T(8,128)(2,1)S(1)}, bf16[44,16,128]{2,1,0:T(8,128)(2,1)S(1)}, u32[]{:S(2)}, u32[]{:S(2)}) collective-permute-start(bf16[44,16,128]{2,1,0:T(8,128)(2,1)S(1)} %get-tuple-element.34), channel_id=1, source_target_pairs={{0,8},{8,16},{16,24},{24,32},{32,40},{40,48},{48,56},{56,64},{64,7... | collective-permute-start | bytes 540680 | tf_op jit(solution)/shard_map/ppermute | solution.py:565
  31.1 4.7 %collective-permute-start.6 = (bf16[16,16,128]{2,1,0:T(8,128)(2,1)S(1)}, bf16[16,16,128]{2,1,0:T(8,128)(2,1)S(1)}, u32[]{:S(2)}, u32[]{:S(2)}) collective-permute-start(bf16[16,16,128]{2,1,0:T(8,128)(2,1)S(1)} %get-tuple-element.33), channel_id=1, source_target_pairs={{16,0},{24,8},{32,16},{40,24},{48,32},{56,40},{64,48},{72,56},{80,... | collective-permute-start | bytes 196616 | tf_op jit(solution)/shard_map/ppermute | solution.py:565
  35.8 2.0 %collective-permute-start.3 = (bf16[16,16,128]{2,1,0:T(8,128)(2,1)S(1)}, bf16[16,16,128]{2,1,0:T(8,128)(2,1)S(1)}, u32[]{:S(2)}, u32[]{:S(2)}) collective-permute-start(bf16[16,16,128]{2,1,0:T(8,128)(2,1)S(1)} %get-tuple-element.33), channel_id=1, source_target_pairs={{0,16},{8,24},{16,32},{24,40},{32,48},{40,56},{48,64},{56,72},{64,... | collective-permute-start | bytes 196616 | tf_op jit(solution)/shard_map/ppermute | solution.py:565
  37.9 2.0 %collective-permute-done.6.far_after_ref = bf16[16,16,128]{2,1,0:T(8,128)(2,1)S(1)} collective-permute-done((bf16[16,16,128]{2,1,0:T(8,128)(2,1)S(1)}, bf16[16,16,128]{2,1,0:T(8,128)(2,1)S(1)}, u32[]{:S(2)}, u32[]{:S(2)}) %collective-permute-start.6) | collective-permute-done | bytes 65568 | tf_op jit(solution)/shard_map/ppermute | solution.py:565
  39.9 6.1 %collective-permute-done.3.far_before_ref = bf16[16,16,128]{2,1,0:T(8,128)(2,1)S(1)} collective-permute-done((bf16[16,16,128]{2,1,0:T(8,128)(2,1)S(1)}, bf16[16,16,128]{2,1,0:T(8,128)(2,1)S(1)}, u32[]{:S(2)}, u32[]{:S(2)}) %collective-permute-start.3) | collective-permute-done | bytes 65568 | tf_op jit(solution)/shard_map/ppermute | solution.py:565
  46.1 1.3 remap.2
  47.3 2.0 %collective-permute-start.7 = (f32[2,16,128]{2,1,0:T(8,128)S(1)}, f32[2,16,128]{2,1,0:T(8,128)S(1)}, u32[]{:S(2)}, u32[]{:S(2)}) collective-permute-start(f32[2,16,128]{2,1,0:T(8,128)S(1)} %get-tuple-element.37), channel_id=1, source_target_pairs={{0,1},{1,2},{2,3},{3,4},{4,5},{5,6},{6,7},{8,9},{9,10},{10,11},{11... | collective-permute-start | bytes 49160 | tf_op jit(solution)/shard_map/ppermute | solution.py:565
  49.4 1.3 collective-permute-start.8
  50.7 4.3 %collective-permute-done.8.right_ref.forcing_right_ref.refs_7_ = f32[2,16,128]{2,1,0:T(8,128)S(1)} collective-permute-done((f32[2,16,128]{2,1,0:T(8,128)S(1)}, f32[2,16,128]{2,1,0:T(8,128)S(1)}, u32[]{:S(2)}, u32[]{:S(2)}) %collective-permute-start.8) | collective-permute-done | bytes 16416 | tf_op jit(solution)/shard_map/ppermute | solution.py:565
  55.0 4.7 %collective-permute-start.10 = (bf16[44,16,128]{2,1,0:T(8,128)(2,1)S(1)}, bf16[44,16,128]{2,1,0:T(8,128)(2,1)S(1)}, u32[]{:S(2)}, u32[]{:S(2)}) collective-permute-start(bf16[44,16,128]{2,1,0:T(8,128)(2,1)S(1)} %get-tuple-element.40), channel_id=1, source_target_pairs={{0,8},{8,16},{16,24},{24,32},{32,40},{40,48},{48,56},{56,64},{64,7... | collective-permute-start | bytes 540680 | tf_op jit(solution)/shard_map/ppermute | solution.py:565
  59.7 3.3 %collective-permute-start.11 = (bf16[44,16,128]{2,1,0:T(8,128)(2,1)S(1)}, bf16[44,16,128]{2,1,0:T(8,128)(2,1)S(1)}, u32[]{:S(2)}, u32[]{:S(2)}) collective-permute-start(bf16[44,16,128]{2,1,0:T(8,128)(2,1)S(1)} %get-tuple-element.41), channel_id=1, source_target_pairs={{8,0},{16,8},{24,16},{32,24},{40,32},{48,40},{56,48},{64,56},{72,6... | collective-permute-start | bytes 540680 | tf_op jit(solution)/shard_map/ppermute | solution.py:565
  62.9 1.9 %collective-permute-start.12 = (bf16[16,16,128]{2,1,0:T(8,128)(2,1)S(1)}, bf16[16,16,128]{2,1,0:T(8,128)(2,1)S(1)}, u32[]{:S(2)}, u32[]{:S(2)}) collective-permute-start(bf16[16,16,128]{2,1,0:T(8,128)(2,1)S(1)} %get-tuple-element.39), channel_id=1, source_target_pairs={{16,0},{24,8},{32,16},{40,24},{48,32},{56,40},{64,48},{72,56},{80,... | collective-permute-start | bytes 196616 | tf_op jit(solution)/shard_map/ppermute | solution.py:565
  64.8 4.8 %collective-permute-start.9 = (bf16[16,16,128]{2,1,0:T(8,128)(2,1)S(1)}, bf16[16,16,128]{2,1,0:T(8,128)(2,1)S(1)}, u32[]{:S(2)}, u32[]{:S(2)}) collective-permute-start(bf16[16,16,128]{2,1,0:T(8,128)(2,1)S(1)} %get-tuple-element.39), channel_id=1, source_target_pairs={{0,16},{8,24},{16,32},{24,40},{32,48},{40,56},{48,64},{56,72},{64,... | collective-permute-start | bytes 196616 | tf_op jit(solution)/shard_map/ppermute | solution.py:565
  69.7 3.8 %tracer_steps.2.refs_15_ = f32[5,16,256]{2,1,0:T(8,128)S(1)} custom-call(f32[14]{0:T(128)S(1)} %pad_maximum_fusion.config_ref.refs_0_, bf16[44,16,128]{2,1,0:T(8,128)(2,1)S(1)} %collective-permute-done.10.forcing_before_ref.refs_4_, f32[8,16,256]{2,1,0:T(8,128)S(1)} %get-tuple-element.36.forcing_ref.refs_5_, ...), custom_call_target="tpu_custom_call" | custom-call | flops 10000000 | bytes 4000000 | tf_op jit(solution)/shard_map/tracer_steps/pallas_call | solution.py:393
  73.5 0.9 collective-permute-done.9.refs_3_
  74.5 2.6 %wave_steps.1 = (f32[8,16,256]{2,1,0:T(8,128)S(1)}, bf16[128,256]{1,0:T(8,128)(2,1)S(1)}, f32[2,16,128]{2,1,0:T(8,128)S(1)}, f32[2,16,128]{2,1,0:T(8,128)S(1)}) custom-call(f32[14]{0:T(128)S(1)} %pad_maximum_fusion.config_ref.refs_0_, f32[8,8]{1,0:T(8,128)S(1)} %bitcast.13, f32[8,8]{1,0:T(8,128)S(1)} %bitcast.15, ...), custom_call_target="tpu_custom_call" | custom-call | tf_op jit(solution)/shard_map/wave_steps/pallas_call | solution.py:552
  77.0 5.8 %collective-permute-start.13 = (bf16[128,256]{1,0:T(8,128)(2,1)S(1)}, bf16[128,256]{1,0:T(8,128)(2,1)S(1)}, u32[]{:S(2)}, u32[]{:S(2)}) collective-permute-start(bf16[128,256]{1,0:T(8,128)(2,1)S(1)} %get-tuple-element.43), channel_id=1, source_target_pairs={{0,256},{256,0},{1,257},{257,1},{2,258},{258,2},{3,259},{259,3},{4... | collective-permute-start | bytes 196616 | tf_op jit(solution)/shard_map/ppermute | solution.py:588
  82.9 2.1 %collective-permute-start.14 = (f32[2,16,128]{2,1,0:T(8,128)S(1)}, f32[2,16,128]{2,1,0:T(8,128)S(1)}, u32[]{:S(2)}, u32[]{:S(2)}) collective-permute-start(f32[2,16,128]{2,1,0:T(8,128)S(1)} %get-tuple-element.45), channel_id=1, source_target_pairs={{0,1},{1,2},{2,3},{3,4},{4,5},{5,6},{6,7},{8,9},{9,10},{10,11},{11... | collective-permute-start | bytes 49160 | tf_op jit(solution)/shard_map/ppermute | solution.py:565
  84.9 1.3 collective-permute-start.15
  86.2 3.8 %collective-permute-done.15.right_ref.refs_11_ = f32[2,16,128]{2,1,0:T(8,128)S(1)} collective-permute-done((f32[2,16,128]{2,1,0:T(8,128)S(1)}, f32[2,16,128]{2,1,0:T(8,128)S(1)}, u32[]{:S(2)}, u32[]{:S(2)}) %collective-permute-start.15) | collective-permute-done | bytes 16416 | tf_op jit(solution)/shard_map/ppermute | solution.py:565
  90.1 3.5 %collective-permute-start.18 = (bf16[44,16,128]{2,1,0:T(8,128)(2,1)S(1)}, bf16[44,16,128]{2,1,0:T(8,128)(2,1)S(1)}, u32[]{:S(2)}, u32[]{:S(2)}) collective-permute-start(bf16[44,16,128]{2,1,0:T(8,128)(2,1)S(1)} %get-tuple-element.48), channel_id=1, source_target_pairs={{8,0},{16,8},{24,16},{32,24},{40,32},{48,40},{56,48},{64,56},{72,6... | collective-permute-start | bytes 540680 | tf_op jit(solution)/shard_map/ppermute | solution.py:565
  93.6 3.0 %collective-permute-start.17 = (bf16[44,16,128]{2,1,0:T(8,128)(2,1)S(1)}, bf16[44,16,128]{2,1,0:T(8,128)(2,1)S(1)}, u32[]{:S(2)}, u32[]{:S(2)}) collective-permute-start(bf16[44,16,128]{2,1,0:T(8,128)(2,1)S(1)} %get-tuple-element.48), channel_id=1, source_target_pairs={{0,8},{8,16},{16,24},{24,32},{32,40},{40,48},{48,56},{56,64},{64,7... | collective-permute-start | bytes 540680 | tf_op jit(solution)/shard_map/ppermute | solution.py:565
  96.6 2.8 %collective-permute-start.19 = (bf16[16,16,128]{2,1,0:T(8,128)(2,1)S(1)}, bf16[16,16,128]{2,1,0:T(8,128)(2,1)S(1)}, u32[]{:S(2)}, u32[]{:S(2)}) collective-permute-start(bf16[16,16,128]{2,1,0:T(8,128)(2,1)S(1)} %get-tuple-element.47), channel_id=1, source_target_pairs={{16,0},{24,8},{32,16},{40,24},{48,32},{56,40},{64,48},{72,56},{80,... | collective-permute-start | bytes 196616 | tf_op jit(solution)/shard_map/ppermute | solution.py:565
  99.3 4.0 %collective-permute-start.16 = (bf16[16,16,128]{2,1,0:T(8,128)(2,1)S(1)}, bf16[16,16,128]{2,1,0:T(8,128)(2,1)S(1)}, u32[]{:S(2)}, u32[]{:S(2)}) collective-permute-start(bf16[16,16,128]{2,1,0:T(8,128)(2,1)S(1)} %get-tuple-element.47), channel_id=1, source_target_pairs={{0,16},{8,24},{16,32},{24,40},{32,48},{40,56},{48,64},{56,72},{64,... | collective-permute-start | bytes 196616 | tf_op jit(solution)/shard_map/ppermute | solution.py:565
  103.3 0.3 collective-permute-done.19.far_after_ref
  103.6 5.0 %collective-permute-done.16.far_before_ref = bf16[16,16,128]{2,1,0:T(8,128)(2,1)S(1)} collective-permute-done((bf16[16,16,128]{2,1,0:T(8,128)(2,1)S(1)}, bf16[16,16,128]{2,1,0:T(8,128)(2,1)S(1)}, u32[]{:S(2)}, u32[]{:S(2)}) %collective-permute-start.16) | collective-permute-done | bytes 65568 | tf_op jit(solution)/shard_map/ppermute | solution.py:565
  108.6 1.8 %remap.3 = (f32[8,16,256]{2,1,0:T(8,128)S(1)}, f32[2,16,128]{2,1,0:T(8,128)S(1)}, f32[2,16,128]{2,1,0:T(8,128)S(1)}, f32[8,16,256]{2,1,0:T(8,128)}) custom-call(s32[128]{0:T(128)S(1)} %multiply_add_fusion.index_ref, bf16[16,16,128]{2,1,0:T(8,128)(2,1)S(1)} %collective-permute-done.16.far_before_ref, ...), custom_call_target="tpu_custom_call" | custom-call | tf_op jit(solution)/shard_map/remap/pallas_call | solution.py:262
  110.4 2.3 %collective-permute-start.20 = (f32[2,16,128]{2,1,0:T(8,128)S(1)}, f32[2,16,128]{2,1,0:T(8,128)S(1)}, u32[]{:S(2)}, u32[]{:S(2)}) collective-permute-start(f32[2,16,128]{2,1,0:T(8,128)S(1)} %get-tuple-element.50), channel_id=1, source_target_pairs={{0,1},{1,2},{2,3},{3,4},{4,5},{5,6},{6,7},{8,9},{9,10},{10,11},{11... | collective-permute-start | bytes 49160 | tf_op jit(solution)/shard_map/ppermute | solution.py:565
  112.8 1.3 collective-permute-start.21
  114.1 3.4 %collective-permute-done.21.right_ref.forcing_right_ref.refs_5_ = f32[2,16,128]{2,1,0:T(8,128)S(1)} collective-permute-done((f32[2,16,128]{2,1,0:T(8,128)S(1)}, f32[2,16,128]{2,1,0:T(8,128)S(1)}, u32[]{:S(2)}, u32[]{:S(2)}) %collective-permute-start.21) | collective-permute-done | bytes 16416 | tf_op jit(solution)/shard_map/ppermute | solution.py:565
  117.6 5.4 %collective-permute-start.23 = (bf16[44,16,128]{2,1,0:T(8,128)(2,1)S(1)}, bf16[44,16,128]{2,1,0:T(8,128)(2,1)S(1)}, u32[]{:S(2)}, u32[]{:S(2)}) collective-permute-start(bf16[44,16,128]{2,1,0:T(8,128)(2,1)S(1)} %get-tuple-element.53), channel_id=1, source_target_pairs={{0,8},{8,16},{16,24},{24,32},{32,40},{40,48},{48,56},{56,64},{64,7... | collective-permute-start | bytes 540680 | tf_op jit(solution)/shard_map/ppermute | solution.py:565
  123.0 2.6 %collective-permute-start.24 = (bf16[44,16,128]{2,1,0:T(8,128)(2,1)S(1)}, bf16[44,16,128]{2,1,0:T(8,128)(2,1)S(1)}, u32[]{:S(2)}, u32[]{:S(2)}) collective-permute-start(bf16[44,16,128]{2,1,0:T(8,128)(2,1)S(1)} %get-tuple-element.54), channel_id=1, source_target_pairs={{8,0},{16,8},{24,16},{32,24},{40,32},{48,40},{56,48},{64,56},{72,6... | collective-permute-start | bytes 540680 | tf_op jit(solution)/shard_map/ppermute | solution.py:565
  125.6 2.9 %collective-permute-start.25 = (bf16[16,16,128]{2,1,0:T(8,128)(2,1)S(1)}, bf16[16,16,128]{2,1,0:T(8,128)(2,1)S(1)}, u32[]{:S(2)}, u32[]{:S(2)}) collective-permute-start(bf16[16,16,128]{2,1,0:T(8,128)(2,1)S(1)} %get-tuple-element.52), channel_id=1, source_target_pairs={{16,0},{24,8},{32,16},{40,24},{48,32},{56,40},{64,48},{72,56},{80,... | collective-permute-start | bytes 196616 | tf_op jit(solution)/shard_map/ppermute | solution.py:565
  128.5 3.8 %collective-permute-start.22 = (bf16[16,16,128]{2,1,0:T(8,128)(2,1)S(1)}, bf16[16,16,128]{2,1,0:T(8,128)(2,1)S(1)}, u32[]{:S(2)}, u32[]{:S(2)}) collective-permute-start(bf16[16,16,128]{2,1,0:T(8,128)(2,1)S(1)} %get-tuple-element.52), channel_id=1, source_target_pairs={{0,16},{8,24},{16,32},{24,40},{32,48},{40,56},{48,64},{56,72},{64,... | collective-permute-start | bytes 196616 | tf_op jit(solution)/shard_map/ppermute | solution.py:565
  132.3 3.8 %tracer_steps.3.refs_13_ = f32[5,16,256]{2,1,0:T(8,128)S(1)} custom-call(f32[14]{0:T(128)S(1)} %pad_maximum_fusion.config_ref.refs_0_, bf16[44,16,128]{2,1,0:T(8,128)(2,1)S(1)} %collective-permute-done.23.forcing_before_ref.refs_2_, f32[8,16,256]{2,1,0:T(8,128)S(1)} %get-tuple-element.49.forcing_ref.refs_3_, ...), custom_call_target="tpu_custom_call" | custom-call | flops 10000000 | bytes 4000000 | tf_op jit(solution)/shard_map/tracer_steps/pallas_call | solution.py:393
  136.1 2.8 %collective-permute-done.22.refs_1_ = bf16[16,16,128]{2,1,0:T(8,128)(2,1)S(1)} collective-permute-done((bf16[16,16,128]{2,1,0:T(8,128)(2,1)S(1)}, bf16[16,16,128]{2,1,0:T(8,128)(2,1)S(1)}, u32[]{:S(2)}, u32[]{:S(2)}) %collective-permute-start.22) | collective-permute-done | bytes 65568 | tf_op jit(solution)/shard_map/ppermute | solution.py:565
  138.9 3.0 %wave_steps_last.1 = f32[8,16,256]{2,1,0:T(8,128)} custom-call(f32[14]{0:T(128)S(1)} %pad_maximum_fusion.config_ref.refs_0_, bf16[16,16,128]{2,1,0:T(8,128)(2,1)S(1)} %collective-permute-done.22.refs_1_, bf16[44,16,128]{2,1,0:T(8,128)(2,1)S(1)} %collective-permute-done.23.forcing_before_ref.refs_2_, f32[8,16,256]{2,1,0:T(8,128)S(1)} %get-tuple-element.49.forcing_ref.refs_3_, ...), custom_call_target="tpu_custom_call" | custom-call | tf_op jit(solution)/shard_map/wave_steps_last/pallas_call | solution.py:552
  (44 shorter events, 0.8 us)
Async XLA Ops:
  3.3 18.9 %collective-permute-start.1 = (f32[2,16,128]{2,1,0:T(8,128)}, f32[2,16,128]{2,1,0:T(8,128)S(1)}, u32[]{:S(2)}, u32[]{:S(2)}) collective-permute-start(f32[2,16,128]{2,1,0:T(8,128)} %get-tuple-element.31), channel_id=1, source_target_pairs={{0,1},{1,2},{2,3},{3,4},{4,5},{5,6},{6,7},{8,9},{9,10},{10,11},{11... | collective-permute-start | bytes 49160 | tf_op jit(solution)/shard_map/ppermute | solution.py:565
  5.0 17.1 %collective-permute-start.2 = (f32[2,16,128]{2,1,0:T(8,128)}, f32[2,16,128]{2,1,0:T(8,128)S(1)}, u32[]{:S(2)}, u32[]{:S(2)}) collective-permute-start(f32[2,16,128]{2,1,0:T(8,128)} %get-tuple-element.32), channel_id=1, source_target_pairs={{1,0},{2,1},{3,2},{4,3},{5,4},{6,5},{7,6},{9,8},{10,9},{11,10},{12... | collective-permute-start | bytes 49160 | tf_op jit(solution)/shard_map/ppermute | solution.py:565
  6.3 15.8 %collective-permute-start = (bf16[128,256]{1,0:T(8,128)(2,1)}, bf16[128,256]{1,0:T(8,128)(2,1)S(1)}, u32[]{:S(2)}, u32[]{:S(2)}) collective-permute-start(bf16[128,256]{1,0:T(8,128)(2,1)} %get-tuple-element.29), channel_id=1, source_target_pairs={{0,256},{256,0},{1,257},{257,1},{2,258},{258,2},{3,259},{259,3},{4... | collective-permute-start | bytes 196616 | tf_op jit(solution)/shard_map/ppermute | solution.py:588
  17.2 0.7 copy-start.7
  18.0 0.7 copy-start.6
  19.1 0.7 copy-start.8
  19.1 0.7 copy-start.9
  19.8 2.3 %copy-start.2 = (f32[8,16,256]{2,1,0:T(8,128)S(1)}, f32[8,16,256]{2,1,0:T(8,128)}, u32[]{:S(2)}) copy-start(f32[8,16,256]{2,1,0:T(8,128)} %get-tuple-element.30.fields_ref.refs_11_) | copy-start | bytes 393220
  22.2 1.2 copy-start
  23.4 22.7 %copy-start.1 = (bf16[16,256,128]{2,1,0:T(8,128)(2,1)S(1)}, bf16[16,256,128]{2,1,0:T(8,128)(2,1)}, u32[]{:S(2)}) copy-start(bf16[16,256,128]{2,1,0:T(8,128)(2,1)} %stage_weights.1.weight_ref) | copy-start | bytes 3145732
  23.4 22.7 %copy-start.3 = (s32[16,256]{1,0:T(8,128)S(1)}, s32[16,256]{1,0:T(8,128)}, u32[]{:S(2)}) copy-start(s32[16,256]{1,0:T(8,128)} %get-tuple-element.35.land_ref.refs_17_) | copy-start | bytes 49156
  23.4 22.6 %collective-permute-start.5 = (bf16[44,16,128]{2,1,0:T(8,128)(2,1)S(1)}, bf16[44,16,128]{2,1,0:T(8,128)(2,1)S(1)}, u32[]{:S(2)}, u32[]{:S(2)}) collective-permute-start(bf16[44,16,128]{2,1,0:T(8,128)(2,1)S(1)} %get-tuple-element.34), channel_id=1, source_target_pairs={{8,0},{16,8},{24,16},{32,24},{40,32},{48,40},{56,48},{64,56},{72,6... | collective-permute-start | bytes 540680 | tf_op jit(solution)/shard_map/ppermute | solution.py:565
  29.2 16.8 %collective-permute-start.4 = (bf16[44,16,128]{2,1,0:T(8,128)(2,1)S(1)}, bf16[44,16,128]{2,1,0:T(8,128)(2,1)S(1)}, u32[]{:S(2)}, u32[]{:S(2)}) collective-permute-start(bf16[44,16,128]{2,1,0:T(8,128)(2,1)S(1)} %get-tuple-element.34), channel_id=1, source_target_pairs={{0,8},{8,16},{16,24},{24,32},{32,40},{40,48},{48,56},{56,64},{64,7... | collective-permute-start | bytes 540680 | tf_op jit(solution)/shard_map/ppermute | solution.py:565
  31.1 8.8 %collective-permute-start.6 = (bf16[16,16,128]{2,1,0:T(8,128)(2,1)S(1)}, bf16[16,16,128]{2,1,0:T(8,128)(2,1)S(1)}, u32[]{:S(2)}, u32[]{:S(2)}) collective-permute-start(bf16[16,16,128]{2,1,0:T(8,128)(2,1)S(1)} %get-tuple-element.33), channel_id=1, source_target_pairs={{16,0},{24,8},{32,16},{40,24},{48,32},{56,40},{64,48},{72,56},{80,... | collective-permute-start | bytes 196616 | tf_op jit(solution)/shard_map/ppermute | solution.py:565
  35.8 10.2 %collective-permute-start.3 = (bf16[16,16,128]{2,1,0:T(8,128)(2,1)S(1)}, bf16[16,16,128]{2,1,0:T(8,128)(2,1)S(1)}, u32[]{:S(2)}, u32[]{:S(2)}) collective-permute-start(bf16[16,16,128]{2,1,0:T(8,128)(2,1)S(1)} %get-tuple-element.33), channel_id=1, source_target_pairs={{0,16},{8,24},{16,32},{24,40},{32,48},{40,56},{48,64},{56,72},{64,... | collective-permute-start | bytes 196616 | tf_op jit(solution)/shard_map/ppermute | solution.py:565
  47.3 3.3 %collective-permute-start.7 = (f32[2,16,128]{2,1,0:T(8,128)S(1)}, f32[2,16,128]{2,1,0:T(8,128)S(1)}, u32[]{:S(2)}, u32[]{:S(2)}) collective-permute-start(f32[2,16,128]{2,1,0:T(8,128)S(1)} %get-tuple-element.37), channel_id=1, source_target_pairs={{0,1},{1,2},{2,3},{3,4},{4,5},{5,6},{6,7},{8,9},{9,10},{10,11},{11... | collective-permute-start | bytes 49160 | tf_op jit(solution)/shard_map/ppermute | solution.py:565
  49.4 5.6 %collective-permute-start.8 = (f32[2,16,128]{2,1,0:T(8,128)S(1)}, f32[2,16,128]{2,1,0:T(8,128)S(1)}, u32[]{:S(2)}, u32[]{:S(2)}) collective-permute-start(f32[2,16,128]{2,1,0:T(8,128)S(1)} %get-tuple-element.38), channel_id=1, source_target_pairs={{1,0},{2,1},{3,2},{4,3},{5,4},{6,5},{7,6},{9,8},{10,9},{11,10},{12... | collective-permute-start | bytes 49160 | tf_op jit(solution)/shard_map/ppermute | solution.py:565
  55.0 14.7 %collective-permute-start.10 = (bf16[44,16,128]{2,1,0:T(8,128)(2,1)S(1)}, bf16[44,16,128]{2,1,0:T(8,128)(2,1)S(1)}, u32[]{:S(2)}, u32[]{:S(2)}) collective-permute-start(bf16[44,16,128]{2,1,0:T(8,128)(2,1)S(1)} %get-tuple-element.40), channel_id=1, source_target_pairs={{0,8},{8,16},{16,24},{24,32},{32,40},{40,48},{48,56},{56,64},{64,7... | collective-permute-start | bytes 540680 | tf_op jit(solution)/shard_map/ppermute | solution.py:565
  59.7 10.0 %collective-permute-start.11 = (bf16[44,16,128]{2,1,0:T(8,128)(2,1)S(1)}, bf16[44,16,128]{2,1,0:T(8,128)(2,1)S(1)}, u32[]{:S(2)}, u32[]{:S(2)}) collective-permute-start(bf16[44,16,128]{2,1,0:T(8,128)(2,1)S(1)} %get-tuple-element.41), channel_id=1, source_target_pairs={{8,0},{16,8},{24,16},{32,24},{40,32},{48,40},{56,48},{64,56},{72,6... | collective-permute-start | bytes 540680 | tf_op jit(solution)/shard_map/ppermute | solution.py:565
  62.9 10.6 %collective-permute-start.12 = (bf16[16,16,128]{2,1,0:T(8,128)(2,1)S(1)}, bf16[16,16,128]{2,1,0:T(8,128)(2,1)S(1)}, u32[]{:S(2)}, u32[]{:S(2)}) collective-permute-start(bf16[16,16,128]{2,1,0:T(8,128)(2,1)S(1)} %get-tuple-element.39), channel_id=1, source_target_pairs={{16,0},{24,8},{32,16},{40,24},{48,32},{56,40},{64,48},{72,56},{80,... | collective-permute-start | bytes 196616 | tf_op jit(solution)/shard_map/ppermute | solution.py:565
  64.8 9.6 %collective-permute-start.9 = (bf16[16,16,128]{2,1,0:T(8,128)(2,1)S(1)}, bf16[16,16,128]{2,1,0:T(8,128)(2,1)S(1)}, u32[]{:S(2)}, u32[]{:S(2)}) collective-permute-start(bf16[16,16,128]{2,1,0:T(8,128)(2,1)S(1)} %get-tuple-element.39), channel_id=1, source_target_pairs={{0,16},{8,24},{16,32},{24,40},{32,48},{40,56},{48,64},{56,72},{64,... | collective-permute-start | bytes 196616 | tf_op jit(solution)/shard_map/ppermute | solution.py:565
  69.7 4.8 %copy-start.4 = (f32[1,8,8]{2,1,0:T(8,128)S(1)}, f32[1,8,8]{2,1,0:T(8,128)}, u32[]{:S(2)}) copy-start(f32[1,8,8]{2,1,0:T(8,128)} %param.13) | copy-start | bytes 772
  69.7 4.8 %copy-start.5 = (f32[1,8,8]{2,1,0:T(8,128)S(1)}, f32[1,8,8]{2,1,0:T(8,128)}, u32[]{:S(2)}) copy-start(f32[1,8,8]{2,1,0:T(8,128)} %param.14) | copy-start | bytes 772
  77.0 13.0 %collective-permute-start.13 = (bf16[128,256]{1,0:T(8,128)(2,1)S(1)}, bf16[128,256]{1,0:T(8,128)(2,1)S(1)}, u32[]{:S(2)}, u32[]{:S(2)}) collective-permute-start(bf16[128,256]{1,0:T(8,128)(2,1)S(1)} %get-tuple-element.43), channel_id=1, source_target_pairs={{0,256},{256,0},{1,257},{257,1},{2,258},{258,2},{3,259},{259,3},{4... | collective-permute-start | bytes 196616 | tf_op jit(solution)/shard_map/ppermute | solution.py:588
  82.9 3.4 %collective-permute-start.14 = (f32[2,16,128]{2,1,0:T(8,128)S(1)}, f32[2,16,128]{2,1,0:T(8,128)S(1)}, u32[]{:S(2)}, u32[]{:S(2)}) collective-permute-start(f32[2,16,128]{2,1,0:T(8,128)S(1)} %get-tuple-element.45), channel_id=1, source_target_pairs={{0,1},{1,2},{2,3},{3,4},{4,5},{5,6},{6,7},{8,9},{9,10},{10,11},{11... | collective-permute-start | bytes 49160 | tf_op jit(solution)/shard_map/ppermute | solution.py:565
  84.9 5.1 %collective-permute-start.15 = (f32[2,16,128]{2,1,0:T(8,128)S(1)}, f32[2,16,128]{2,1,0:T(8,128)S(1)}, u32[]{:S(2)}, u32[]{:S(2)}) collective-permute-start(f32[2,16,128]{2,1,0:T(8,128)S(1)} %get-tuple-element.46), channel_id=1, source_target_pairs={{1,0},{2,1},{3,2},{4,3},{5,4},{6,5},{7,6},{9,8},{10,9},{11,10},{12... | collective-permute-start | bytes 49160 | tf_op jit(solution)/shard_map/ppermute | solution.py:565
  90.1 18.5 %collective-permute-start.18 = (bf16[44,16,128]{2,1,0:T(8,128)(2,1)S(1)}, bf16[44,16,128]{2,1,0:T(8,128)(2,1)S(1)}, u32[]{:S(2)}, u32[]{:S(2)}) collective-permute-start(bf16[44,16,128]{2,1,0:T(8,128)(2,1)S(1)} %get-tuple-element.48), channel_id=1, source_target_pairs={{8,0},{16,8},{24,16},{32,24},{40,32},{48,40},{56,48},{64,56},{72,6... | collective-permute-start | bytes 540680 | tf_op jit(solution)/shard_map/ppermute | solution.py:565
  93.6 15.0 %collective-permute-start.17 = (bf16[44,16,128]{2,1,0:T(8,128)(2,1)S(1)}, bf16[44,16,128]{2,1,0:T(8,128)(2,1)S(1)}, u32[]{:S(2)}, u32[]{:S(2)}) collective-permute-start(bf16[44,16,128]{2,1,0:T(8,128)(2,1)S(1)} %get-tuple-element.48), channel_id=1, source_target_pairs={{0,8},{8,16},{16,24},{24,32},{32,40},{40,48},{48,56},{56,64},{64,7... | collective-permute-start | bytes 540680 | tf_op jit(solution)/shard_map/ppermute | solution.py:565
  96.6 7.1 %collective-permute-start.19 = (bf16[16,16,128]{2,1,0:T(8,128)(2,1)S(1)}, bf16[16,16,128]{2,1,0:T(8,128)(2,1)S(1)}, u32[]{:S(2)}, u32[]{:S(2)}) collective-permute-start(bf16[16,16,128]{2,1,0:T(8,128)(2,1)S(1)} %get-tuple-element.47), channel_id=1, source_target_pairs={{16,0},{24,8},{32,16},{40,24},{48,32},{56,40},{64,48},{72,56},{80,... | collective-permute-start | bytes 196616 | tf_op jit(solution)/shard_map/ppermute | solution.py:565
  99.3 9.2 %collective-permute-start.16 = (bf16[16,16,128]{2,1,0:T(8,128)(2,1)S(1)}, bf16[16,16,128]{2,1,0:T(8,128)(2,1)S(1)}, u32[]{:S(2)}, u32[]{:S(2)}) collective-permute-start(bf16[16,16,128]{2,1,0:T(8,128)(2,1)S(1)} %get-tuple-element.47), channel_id=1, source_target_pairs={{0,16},{8,24},{16,32},{24,40},{32,48},{40,56},{48,64},{56,72},{64,... | collective-permute-start | bytes 196616 | tf_op jit(solution)/shard_map/ppermute | solution.py:565
  110.4 3.6 %collective-permute-start.20 = (f32[2,16,128]{2,1,0:T(8,128)S(1)}, f32[2,16,128]{2,1,0:T(8,128)S(1)}, u32[]{:S(2)}, u32[]{:S(2)}) collective-permute-start(f32[2,16,128]{2,1,0:T(8,128)S(1)} %get-tuple-element.50), channel_id=1, source_target_pairs={{0,1},{1,2},{2,3},{3,4},{4,5},{5,6},{6,7},{8,9},{9,10},{10,11},{11... | collective-permute-start | bytes 49160 | tf_op jit(solution)/shard_map/ppermute | solution.py:565
  112.8 4.8 %collective-permute-start.21 = (f32[2,16,128]{2,1,0:T(8,128)S(1)}, f32[2,16,128]{2,1,0:T(8,128)S(1)}, u32[]{:S(2)}, u32[]{:S(2)}) collective-permute-start(f32[2,16,128]{2,1,0:T(8,128)S(1)} %get-tuple-element.51), channel_id=1, source_target_pairs={{1,0},{2,1},{3,2},{4,3},{5,4},{6,5},{7,6},{9,8},{10,9},{11,10},{12... | collective-permute-start | bytes 49160 | tf_op jit(solution)/shard_map/ppermute | solution.py:565
  117.6 14.7 %collective-permute-start.23 = (bf16[44,16,128]{2,1,0:T(8,128)(2,1)S(1)}, bf16[44,16,128]{2,1,0:T(8,128)(2,1)S(1)}, u32[]{:S(2)}, u32[]{:S(2)}) collective-permute-start(bf16[44,16,128]{2,1,0:T(8,128)(2,1)S(1)} %get-tuple-element.53), channel_id=1, source_target_pairs={{0,8},{8,16},{16,24},{24,32},{32,40},{40,48},{48,56},{56,64},{64,7... | collective-permute-start | bytes 540680 | tf_op jit(solution)/shard_map/ppermute | solution.py:565
  123.0 9.3 %collective-permute-start.24 = (bf16[44,16,128]{2,1,0:T(8,128)(2,1)S(1)}, bf16[44,16,128]{2,1,0:T(8,128)(2,1)S(1)}, u32[]{:S(2)}, u32[]{:S(2)}) collective-permute-start(bf16[44,16,128]{2,1,0:T(8,128)(2,1)S(1)} %get-tuple-element.54), channel_id=1, source_target_pairs={{8,0},{16,8},{24,16},{32,24},{40,32},{48,40},{56,48},{64,56},{72,6... | collective-permute-start | bytes 540680 | tf_op jit(solution)/shard_map/ppermute | solution.py:565
  125.6 10.6 %collective-permute-start.25 = (bf16[16,16,128]{2,1,0:T(8,128)(2,1)S(1)}, bf16[16,16,128]{2,1,0:T(8,128)(2,1)S(1)}, u32[]{:S(2)}, u32[]{:S(2)}) collective-permute-start(bf16[16,16,128]{2,1,0:T(8,128)(2,1)S(1)} %get-tuple-element.52), channel_id=1, source_target_pairs={{16,0},{24,8},{32,16},{40,24},{48,32},{56,40},{64,48},{72,56},{80,... | collective-permute-start | bytes 196616 | tf_op jit(solution)/shard_map/ppermute | solution.py:565
  128.5 10.4 %collective-permute-start.22 = (bf16[16,16,128]{2,1,0:T(8,128)(2,1)S(1)}, bf16[16,16,128]{2,1,0:T(8,128)(2,1)S(1)}, u32[]{:S(2)}, u32[]{:S(2)}) collective-permute-start(bf16[16,16,128]{2,1,0:T(8,128)(2,1)S(1)} %get-tuple-element.52), channel_id=1, source_target_pairs={{0,16},{8,24},{16,32},{24,40},{32,48},{40,56},{48,64},{56,72},{64,... | collective-permute-start | bytes 196616 | tf_op jit(solution)/shard_map/ppermute | solution.py:565

commit v4 on v3

--- a/solution.py
+++ b/solution.py
@@ -20,14 +20,16 @@
 STRIP = 32
 STEPS_PER_PHASE = 4
 
-T_PLANES = 12
-W_PLANES = 8
-A_WAVE = T_PLANES
-A_EXPORT = A_WAVE + 2 * W_PLANES
-A_PLANES = A_EXPORT + 16
-B_WAVE = T_PLANES
-B_BEHIND = B_WAVE + 2 * W_PLANES
-B_PLANES = B_BEHIND + 2 * W_PLANES
+A_WAVE = 10
+A_EXPORT = 22
+A_PLANES = 38
+B_WAVE = 12
+B_STRIP_T = 28
+B_STRIP_W = 30
+B_BEHIND = 34
+B_PLANES = 46
+C_STRIP_W = 16
+C_PLANES = 20
 
 PAD = 8
 WAVE_SPEED = 8
@@ -68,7 +70,7 @@
         out_ref[:, half * LANES : (half + 1) * LANES] = turned[half].astype(bf16)
 
 
-def write_strips(fields, low_ref, high_ref):
+def write_strips(fields, at, low_ref, high_ref):
     lane = lax.broadcasted_iota(jnp.int32, (ROWS, LANES), 1)
     groups = [fields[3:7], [fields[7]] + fields[0:3]]
     for p, group in enumerate(groups):
@@ -79,13 +81,13 @@
             first = jnp.where(here, pltpu.roll(group[j][0], STRIP * j, 1), first)
             moved = group[j][1] if j == 3 else pltpu.roll(group[j][1], STRIP * (j + 1), 1)
             last = jnp.where(here, moved, last)
-        low_ref[p] = first
-        high_ref[p] = last
+        low_ref[at + p] = first
+        high_ref[at + p] = last
 
 
 def export_kernel(
     smix_ref, imix_ref, fields_ref, received_ref, land_ref,
-    out_ref, low_ref, high_ref, fields_out, land_out, turned, received_buf, sems,
+    out_ref, fields_out, land_out, turned, received_buf, sems,
 ):
     copies = [
         pltpu.make_async_copy(fields_ref, fields_out, sems.at[0]),
@@ -99,18 +101,16 @@
     fields = [fields_out[c] for c in range(FIELDS)]
     received = [received_buf[c] for c in range(FIELDS)]
     write_export(fields, received, land_out[...].astype(f32), smix_ref, imix_ref, turned, out_ref)
-    write_strips([[half_of(v, 0), half_of(v, 1)] for v in fields], low_ref, high_ref)
 
 
 def export(fields, received, land, smix, imix):
-    strips = shaped((2, ROWS, LANES))
     return pl.pallas_call(
         export_kernel,
         out_shape=(
-            shaped((TURNED, COLS), bf16), strips, strips, shaped((FIELDS, ROWS, COLS)), shaped((ROWS, COLS), jnp.int32),
+            shaped((TURNED, COLS), bf16), shaped((FIELDS, ROWS, COLS)), shaped((ROWS, COLS), jnp.int32),
         ),
         in_specs=[SMEM, SMEM, HBM, HBM, HBM],
-        out_specs=(VMEM,) * 5,
+        out_specs=(VMEM,) * 3,
         scratch_shapes=[
             pltpu.VMEM((2, TURNED, LANES), f32),
             pltpu.VMEM((FIELDS, ROWS, COLS), f32),
@@ -121,86 +121,63 @@
     )(smix, imix, fields, received, land)
 
 
-def stage_kernel(weight_ref, out_ref, sem):
-    copy = pltpu.make_async_copy(weight_ref, out_ref, sem)
-    copy.start()
-    copy.wait()
-
-
-def stage(weight):
-    return pl.pallas_call(
-        stage_kernel,
-        out_shape=shaped(weight.shape, weight.dtype),
-        in_specs=[HBM],
-        out_specs=VMEM,
-        scratch_shapes=[pltpu.SemaphoreType.DMA],
-        compiler_params=params(56),
-        cost_estimate=pl.CostEstimate(flops=0, bytes_accessed=4_000_000, transcendentals=0),
-        name="stage_weights",
-    )(weight)
-
-
 def split_to(ref, at, low_at, value):
     high = value.astype(bf16)
     ref[at] = high
     ref[low_at] = (value - high.astype(f32)).astype(bf16)
 
 
-def write_halo(ref, base, fields, left, right):
-    for i in range(TRACERS):
-        for half in range(2):
-            ref[2 * i + half] = fields(WAVES + i, half).astype(bf16)
-    ref[10] = left[0].astype(bf16)
-    ref[11] = right[0].astype(bf16)
-    split_to(ref, base, base + W_PLANES, left[1])
-    split_to(ref, base + 1, base + 1 + W_PLANES, right[1])
-    for i in range(WAVES):
-        for half in range(2):
-            at = base + 2 + 2 * i + half
-            split_to(ref, at, at + W_PLANES, fields(i, half))
-
-
-def pack_kernel(opposite_ref, fields_ref, left_ref, right_ref, index_ref, config_ref, weight_ref, near_ref, far_ref):
-    del index_ref, config_ref, weight_ref
-    write_halo(
-        near_ref, A_WAVE, lambda i, half: fields_ref[i, :, half * LANES : (half + 1) * LANES], left_ref, right_ref
-    )
+def write_main(ref, tracer_at, wave_at, wave_low_at, fields_ref):
+    for half in range(2):
+        cols = slice(half * LANES, (half + 1) * LANES)
+        for i in range(TRACERS):
+            ref[tracer_at + 2 * i + half] = fields_ref[WAVES + i, :, cols].astype(bf16)
+        for i in range(WAVES):
+            split_to(ref, wave_at + 2 * i + half, wave_low_at + 2 * i + half, fields_ref[i, :, cols])
+
+
+def pack_kernel(opposite_ref, fields_ref, index_ref, config_ref, near_ref):
+    del index_ref, config_ref
+    write_main(near_ref, 0, A_WAVE, A_WAVE + 6, fields_ref)
     for half in range(2):
         for i in range(TURNED // 16):
-            part = opposite_ref[16 * i : 16 * i + 16, half * LANES : (half + 1) * LANES]
-            near_ref[A_EXPORT + half * 8 + i] = part
-            far_ref[half * 8 + i] = part
-
-
-def pack(opposite, fields, left, right, index, config, weight):
+            near_ref[A_EXPORT + half * 8 + i] = opposite_ref[16 * i : 16 * i + 16, half * LANES : (half + 1) * LANES]
+
+
+def pack(opposite, fields, index, config):
     return pl.pallas_call(
         pack_kernel,
-        out_shape=(shaped((A_PLANES, ROWS, LANES), bf16), shaped((16, ROWS, LANES), bf16)),
-        in_specs=[VMEM] * 4 + [HBM] * 3,
-        out_specs=(VMEM,) * 2,
+        out_shape=shaped((A_PLANES, ROWS, LANES), bf16),
+        in_specs=[VMEM] * 2 + [HBM] * 2,
+        out_specs=VMEM,
         compiler_params=params(),
         name="pack",
-    )(opposite, fields, left, right, index, config, weight)
+    )(opposite, fields, index, config)
 
 
 def pack_forcing_kernel(
     forcing_ref, left_ref, right_ref, before_ref, after_ref, forward_ref, backward_ref, far_ref,
 ):
     for ref, behind in ((forward_ref, before_ref), (backward_ref, after_ref)):
-        write_halo(
-            ref, B_WAVE, lambda i, half: forcing_ref[i, :, half * LANES : (half + 1) * LANES], left_ref, right_ref
-        )
-        for p in range(2 * W_PLANES):
+        write_main(ref, 0, B_WAVE + 2, B_WAVE + 10, forcing_ref)
+        for k, strips in enumerate((left_ref, right_ref)):
+            ref[10 + k] = strips[0].astype(bf16)
+            split_to(ref, B_WAVE + k, B_WAVE + 8 + k, strips[1])
+            ref[B_STRIP_T + k] = strips[2].astype(bf16)
+            split_to(ref, B_STRIP_W + k, B_STRIP_W + 2 + k, strips[3])
+        for p in range(12):
             ref[B_BEHIND + p] = behind[A_WAVE + p]
-    for p in range(2 * W_PLANES):
+    for p in range(16):
         far_ref[p] = forward_ref[B_WAVE + p]
+    for p in range(4):
+        far_ref[C_STRIP_W + p] = forward_ref[B_STRIP_W + p]
 
 
 def pack_forcing(forcing, left, right, before, after):
     payload = shaped((B_PLANES, ROWS, LANES), bf16)
     return pl.pallas_call(
         pack_forcing_kernel,
-        out_shape=(payload, payload, shaped((2 * W_PLANES, ROWS, LANES), bf16)),
+        out_shape=(payload, payload, shaped((C_PLANES, ROWS, LANES), bf16)),
         in_specs=[VMEM] * 5,
         out_specs=(VMEM,) * 3,
         compiler_params=params(),
@@ -209,18 +186,20 @@
 
 
 def remap_kernel(
-    index_ref, far_before_ref, before_ref, opposite_ref, after_ref, far_after_ref, weight_ref, land_ref,
-    forcing_ref, low_ref, high_ref, import_ref, table, turned,
+    index_ref, far_before_ref, before_ref, opposite_ref, after_ref, far_after_ref, weight_hbm, land_ref, fields_ref,
+    forcing_ref, low_ref, high_ref, import_ref, table, turned, weight_ref, sem,
 ):
+    copy = pltpu.make_async_copy(weight_hbm, weight_ref, sem)
+    copy.start()
     half_count = 5 * ROWS * 2
     windows = [far_before_ref, before_ref, opposite_ref, after_ref, far_after_ref]
     for w, ref in enumerate(windows):
         for half in range(2):
             for i in range(TURNED // 16):
-                if w == 2:
+                if w in (1, 3):
+                    chunk = ref[A_EXPORT + half * 8 + i]
+                else:
                     chunk = ref[16 * i : 16 * i + 16, half * LANES : (half + 1) * LANES]
-                else:
-                    chunk = ref[(0 if w in (0, 4) else A_EXPORT) + half * 8 + i]
                 chunk = chunk.astype(f32)
                 for sub in range(2):
                     part = chunk[sub * 8 : sub * 8 + 8]
@@ -230,6 +209,7 @@
     lane8 = lax.broadcasted_iota(jnp.int32, (8, LANES), 1)
     low_half = lane8 < 64
     ones = jnp.ones((8, LANES), f32)
+    copy.wait()
     for x in range(ROWS):
         pieces = []
         for seg in range(4):
@@ -254,23 +234,27 @@
             forcing_ref[c, :, half * LANES : (half + 1) * LANES] = part
             parts.append(part)
         forcing.append(parts)
-    write_strips(forcing, low_ref, high_ref)
-
-
-def remap(index, windows, weight, land):
-    strips = shaped((2, ROWS, LANES))
+    state = [[half_of(fields_ref[c], half) for half in range(2)] for c in range(FIELDS)]
+    write_strips(forcing, 0, low_ref, high_ref)
+    write_strips(state, 2, low_ref, high_ref)
+
+
+def remap(index, windows, weight, land, fields):
+    strips = shaped((4, ROWS, LANES))
     return pl.pallas_call(
         remap_kernel,
         out_shape=(shaped((FIELDS, ROWS, COLS)), strips, strips, shaped((FIELDS, ROWS, COLS))),
-        in_specs=[SMEM] + [VMEM] * 7,
+        in_specs=[SMEM] + [VMEM] * 5 + [HBM] + [VMEM] * 2,
         out_specs=(VMEM,) * 4,
         scratch_shapes=[
             pltpu.VMEM((2 * 5 * ROWS * 2, FIELDS, LANES), f32),
             pltpu.VMEM((2, TURNED, LANES), f32),
+            pltpu.VMEM((ROWS, COLS, 128), bf16),
+            pltpu.SemaphoreType.DMA,
         ],
-        compiler_params=params(),
+        compiler_params=params(52),
         name="remap",
-    )(index, *windows, weight, land)
+    )(index, *windows, weight, land, fields)
 
 
 def sides(left, right, j):
@@ -312,41 +296,41 @@
     return [jnp.where(lane >= LANES - by, moved[(j + 1) % 3], moved[j]) for j in range(3)]
 
 
-def own_parts(fields_ref, left_ref, right_ref, i):
+def own_parts(fields_ref, left_ref, right_ref, at, i):
     p, j = (0, i - WAVES) if WAVES <= i < FIELDS - 1 else (1, (i + 1) % FIELDS)
     return [
-        fields_ref[i, :, :LANES], fields_ref[i, :, LANES:], sides(left_ref[p], right_ref[p], j),
+        fields_ref[i, :, :LANES], fields_ref[i, :, LANES:], sides(left_ref[at + p], right_ref[at + p], j),
     ]
 
 
-def tracer_parts(ref, wave_base, i):
-    parts = [ref[2 * i].astype(f32), ref[2 * i + 1].astype(f32)]
-    at = 10 if i < 4 else wave_base
-    return parts + [sides(ref[at].astype(f32), ref[at + 1].astype(f32), i % 4)]
-
-
-def wave_parts(ref, base, i):
-    planes = [base + 2 + 2 * i, base + 3 + 2 * i, base, base + 1]
-    first, second, left, right = [joined(ref, p, p + W_PLANES) for p in planes]
+def tracer_parts(ref, strip_ref, strip_at, wave_strip_at, i):
+    at = strip_at if i < 4 else wave_strip_at
+    beside = sides(strip_ref[at].astype(f32), strip_ref[at + 1].astype(f32), i % 4)
+    return [ref[2 * i].astype(f32), ref[2 * i + 1].astype(f32), beside]
+
+
+def wave_parts(ref, at, low_at, strip_ref, strip_at, strip_low_at, i):
+    first, second = [joined(ref, at + 2 * i + half, low_at + 2 * i + half) for half in range(2)]
+    left, right = [joined(strip_ref, strip_at + k, strip_low_at + k) for k in range(2)]
     return [first, second, sides(left, right, i + 1)]
 
 
 def tracer_kernel(
-    config_ref, forcing_before_ref, forcing_ref, forcing_left_ref, forcing_right_ref, forcing_after_ref,
-    state_before_ref, fields_ref, left_ref, right_ref, state_after_ref, out_ref, state, forcing, coef,
+    config_ref, near_before_ref, forcing_ref, left_ref, right_ref, near_after_ref,
+    state_before_ref, fields_ref, state_after_ref, out_ref, state, forcing, coef,
 ):
-    own_forcing = (forcing_ref, forcing_left_ref, forcing_right_ref)
-    own_state = (fields_ref, left_ref, right_ref)
-    for t, ref in enumerate((forcing_before_ref, None, forcing_after_ref)):
-        rows = slice(t * ROWS, (t + 1) * ROWS)
+    for t, (near, main) in enumerate(
+        ((near_before_ref, state_before_ref), (None, None), (near_after_ref, state_after_ref))
+    ):
         for i in range(TRACERS):
-            parts = own_parts(*own_forcing, WAVES + i) if ref is None else tracer_parts(ref, B_WAVE, i)
-            place_field(forcing.at[i], rows, parts)
-    for t, ref in enumerate((state_before_ref, None, state_after_ref)):
-        rows = slice(PAD + t * ROWS, PAD + (t + 1) * ROWS)
-        for i in range(TRACERS):
-            parts = own_parts(*own_state, WAVES + i) if ref is None else tracer_parts(ref, A_WAVE, i)
-            place_field(state.at[0, i], rows, parts)
+            if near is None:
+                pushed = own_parts(forcing_ref, left_ref, right_ref, 0, WAVES + i)
+                parts = own_parts(fields_ref, left_ref, right_ref, 2, WAVES + i)
+            else:
+                pushed = tracer_parts(near, near, 10, B_WAVE, i)
+                parts = tracer_parts(main, near, B_STRIP_T, B_STRIP_W, i)
+            place_field(forcing.at[i], slice(t * ROWS, (t + 1) * ROWS), pushed)
+            place_field(state.at[0, i], slice(PAD + t * ROWS, PAD + (t + 1) * ROWS), parts)
     height = 3 * ROWS
     for k in range(2):
         for i in range(TRACERS):
@@ -409,25 +393,29 @@
 def wave_kernel(last, config_ref, *refs):
     if not last:
         smix_ref, imix_ref, *refs = refs
-    (far_before, near_before, forcing_ref, forcing_left_ref, forcing_right_ref, near_after, far_after,
-     state_before, fields_ref, left_ref, right_ref, state_after, tracers_ref, *refs) = refs
+    (far_before, near_before, forcing_ref, left_ref, right_ref, near_after, far_after,
+     state_before, fields_ref, state_after, tracers_ref, *refs) = refs
     if last:
         out_ref, state, forcing, coef = refs
     else:
-        received_ref, land_ref, out_ref, export_ref, low_ref, high_ref, state, forcing, coef, turned = refs
+        received_ref, land_ref, out_ref, export_ref, state, forcing, coef, turned = refs
     height = 5 * ROWS
     tiles = height // 8
 
     for i in range(WAVES):
         forcing_tiles = [
-            wave_parts(far_before, 0, i), wave_parts(near_before, B_WAVE, i),
-            own_parts(forcing_ref, forcing_left_ref, forcing_right_ref, i),
-            wave_parts(near_after, B_WAVE, i), wave_parts(far_after, 0, i),
+            wave_parts(far_before, 2, 10, far_before, 0, 8, i),
+            wave_parts(near_before, B_WAVE + 2, B_WAVE + 10, near_before, B_WAVE, B_WAVE + 8, i),
+            own_parts(forcing_ref, left_ref, right_ref, 0, i),
+            wave_parts(near_after, B_WAVE + 2, B_WAVE + 10, near_after, B_WAVE, B_WAVE + 8, i),
+            wave_parts(far_after, 2, 10, far_after, 0, 8, i),
         ]
         state_tiles = [
-            wave_parts(near_before, B_BEHIND, i), wave_parts(state_before, A_WAVE, i),
-            own_parts(fields_ref, left_ref, right_ref, i),
-            wave_parts(state_after, A_WAVE, i), wave_parts(near_after, B_BEHIND, i),
+            wave_parts(near_before, B_BEHIND, B_BEHIND + 6, far_before, C_STRIP_W, C_STRIP_W + 2, i),
+            wave_parts(state_before, A_WAVE, A_WAVE + 6, near_before, B_STRIP_W, B_STRIP_W + 2, i),
+            own_parts(fields_ref, left_ref, right_ref, 2, i),
+            wave_parts(state_after, A_WAVE, A_WAVE + 6, near_after, B_STRIP_W, B_STRIP_W + 2, i),
+            wave_parts(near_after, B_BEHIND, B_BEHIND + 6, far_after, C_STRIP_W, C_STRIP_W + 2, i),
         ]
         for t in range(5):
             rows = slice(PAD + t * ROWS, PAD + (t + 1) * ROWS)
@@ -536,12 +524,10 @@
         fields = [out_ref[c] for c in range(FIELDS)]
         received = [received_ref[c] for c in range(FIELDS)]
         write_export(fields, received, land_ref[...].astype(f32), smix_ref, imix_ref, turned, export_ref)
-        write_strips([[half_of(v, 0), half_of(v, 1)] for v in fields], low_ref, high_ref)
 
 
 def wave_steps(last, config, mixes, operands):
     state = shaped((FIELDS, ROWS, COLS))
-    strips = shaped((2, ROWS, LANES))
     scratch = [
         pltpu.VMEM((WAVES, 3, 5 * ROWS + 2 * PAD, LANES), f32),
         pltpu.VMEM((WAVES, 3, 5 * ROWS + 2 * PAD, LANES), f32),
@@ -551,9 +537,9 @@
         scratch.append(pltpu.VMEM((2, TURNED, LANES), f32))
     return pl.pallas_call(
         lambda *refs: wave_kernel(last, *refs),
-        out_shape=state if last else (state, shaped((TURNED, COLS), bf16), strips, strips),
+        out_shape=state if last else (state, shaped((TURNED, COLS), bf16)),
         in_specs=[SMEM] * (1 + len(mixes)) + [VMEM] * len(operands),
-        out_specs=VMEM if last else (VMEM,) * 4,
+        out_specs=VMEM if last else (VMEM,) * 2,
         scratch_shapes=scratch,
         compiler_params=params(),
         name="wave_steps_last" if last else "wave_steps",
@@ -581,37 +567,36 @@
     second = lax.iota(jnp.int32, owner.shape[0]) % 2
     index = entry + ((slot % 2) ^ second) * (5 * ROWS * 2)
 
-    exported, low, high, fields, land = export(section_state[0], prev_import[0], land_mask[0], smix, imix)
-    weight = stage(remap_weight[0].reshape(ROWS, COLS, 128))
+    weight = remap_weight[0].reshape(ROWS, COLS, 128)
+
+    exported, fields, land = export(section_state[0], prev_import[0], land_mask[0], smix, imix)
     for interval in range(ITERS):
         last = interval == ITERS - 1
         opposite = lax.ppermute(exported, "sec", [(0, 1), (1, 0)])
+        near = pack(opposite, fields, index, config)
+        far_before = line(opposite, "gx", 2)
+        far_after = line(opposite, "gx", -2)
+        before = line(near, "gx", 1)
+        after = line(near, "gx", -1)
+        forcing, low, high, received = remap(
+            index, (far_before, before, opposite, after, far_after), weight, land, fields
+        )
         left = line(high, "gy", 1)
         right = line(low, "gy", -1)
-        near, far = pack(opposite, fields, left, right, index, config, weight)
-        before = line(near, "gx", 1)
-        after = line(near, "gx", -1)
-        far_before = line(far, "gx", 2)
-        far_after = line(far, "gx", -2)
-        forcing, low, high, received = remap(
-            index, (far_before, before, opposite, after, far_after), weight, land
-        )
-        forcing_left = line(high, "gy", 1)
-        forcing_right = line(low, "gy", -1)
-        forward, backward, outer = pack_forcing(forcing, forcing_left, forcing_right, before, after)
+        forward, backward, outer = pack_forcing(forcing, left, right, before, after)
         near_before = line(forward, "gx", 1)
         near_after = line(backward, "gx", -1)
         outer_before = line(outer, "gx", 2)
         outer_after = line(outer, "gx", -2)
-        own = (forcing, forcing_left, forcing_right)
-        state = (before, fields, left, right, after)
+        own = (forcing, left, right)
+        state = (before, fields, after)
         tracers = tracer_steps(config, (near_before, *own, near_after, *state))
         operands = (outer_before, near_before, *own, near_after, outer_after, *state, tracers)
         if last:
             fields = wave_steps(last, config, (), operands)
         else:
             operands += (received, land)
-            fields, exported, low, high = wave_steps(last, config, (smix, imix), operands)
+            fields, exported = wave_steps(last, config, (smix, imix), operands)
     return (fields[None], received[None])
 
 

time: 143 us -> 135 us (0.944)
  starting transfers between devices: 87.1 us -> 80.3 us
  local copies, waits for them, and re-layouts: 3.64 us -> 1.22 us
    ppermute x24 -> x20, starting transfers between devices: 70.4 us -> 61.4 us  [line(): lax.ppermute(block, axis, [(i, i + by) for i in range(count) if 0 <= i +...]
    ppermute x2, waiting for transfers between devices: 0.01 us -> 5.14 us  [local(): opposite = lax.ppermute(exported, 'sec', [(0, 1), (1, 0)])]
    ppermute x24 -> x20, waiting for transfers between devices: 28.7 us -> 24.4 us  [line(): lax.ppermute(block, axis, [(i, i + by) for i in range(count) if 0 <= i +...]
    unnamed x21 -> x19, local copies, waits for them, and re-layouts: 3.24 us -> 0.82 us
    pallas_call x4 -> x3, Pallas kernels: 4.94 us -> 2.77 us  [the longest x1 2.73 us: export(): pl.pallas_call(export_kernel, out_shape=(shaped((TURNED, COLS), bf16), sh...]
    ppermute x2, starting transfers between devices: 16.7 us -> 18.9 us  [local(): opposite = lax.ppermute(exported, 'sec', [(0, 1), (1, 0)])]
  transfers between devices with their start and end apart: 26 -> 22, of which waited for: 9 -> 10; matrix products, arithmetic and copies ran while one was open for 0% -> 1% of each run, Pallas kernels for 7% -> 6%
where the time goes in v4:
time: 135 us; the launch traced here: 133 us
  starting transfers between devices  80.3 us (59%)
  waiting for transfers between devices  29.5 us (22%)
  Pallas kernels  20.3 us (15%)
    ppermute x20, starting transfers between devices, line(): lax.ppermute(block, axis, [(i, i + by) for i in range(count) if 0 <= i +...  61.4 us
    ppermute x20, waiting for transfers between devices, line(): lax.ppermute(block, axis, [(i, i + by) for i in range(count) if 0 <= i +...  24.4 us
    ppermute x2, starting transfers between devices, local(): opposite = lax.ppermute(exported, 'sec', [(0, 1), (1, 0)])  18.9 us
    pallas_call x2, Pallas kernels, tracer_steps(): pl.pallas_call(tracer_kernel, out_shape=shaped((TRACERS, ROWS, COLS)), in...  7.55 us
    pallas_call x2, Pallas kernels, wave_steps(): pl.pallas_call(lambda *refs: wave_kernel(last, *refs), out_shape=state if...  5.55 us
    ppermute x2, waiting for transfers between devices, local(): opposite = lax.ppermute(exported, 'sec', [(0, 1), (1, 0)])  5.14 us
    pallas_call x2, Pallas kernels, remap(): pl.pallas_call(remap_kernel, out_shape=(shaped((FIELDS, ROWS, COLS)), str...  4.36 us
    pallas_call x1, Pallas kernels, export(): pl.pallas_call(export_kernel, out_shape=(shaped((TURNED, COLS), bf16), sh...  2.73 us
  transfers between devices with their start and end apart: 22, of which 10 were waited for; matrix products, arithmetic and copies ran while one was open for 1% of the time, Pallas kernels for 6%

profile of v4, /device:TPU:6, one launch (start us, length us, event | category | flops | bytes accessed | tf_op | source)
XLA Modules:
  0.0 132.6 jit_solution(4436564102265459527)
XLA Ops:
  0.7 2.7 %export.1 = (bf16[128,256]{1,0:T(8,128)(2,1)}, f32[8,16,256]{2,1,0:T(8,128)}, s32[16,256]{1,0:T(8,128)}) custom-call(f32[8,8]{1,0:T(8,128)} %bitcast.14, f32[8,8]{1,0:T(8,128)} %bitcast.16, f32[8,16,256]{2,1,0:T(8,128)} %bitcast.19, f32[8,16,256]{2,1,0:T(8,128)} %bitcast.20, s32[16,256]{1,0:T(8,128)} %bitcast.21), custom_call_target="tpu_custom_call" | custom-call | tf_op jit(solution)/shard_map/export/pallas_call | solution.py:107
  3.4 11.0 %collective-permute-start = (bf16[128,256]{1,0:T(8,128)(2,1)}, bf16[128,256]{1,0:T(8,128)(2,1)S(1)}, u32[]{:S(2)}, u32[]{:S(2)}) collective-permute-start(bf16[128,256]{1,0:T(8,128)(2,1)} %get-tuple-element.21), channel_id=1, source_target_pairs={{0,256},{256,0},{1,257},{257,1},{2,258},{258,2},{3,259},{259,3},{4... | collective-permute-start | bytes 196616 | tf_op jit(solution)/shard_map/ppermute | solution.py:575
  14.5 0.1 copy.14
  14.6 0.1 mul.28
  14.8 0.1 copy.15
  14.9 0.1 reshape_squeeze.7
  15.0 0.1 add_convert_fusion
  15.1 0.7 copy-done.7
  15.8 0.0 copy-done.8
  15.8 0.1 pad_maximum_fusion.config_ref.refs_0_
  15.9 1.9 %collective-permute-done.opposite_ref = bf16[128,256]{1,0:T(8,128)(2,1)S(1)} collective-permute-done((bf16[128,256]{1,0:T(8,128)(2,1)}, bf16[128,256]{1,0:T(8,128)(2,1)S(1)}, u32[]{:S(2)}, u32[]{:S(2)}) %collective-permute-start) | collective-permute-done | bytes 65568 | tf_op jit(solution)/shard_map/ppermute | solution.py:575
  17.8 5.6 %collective-permute-start.3 = (bf16[38,16,128]{2,1,0:T(8,128)(2,1)S(1)}, bf16[38,16,128]{2,1,0:T(8,128)(2,1)S(1)}, u32[]{:S(2)}, u32[]{:S(2)}) collective-permute-start(bf16[38,16,128]{2,1,0:T(8,128)(2,1)S(1)} %pack.2), channel_id=1, source_target_pairs={{8,0},{16,8},{24,16},{32,24},{40,32},{48,40},{56,48},{64,56},{72,6... | collective-permute-start | bytes 466952 | tf_op jit(solution)/shard_map/ppermute | solution.py:551
  23.5 1.9 %collective-permute-start.2 = (bf16[38,16,128]{2,1,0:T(8,128)(2,1)S(1)}, bf16[38,16,128]{2,1,0:T(8,128)(2,1)S(1)}, u32[]{:S(2)}, u32[]{:S(2)}) collective-permute-start(bf16[38,16,128]{2,1,0:T(8,128)(2,1)S(1)} %pack.2), channel_id=1, source_target_pairs={{0,8},{8,16},{16,24},{24,32},{32,40},{40,48},{48,56},{56,64},{64,7... | collective-permute-start | bytes 466952 | tf_op jit(solution)/shard_map/ppermute | solution.py:551
  25.4 4.7 %collective-permute-start.4 = (bf16[128,256]{1,0:T(8,128)(2,1)S(1)}, bf16[128,256]{1,0:T(8,128)(2,1)S(1)}, u32[]{:S(2)}, u32[]{:S(2)}) collective-permute-start(bf16[128,256]{1,0:T(8,128)(2,1)S(1)} %collective-permute-done.opposite_ref), channel_id=1, source_target_pairs={{16,0},{24,8},{32,16},{40,24},{48,32},{56,40},{64,48},{72,56},{80,... | collective-permute-start | bytes 196616 | tf_op jit(solution)/shard_map/ppermute | solution.py:551
  30.1 2.0 %collective-permute-start.1 = (bf16[128,256]{1,0:T(8,128)(2,1)S(1)}, bf16[128,256]{1,0:T(8,128)(2,1)S(1)}, u32[]{:S(2)}, u32[]{:S(2)}) collective-permute-start(bf16[128,256]{1,0:T(8,128)(2,1)S(1)} %collective-permute-done.opposite_ref), channel_id=1, source_target_pairs={{0,16},{8,24},{16,32},{24,40},{32,48},{40,56},{48,64},{56,72},{64,... | collective-permute-start | bytes 196616 | tf_op jit(solution)/shard_map/ppermute | solution.py:551
  32.2 1.0 collective-permute-done.4.far_after_ref
  33.2 6.1 %collective-permute-done.1.far_before_ref = bf16[128,256]{1,0:T(8,128)(2,1)S(1)} collective-permute-done((bf16[128,256]{1,0:T(8,128)(2,1)S(1)}, bf16[128,256]{1,0:T(8,128)(2,1)S(1)}, u32[]{:S(2)}, u32[]{:S(2)}) %collective-permute-start.1) | collective-permute-done | bytes 65568 | tf_op jit(solution)/shard_map/ppermute | solution.py:551
  39.3 2.4 %remap.2 = (f32[8,16,256]{2,1,0:T(8,128)S(1)}, f32[4,16,128]{2,1,0:T(8,128)S(1)}, f32[4,16,128]{2,1,0:T(8,128)S(1)}, f32[8,16,256]{2,1,0:T(8,128)S(1)}) custom-call(s32[128]{0:T(128)S(1)} %multiply_add_fusion.index_ref, bf16[128,256]{1,0:T(8,128)(2,1)S(1)} %collective-permute-done.1.far_before_ref, ...), custom_call_target="tpu_custom_call" | custom-call | tf_op jit(solution)/shard_map/remap/pallas_call | solution.py:244
  41.7 1.3 collective-permute-start.5
  43.0 1.3 collective-permute-start.6
  44.3 2.6 %collective-permute-done.6.right_ref.refs_7_ = f32[4,16,128]{2,1,0:T(8,128)S(1)} collective-permute-done((f32[4,16,128]{2,1,0:T(8,128)S(1)}, f32[4,16,128]{2,1,0:T(8,128)S(1)}, u32[]{:S(2)}, u32[]{:S(2)}) %collective-permute-start.6) | collective-permute-done | bytes 32800 | tf_op jit(solution)/shard_map/ppermute | solution.py:551
  47.0 4.7 %collective-permute-start.8 = (bf16[46,16,128]{2,1,0:T(8,128)(2,1)S(1)}, bf16[46,16,128]{2,1,0:T(8,128)(2,1)S(1)}, u32[]{:S(2)}, u32[]{:S(2)}) collective-permute-start(bf16[46,16,128]{2,1,0:T(8,128)(2,1)S(1)} %get-tuple-element.28), channel_id=1, source_target_pairs={{0,8},{8,16},{16,24},{24,32},{32,40},{40,48},{48,56},{56,64},{64,7... | collective-permute-start | bytes 565256 | tf_op jit(solution)/shard_map/ppermute | solution.py:551
  51.7 3.3 %collective-permute-start.9 = (bf16[46,16,128]{2,1,0:T(8,128)(2,1)S(1)}, bf16[46,16,128]{2,1,0:T(8,128)(2,1)S(1)}, u32[]{:S(2)}, u32[]{:S(2)}) collective-permute-start(bf16[46,16,128]{2,1,0:T(8,128)(2,1)S(1)} %get-tuple-element.29), channel_id=1, source_target_pairs={{8,0},{16,8},{24,16},{32,24},{40,32},{48,40},{56,48},{64,56},{72,6... | collective-permute-start | bytes 565256 | tf_op jit(solution)/shard_map/ppermute | solution.py:551
  54.9 1.9 %collective-permute-start.10 = (bf16[20,16,128]{2,1,0:T(8,128)(2,1)S(1)}, bf16[20,16,128]{2,1,0:T(8,128)(2,1)S(1)}, u32[]{:S(2)}, u32[]{:S(2)}) collective-permute-start(bf16[20,16,128]{2,1,0:T(8,128)(2,1)S(1)} %get-tuple-element.27), channel_id=1, source_target_pairs={{16,0},{24,8},{32,16},{40,24},{48,32},{56,40},{64,48},{72,56},{80,... | collective-permute-start | bytes 245768 | tf_op jit(solution)/shard_map/ppermute | solution.py:551
  56.9 4.8 %collective-permute-start.7 = (bf16[20,16,128]{2,1,0:T(8,128)(2,1)S(1)}, bf16[20,16,128]{2,1,0:T(8,128)(2,1)S(1)}, u32[]{:S(2)}, u32[]{:S(2)}) collective-permute-start(bf16[20,16,128]{2,1,0:T(8,128)(2,1)S(1)} %get-tuple-element.27), channel_id=1, source_target_pairs={{0,16},{8,24},{16,32},{24,40},{32,48},{40,56},{48,64},{56,72},{64,... | collective-permute-start | bytes 245768 | tf_op jit(solution)/shard_map/ppermute | solution.py:551
  61.7 0.0 copy-start.3
  61.7 3.8 %tracer_steps.2.refs_13_ = f32[5,16,256]{2,1,0:T(8,128)S(1)} custom-call(f32[14]{0:T(128)S(1)} %pad_maximum_fusion.config_ref.refs_0_, bf16[46,16,128]{2,1,0:T(8,128)(2,1)S(1)} %collective-permute-done.8.near_before_ref.refs_4_, f32[8,16,256]{2,1,0:T(8,128)S(1)} %get-tuple-element.24.forcing_ref.refs_5_, ...), custom_call_target="tpu_custom_call" | custom-call | flops 10000000 | bytes 4000000 | tf_op jit(solution)/shard_map/tracer_steps/pallas_call | solution.py:377
  65.5 1.9 %collective-permute-done.7.refs_3_ = bf16[20,16,128]{2,1,0:T(8,128)(2,1)S(1)} collective-permute-done((bf16[20,16,128]{2,1,0:T(8,128)(2,1)S(1)}, bf16[20,16,128]{2,1,0:T(8,128)(2,1)S(1)}, u32[]{:S(2)}, u32[]{:S(2)}) %collective-permute-start.7) | collective-permute-done | bytes 81952 | tf_op jit(solution)/shard_map/ppermute | solution.py:551
  67.4 2.6 %wave_steps.1 = (f32[8,16,256]{2,1,0:T(8,128)S(1)}, bf16[128,256]{1,0:T(8,128)(2,1)S(1)}) custom-call(f32[14]{0:T(128)S(1)} %pad_maximum_fusion.config_ref.refs_0_, f32[8,8]{1,0:T(8,128)S(1)} %bitcast.15, f32[8,8]{1,0:T(8,128)S(1)} %bitcast.17, bf16[20,16,128]{2,1,0:T(8,128)(2,1)S(1)} %collective-permute-done.7.refs_3_, ...), custom_call_target="tpu_custom_call" | custom-call | tf_op jit(solution)/shard_map/wave_steps/pallas_call | solution.py:538
  70.0 7.8 %collective-permute-start.11 = (bf16[128,256]{1,0:T(8,128)(2,1)S(1)}, bf16[128,256]{1,0:T(8,128)(2,1)S(1)}, u32[]{:S(2)}, u32[]{:S(2)}) collective-permute-start(bf16[128,256]{1,0:T(8,128)(2,1)S(1)} %get-tuple-element.31), channel_id=1, source_target_pairs={{0,256},{256,0},{1,257},{257,1},{2,258},{258,2},{3,259},{259,3},{4... | collective-permute-start | bytes 196616 | tf_op jit(solution)/shard_map/ppermute | solution.py:575
  77.9 3.2 %collective-permute-done.11.opposite_ref = bf16[128,256]{1,0:T(8,128)(2,1)S(1)} collective-permute-done((bf16[128,256]{1,0:T(8,128)(2,1)S(1)}, bf16[128,256]{1,0:T(8,128)(2,1)S(1)}, u32[]{:S(2)}, u32[]{:S(2)}) %collective-permute-start.11) | collective-permute-done | bytes 65568 | tf_op jit(solution)/shard_map/ppermute | solution.py:575
  81.1 1.9 %collective-permute-start.14 = (bf16[38,16,128]{2,1,0:T(8,128)(2,1)S(1)}, bf16[38,16,128]{2,1,0:T(8,128)(2,1)S(1)}, u32[]{:S(2)}, u32[]{:S(2)}) collective-permute-start(bf16[38,16,128]{2,1,0:T(8,128)(2,1)S(1)} %pack.3), channel_id=1, source_target_pairs={{8,0},{16,8},{24,16},{32,24},{40,32},{48,40},{56,48},{64,56},{72,6... | collective-permute-start | bytes 466952 | tf_op jit(solution)/shard_map/ppermute | solution.py:551
  83.0 3.9 %collective-permute-start.13 = (bf16[38,16,128]{2,1,0:T(8,128)(2,1)S(1)}, bf16[38,16,128]{2,1,0:T(8,128)(2,1)S(1)}, u32[]{:S(2)}, u32[]{:S(2)}) collective-permute-start(bf16[38,16,128]{2,1,0:T(8,128)(2,1)S(1)} %pack.3), channel_id=1, source_target_pairs={{0,8},{8,16},{16,24},{24,32},{32,40},{40,48},{48,56},{56,64},{64,7... | collective-permute-start | bytes 466952 | tf_op jit(solution)/shard_map/ppermute | solution.py:551
  86.9 1.9 %collective-permute-start.15 = (bf16[128,256]{1,0:T(8,128)(2,1)S(1)}, bf16[128,256]{1,0:T(8,128)(2,1)S(1)}, u32[]{:S(2)}, u32[]{:S(2)}) collective-permute-start(bf16[128,256]{1,0:T(8,128)(2,1)S(1)} %collective-permute-done.11.opposite_ref), channel_id=1, source_target_pairs={{16,0},{24,8},{32,16},{40,24},{48,32},{56,40},{64,48},{72,56},{80,... | collective-permute-start | bytes 196616 | tf_op jit(solution)/shard_map/ppermute | solution.py:551
  88.9 4.8 %collective-permute-start.12 = (bf16[128,256]{1,0:T(8,128)(2,1)S(1)}, bf16[128,256]{1,0:T(8,128)(2,1)S(1)}, u32[]{:S(2)}, u32[]{:S(2)}) collective-permute-start(bf16[128,256]{1,0:T(8,128)(2,1)S(1)} %collective-permute-done.11.opposite_ref), channel_id=1, source_target_pairs={{0,16},{8,24},{16,32},{24,40},{32,48},{40,56},{48,64},{56,72},{64,... | collective-permute-start | bytes 196616 | tf_op jit(solution)/shard_map/ppermute | solution.py:551
  93.7 0.7 collective-permute-done.15.far_after_ref
  94.4 4.9 %collective-permute-done.12.far_before_ref = bf16[128,256]{1,0:T(8,128)(2,1)S(1)} collective-permute-done((bf16[128,256]{1,0:T(8,128)(2,1)S(1)}, bf16[128,256]{1,0:T(8,128)(2,1)S(1)}, u32[]{:S(2)}, u32[]{:S(2)}) %collective-permute-start.12) | collective-permute-done | bytes 65568 | tf_op jit(solution)/shard_map/ppermute | solution.py:551
  99.3 2.0 %remap.3 = (f32[8,16,256]{2,1,0:T(8,128)S(1)}, f32[4,16,128]{2,1,0:T(8,128)S(1)}, f32[4,16,128]{2,1,0:T(8,128)S(1)}, f32[8,16,256]{2,1,0:T(8,128)}) custom-call(s32[128]{0:T(128)S(1)} %multiply_add_fusion.index_ref, bf16[128,256]{1,0:T(8,128)(2,1)S(1)} %collective-permute-done.12.far_before_ref, ...), custom_call_target="tpu_custom_call" | custom-call | tf_op jit(solution)/shard_map/remap/pallas_call | solution.py:244
  101.3 1.3 collective-permute-start.16
  102.6 1.3 collective-permute-start.17
  103.9 5.1 %collective-permute-done.17.right_ref.refs_5_ = f32[4,16,128]{2,1,0:T(8,128)S(1)} collective-permute-done((f32[4,16,128]{2,1,0:T(8,128)S(1)}, f32[4,16,128]{2,1,0:T(8,128)S(1)}, u32[]{:S(2)}, u32[]{:S(2)}) %collective-permute-start.17) | collective-permute-done | bytes 32800 | tf_op jit(solution)/shard_map/ppermute | solution.py:551
  109.0 4.6 %collective-permute-start.19 = (bf16[46,16,128]{2,1,0:T(8,128)(2,1)S(1)}, bf16[46,16,128]{2,1,0:T(8,128)(2,1)S(1)}, u32[]{:S(2)}, u32[]{:S(2)}) collective-permute-start(bf16[46,16,128]{2,1,0:T(8,128)(2,1)S(1)} %get-tuple-element.37), channel_id=1, source_target_pairs={{0,8},{8,16},{16,24},{24,32},{32,40},{40,48},{48,56},{56,64},{64,7... | collective-permute-start | bytes 565256 | tf_op jit(solution)/shard_map/ppermute | solution.py:551
  113.7 3.4 %collective-permute-start.20 = (bf16[46,16,128]{2,1,0:T(8,128)(2,1)S(1)}, bf16[46,16,128]{2,1,0:T(8,128)(2,1)S(1)}, u32[]{:S(2)}, u32[]{:S(2)}) collective-permute-start(bf16[46,16,128]{2,1,0:T(8,128)(2,1)S(1)} %get-tuple-element.38), channel_id=1, source_target_pairs={{8,0},{16,8},{24,16},{32,24},{40,32},{48,40},{56,48},{64,56},{72,6... | collective-permute-start | bytes 565256 | tf_op jit(solution)/shard_map/ppermute | solution.py:551
  117.0 1.9 %collective-permute-start.21 = (bf16[20,16,128]{2,1,0:T(8,128)(2,1)S(1)}, bf16[20,16,128]{2,1,0:T(8,128)(2,1)S(1)}, u32[]{:S(2)}, u32[]{:S(2)}) collective-permute-start(bf16[20,16,128]{2,1,0:T(8,128)(2,1)S(1)} %get-tuple-element.36), channel_id=1, source_target_pairs={{16,0},{24,8},{32,16},{40,24},{48,32},{56,40},{64,48},{72,56},{80,... | collective-permute-start | bytes 245768 | tf_op jit(solution)/shard_map/ppermute | solution.py:551
  118.9 4.8 %collective-permute-start.18 = (bf16[20,16,128]{2,1,0:T(8,128)(2,1)S(1)}, bf16[20,16,128]{2,1,0:T(8,128)(2,1)S(1)}, u32[]{:S(2)}, u32[]{:S(2)}) collective-permute-start(bf16[20,16,128]{2,1,0:T(8,128)(2,1)S(1)} %get-tuple-element.36), channel_id=1, source_target_pairs={{0,16},{8,24},{16,32},{24,40},{32,48},{40,56},{48,64},{56,72},{64,... | collective-permute-start | bytes 245768 | tf_op jit(solution)/shard_map/ppermute | solution.py:551
  123.8 3.8 %tracer_steps.3.refs_11_ = f32[5,16,256]{2,1,0:T(8,128)S(1)} custom-call(f32[14]{0:T(128)S(1)} %pad_maximum_fusion.config_ref.refs_0_, bf16[46,16,128]{2,1,0:T(8,128)(2,1)S(1)} %collective-permute-done.19.near_before_ref.refs_2_, f32[8,16,256]{2,1,0:T(8,128)S(1)} %get-tuple-element.33.forcing_ref.refs_3_, ...), custom_call_target="tpu_custom_call" | custom-call | flops 10000000 | bytes 4000000 | tf_op jit(solution)/shard_map/tracer_steps/pallas_call | solution.py:377
  127.6 2.0 %collective-permute-done.18.refs_1_ = bf16[20,16,128]{2,1,0:T(8,128)(2,1)S(1)} collective-permute-done((bf16[20,16,128]{2,1,0:T(8,128)(2,1)S(1)}, bf16[20,16,128]{2,1,0:T(8,128)(2,1)S(1)}, u32[]{:S(2)}, u32[]{:S(2)}) %collective-permute-start.18) | collective-permute-done | bytes 81952 | tf_op jit(solution)/shard_map/ppermute | solution.py:551
  129.6 3.0 %wave_steps_last.1 = f32[8,16,256]{2,1,0:T(8,128)} custom-call(f32[14]{0:T(128)S(1)} %pad_maximum_fusion.config_ref.refs_0_, bf16[20,16,128]{2,1,0:T(8,128)(2,1)S(1)} %collective-permute-done.18.refs_1_, bf16[46,16,128]{2,1,0:T(8,128)(2,1)S(1)} %collective-permute-done.19.near_before_ref.refs_2_, f32[8,16,256]{2,1,0:T(8,128)S(1)} %get-tuple-element.33.forcing_ref.refs_3_, ...), custom_call_target="tpu_custom_call" | custom-call | tf_op jit(solution)/shard_map/wave_steps_last/pallas_call | solution.py:538
  (33 shorter events, 0.2 us)
Async XLA Ops:
  0.6 13.8 %copy-start.6 = (s32[1,16,4,2]{1,3,2,0:T(2,128)S(1)}, s32[1,16,4,2]{1,3,2,0:T(2,128)}, u32[]{:S(2)}) copy-start(s32[1,16,4,2]{1,3,2,0:T(2,128)} %param.17) | copy-start | bytes 1540
  0.6 14.1 %copy-start.5 = (s32[1,16,4,2]{1,3,2,0:T(2,128)S(1)}, s32[1,16,4,2]{1,3,2,0:T(2,128)}, u32[]{:S(2)}) copy-start(s32[1,16,4,2]{1,3,2,0:T(2,128)} %param.18) | copy-start | bytes 1540
  3.4 14.4 %copy-start.1 = (f32[8,16,256]{2,1,0:T(8,128)S(1)}, f32[8,16,256]{2,1,0:T(8,128)}, u32[]{:S(2)}) copy-start(f32[8,16,256]{2,1,0:T(8,128)} %get-tuple-element.22.fields_ref.refs_11_) | copy-start | bytes 393220
  3.4 14.4 %collective-permute-start = (bf16[128,256]{1,0:T(8,128)(2,1)}, bf16[128,256]{1,0:T(8,128)(2,1)S(1)}, u32[]{:S(2)}, u32[]{:S(2)}) collective-permute-start(bf16[128,256]{1,0:T(8,128)(2,1)} %get-tuple-element.21), channel_id=1, source_target_pairs={{0,256},{256,0},{1,257},{257,1},{2,258},{258,2},{3,259},{259,3},{4... | collective-permute-start | bytes 196616 | tf_op jit(solution)/shard_map/ppermute | solution.py:575
  15.1 0.7 copy-start.7
  15.1 0.7 copy-start.8
  17.8 21.5 %copy-start.2 = (s32[16,256]{1,0:T(8,128)S(1)}, s32[16,256]{1,0:T(8,128)}, u32[]{:S(2)}) copy-start(s32[16,256]{1,0:T(8,128)} %get-tuple-element.23.land_ref.refs_15_) | copy-start | bytes 49156
  17.8 21.5 %collective-permute-start.3 = (bf16[38,16,128]{2,1,0:T(8,128)(2,1)S(1)}, bf16[38,16,128]{2,1,0:T(8,128)(2,1)S(1)}, u32[]{:S(2)}, u32[]{:S(2)}) collective-permute-start(bf16[38,16,128]{2,1,0:T(8,128)(2,1)S(1)} %pack.2), channel_id=1, source_target_pairs={{8,0},{16,8},{24,16},{32,24},{40,32},{48,40},{56,48},{64,56},{72,6... | collective-permute-start | bytes 466952 | tf_op jit(solution)/shard_map/ppermute | solution.py:551
  23.5 15.8 %collective-permute-start.2 = (bf16[38,16,128]{2,1,0:T(8,128)(2,1)S(1)}, bf16[38,16,128]{2,1,0:T(8,128)(2,1)S(1)}, u32[]{:S(2)}, u32[]{:S(2)}) collective-permute-start(bf16[38,16,128]{2,1,0:T(8,128)(2,1)S(1)} %pack.2), channel_id=1, source_target_pairs={{0,8},{8,16},{16,24},{24,32},{32,40},{40,48},{48,56},{56,64},{64,7... | collective-permute-start | bytes 466952 | tf_op jit(solution)/shard_map/ppermute | solution.py:551
  25.4 7.8 %collective-permute-start.4 = (bf16[128,256]{1,0:T(8,128)(2,1)S(1)}, bf16[128,256]{1,0:T(8,128)(2,1)S(1)}, u32[]{:S(2)}, u32[]{:S(2)}) collective-permute-start(bf16[128,256]{1,0:T(8,128)(2,1)S(1)} %collective-permute-done.opposite_ref), channel_id=1, source_target_pairs={{16,0},{24,8},{32,16},{40,24},{48,32},{56,40},{64,48},{72,56},{80,... | collective-permute-start | bytes 196616 | tf_op jit(solution)/shard_map/ppermute | solution.py:551
  30.1 9.2 %collective-permute-start.1 = (bf16[128,256]{1,0:T(8,128)(2,1)S(1)}, bf16[128,256]{1,0:T(8,128)(2,1)S(1)}, u32[]{:S(2)}, u32[]{:S(2)}) collective-permute-start(bf16[128,256]{1,0:T(8,128)(2,1)S(1)} %collective-permute-done.opposite_ref), channel_id=1, source_target_pairs={{0,16},{8,24},{16,32},{24,40},{32,48},{40,56},{48,64},{56,72},{64,... | collective-permute-start | bytes 196616 | tf_op jit(solution)/shard_map/ppermute | solution.py:551
  41.7 2.6 %collective-permute-start.5 = (f32[4,16,128]{2,1,0:T(8,128)S(1)}, f32[4,16,128]{2,1,0:T(8,128)S(1)}, u32[]{:S(2)}, u32[]{:S(2)}) collective-permute-start(f32[4,16,128]{2,1,0:T(8,128)S(1)} %get-tuple-element.25), channel_id=1, source_target_pairs={{0,1},{1,2},{2,3},{3,4},{4,5},{5,6},{6,7},{8,9},{9,10},{10,11},{11... | collective-permute-start | bytes 98312 | tf_op jit(solution)/shard_map/ppermute | solution.py:551
  43.0 3.9 %collective-permute-start.6 = (f32[4,16,128]{2,1,0:T(8,128)S(1)}, f32[4,16,128]{2,1,0:T(8,128)S(1)}, u32[]{:S(2)}, u32[]{:S(2)}) collective-permute-start(f32[4,16,128]{2,1,0:T(8,128)S(1)} %get-tuple-element.26), channel_id=1, source_target_pairs={{1,0},{2,1},{3,2},{4,3},{5,4},{6,5},{7,6},{9,8},{10,9},{11,10},{12... | collective-permute-start | bytes 98312 | tf_op jit(solution)/shard_map/ppermute | solution.py:551
  47.0 14.7 %collective-permute-start.8 = (bf16[46,16,128]{2,1,0:T(8,128)(2,1)S(1)}, bf16[46,16,128]{2,1,0:T(8,128)(2,1)S(1)}, u32[]{:S(2)}, u32[]{:S(2)}) collective-permute-start(bf16[46,16,128]{2,1,0:T(8,128)(2,1)S(1)} %get-tuple-element.28), channel_id=1, source_target_pairs={{0,8},{8,16},{16,24},{24,32},{32,40},{40,48},{48,56},{56,64},{64,7... | collective-permute-start | bytes 565256 | tf_op jit(solution)/shard_map/ppermute | solution.py:551
  51.7 10.0 %collective-permute-start.9 = (bf16[46,16,128]{2,1,0:T(8,128)(2,1)S(1)}, bf16[46,16,128]{2,1,0:T(8,128)(2,1)S(1)}, u32[]{:S(2)}, u32[]{:S(2)}) collective-permute-start(bf16[46,16,128]{2,1,0:T(8,128)(2,1)S(1)} %get-tuple-element.29), channel_id=1, source_target_pairs={{8,0},{16,8},{24,16},{32,24},{40,32},{48,40},{56,48},{64,56},{72,6... | collective-permute-start | bytes 565256 | tf_op jit(solution)/shard_map/ppermute | solution.py:551
  54.9 10.6 %collective-permute-start.10 = (bf16[20,16,128]{2,1,0:T(8,128)(2,1)S(1)}, bf16[20,16,128]{2,1,0:T(8,128)(2,1)S(1)}, u32[]{:S(2)}, u32[]{:S(2)}) collective-permute-start(bf16[20,16,128]{2,1,0:T(8,128)(2,1)S(1)} %get-tuple-element.27), channel_id=1, source_target_pairs={{16,0},{24,8},{32,16},{40,24},{48,32},{56,40},{64,48},{72,56},{80,... | collective-permute-start | bytes 245768 | tf_op jit(solution)/shard_map/ppermute | solution.py:551
  56.9 10.6 %collective-permute-start.7 = (bf16[20,16,128]{2,1,0:T(8,128)(2,1)S(1)}, bf16[20,16,128]{2,1,0:T(8,128)(2,1)S(1)}, u32[]{:S(2)}, u32[]{:S(2)}) collective-permute-start(bf16[20,16,128]{2,1,0:T(8,128)(2,1)S(1)} %get-tuple-element.27), channel_id=1, source_target_pairs={{0,16},{8,24},{16,32},{24,40},{32,48},{40,56},{48,64},{56,72},{64,... | collective-permute-start | bytes 245768 | tf_op jit(solution)/shard_map/ppermute | solution.py:551
  61.7 5.7 %copy-start.3 = (f32[1,8,8]{2,1,0:T(8,128)S(1)}, f32[1,8,8]{2,1,0:T(8,128)}, u32[]{:S(2)}) copy-start(f32[1,8,8]{2,1,0:T(8,128)} %param.13) | copy-start | bytes 772
  61.7 5.7 %copy-start.4 = (f32[1,8,8]{2,1,0:T(8,128)S(1)}, f32[1,8,8]{2,1,0:T(8,128)}, u32[]{:S(2)}) copy-start(f32[1,8,8]{2,1,0:T(8,128)} %param.14) | copy-start | bytes 772
  65.5 33.8 %copy-start = (bf16[1,16,4,64,128]{4,3,2,1,0:T(8,128)(2,1)S(1)}, bf16[1,16,4,64,128]{4,3,2,1,0:T(8,128)(2,1)}, u32[]{:S(2)}) copy-start(bf16[1,16,4,64,128]{4,3,2,1,0:T(8,128)(2,1)} %param.19) | copy-start | bytes 3145732
  70.0 11.0 %collective-permute-start.11 = (bf16[128,256]{1,0:T(8,128)(2,1)S(1)}, bf16[128,256]{1,0:T(8,128)(2,1)S(1)}, u32[]{:S(2)}, u32[]{:S(2)}) collective-permute-start(bf16[128,256]{1,0:T(8,128)(2,1)S(1)} %get-tuple-element.31), channel_id=1, source_target_pairs={{0,256},{256,0},{1,257},{257,1},{2,258},{258,2},{3,259},{259,3},{4... | collective-permute-start | bytes 196616 | tf_op jit(solution)/shard_map/ppermute | solution.py:575
  81.1 18.2 %collective-permute-start.14 = (bf16[38,16,128]{2,1,0:T(8,128)(2,1)S(1)}, bf16[38,16,128]{2,1,0:T(8,128)(2,1)S(1)}, u32[]{:S(2)}, u32[]{:S(2)}) collective-permute-start(bf16[38,16,128]{2,1,0:T(8,128)(2,1)S(1)} %pack.3), channel_id=1, source_target_pairs={{8,0},{16,8},{24,16},{32,24},{40,32},{48,40},{56,48},{64,56},{72,6... | collective-permute-start | bytes 466952 | tf_op jit(solution)/shard_map/ppermute | solution.py:551
  83.0 16.3 %collective-permute-start.13 = (bf16[38,16,128]{2,1,0:T(8,128)(2,1)S(1)}, bf16[38,16,128]{2,1,0:T(8,128)(2,1)S(1)}, u32[]{:S(2)}, u32[]{:S(2)}) collective-permute-start(bf16[38,16,128]{2,1,0:T(8,128)(2,1)S(1)} %pack.3), channel_id=1, source_target_pairs={{0,8},{8,16},{16,24},{24,32},{32,40},{40,48},{48,56},{56,64},{64,7... | collective-permute-start | bytes 466952 | tf_op jit(solution)/shard_map/ppermute | solution.py:551
  86.9 7.5 %collective-permute-start.15 = (bf16[128,256]{1,0:T(8,128)(2,1)S(1)}, bf16[128,256]{1,0:T(8,128)(2,1)S(1)}, u32[]{:S(2)}, u32[]{:S(2)}) collective-permute-start(bf16[128,256]{1,0:T(8,128)(2,1)S(1)} %collective-permute-done.11.opposite_ref), channel_id=1, source_target_pairs={{16,0},{24,8},{32,16},{40,24},{48,32},{56,40},{64,48},{72,56},{80,... | collective-permute-start | bytes 196616 | tf_op jit(solution)/shard_map/ppermute | solution.py:551
  88.9 10.4 %collective-permute-start.12 = (bf16[128,256]{1,0:T(8,128)(2,1)S(1)}, bf16[128,256]{1,0:T(8,128)(2,1)S(1)}, u32[]{:S(2)}, u32[]{:S(2)}) collective-permute-start(bf16[128,256]{1,0:T(8,128)(2,1)S(1)} %collective-permute-done.11.opposite_ref), channel_id=1, source_target_pairs={{0,16},{8,24},{16,32},{24,40},{32,48},{40,56},{48,64},{56,72},{64,... | collective-permute-start | bytes 196616 | tf_op jit(solution)/shard_map/ppermute | solution.py:551
  101.3 2.6 %collective-permute-start.16 = (f32[4,16,128]{2,1,0:T(8,128)S(1)}, f32[4,16,128]{2,1,0:T(8,128)S(1)}, u32[]{:S(2)}, u32[]{:S(2)}) collective-permute-start(f32[4,16,128]{2,1,0:T(8,128)S(1)} %get-tuple-element.34), channel_id=1, source_target_pairs={{0,1},{1,2},{2,3},{3,4},{4,5},{5,6},{6,7},{8,9},{9,10},{10,11},{11... | collective-permute-start | bytes 98312 | tf_op jit(solution)/shard_map/ppermute | solution.py:551
  102.6 6.5 %collective-permute-start.17 = (f32[4,16,128]{2,1,0:T(8,128)S(1)}, f32[4,16,128]{2,1,0:T(8,128)S(1)}, u32[]{:S(2)}, u32[]{:S(2)}) collective-permute-start(f32[4,16,128]{2,1,0:T(8,128)S(1)} %get-tuple-element.35), channel_id=1, source_target_pairs={{1,0},{2,1},{3,2},{4,3},{5,4},{6,5},{7,6},{9,8},{10,9},{11,10},{12... | collective-permute-start | bytes 98312 | tf_op jit(solution)/shard_map/ppermute | solution.py:551
  109.0 14.7 %collective-permute-start.19 = (bf16[46,16,128]{2,1,0:T(8,128)(2,1)S(1)}, bf16[46,16,128]{2,1,0:T(8,128)(2,1)S(1)}, u32[]{:S(2)}, u32[]{:S(2)}) collective-permute-start(bf16[46,16,128]{2,1,0:T(8,128)(2,1)S(1)} %get-tuple-element.37), channel_id=1, source_target_pairs={{0,8},{8,16},{16,24},{24,32},{32,40},{40,48},{48,56},{56,64},{64,7... | collective-permute-start | bytes 565256 | tf_op jit(solution)/shard_map/ppermute | solution.py:551
  113.7 10.1 %collective-permute-start.20 = (bf16[46,16,128]{2,1,0:T(8,128)(2,1)S(1)}, bf16[46,16,128]{2,1,0:T(8,128)(2,1)S(1)}, u32[]{:S(2)}, u32[]{:S(2)}) collective-permute-start(bf16[46,16,128]{2,1,0:T(8,128)(2,1)S(1)} %get-tuple-element.38), channel_id=1, source_target_pairs={{8,0},{16,8},{24,16},{32,24},{40,32},{48,40},{56,48},{64,56},{72,6... | collective-permute-start | bytes 565256 | tf_op jit(solution)/shard_map/ppermute | solution.py:551
  117.0 10.6 %collective-permute-start.21 = (bf16[20,16,128]{2,1,0:T(8,128)(2,1)S(1)}, bf16[20,16,128]{2,1,0:T(8,128)(2,1)S(1)}, u32[]{:S(2)}, u32[]{:S(2)}) collective-permute-start(bf16[20,16,128]{2,1,0:T(8,128)(2,1)S(1)} %get-tuple-element.36), channel_id=1, source_target_pairs={{16,0},{24,8},{32,16},{40,24},{48,32},{56,40},{64,48},{72,56},{80,... | collective-permute-start | bytes 245768 | tf_op jit(solution)/shard_map/ppermute | solution.py:551
  118.9 10.6 %collective-permute-start.18 = (bf16[20,16,128]{2,1,0:T(8,128)(2,1)S(1)}, bf16[20,16,128]{2,1,0:T(8,128)(2,1)S(1)}, u32[]{:S(2)}, u32[]{:S(2)}) collective-permute-start(bf16[20,16,128]{2,1,0:T(8,128)(2,1)S(1)} %get-tuple-element.36), channel_id=1, source_target_pairs={{0,16},{8,24},{16,32},{24,40},{32,48},{40,56},{48,64},{56,72},{64,... | collective-permute-start | bytes 245768 | tf_op jit(solution)/shard_map/ppermute | solution.py:551

commit v5 on v4

--- a/solution.py
+++ b/solution.py
@@ -32,8 +32,9 @@
 C_PLANES = 20
 
 PAD = 8
+WEIGHT_CHUNKS = 8
 WAVE_SPEED = 8
-ROW0, COL0, ROW_END, COL_END = 10, 11, 12, 13
+ROW0, COL0, ROW_END, COL_END, NEAR_C, NEAR_I, FAR_C, FAR_I = range(8)
 SMEM = pl.BlockSpec(memory_space=pltpu.SMEM)
 VMEM = pl.BlockSpec(memory_space=pltpu.VMEM)
 HBM = pl.BlockSpec(memory_space=pl.ANY)
@@ -136,29 +137,29 @@
             split_to(ref, wave_at + 2 * i + half, wave_low_at + 2 * i + half, fields_ref[i, :, cols])
 
 
-def pack_kernel(opposite_ref, fields_ref, index_ref, config_ref, near_ref):
-    del index_ref, config_ref
+def pack_kernel(opposite_ref, fields_ref, index_ref, place_ref, config_ref, near_ref):
+    del index_ref, place_ref, config_ref
     write_main(near_ref, 0, A_WAVE, A_WAVE + 6, fields_ref)
     for half in range(2):
         for i in range(TURNED // 16):
             near_ref[A_EXPORT + half * 8 + i] = opposite_ref[16 * i : 16 * i + 16, half * LANES : (half + 1) * LANES]
 
 
-def pack(opposite, fields, index, config):
+def pack(opposite, fields, index, place, config):
     return pl.pallas_call(
         pack_kernel,
         out_shape=shaped((A_PLANES, ROWS, LANES), bf16),
-        in_specs=[VMEM] * 2 + [HBM] * 2,
+        in_specs=[VMEM] * 2 + [HBM] * 3,
         out_specs=VMEM,
         compiler_params=params(),
         name="pack",
-    )(opposite, fields, index, config)
+    )(opposite, fields, index, place, config)
 
 
 def pack_forcing_kernel(
-    forcing_ref, left_ref, right_ref, before_ref, after_ref, forward_ref, backward_ref, far_ref,
+    forcing_ref, left_ref, right_ref, state_c_ref, state_i_ref, out_c_ref, out_i_ref, far_ref,
 ):
-    for ref, behind in ((forward_ref, before_ref), (backward_ref, after_ref)):
+    for ref, behind in ((out_c_ref, state_i_ref), (out_i_ref, state_c_ref)):
         write_main(ref, 0, B_WAVE + 2, B_WAVE + 10, forcing_ref)
         for k, strips in enumerate((left_ref, right_ref)):
             ref[10 + k] = strips[0].astype(bf16)
@@ -168,12 +169,12 @@
         for p in range(12):
             ref[B_BEHIND + p] = behind[A_WAVE + p]
     for p in range(16):
-        far_ref[p] = forward_ref[B_WAVE + p]
+        far_ref[p] = out_c_ref[B_WAVE + p]
     for p in range(4):
-        far_ref[C_STRIP_W + p] = forward_ref[B_STRIP_W + p]
-
-
-def pack_forcing(forcing, left, right, before, after):
+        far_ref[C_STRIP_W + p] = out_c_ref[B_STRIP_W + p]
+
+
+def pack_forcing(forcing, left, right, state_c, state_i):
     payload = shaped((B_PLANES, ROWS, LANES), bf16)
     return pl.pallas_call(
         pack_forcing_kernel,
@@ -182,17 +183,21 @@
         out_specs=(VMEM,) * 3,
         compiler_params=params(),
         name="pack_forcing",
-    )(forcing, left, right, before, after)
+    )(forcing, left, right, state_c, state_i)
 
 
 def remap_kernel(
-    index_ref, far_before_ref, before_ref, opposite_ref, after_ref, far_after_ref, weight_hbm, land_ref, fields_ref,
-    forcing_ref, low_ref, high_ref, import_ref, table, turned, weight_ref, sem,
+    index_ref, far_i_ref, near_i_ref, opposite_ref, near_c_ref, far_c_ref, weight_hbm, land_ref, fields_ref,
+    forcing_ref, low_ref, high_ref, import_ref, table, turned, weight_ref, sems,
 ):
-    copy = pltpu.make_async_copy(weight_hbm, weight_ref, sem)
-    copy.start()
+    chunk_rows = ROWS // WEIGHT_CHUNKS
+    copies = []
+    for k in range(WEIGHT_CHUNKS):
+        rows = pl.ds(k * chunk_rows, chunk_rows)
+        copies.append(pltpu.make_async_copy(weight_hbm.at[rows], weight_ref.at[rows], sems.at[k]))
+        copies[k].start()
     half_count = 5 * ROWS * 2
-    windows = [far_before_ref, before_ref, opposite_ref, after_ref, far_after_ref]
+    windows = [far_c_ref, near_c_ref, opposite_ref, near_i_ref, far_i_ref]
     for w, ref in enumerate(windows):
         for half in range(2):
             for i in range(TURNED // 16):
@@ -209,8 +214,9 @@
     lane8 = lax.broadcasted_iota(jnp.int32, (8, LANES), 1)
     low_half = lane8 < 64
     ones = jnp.ones((8, LANES), f32)
-    copy.wait()
     for x in range(ROWS):
+        if x % chunk_rows == 0:
+            copies[x // chunk_rows].wait()
         pieces = []
         for seg in range(4):
             at = (x * 4 + seg) * 2
@@ -250,7 +256,7 @@
             pltpu.VMEM((2 * 5 * ROWS * 2, FIELDS, LANES), f32),
             pltpu.VMEM((2, TURNED, LANES), f32),
             pltpu.VMEM((ROWS, COLS, 128), bf16),
-            pltpu.SemaphoreType.DMA,
+            pltpu.SemaphoreType.DMA((WEIGHT_CHUNKS,)),
         ],
         compiler_params=params(52),
         name="remap",
@@ -266,23 +272,25 @@
     return jnp.where(lane < STRIP, right, jnp.where(lane >= 96, left, 0.0))
 
 
-def place_field(dest, rows, parts):
+def place_field(dest, start, parts, strip_start=None):
     for j, part in enumerate(parts):
-        dest[j, rows, :] = part
+        at = strip_start if j == 2 and strip_start is not None else start
+        at = at if isinstance(at, int) else pl.multiple_of(at, 8)
+        dest[j, pl.ds(at, ROWS), :] = part
 
 
 def joined(ref, at, low_at):
     return ref[at].astype(f32) + ref[low_at].astype(f32)
 
 
-def inside_tile(config_ref, first_row, count, j, shift=0):
+def inside_tile(place_ref, first_row, count, j, shift=0):
     shape = (count, LANES)
-    row = lax.broadcasted_iota(jnp.int32, shape, 0).astype(f32) + (config_ref[ROW0] + first_row)
+    row = lax.broadcasted_iota(jnp.int32, shape, 0) + (place_ref[ROW0] + first_row)
     col = lax.broadcasted_iota(jnp.int32, shape, 1) + j * LANES
     if j == 2:
         col = jnp.where(col >= 3 * LANES - STRIP, col - 3 * LANES, col)
-    col = (col + shift).astype(f32) + config_ref[COL0]
-    ok = (row >= 0.0) & (row < config_ref[ROW_END]) & (col >= 0.0) & (col < config_ref[COL_END])
+    col = col + (place_ref[COL0] + shift)
+    ok = (row >= 0) & (row < place_ref[ROW_END]) & (col >= 0) & (col < place_ref[COL_END])
     return jnp.where(ok, 1.0, 0.0)
 
 
@@ -316,12 +324,15 @@
 
 
 def tracer_kernel(
-    config_ref, near_before_ref, forcing_ref, left_ref, right_ref, near_after_ref,
-    state_before_ref, fields_ref, state_after_ref, out_ref, state, forcing, coef,
+    place_ref, config_ref, near_c_ref, forcing_ref, left_ref, right_ref, near_i_ref,
+    state_c_ref, fields_ref, state_i_ref, out_ref, state, forcing, coef,
 ):
-    for t, (near, main) in enumerate(
-        ((near_before_ref, state_before_ref), (None, None), (near_after_ref, state_after_ref))
-    ):
+    pairs = (
+        ((place_ref[NEAR_C] - 1) * ROWS, near_c_ref, state_c_ref),
+        ((place_ref[NEAR_I] - 1) * ROWS, near_i_ref, state_i_ref),
+        (ROWS, None, None),
+    )
+    for start, near, main in pairs:
         for i in range(TRACERS):
             if near is None:
                 pushed = own_parts(forcing_ref, left_ref, right_ref, 0, WAVES + i)
@@ -329,8 +340,8 @@
             else:
                 pushed = tracer_parts(near, near, 10, B_WAVE, i)
                 parts = tracer_parts(main, near, B_STRIP_T, B_STRIP_W, i)
-            place_field(forcing.at[i], slice(t * ROWS, (t + 1) * ROWS), pushed)
-            place_field(state.at[0, i], slice(PAD + t * ROWS, PAD + (t + 1) * ROWS), parts)
+            place_field(forcing.at[i], start, pushed)
+            place_field(state.at[0, i], start + PAD, parts)
     height = 3 * ROWS
     for k in range(2):
         for i in range(TRACERS):
@@ -338,7 +349,7 @@
                 state[k, i, j, 0:PAD, :] = jnp.zeros((PAD, LANES), f32)
                 state[k, i, j, PAD + height : height + 2 * PAD, :] = jnp.zeros((PAD, LANES), f32)
     for j in range(3):
-        coef[j] = inside_tile(config_ref, -ROWS, height, j) * DIFFUSION
+        coef[j] = inside_tile(place_ref, -ROWS, height, j) * DIFFUSION
 
     lane = lax.broadcasted_iota(jnp.int32, (8, LANES), 1)
     keep = [(1.0 - config_ref[WAVES + c]) - 4.0 * DIFFUSION for c in range(TRACERS)]
@@ -373,11 +384,11 @@
             out_ref[i, :, half * LANES : (half + 1) * LANES] = state[0, i, half, PAD + ROWS : PAD + 2 * ROWS, :]
 
 
-def tracer_steps(config, operands):
+def tracer_steps(place, config, operands):
     return pl.pallas_call(
         tracer_kernel,
         out_shape=shaped((TRACERS, ROWS, COLS)),
-        in_specs=[SMEM] + [VMEM] * len(operands),
+        in_specs=[SMEM] * 2 + [VMEM] * len(operands),
         out_specs=VMEM,
         scratch_shapes=[
             pltpu.VMEM((2, TRACERS, 3, 3 * ROWS + 2 * PAD, LANES), f32),
@@ -387,14 +398,14 @@
         compiler_params=params(),
         cost_estimate=pl.CostEstimate(flops=10_000_000, bytes_accessed=4_000_000, transcendentals=0),
         name="tracer_steps",
-    )(config, *operands)
-
-
-def wave_kernel(last, config_ref, *refs):
+    )(place, config, *operands)
+
+
+def wave_kernel(last, place_ref, config_ref, *refs):
     if not last:
         smix_ref, imix_ref, *refs = refs
-    (far_before, near_before, forcing_ref, left_ref, right_ref, near_after, far_after,
-     state_before, fields_ref, state_after, tracers_ref, *refs) = refs
+    (far_i, near_c, forcing_ref, left_ref, right_ref, near_i, far_c,
+     state_c, fields_ref, state_i, tracers_ref, *refs) = refs
     if last:
         out_ref, state, forcing, coef = refs
     else:
@@ -402,38 +413,34 @@
     height = 5 * ROWS
     tiles = height // 8
 
+    row_of = {k: PAD + place_ref[k] * ROWS for k in (NEAR_C, NEAR_I, FAR_C, FAR_I)}
     for i in range(WAVES):
-        forcing_tiles = [
-            wave_parts(far_before, 2, 10, far_before, 0, 8, i),
-            wave_parts(near_before, B_WAVE + 2, B_WAVE + 10, near_before, B_WAVE, B_WAVE + 8, i),
-            own_parts(forcing_ref, left_ref, right_ref, 0, i),
-            wave_parts(near_after, B_WAVE + 2, B_WAVE + 10, near_after, B_WAVE, B_WAVE + 8, i),
-            wave_parts(far_after, 2, 10, far_after, 0, 8, i),
-        ]
-        state_tiles = [
-            wave_parts(near_before, B_BEHIND, B_BEHIND + 6, far_before, C_STRIP_W, C_STRIP_W + 2, i),
-            wave_parts(state_before, A_WAVE, A_WAVE + 6, near_before, B_STRIP_W, B_STRIP_W + 2, i),
-            own_parts(fields_ref, left_ref, right_ref, 2, i),
-            wave_parts(state_after, A_WAVE, A_WAVE + 6, near_after, B_STRIP_W, B_STRIP_W + 2, i),
-            wave_parts(near_after, B_BEHIND, B_BEHIND + 6, far_after, C_STRIP_W, C_STRIP_W + 2, i),
-        ]
-        for t in range(5):
-            rows = slice(PAD + t * ROWS, PAD + (t + 1) * ROWS)
-            place_field(forcing.at[i], rows, forcing_tiles[t])
-            place_field(state.at[i], rows, state_tiles[t])
+        place_field(forcing.at[i], PAD + 2 * ROWS, own_parts(forcing_ref, left_ref, right_ref, 0, i))
+        place_field(state.at[i], PAD + 2 * ROWS, own_parts(fields_ref, left_ref, right_ref, 2, i))
+        for near, main, at in ((near_c, state_c, row_of[NEAR_C]), (near_i, state_i, row_of[NEAR_I])):
+            pushed = wave_parts(near, B_WAVE + 2, B_WAVE + 10, near, B_WAVE, B_WAVE + 8, i)
+            place_field(forcing.at[i], at, pushed)
+            place_field(state.at[i], at, wave_parts(main, A_WAVE, A_WAVE + 6, near, B_STRIP_W, B_STRIP_W + 2, i))
+        for far, near, at, main_at in (
+            (far_c, near_c, row_of[FAR_C], 2 * row_of[NEAR_C] - (PAD + 2 * ROWS)),
+            (far_i, near_i, row_of[FAR_I], 2 * row_of[NEAR_I] - (PAD + 2 * ROWS)),
+        ):
+            place_field(forcing.at[i], at, wave_parts(far, 2, 10, far, 0, 8, i))
+            parts = wave_parts(near, B_BEHIND, B_BEHIND + 6, far, C_STRIP_W, C_STRIP_W + 2, i)
+            place_field(state.at[i], main_at, parts, at)
         for j in range(3):
             for ref in (state, forcing):
                 ref[i, j, 0:PAD, :] = jnp.zeros((PAD, LANES), f32)
                 ref[i, j, PAD + height : height + 2 * PAD, :] = jnp.zeros((PAD, LANES), f32)
     half_a = 0.5 * config_ref[WAVE_SPEED]
     half_b = 0.5 * config_ref[WAVE_SPEED + 1]
-    first_row = -2.0 * ROWS
+    first_row = -2 * ROWS
     for j in range(3):
-        coef[0, j] = inside_tile(config_ref, first_row, height, j) * half_a
-        coef[1, j] = inside_tile(config_ref, first_row + 1.0, height, j) * half_b
-        coef[2, j] = inside_tile(config_ref, first_row - 1.0, height, j) * half_b
-        coef[3, j] = inside_tile(config_ref, first_row, height, j, 1) * half_b
-        coef[4, j] = inside_tile(config_ref, first_row, height, j, -1) * half_b
+        coef[0, j] = inside_tile(place_ref, first_row, height, j) * half_a
+        coef[1, j] = inside_tile(place_ref, first_row + 1, height, j) * half_b
+        coef[2, j] = inside_tile(place_ref, first_row - 1, height, j) * half_b
+        coef[3, j] = inside_tile(place_ref, first_row, height, j, 1) * half_b
+        coef[4, j] = inside_tile(place_ref, first_row, height, j, -1) * half_b
 
     lane = lax.broadcasted_iota(jnp.int32, (8, LANES), 1)
     keep = [1.0 - config_ref[c] for c in range(WAVES)]
@@ -505,7 +512,7 @@
     power_u, total_u = decays(keep[1])
     power_v, total_v = decays(keep[2])
     for j in range(2):
-        inside = inside_tile(config_ref, 0.0, ROWS, j) * half_b
+        inside = inside_tile(place_ref, 0, ROWS, j) * half_b
         for t in own:
             at = PAD + 8 * t
             rows = slice(8 * (t - 4), 8 * (t - 4) + 8)
@@ -526,7 +533,7 @@
         write_export(fields, received, land_ref[...].astype(f32), smix_ref, imix_ref, turned, export_ref)
 
 
-def wave_steps(last, config, mixes, operands):
+def wave_steps(last, place, config, mixes, operands):
     state = shaped((FIELDS, ROWS, COLS))
     scratch = [
         pltpu.VMEM((WAVES, 3, 5 * ROWS + 2 * PAD, LANES), f32),
@@ -538,17 +545,26 @@
     return pl.pallas_call(
         lambda *refs: wave_kernel(last, *refs),
         out_shape=state if last else (state, shaped((TURNED, COLS), bf16)),
-        in_specs=[SMEM] * (1 + len(mixes)) + [VMEM] * len(operands),
+        in_specs=[SMEM] * (2 + len(mixes)) + [VMEM] * len(operands),
         out_specs=VMEM if last else (VMEM,) * 2,
         scratch_shapes=scratch,
         compiler_params=params(),
         name="wave_steps_last" if last else "wave_steps",
-    )(config, *mixes, *operands)
+    )(place, config, *mixes, *operands)
 
 
 def line(block, axis, by):
     count = lax.axis_size(axis)
     return lax.ppermute(block, axis, [(i, i + by) for i in range(count) if 0 <= i + by < count])
+
+
+def exchanged(block, distance, phase):
+    count = lax.axis_size("gx")
+    route = []
+    for low in range(count - distance):
+        if (low // distance) % 2 == phase:
+            route += [(low, low + distance), (low + distance, low)]
+    return lax.ppermute(block, "gx", route)
 
 
 def local(
@@ -559,44 +575,50 @@
     imix = import_mix[0]
     gx = lax.axis_index("gx")
     gy = lax.axis_index("gy")
-    place = jnp.stack([gx * ROWS, gy * COLS, lax.axis_size("gx") * ROWS, lax.axis_size("gy") * COLS])
-    config = jnp.concatenate([damping[0], wave_speed[0], place.astype(f32)])
+    side_near = 1 - 2 * (gx % 2)
+    side_far = 1 - 2 * ((gx // 2) % 2)
+    place = jnp.stack([
+        gx * ROWS, gy * COLS, lax.axis_size("gx") * ROWS, lax.axis_size("gy") * COLS,
+        2 - side_near, 2 + side_near, 2 - 2 * side_far, 2 + 2 * side_far,
+    ]).astype(jnp.int32)
+    config = jnp.concatenate([damping[0], wave_speed[0]])
     owner = remap_owner[0].reshape(-1)
     slot = remap_slot[0].reshape(-1)
-    entry = ((owner - gx + 2) * ROWS + slot // 4) * 2 + (slot % 4) // 2
+    away = owner - gx
+    window = 2 + away * jnp.where(away % 2 == 1, side_near, side_far)
+    entry = (window * ROWS + slot // 4) * 2 + (slot % 4) // 2
     second = lax.iota(jnp.int32, owner.shape[0]) % 2
     index = entry + ((slot % 2) ^ second) * (5 * ROWS * 2)
-
     weight = remap_weight[0].reshape(ROWS, COLS, 128)
 
     exported, fields, land = export(section_state[0], prev_import[0], land_mask[0], smix, imix)
     for interval in range(ITERS):
         last = interval == ITERS - 1
         opposite = lax.ppermute(exported, "sec", [(0, 1), (1, 0)])
-        near = pack(opposite, fields, index, config)
-        far_before = line(opposite, "gx", 2)
-        far_after = line(opposite, "gx", -2)
-        before = line(near, "gx", 1)
-        after = line(near, "gx", -1)
+        near = pack(opposite, fields, index, place, config)
+        state_c = exchanged(near, 1, 1)
+        state_i = exchanged(near, 1, 0)
+        export_c = exchanged(opposite, 2, 1)
+        export_i = exchanged(opposite, 2, 0)
         forcing, low, high, received = remap(
-            index, (far_before, before, opposite, after, far_after), weight, land, fields
+            index, (export_i, state_i, opposite, state_c, export_c), weight, land, fields
         )
         left = line(high, "gy", 1)
         right = line(low, "gy", -1)
-        forward, backward, outer = pack_forcing(forcing, left, right, before, after)
-        near_before = line(forward, "gx", 1)
-        near_after = line(backward, "gx", -1)
-        outer_before = line(outer, "gx", 2)
-        outer_after = line(outer, "gx", -2)
+        out_c, out_i, outer = pack_forcing(forcing, left, right, state_c, state_i)
+        near_c = exchanged(out_c, 1, 1)
+        near_i = exchanged(out_i, 1, 0)
+        far_c = exchanged(outer, 2, 1)
+        far_i = exchanged(outer, 2, 0)
         own = (forcing, left, right)
-        state = (before, fields, after)
-        tracers = tracer_steps(config, (near_before, *own, near_after, *state))
-        operands = (outer_before, near_before, *own, near_after, outer_after, *state, tracers)
+        state = (state_c, fields, state_i)
+        tracers = tracer_steps(place, config, (near_c, *own, near_i, *state))
+        operands = (far_i, near_c, *own, near_i, far_c, *state, tracers)
         if last:
-            fields = wave_steps(last, config, (), operands)
+            fields = wave_steps(last, place, config, (), operands)
         else:
             operands += (received, land)
-            fields, exported = wave_steps(last, config, (smix, imix), operands)
+            fields, exported = wave_steps(last, place, config, (smix, imix), operands)
     return (fields[None], received[None])
 
 

time: 135 us -> 134 us (level); the launches traced: 133 us -> 133 us
  waiting for transfers between devices: 29.5 us -> 26.8 us
  Pallas kernels: 20.3 us -> 22.9 us
    ppermute x20 -> x4, starting transfers between devices: 61.4 us -> 5.17 us  [line(): lax.ppermute(block, axis, [(i, i + by) for i in range(count) if 0 <= i +...]
    ppermute x0 -> x16, starting transfers between devices: none -> 55.9 us  [exchanged(): return lax.ppermute(block, 'gx', route)]
    ppermute x20 -> x4, waiting for transfers between devices: 24.4 us -> 7.45 us  [line(): lax.ppermute(block, axis, [(i, i + by) for i in range(count) if 0 <= i +...]
    ppermute x0 -> x16, waiting for transfers between devices: none -> 15.4 us  [exchanged(): return lax.ppermute(block, 'gx', route)]
    pallas_call x2, Pallas kernels: 4.36 us -> 7.13 us  [remap(): pl.pallas_call(remap_kernel, out_shape=(shaped((FIELDS, ROWS, COLS)), str...]
where the time goes in v5:
time: 134 us; the launch traced here: 133 us
  starting transfers between devices  79.6 us (59%)
  waiting for transfers between devices  26.8 us (20%)
  Pallas kernels  22.9 us (17%)
  local copies, waits for them, and re-layouts  2.47 us (2%)
    ppermute x16, starting transfers between devices, exchanged(): return lax.ppermute(block, 'gx', route)  55.9 us
    ppermute x2, starting transfers between devices, local(): opposite = lax.ppermute(exported, 'sec', [(0, 1), (1, 0)])  18.6 us
    ppermute x16, waiting for transfers between devices, exchanged(): return lax.ppermute(block, 'gx', route)  15.4 us
    pallas_call x2, Pallas kernels, tracer_steps(): pl.pallas_call(tracer_kernel, out_shape=shaped((TRACERS, ROWS, COLS)), in...  7.56 us
    ppermute x4, waiting for transfers between devices, line(): lax.ppermute(block, axis, [(i, i + by) for i in range(count) if 0 <= i +...  7.45 us
    pallas_call x2, Pallas kernels, remap(): pl.pallas_call(remap_kernel, out_shape=(shaped((FIELDS, ROWS, COLS)), str...  7.13 us
    pallas_call x2, Pallas kernels, wave_steps(): pl.pallas_call(lambda *refs: wave_kernel(last, *refs), out_shape=state if...  5.53 us
    ppermute x4, starting transfers between devices, line(): lax.ppermute(block, axis, [(i, i + by) for i in range(count) if 0 <= i +...  5.17 us
  transfers between devices with their start and end apart: 22, of which 10 were waited for; matrix products, arithmetic and copies ran while one was open for 1% of the time, Pallas kernels for 6%

profile of v5, /device:TPU:6, one launch (start us, length us, event | category | flops | bytes accessed | tf_op | source)
XLA Modules:
  0.0 132.9 jit_solution(3185747036054562661)
XLA Ops:
  0.6 2.6 %export.1 = (bf16[128,256]{1,0:T(8,128)(2,1)}, f32[8,16,256]{2,1,0:T(8,128)}, s32[16,256]{1,0:T(8,128)}) custom-call(f32[8,8]{1,0:T(8,128)} %bitcast.20, f32[8,8]{1,0:T(8,128)} %bitcast.22, f32[8,16,256]{2,1,0:T(8,128)} %bitcast.25, f32[8,16,256]{2,1,0:T(8,128)} %bitcast.26, s32[16,256]{1,0:T(8,128)} %bitcast.27), custom_call_target="tpu_custom_call" | custom-call | tf_op jit(solution)/shard_map/export/pallas_call | solution.py:108
  3.2 10.9 %collective-permute-start = (bf16[128,256]{1,0:T(8,128)(2,1)}, bf16[128,256]{1,0:T(8,128)(2,1)S(1)}, u32[]{:S(2)}, u32[]{:S(2)}) collective-permute-start(bf16[128,256]{1,0:T(8,128)(2,1)} %get-tuple-element.21), channel_id=1, source_target_pairs={{0,256},{256,0},{1,257},{257,1},{2,258},{258,2},{3,259},{259,3},{4... | collective-permute-start | bytes 196616 | tf_op jit(solution)/shard_map/ppermute | solution.py:597
  14.2 0.6 copy-done.6
  14.9 0.1 copy.14
  15.0 0.1 sub.42
  15.1 0.5 copy-done.5
  15.7 0.1 copy.15
  15.8 0.1 reshape_squeeze.7
  15.9 0.1 stack.27.place_ref.refs_0_
  16.0 0.7 copy-done.7
  16.7 0.1 pad_maximum_fusion.config_ref.refs_1_
  16.8 0.7 collective-permute-done.opposite_ref
  17.5 5.6 %collective-permute-start.3 = (bf16[38,16,128]{2,1,0:T(8,128)(2,1)S(1)}, bf16[38,16,128]{2,1,0:T(8,128)(2,1)S(1)}, u32[]{:S(2)}, u32[]{:S(2)}) collective-permute-start(bf16[38,16,128]{2,1,0:T(8,128)(2,1)S(1)} %pack.2), channel_id=1, source_target_pairs={{8,16},{16,8},{24,32},{32,24},{40,48},{48,40},{56,64},{64,56},{72,... | collective-permute-start | bytes 466952 | tf_op jit(solution)/shard_map/ppermute | solution.py:567
  23.2 1.9 %collective-permute-start.2 = (bf16[38,16,128]{2,1,0:T(8,128)(2,1)S(1)}, bf16[38,16,128]{2,1,0:T(8,128)(2,1)S(1)}, u32[]{:S(2)}, u32[]{:S(2)}) collective-permute-start(bf16[38,16,128]{2,1,0:T(8,128)(2,1)S(1)} %pack.2), channel_id=1, source_target_pairs={{0,8},{8,0},{16,24},{24,16},{32,40},{40,32},{48,56},{56,48},{64,72... | collective-permute-start | bytes 466952 | tf_op jit(solution)/shard_map/ppermute | solution.py:567
  25.1 4.0 %collective-permute-start.4 = (bf16[128,256]{1,0:T(8,128)(2,1)S(1)}, bf16[128,256]{1,0:T(8,128)(2,1)S(1)}, u32[]{:S(2)}, u32[]{:S(2)}) collective-permute-start(bf16[128,256]{1,0:T(8,128)(2,1)S(1)} %collective-permute-done.opposite_ref), channel_id=1, source_target_pairs={{16,32},{32,16},{24,40},{40,24},{48,64},{64,48},{56,72},{72,56},{8... | collective-permute-start | bytes 196616 | tf_op jit(solution)/shard_map/ppermute | solution.py:567
  29.2 3.8 %collective-permute-start.1 = (bf16[128,256]{1,0:T(8,128)(2,1)S(1)}, bf16[128,256]{1,0:T(8,128)(2,1)S(1)}, u32[]{:S(2)}, u32[]{:S(2)}) collective-permute-start(bf16[128,256]{1,0:T(8,128)(2,1)S(1)} %collective-permute-done.opposite_ref), channel_id=1, source_target_pairs={{0,16},{16,0},{8,24},{24,8},{32,48},{48,32},{40,56},{56,40},{64,80... | collective-permute-start | bytes 196616 | tf_op jit(solution)/shard_map/ppermute | solution.py:567
  33.0 1.3 %collective-permute-done.4.far_c_ref = bf16[128,256]{1,0:T(8,128)(2,1)S(1)} collective-permute-done((bf16[128,256]{1,0:T(8,128)(2,1)S(1)}, bf16[128,256]{1,0:T(8,128)(2,1)S(1)}, u32[]{:S(2)}, u32[]{:S(2)}) %collective-permute-start.4) | collective-permute-done | bytes 65568 | tf_op jit(solution)/shard_map/ppermute | solution.py:567
  34.3 1.9 %collective-permute-done.1.far_i_ref = bf16[128,256]{1,0:T(8,128)(2,1)S(1)} collective-permute-done((bf16[128,256]{1,0:T(8,128)(2,1)S(1)}, bf16[128,256]{1,0:T(8,128)(2,1)S(1)}, u32[]{:S(2)}, u32[]{:S(2)}) %collective-permute-start.1) | collective-permute-done | bytes 65568 | tf_op jit(solution)/shard_map/ppermute | solution.py:567
  36.2 3.0 %remap.2 = (f32[8,16,256]{2,1,0:T(8,128)S(1)}, f32[4,16,128]{2,1,0:T(8,128)S(1)}, f32[4,16,128]{2,1,0:T(8,128)S(1)}, f32[8,16,256]{2,1,0:T(8,128)S(1)}) custom-call(s32[128]{0:T(128)S(1)} %multiply_add_fusion.index_ref, bf16[128,256]{1,0:T(8,128)(2,1)S(1)} %collective-permute-done.1.far_i_ref, ...), custom_call_target="tpu_custom_call" | custom-call | tf_op jit(solution)/shard_map/remap/pallas_call | solution.py:250
  39.2 1.3 collective-permute-start.5
  40.5 1.3 collective-permute-start.6
  41.9 2.8 %collective-permute-done.6.right_ref.refs_8_ = f32[4,16,128]{2,1,0:T(8,128)S(1)} collective-permute-done((f32[4,16,128]{2,1,0:T(8,128)S(1)}, f32[4,16,128]{2,1,0:T(8,128)S(1)}, u32[]{:S(2)}, u32[]{:S(2)}) %collective-permute-start.6) | collective-permute-done | bytes 32800 | tf_op jit(solution)/shard_map/ppermute | solution.py:558
  44.7 5.5 %collective-permute-start.8 = (bf16[46,16,128]{2,1,0:T(8,128)(2,1)S(1)}, bf16[46,16,128]{2,1,0:T(8,128)(2,1)S(1)}, u32[]{:S(2)}, u32[]{:S(2)}) collective-permute-start(bf16[46,16,128]{2,1,0:T(8,128)(2,1)S(1)} %get-tuple-element.28), channel_id=1, source_target_pairs={{8,16},{16,8},{24,32},{32,24},{40,48},{48,40},{56,64},{64,56},{72,... | collective-permute-start | bytes 565256 | tf_op jit(solution)/shard_map/ppermute | solution.py:567
  50.2 1.9 %collective-permute-start.9 = (bf16[46,16,128]{2,1,0:T(8,128)(2,1)S(1)}, bf16[46,16,128]{2,1,0:T(8,128)(2,1)S(1)}, u32[]{:S(2)}, u32[]{:S(2)}) collective-permute-start(bf16[46,16,128]{2,1,0:T(8,128)(2,1)S(1)} %get-tuple-element.29), channel_id=1, source_target_pairs={{0,8},{8,0},{16,24},{24,16},{32,40},{40,32},{48,56},{56,48},{64,72... | collective-permute-start | bytes 565256 | tf_op jit(solution)/shard_map/ppermute | solution.py:567
  52.1 3.9 %collective-permute-start.10 = (bf16[20,16,128]{2,1,0:T(8,128)(2,1)S(1)}, bf16[20,16,128]{2,1,0:T(8,128)(2,1)S(1)}, u32[]{:S(2)}, u32[]{:S(2)}) collective-permute-start(bf16[20,16,128]{2,1,0:T(8,128)(2,1)S(1)} %get-tuple-element.27), channel_id=1, source_target_pairs={{16,32},{32,16},{24,40},{40,24},{48,64},{64,48},{56,72},{72,56},{8... | collective-permute-start | bytes 245768 | tf_op jit(solution)/shard_map/ppermute | solution.py:567
  56.0 2.7 %collective-permute-start.7 = (bf16[20,16,128]{2,1,0:T(8,128)(2,1)S(1)}, bf16[20,16,128]{2,1,0:T(8,128)(2,1)S(1)}, u32[]{:S(2)}, u32[]{:S(2)}) collective-permute-start(bf16[20,16,128]{2,1,0:T(8,128)(2,1)S(1)} %get-tuple-element.27), channel_id=1, source_target_pairs={{0,16},{16,0},{8,24},{24,8},{32,48},{48,32},{40,56},{56,40},{64,80... | collective-permute-start | bytes 245768 | tf_op jit(solution)/shard_map/ppermute | solution.py:567
  58.7 3.8 %tracer_steps.2.refs_14_ = f32[5,16,256]{2,1,0:T(8,128)S(1)} custom-call(s32[8]{0:T(128)S(1)} %stack.27.place_ref.refs_0_, f32[10]{0:T(128)S(1)} %pad_maximum_fusion.config_ref.refs_1_, bf16[46,16,128]{2,1,0:T(8,128)(2,1)S(1)} %collective-permute-done.8.near_c_ref.refs_5_, f32[8,16,256]{2,1,0:T(8,128)S(1)} %get-tuple-element.24.forcing_ref.refs_6_, ...), custom_call_target="tpu_custom_call" | custom-call | flops 10000000 | bytes 4000000 | tf_op jit(solution)/shard_map/tracer_steps/pallas_call | solution.py:388
  62.6 3.1 %collective-permute-done.7.refs_4_ = bf16[20,16,128]{2,1,0:T(8,128)(2,1)S(1)} collective-permute-done((bf16[20,16,128]{2,1,0:T(8,128)(2,1)S(1)}, bf16[20,16,128]{2,1,0:T(8,128)(2,1)S(1)}, u32[]{:S(2)}, u32[]{:S(2)}) %collective-permute-start.7) | collective-permute-done | bytes 81952 | tf_op jit(solution)/shard_map/ppermute | solution.py:567
  65.7 2.6 %wave_steps.1 = (f32[8,16,256]{2,1,0:T(8,128)S(1)}, bf16[128,256]{1,0:T(8,128)(2,1)S(1)}) custom-call(s32[8]{0:T(128)S(1)} %stack.27.place_ref.refs_0_, f32[10]{0:T(128)S(1)} %pad_maximum_fusion.config_ref.refs_1_, f32[8,8]{1,0:T(8,128)S(1)} %bitcast.21, f32[8,8]{1,0:T(8,128)S(1)} %bitcast.23, bf16[20,16,128]{2,1,0:T(8,128)(2,1)S(1)} %collective-permute-done.7.refs_4_, ...), custom_call_target="tpu_custom_call" | custom-call | tf_op jit(solution)/shard_map/wave_steps/pallas_call | solution.py:545
  68.3 7.7 %collective-permute-start.11 = (bf16[128,256]{1,0:T(8,128)(2,1)S(1)}, bf16[128,256]{1,0:T(8,128)(2,1)S(1)}, u32[]{:S(2)}, u32[]{:S(2)}) collective-permute-start(bf16[128,256]{1,0:T(8,128)(2,1)S(1)} %get-tuple-element.31), channel_id=1, source_target_pairs={{0,256},{256,0},{1,257},{257,1},{2,258},{258,2},{3,259},{259,3},{4... | collective-permute-start | bytes 196616 | tf_op jit(solution)/shard_map/ppermute | solution.py:597
  75.9 3.2 %collective-permute-done.11.opposite_ref = bf16[128,256]{1,0:T(8,128)(2,1)S(1)} collective-permute-done((bf16[128,256]{1,0:T(8,128)(2,1)S(1)}, bf16[128,256]{1,0:T(8,128)(2,1)S(1)}, u32[]{:S(2)}, u32[]{:S(2)}) %collective-permute-start.11) | collective-permute-done | bytes 65568 | tf_op jit(solution)/shard_map/ppermute | solution.py:597
  79.1 5.1 %collective-permute-start.14 = (bf16[38,16,128]{2,1,0:T(8,128)(2,1)S(1)}, bf16[38,16,128]{2,1,0:T(8,128)(2,1)S(1)}, u32[]{:S(2)}, u32[]{:S(2)}) collective-permute-start(bf16[38,16,128]{2,1,0:T(8,128)(2,1)S(1)} %pack.3), channel_id=1, source_target_pairs={{8,16},{16,8},{24,32},{32,24},{40,48},{48,40},{56,64},{64,56},{72,... | collective-permute-start | bytes 466952 | tf_op jit(solution)/shard_map/ppermute | solution.py:567
  84.2 1.9 %collective-permute-start.13 = (bf16[38,16,128]{2,1,0:T(8,128)(2,1)S(1)}, bf16[38,16,128]{2,1,0:T(8,128)(2,1)S(1)}, u32[]{:S(2)}, u32[]{:S(2)}) collective-permute-start(bf16[38,16,128]{2,1,0:T(8,128)(2,1)S(1)} %pack.3), channel_id=1, source_target_pairs={{0,8},{8,0},{16,24},{24,16},{32,40},{40,32},{48,56},{56,48},{64,72... | collective-permute-start | bytes 466952 | tf_op jit(solution)/shard_map/ppermute | solution.py:567
  86.2 4.3 %collective-permute-start.15 = (bf16[128,256]{1,0:T(8,128)(2,1)S(1)}, bf16[128,256]{1,0:T(8,128)(2,1)S(1)}, u32[]{:S(2)}, u32[]{:S(2)}) collective-permute-start(bf16[128,256]{1,0:T(8,128)(2,1)S(1)} %collective-permute-done.11.opposite_ref), channel_id=1, source_target_pairs={{16,32},{32,16},{24,40},{40,24},{48,64},{64,48},{56,72},{72,56},{8... | collective-permute-start | bytes 196616 | tf_op jit(solution)/shard_map/ppermute | solution.py:567
  90.5 1.9 %collective-permute-start.12 = (bf16[128,256]{1,0:T(8,128)(2,1)S(1)}, bf16[128,256]{1,0:T(8,128)(2,1)S(1)}, u32[]{:S(2)}, u32[]{:S(2)}) collective-permute-start(bf16[128,256]{1,0:T(8,128)(2,1)S(1)} %collective-permute-done.11.opposite_ref), channel_id=1, source_target_pairs={{0,16},{16,0},{8,24},{24,8},{32,48},{48,32},{40,56},{56,40},{64,80... | collective-permute-start | bytes 196616 | tf_op jit(solution)/shard_map/ppermute | solution.py:567
  92.4 2.9 %collective-permute-done.15.far_c_ref = bf16[128,256]{1,0:T(8,128)(2,1)S(1)} collective-permute-done((bf16[128,256]{1,0:T(8,128)(2,1)S(1)}, bf16[128,256]{1,0:T(8,128)(2,1)S(1)}, u32[]{:S(2)}, u32[]{:S(2)}) %collective-permute-start.15) | collective-permute-done | bytes 65568 | tf_op jit(solution)/shard_map/ppermute | solution.py:567
  95.3 2.4 %collective-permute-done.12.far_i_ref = bf16[128,256]{1,0:T(8,128)(2,1)S(1)} collective-permute-done((bf16[128,256]{1,0:T(8,128)(2,1)S(1)}, bf16[128,256]{1,0:T(8,128)(2,1)S(1)}, u32[]{:S(2)}, u32[]{:S(2)}) %collective-permute-start.12) | collective-permute-done | bytes 65568 | tf_op jit(solution)/shard_map/ppermute | solution.py:567
  97.7 4.1 %remap.3 = (f32[8,16,256]{2,1,0:T(8,128)S(1)}, f32[4,16,128]{2,1,0:T(8,128)S(1)}, f32[4,16,128]{2,1,0:T(8,128)S(1)}, f32[8,16,256]{2,1,0:T(8,128)}) custom-call(s32[128]{0:T(128)S(1)} %multiply_add_fusion.index_ref, bf16[128,256]{1,0:T(8,128)(2,1)S(1)} %collective-permute-done.12.far_i_ref, ...), custom_call_target="tpu_custom_call" | custom-call | tf_op jit(solution)/shard_map/remap/pallas_call | solution.py:250
  101.9 1.3 collective-permute-start.16
  103.2 1.3 collective-permute-start.17
  104.5 4.7 %collective-permute-done.17.right_ref.refs_6_ = f32[4,16,128]{2,1,0:T(8,128)S(1)} collective-permute-done((f32[4,16,128]{2,1,0:T(8,128)S(1)}, f32[4,16,128]{2,1,0:T(8,128)S(1)}, u32[]{:S(2)}, u32[]{:S(2)}) %collective-permute-start.17) | collective-permute-done | bytes 32800 | tf_op jit(solution)/shard_map/ppermute | solution.py:558
  109.2 5.1 %collective-permute-start.19 = (bf16[46,16,128]{2,1,0:T(8,128)(2,1)S(1)}, bf16[46,16,128]{2,1,0:T(8,128)(2,1)S(1)}, u32[]{:S(2)}, u32[]{:S(2)}) collective-permute-start(bf16[46,16,128]{2,1,0:T(8,128)(2,1)S(1)} %get-tuple-element.37), channel_id=1, source_target_pairs={{8,16},{16,8},{24,32},{32,24},{40,48},{48,40},{56,64},{64,56},{72,... | collective-permute-start | bytes 565256 | tf_op jit(solution)/shard_map/ppermute | solution.py:567
  114.3 1.9 %collective-permute-start.20 = (bf16[46,16,128]{2,1,0:T(8,128)(2,1)S(1)}, bf16[46,16,128]{2,1,0:T(8,128)(2,1)S(1)}, u32[]{:S(2)}, u32[]{:S(2)}) collective-permute-start(bf16[46,16,128]{2,1,0:T(8,128)(2,1)S(1)} %get-tuple-element.38), channel_id=1, source_target_pairs={{0,8},{8,0},{16,24},{24,16},{32,40},{40,32},{48,56},{56,48},{64,72... | collective-permute-start | bytes 565256 | tf_op jit(solution)/shard_map/ppermute | solution.py:567
  116.2 4.3 %collective-permute-start.21 = (bf16[20,16,128]{2,1,0:T(8,128)(2,1)S(1)}, bf16[20,16,128]{2,1,0:T(8,128)(2,1)S(1)}, u32[]{:S(2)}, u32[]{:S(2)}) collective-permute-start(bf16[20,16,128]{2,1,0:T(8,128)(2,1)S(1)} %get-tuple-element.36), channel_id=1, source_target_pairs={{16,32},{32,16},{24,40},{40,24},{48,64},{64,48},{56,72},{72,56},{8... | collective-permute-start | bytes 245768 | tf_op jit(solution)/shard_map/ppermute | solution.py:567
  120.5 1.9 %collective-permute-start.18 = (bf16[20,16,128]{2,1,0:T(8,128)(2,1)S(1)}, bf16[20,16,128]{2,1,0:T(8,128)(2,1)S(1)}, u32[]{:S(2)}, u32[]{:S(2)}) collective-permute-start(bf16[20,16,128]{2,1,0:T(8,128)(2,1)S(1)} %get-tuple-element.36), channel_id=1, source_target_pairs={{0,16},{16,0},{8,24},{24,8},{32,48},{48,32},{40,56},{56,40},{64,80... | collective-permute-start | bytes 245768 | tf_op jit(solution)/shard_map/ppermute | solution.py:567
  122.5 3.8 %tracer_steps.3.refs_12_ = f32[5,16,256]{2,1,0:T(8,128)S(1)} custom-call(s32[8]{0:T(128)S(1)} %stack.27.place_ref.refs_0_, f32[10]{0:T(128)S(1)} %pad_maximum_fusion.config_ref.refs_1_, bf16[46,16,128]{2,1,0:T(8,128)(2,1)S(1)} %collective-permute-done.19.near_c_ref.refs_3_, f32[8,16,256]{2,1,0:T(8,128)S(1)} %get-tuple-element.33.forcing_ref.refs_4_, ...), custom_call_target="tpu_custom_call" | custom-call | flops 10000000 | bytes 4000000 | tf_op jit(solution)/shard_map/tracer_steps/pallas_call | solution.py:388
  126.3 3.7 %collective-permute-done.18.refs_2_ = bf16[20,16,128]{2,1,0:T(8,128)(2,1)S(1)} collective-permute-done((bf16[20,16,128]{2,1,0:T(8,128)(2,1)S(1)}, bf16[20,16,128]{2,1,0:T(8,128)(2,1)S(1)}, u32[]{:S(2)}, u32[]{:S(2)}) %collective-permute-start.18) | collective-permute-done | bytes 81952 | tf_op jit(solution)/shard_map/ppermute | solution.py:567
  130.0 3.0 %wave_steps_last.1 = f32[8,16,256]{2,1,0:T(8,128)} custom-call(s32[8]{0:T(128)S(1)} %stack.27.place_ref.refs_0_, f32[10]{0:T(128)S(1)} %pad_maximum_fusion.config_ref.refs_1_, bf16[20,16,128]{2,1,0:T(8,128)(2,1)S(1)} %collective-permute-done.18.refs_2_, bf16[46,16,128]{2,1,0:T(8,128)(2,1)S(1)} %collective-permute-done.19.near_c_ref.refs_3_, ...), custom_call_target="tpu_custom_call" | custom-call | tf_op jit(solution)/shard_map/wave_steps_last/pallas_call | solution.py:545
  (33 shorter events, 0.2 us)
Async XLA Ops:
  3.2 14.3 %collective-permute-start = (bf16[128,256]{1,0:T(8,128)(2,1)}, bf16[128,256]{1,0:T(8,128)(2,1)S(1)}, u32[]{:S(2)}, u32[]{:S(2)}) collective-permute-start(bf16[128,256]{1,0:T(8,128)(2,1)} %get-tuple-element.21), channel_id=1, source_target_pairs={{0,256},{256,0},{1,257},{257,1},{2,258},{258,2},{3,259},{259,3},{4... | collective-permute-start | bytes 196616 | tf_op jit(solution)/shard_map/ppermute | solution.py:597
  14.2 0.7 copy-start.6
  14.2 3.3 %copy-start.1 = (f32[8,16,256]{2,1,0:T(8,128)S(1)}, f32[8,16,256]{2,1,0:T(8,128)}, u32[]{:S(2)}) copy-start(f32[8,16,256]{2,1,0:T(8,128)} %get-tuple-element.22.fields_ref.refs_12_) | copy-start | bytes 393220
  15.0 0.7 copy-start.5
  16.0 0.7 copy-start.7
  16.0 0.7 copy-start.8
  17.5 18.7 %copy-start.2 = (s32[16,256]{1,0:T(8,128)S(1)}, s32[16,256]{1,0:T(8,128)}, u32[]{:S(2)}) copy-start(s32[16,256]{1,0:T(8,128)} %get-tuple-element.23.land_ref.refs_16_) | copy-start | bytes 49156
  17.5 18.7 %collective-permute-start.3 = (bf16[38,16,128]{2,1,0:T(8,128)(2,1)S(1)}, bf16[38,16,128]{2,1,0:T(8,128)(2,1)S(1)}, u32[]{:S(2)}, u32[]{:S(2)}) collective-permute-start(bf16[38,16,128]{2,1,0:T(8,128)(2,1)S(1)} %pack.2), channel_id=1, source_target_pairs={{8,16},{16,8},{24,32},{32,24},{40,48},{48,40},{56,64},{64,56},{72,... | collective-permute-start | bytes 466952 | tf_op jit(solution)/shard_map/ppermute | solution.py:567
  23.2 13.0 %collective-permute-start.2 = (bf16[38,16,128]{2,1,0:T(8,128)(2,1)S(1)}, bf16[38,16,128]{2,1,0:T(8,128)(2,1)S(1)}, u32[]{:S(2)}, u32[]{:S(2)}) collective-permute-start(bf16[38,16,128]{2,1,0:T(8,128)(2,1)S(1)} %pack.2), channel_id=1, source_target_pairs={{0,8},{8,0},{16,24},{24,16},{32,40},{40,32},{48,56},{56,48},{64,72... | collective-permute-start | bytes 466952 | tf_op jit(solution)/shard_map/ppermute | solution.py:567
  25.1 9.2 %collective-permute-start.4 = (bf16[128,256]{1,0:T(8,128)(2,1)S(1)}, bf16[128,256]{1,0:T(8,128)(2,1)S(1)}, u32[]{:S(2)}, u32[]{:S(2)}) collective-permute-start(bf16[128,256]{1,0:T(8,128)(2,1)S(1)} %collective-permute-done.opposite_ref), channel_id=1, source_target_pairs={{16,32},{32,16},{24,40},{40,24},{48,64},{64,48},{56,72},{72,56},{8... | collective-permute-start | bytes 196616 | tf_op jit(solution)/shard_map/ppermute | solution.py:567
  29.2 7.1 %collective-permute-start.1 = (bf16[128,256]{1,0:T(8,128)(2,1)S(1)}, bf16[128,256]{1,0:T(8,128)(2,1)S(1)}, u32[]{:S(2)}, u32[]{:S(2)}) collective-permute-start(bf16[128,256]{1,0:T(8,128)(2,1)S(1)} %collective-permute-done.opposite_ref), channel_id=1, source_target_pairs={{0,16},{16,0},{8,24},{24,8},{32,48},{48,32},{40,56},{56,40},{64,80... | collective-permute-start | bytes 196616 | tf_op jit(solution)/shard_map/ppermute | solution.py:567
  39.2 2.6 %collective-permute-start.5 = (f32[4,16,128]{2,1,0:T(8,128)S(1)}, f32[4,16,128]{2,1,0:T(8,128)S(1)}, u32[]{:S(2)}, u32[]{:S(2)}) collective-permute-start(f32[4,16,128]{2,1,0:T(8,128)S(1)} %get-tuple-element.25), channel_id=1, source_target_pairs={{0,1},{1,2},{2,3},{3,4},{4,5},{5,6},{6,7},{8,9},{9,10},{10,11},{11... | collective-permute-start | bytes 98312 | tf_op jit(solution)/shard_map/ppermute | solution.py:558
  40.5 4.1 %collective-permute-start.6 = (f32[4,16,128]{2,1,0:T(8,128)S(1)}, f32[4,16,128]{2,1,0:T(8,128)S(1)}, u32[]{:S(2)}, u32[]{:S(2)}) collective-permute-start(f32[4,16,128]{2,1,0:T(8,128)S(1)} %get-tuple-element.26), channel_id=1, source_target_pairs={{1,0},{2,1},{3,2},{4,3},{5,4},{6,5},{7,6},{9,8},{10,9},{11,10},{12... | collective-permute-start | bytes 98312 | tf_op jit(solution)/shard_map/ppermute | solution.py:558
  44.7 14.0 %collective-permute-start.8 = (bf16[46,16,128]{2,1,0:T(8,128)(2,1)S(1)}, bf16[46,16,128]{2,1,0:T(8,128)(2,1)S(1)}, u32[]{:S(2)}, u32[]{:S(2)}) collective-permute-start(bf16[46,16,128]{2,1,0:T(8,128)(2,1)S(1)} %get-tuple-element.28), channel_id=1, source_target_pairs={{8,16},{16,8},{24,32},{32,24},{40,48},{48,40},{56,64},{64,56},{72,... | collective-permute-start | bytes 565256 | tf_op jit(solution)/shard_map/ppermute | solution.py:567
  50.2 8.5 %collective-permute-start.9 = (bf16[46,16,128]{2,1,0:T(8,128)(2,1)S(1)}, bf16[46,16,128]{2,1,0:T(8,128)(2,1)S(1)}, u32[]{:S(2)}, u32[]{:S(2)}) collective-permute-start(bf16[46,16,128]{2,1,0:T(8,128)(2,1)S(1)} %get-tuple-element.29), channel_id=1, source_target_pairs={{0,8},{8,0},{16,24},{24,16},{32,40},{40,32},{48,56},{56,48},{64,72... | collective-permute-start | bytes 565256 | tf_op jit(solution)/shard_map/ppermute | solution.py:567
  52.1 10.4 %collective-permute-start.10 = (bf16[20,16,128]{2,1,0:T(8,128)(2,1)S(1)}, bf16[20,16,128]{2,1,0:T(8,128)(2,1)S(1)}, u32[]{:S(2)}, u32[]{:S(2)}) collective-permute-start(bf16[20,16,128]{2,1,0:T(8,128)(2,1)S(1)} %get-tuple-element.27), channel_id=1, source_target_pairs={{16,32},{32,16},{24,40},{40,24},{48,64},{64,48},{56,72},{72,56},{8... | collective-permute-start | bytes 245768 | tf_op jit(solution)/shard_map/ppermute | solution.py:567
  56.0 9.7 %collective-permute-start.7 = (bf16[20,16,128]{2,1,0:T(8,128)(2,1)S(1)}, bf16[20,16,128]{2,1,0:T(8,128)(2,1)S(1)}, u32[]{:S(2)}, u32[]{:S(2)}) collective-permute-start(bf16[20,16,128]{2,1,0:T(8,128)(2,1)S(1)} %get-tuple-element.27), channel_id=1, source_target_pairs={{0,16},{16,0},{8,24},{24,8},{32,48},{48,32},{40,56},{56,40},{64,80... | collective-permute-start | bytes 245768 | tf_op jit(solution)/shard_map/ppermute | solution.py:567
  58.7 7.0 %copy-start.3 = (f32[1,8,8]{2,1,0:T(8,128)S(1)}, f32[1,8,8]{2,1,0:T(8,128)}, u32[]{:S(2)}) copy-start(f32[1,8,8]{2,1,0:T(8,128)} %param.13) | copy-start | bytes 772
  58.7 7.0 %copy-start.4 = (f32[1,8,8]{2,1,0:T(8,128)S(1)}, f32[1,8,8]{2,1,0:T(8,128)}, u32[]{:S(2)}) copy-start(f32[1,8,8]{2,1,0:T(8,128)} %param.14) | copy-start | bytes 772
  62.5 35.2 %copy-start = (bf16[1,16,4,64,128]{4,3,2,1,0:T(8,128)(2,1)S(1)}, bf16[1,16,4,64,128]{4,3,2,1,0:T(8,128)(2,1)}, u32[]{:S(2)}) copy-start(bf16[1,16,4,64,128]{4,3,2,1,0:T(8,128)(2,1)} %param.19) | copy-start | bytes 3145732
  68.3 10.8 %collective-permute-start.11 = (bf16[128,256]{1,0:T(8,128)(2,1)S(1)}, bf16[128,256]{1,0:T(8,128)(2,1)S(1)}, u32[]{:S(2)}, u32[]{:S(2)}) collective-permute-start(bf16[128,256]{1,0:T(8,128)(2,1)S(1)} %get-tuple-element.31), channel_id=1, source_target_pairs={{0,256},{256,0},{1,257},{257,1},{2,258},{258,2},{3,259},{259,3},{4... | collective-permute-start | bytes 196616 | tf_op jit(solution)/shard_map/ppermute | solution.py:597
  79.1 18.6 %collective-permute-start.14 = (bf16[38,16,128]{2,1,0:T(8,128)(2,1)S(1)}, bf16[38,16,128]{2,1,0:T(8,128)(2,1)S(1)}, u32[]{:S(2)}, u32[]{:S(2)}) collective-permute-start(bf16[38,16,128]{2,1,0:T(8,128)(2,1)S(1)} %pack.3), channel_id=1, source_target_pairs={{8,16},{16,8},{24,32},{32,24},{40,48},{48,40},{56,64},{64,56},{72,... | collective-permute-start | bytes 466952 | tf_op jit(solution)/shard_map/ppermute | solution.py:567
  84.2 13.5 %collective-permute-start.13 = (bf16[38,16,128]{2,1,0:T(8,128)(2,1)S(1)}, bf16[38,16,128]{2,1,0:T(8,128)(2,1)S(1)}, u32[]{:S(2)}, u32[]{:S(2)}) collective-permute-start(bf16[38,16,128]{2,1,0:T(8,128)(2,1)S(1)} %pack.3), channel_id=1, source_target_pairs={{0,8},{8,0},{16,24},{24,16},{32,40},{40,32},{48,56},{56,48},{64,72... | collective-permute-start | bytes 466952 | tf_op jit(solution)/shard_map/ppermute | solution.py:567
  86.2 9.2 %collective-permute-start.15 = (bf16[128,256]{1,0:T(8,128)(2,1)S(1)}, bf16[128,256]{1,0:T(8,128)(2,1)S(1)}, u32[]{:S(2)}, u32[]{:S(2)}) collective-permute-start(bf16[128,256]{1,0:T(8,128)(2,1)S(1)} %collective-permute-done.11.opposite_ref), channel_id=1, source_target_pairs={{16,32},{32,16},{24,40},{40,24},{48,64},{64,48},{56,72},{72,56},{8... | collective-permute-start | bytes 196616 | tf_op jit(solution)/shard_map/ppermute | solution.py:567
  90.5 7.2 %collective-permute-start.12 = (bf16[128,256]{1,0:T(8,128)(2,1)S(1)}, bf16[128,256]{1,0:T(8,128)(2,1)S(1)}, u32[]{:S(2)}, u32[]{:S(2)}) collective-permute-start(bf16[128,256]{1,0:T(8,128)(2,1)S(1)} %collective-permute-done.11.opposite_ref), channel_id=1, source_target_pairs={{0,16},{16,0},{8,24},{24,8},{32,48},{48,32},{40,56},{56,40},{64,80... | collective-permute-start | bytes 196616 | tf_op jit(solution)/shard_map/ppermute | solution.py:567
  101.9 2.6 %collective-permute-start.16 = (f32[4,16,128]{2,1,0:T(8,128)S(1)}, f32[4,16,128]{2,1,0:T(8,128)S(1)}, u32[]{:S(2)}, u32[]{:S(2)}) collective-permute-start(f32[4,16,128]{2,1,0:T(8,128)S(1)} %get-tuple-element.34), channel_id=1, source_target_pairs={{0,1},{1,2},{2,3},{3,4},{4,5},{5,6},{6,7},{8,9},{9,10},{10,11},{11... | collective-permute-start | bytes 98312 | tf_op jit(solution)/shard_map/ppermute | solution.py:558
  103.2 6.0 %collective-permute-start.17 = (f32[4,16,128]{2,1,0:T(8,128)S(1)}, f32[4,16,128]{2,1,0:T(8,128)S(1)}, u32[]{:S(2)}, u32[]{:S(2)}) collective-permute-start(f32[4,16,128]{2,1,0:T(8,128)S(1)} %get-tuple-element.35), channel_id=1, source_target_pairs={{1,0},{2,1},{3,2},{4,3},{5,4},{6,5},{7,6},{9,8},{10,9},{11,10},{12... | collective-permute-start | bytes 98312 | tf_op jit(solution)/shard_map/ppermute | solution.py:558
  109.2 13.3 %collective-permute-start.19 = (bf16[46,16,128]{2,1,0:T(8,128)(2,1)S(1)}, bf16[46,16,128]{2,1,0:T(8,128)(2,1)S(1)}, u32[]{:S(2)}, u32[]{:S(2)}) collective-permute-start(bf16[46,16,128]{2,1,0:T(8,128)(2,1)S(1)} %get-tuple-element.37), channel_id=1, source_target_pairs={{8,16},{16,8},{24,32},{32,24},{40,48},{48,40},{56,64},{64,56},{72,... | collective-permute-start | bytes 565256 | tf_op jit(solution)/shard_map/ppermute | solution.py:567
  114.3 8.2 %collective-permute-start.20 = (bf16[46,16,128]{2,1,0:T(8,128)(2,1)S(1)}, bf16[46,16,128]{2,1,0:T(8,128)(2,1)S(1)}, u32[]{:S(2)}, u32[]{:S(2)}) collective-permute-start(bf16[46,16,128]{2,1,0:T(8,128)(2,1)S(1)} %get-tuple-element.38), channel_id=1, source_target_pairs={{0,8},{8,0},{16,24},{24,16},{32,40},{40,32},{48,56},{56,48},{64,72... | collective-permute-start | bytes 565256 | tf_op jit(solution)/shard_map/ppermute | solution.py:567
  116.2 10.1 %collective-permute-start.21 = (bf16[20,16,128]{2,1,0:T(8,128)(2,1)S(1)}, bf16[20,16,128]{2,1,0:T(8,128)(2,1)S(1)}, u32[]{:S(2)}, u32[]{:S(2)}) collective-permute-start(bf16[20,16,128]{2,1,0:T(8,128)(2,1)S(1)} %get-tuple-element.36), channel_id=1, source_target_pairs={{16,32},{32,16},{24,40},{40,24},{48,64},{64,48},{56,72},{72,56},{8... | collective-permute-start | bytes 245768 | tf_op jit(solution)/shard_map/ppermute | solution.py:567
  120.5 9.4 %collective-permute-start.18 = (bf16[20,16,128]{2,1,0:T(8,128)(2,1)S(1)}, bf16[20,16,128]{2,1,0:T(8,128)(2,1)S(1)}, u32[]{:S(2)}, u32[]{:S(2)}) collective-permute-start(bf16[20,16,128]{2,1,0:T(8,128)(2,1)S(1)} %get-tuple-element.36), channel_id=1, source_target_pairs={{0,16},{16,0},{8,24},{24,8},{32,48},{48,32},{40,56},{56,40},{64,80... | collective-permute-start | bytes 245768 | tf_op jit(solution)/shard_map/ppermute | solution.py:567

commit v6 on v5

--- a/solution.py
+++ b/solution.py
@@ -32,9 +32,8 @@
 C_PLANES = 20
 
 PAD = 8
-WEIGHT_CHUNKS = 8
 WAVE_SPEED = 8
-ROW0, COL0, ROW_END, COL_END, NEAR_C, NEAR_I, FAR_C, FAR_I = range(8)
+ROW0, COL0, ROW_END, COL_END, NEAR_C, NEAR_I, FAR_C, FAR_I, GY_ODD = range(9)
 SMEM = pl.BlockSpec(memory_space=pltpu.SMEM)
 VMEM = pl.BlockSpec(memory_space=pltpu.VMEM)
 HBM = pl.BlockSpec(memory_space=pl.ANY)
@@ -71,7 +70,7 @@
         out_ref[:, half * LANES : (half + 1) * LANES] = turned[half].astype(bf16)
 
 
-def write_strips(fields, at, low_ref, high_ref):
+def write_strips(fields, at, odd, chip_ref, outer_ref):
     lane = lax.broadcasted_iota(jnp.int32, (ROWS, LANES), 1)
     groups = [fields[3:7], [fields[7]] + fields[0:3]]
     for p, group in enumerate(groups):
@@ -82,8 +81,8 @@
             first = jnp.where(here, pltpu.roll(group[j][0], STRIP * j, 1), first)
             moved = group[j][1] if j == 3 else pltpu.roll(group[j][1], STRIP * (j + 1), 1)
             last = jnp.where(here, moved, last)
-        low_ref[at + p] = first
-        high_ref[at + p] = last
+        chip_ref[at + p] = jnp.where(odd, first, last)
+        outer_ref[at + p] = jnp.where(odd, last, first)
 
 
 def export_kernel(
@@ -157,8 +156,12 @@
 
 
 def pack_forcing_kernel(
-    forcing_ref, left_ref, right_ref, state_c_ref, state_i_ref, out_c_ref, out_i_ref, far_ref,
+    place_ref, forcing_ref, outer_ref, chip_ref, state_c_ref, state_i_ref,
+    out_c_ref, out_i_ref, far_ref, left_ref, right_ref,
 ):
+    odd = place_ref[GY_ODD] == 1
+    left_ref[...] = jnp.where(odd, chip_ref[...], outer_ref[...])
+    right_ref[...] = jnp.where(odd, outer_ref[...], chip_ref[...])
     for ref, behind in ((out_c_ref, state_i_ref), (out_i_ref, state_c_ref)):
         write_main(ref, 0, B_WAVE + 2, B_WAVE + 10, forcing_ref)
         for k, strips in enumerate((left_ref, right_ref)):
@@ -174,28 +177,38 @@
         far_ref[C_STRIP_W + p] = out_c_ref[B_STRIP_W + p]
 
 
-def pack_forcing(forcing, left, right, state_c, state_i):
-    payload = shaped((B_PLANES, ROWS, LANES), bf16)
+def pack_forcing(place, forcing, outer, chip, state_c, state_i):
+    payload, strips = shaped((B_PLANES, ROWS, LANES), bf16), shaped((4, ROWS, LANES))
     return pl.pallas_call(
         pack_forcing_kernel,
-        out_shape=(payload, payload, shaped((C_PLANES, ROWS, LANES), bf16)),
-        in_specs=[VMEM] * 5,
-        out_specs=(VMEM,) * 3,
+        out_shape=(payload, payload, shaped((C_PLANES, ROWS, LANES), bf16), strips, strips),
+        in_specs=[SMEM] + [VMEM] * 5,
+        out_specs=(VMEM,) * 5,
         compiler_params=params(),
         name="pack_forcing",
-    )(forcing, left, right, state_c, state_i)
+    )(place, forcing, outer, chip, state_c, state_i)
+
+
+def stage_kernel(weight_ref, near_c_ref, near_i_ref, out_ref):
+    del near_c_ref, near_i_ref
+    out_ref[...] = weight_ref[...]
+
+
+def stage(weight, near_c, near_i):
+    return pl.pallas_call(
+        stage_kernel,
+        out_shape=shaped(weight.shape, weight.dtype),
+        in_specs=[VMEM, HBM, HBM],
+        out_specs=VMEM,
+        compiler_params=params(),
+        name="stage_weights",
+    )(weight, near_c, near_i)
 
 
 def remap_kernel(
-    index_ref, far_i_ref, near_i_ref, opposite_ref, near_c_ref, far_c_ref, weight_hbm, land_ref, fields_ref,
-    forcing_ref, low_ref, high_ref, import_ref, table, turned, weight_ref, sems,
+    index_ref, far_i_ref, near_i_ref, opposite_ref, near_c_ref, far_c_ref, weight_ref, land_ref, fields_ref,
+    forcing_ref, chip_ref, outer_ref, import_ref, table, turned,
 ):
-    chunk_rows = ROWS // WEIGHT_CHUNKS
-    copies = []
-    for k in range(WEIGHT_CHUNKS):
-        rows = pl.ds(k * chunk_rows, chunk_rows)
-        copies.append(pltpu.make_async_copy(weight_hbm.at[rows], weight_ref.at[rows], sems.at[k]))
-        copies[k].start()
     half_count = 5 * ROWS * 2
     windows = [far_c_ref, near_c_ref, opposite_ref, near_i_ref, far_i_ref]
     for w, ref in enumerate(windows):
@@ -215,8 +228,6 @@
     low_half = lane8 < 64
     ones = jnp.ones((8, LANES), f32)
     for x in range(ROWS):
-        if x % chunk_rows == 0:
-            copies[x // chunk_rows].wait()
         pieces = []
         for seg in range(4):
             at = (x * 4 + seg) * 2
@@ -241,8 +252,9 @@
             parts.append(part)
         forcing.append(parts)
     state = [[half_of(fields_ref[c], half) for half in range(2)] for c in range(FIELDS)]
-    write_strips(forcing, 0, low_ref, high_ref)
-    write_strips(state, 2, low_ref, high_ref)
+    odd = index_ref[TURNED] == 1
+    write_strips(forcing, 0, odd, chip_ref, outer_ref)
+    write_strips(state, 2, odd, chip_ref, outer_ref)
 
 
 def remap(index, windows, weight, land, fields):
@@ -250,15 +262,13 @@
     return pl.pallas_call(
         remap_kernel,
         out_shape=(shaped((FIELDS, ROWS, COLS)), strips, strips, shaped((FIELDS, ROWS, COLS))),
-        in_specs=[SMEM] + [VMEM] * 5 + [HBM] + [VMEM] * 2,
+        in_specs=[SMEM] + [VMEM] * 8,
         out_specs=(VMEM,) * 4,
         scratch_shapes=[
             pltpu.VMEM((2 * 5 * ROWS * 2, FIELDS, LANES), f32),
             pltpu.VMEM((2, TURNED, LANES), f32),
-            pltpu.VMEM((ROWS, COLS, 128), bf16),
-            pltpu.SemaphoreType.DMA((WEIGHT_CHUNKS,)),
         ],
-        compiler_params=params(52),
+        compiler_params=params(),
         name="remap",
     )(index, *windows, weight, land, fields)
 
@@ -324,9 +334,14 @@
 
 
 def tracer_kernel(
-    place_ref, config_ref, near_c_ref, forcing_ref, left_ref, right_ref, near_i_ref,
-    state_c_ref, fields_ref, state_i_ref, out_ref, state, forcing, coef,
+    last, place_ref, config_ref, near_c_ref, forcing_ref, left_ref, right_ref, near_i_ref,
+    state_c_ref, fields_ref, state_i_ref, *refs
 ):
+    if last:
+        received_ref, out_ref, received_out, state, forcing, coef = refs
+        received_out[...] = received_ref[...]
+    else:
+        out_ref, state, forcing, coef = refs
     pairs = (
         ((place_ref[NEAR_C] - 1) * ROWS, near_c_ref, state_c_ref),
         ((place_ref[NEAR_I] - 1) * ROWS, near_i_ref, state_i_ref),
@@ -384,12 +399,13 @@
             out_ref[i, :, half * LANES : (half + 1) * LANES] = state[0, i, half, PAD + ROWS : PAD + 2 * ROWS, :]
 
 
-def tracer_steps(place, config, operands):
+def tracer_steps(last, place, config, operands):
+    tracers, received = shaped((TRACERS, ROWS, COLS)), shaped((FIELDS, ROWS, COLS))
     return pl.pallas_call(
-        tracer_kernel,
-        out_shape=shaped((TRACERS, ROWS, COLS)),
+        lambda *refs: tracer_kernel(last, *refs),
+        out_shape=(tracers, received) if last else tracers,
         in_specs=[SMEM] * 2 + [VMEM] * len(operands),
-        out_specs=VMEM,
+        out_specs=(VMEM, VMEM) if last else VMEM,
         scratch_shapes=[
             pltpu.VMEM((2, TRACERS, 3, 3 * ROWS + 2 * PAD, LANES), f32),
             pltpu.VMEM((TRACERS, 3, 3 * ROWS, LANES), f32),
@@ -553,18 +569,13 @@
     )(place, config, *mixes, *operands)
 
 
-def line(block, axis, by):
+def exchanged(block, axis, distance, phase):
     count = lax.axis_size(axis)
-    return lax.ppermute(block, axis, [(i, i + by) for i in range(count) if 0 <= i + by < count])
-
-
-def exchanged(block, distance, phase):
-    count = lax.axis_size("gx")
     route = []
     for low in range(count - distance):
         if (low // distance) % 2 == phase:
             route += [(low, low + distance), (low + distance, low)]
-    return lax.ppermute(block, "gx", route)
+    return lax.ppermute(block, axis, route)
 
 
 def local(
@@ -579,7 +590,7 @@
     side_far = 1 - 2 * ((gx // 2) % 2)
     place = jnp.stack([
         gx * ROWS, gy * COLS, lax.axis_size("gx") * ROWS, lax.axis_size("gy") * COLS,
-        2 - side_near, 2 + side_near, 2 - 2 * side_far, 2 + 2 * side_far,
+        2 - side_near, 2 + side_near, 2 - 2 * side_far, 2 + 2 * side_far, gy % 2,
     ]).astype(jnp.int32)
     config = jnp.concatenate([damping[0], wave_speed[0]])
     owner = remap_owner[0].reshape(-1)
@@ -589,6 +600,7 @@
     entry = (window * ROWS + slot // 4) * 2 + (slot % 4) // 2
     second = lax.iota(jnp.int32, owner.shape[0]) % 2
     index = entry + ((slot % 2) ^ second) * (5 * ROWS * 2)
+    index = jnp.concatenate([index, (gy % 2).astype(jnp.int32)[None]])
     weight = remap_weight[0].reshape(ROWS, COLS, 128)
 
     exported, fields, land = export(section_state[0], prev_import[0], land_mask[0], smix, imix)
@@ -596,23 +608,29 @@
         last = interval == ITERS - 1
         opposite = lax.ppermute(exported, "sec", [(0, 1), (1, 0)])
         near = pack(opposite, fields, index, place, config)
-        state_c = exchanged(near, 1, 1)
-        state_i = exchanged(near, 1, 0)
-        export_c = exchanged(opposite, 2, 1)
-        export_i = exchanged(opposite, 2, 0)
-        forcing, low, high, received = remap(
+        state_c = exchanged(near, "gx", 1, 1)
+        state_i = exchanged(near, "gx", 1, 0)
+        export_c = exchanged(opposite, "gx", 2, 1)
+        export_i = exchanged(opposite, "gx", 2, 0)
+        if interval == 0:
+            weight = stage(weight, state_c, state_i)
+        forcing, to_chip, to_outer, received = remap(
             index, (export_i, state_i, opposite, state_c, export_c), weight, land, fields
         )
-        left = line(high, "gy", 1)
-        right = line(low, "gy", -1)
-        out_c, out_i, outer = pack_forcing(forcing, left, right, state_c, state_i)
-        near_c = exchanged(out_c, 1, 1)
-        near_i = exchanged(out_i, 1, 0)
-        far_c = exchanged(outer, 2, 1)
-        far_i = exchanged(outer, 2, 0)
+        outer = exchanged(to_outer, "gy", 1, 1)
+        chip = exchanged(to_chip, "gy", 1, 0)
+        out_c, out_i, outer, left, right = pack_forcing(place, forcing, outer, chip, state_c, state_i)
+        near_c = exchanged(out_c, "gx", 1, 1)
+        near_i = exchanged(out_i, "gx", 1, 0)
+        far_c = exchanged(outer, "gx", 2, 1)
+        far_i = exchanged(outer, "gx", 2, 0)
         own = (forcing, left, right)
         state = (state_c, fields, state_i)
-        tracers = tracer_steps(place, config, (near_c, *own, near_i, *state))
+        operands = (near_c, *own, near_i, *state)
+        if last:
+            tracers, received = tracer_steps(last, place, config, operands + (received,))
+        else:
+            tracers = tracer_steps(last, place, config, operands)
         operands = (far_i, near_c, *own, near_i, far_c, *state, tracers)
         if last:
             fields = wave_steps(last, place, config, (), operands)

time: 134 us -> 128 us (0.955)
  waiting for transfers between devices: 26.8 us -> 16.2 us
  starting transfers between devices: 79.6 us -> 85.7 us
  Pallas kernels: 22.9 us -> 19.8 us
    ppermute x20, waiting for transfers between devices: 22.9 us -> 13 us  [exchanged(): return lax.ppermute(block, axis, route)]
    ppermute x20, starting transfers between devices: 61 us -> 67.2 us  [exchanged(): return lax.ppermute(block, axis, route)]
    pallas_call x2, Pallas kernels: 7.13 us -> 2.56 us  [remap(): pl.pallas_call(remap_kernel, out_shape=(shaped((FIELDS, ROWS, COLS)), str...]
    pallas_call x2 -> x3, Pallas kernels: 7.56 us -> 7.96 us  [the longest x2 7.89 us: tracer_steps(): pl.pallas_call(lambda *refs: tracer_kernel(last, *refs), out_shape=(trace...]
  transfers between devices with their start and end apart: 22 -> 22, of which waited for: 10 -> 11; matrix products, arithmetic and copies ran while one was open for 1% -> 1% of each run, Pallas kernels for 6% -> 6%
where the time goes in v6:
time: 128 us; the launch traced here: 127 us
  starting transfers between devices  85.7 us (67%)
  Pallas kernels  19.8 us (15%)
  waiting for transfers between devices  16.2 us (13%)
  local copies, waits for them, and re-layouts  3.68 us (3%)
    ppermute x20, starting transfers between devices, exchanged(): return lax.ppermute(block, axis, route)  67.2 us
    ppermute x2, starting transfers between devices, local(): opposite = lax.ppermute(exported, 'sec', [(0, 1), (1, 0)])  18.5 us
    ppermute x20, waiting for transfers between devices, exchanged(): return lax.ppermute(block, axis, route)  13 us
    pallas_call x2, Pallas kernels, tracer_steps(): pl.pallas_call(lambda *refs: tracer_kernel(last, *refs), out_shape=(trace...  7.89 us
    pallas_call x2, Pallas kernels, wave_steps(): pl.pallas_call(lambda *refs: wave_kernel(last, *refs), out_shape=state if...  5.53 us
    ppermute x2, waiting for transfers between devices, local(): opposite = lax.ppermute(exported, 'sec', [(0, 1), (1, 0)])  3.22 us
    unnamed x19, local copies, waits for them, and re-layouts  3.19 us
    pallas_call x1, Pallas kernels, export(): pl.pallas_call(export_kernel, out_shape=(shaped((TURNED, COLS), bf16), sh...  2.6 us
  transfers between devices with their start and end apart: 22, of which 11 were waited for; matrix products, arithmetic and copies ran while one was open for 1% of the time, Pallas kernels for 6%

profile of v6, /device:TPU:6, one launch (start us, length us, event | category | flops | bytes accessed | tf_op | source)
XLA Modules:
  0.0 126.6 jit_solution(290985216925217998)
XLA Ops:
  0.6 2.6 %export.1 = (bf16[128,256]{1,0:T(8,128)(2,1)}, f32[8,16,256]{2,1,0:T(8,128)}, s32[16,256]{1,0:T(8,128)}) custom-call(f32[8,8]{1,0:T(8,128)} %bitcast.20, f32[8,8]{1,0:T(8,128)} %bitcast.22, f32[8,16,256]{2,1,0:T(8,128)} %bitcast.25, f32[8,16,256]{2,1,0:T(8,128)} %bitcast.26, s32[16,256]{1,0:T(8,128)} %bitcast.27), custom_call_target="tpu_custom_call" | custom-call | tf_op jit(solution)/shard_map/export/pallas_call | solution.py:107
  3.2 10.9 %collective-permute-start = (bf16[128,256]{1,0:T(8,128)(2,1)}, bf16[128,256]{1,0:T(8,128)(2,1)S(1)}, u32[]{:S(2)}, u32[]{:S(2)}) collective-permute-start(bf16[128,256]{1,0:T(8,128)(2,1)} %get-tuple-element.27), channel_id=1, source_target_pairs={{0,256},{256,0},{1,257},{257,1},{2,258},{258,2},{3,259},{259,3},{4... | collective-permute-start | bytes 196616 | tf_op jit(solution)/shard_map/ppermute | solution.py:609
  14.2 0.6 copy-done.6
  15.0 0.1 sub.42
  15.1 0.5 copy-done.5
  15.8 0.1 reshape_squeeze.7
  16.1 0.7 copy-done.7
  16.8 0.7 collective-permute-done.opposite_ref
  17.5 5.6 %collective-permute-start.3 = (bf16[38,16,128]{2,1,0:T(8,128)(2,1)S(1)}, bf16[38,16,128]{2,1,0:T(8,128)(2,1)S(1)}, u32[]{:S(2)}, u32[]{:S(2)}) collective-permute-start(bf16[38,16,128]{2,1,0:T(8,128)(2,1)S(1)} %pack.2), channel_id=1, source_target_pairs={{8,16},{16,8},{24,32},{32,24},{40,48},{48,40},{56,64},{64,56},{72,... | collective-permute-start | bytes 466952 | tf_op jit(solution)/shard_map/ppermute | solution.py:578
  23.2 1.9 %collective-permute-start.2 = (bf16[38,16,128]{2,1,0:T(8,128)(2,1)S(1)}, bf16[38,16,128]{2,1,0:T(8,128)(2,1)S(1)}, u32[]{:S(2)}, u32[]{:S(2)}) collective-permute-start(bf16[38,16,128]{2,1,0:T(8,128)(2,1)S(1)} %pack.2), channel_id=1, source_target_pairs={{0,8},{8,0},{16,24},{24,16},{32,40},{40,32},{48,56},{56,48},{64,72... | collective-permute-start | bytes 466952 | tf_op jit(solution)/shard_map/ppermute | solution.py:578
  25.1 4.0 %collective-permute-start.4 = (bf16[128,256]{1,0:T(8,128)(2,1)S(1)}, bf16[128,256]{1,0:T(8,128)(2,1)S(1)}, u32[]{:S(2)}, u32[]{:S(2)}) collective-permute-start(bf16[128,256]{1,0:T(8,128)(2,1)S(1)} %collective-permute-done.opposite_ref), channel_id=1, source_target_pairs={{16,32},{32,16},{24,40},{40,24},{48,64},{64,48},{56,72},{72,56},{8... | collective-permute-start | bytes 196616 | tf_op jit(solution)/shard_map/ppermute | solution.py:578
  29.2 3.8 %collective-permute-start.1 = (bf16[128,256]{1,0:T(8,128)(2,1)S(1)}, bf16[128,256]{1,0:T(8,128)(2,1)S(1)}, u32[]{:S(2)}, u32[]{:S(2)}) collective-permute-start(bf16[128,256]{1,0:T(8,128)(2,1)S(1)} %collective-permute-done.opposite_ref), channel_id=1, source_target_pairs={{0,16},{16,0},{8,24},{24,8},{32,48},{48,32},{40,56},{56,40},{64,80... | collective-permute-start | bytes 196616 | tf_op jit(solution)/shard_map/ppermute | solution.py:578
  33.0 1.2 copy-done.1
  34.3 1.9 %collective-permute-done.1.far_i_ref = bf16[128,256]{1,0:T(8,128)(2,1)S(1)} collective-permute-done((bf16[128,256]{1,0:T(8,128)(2,1)S(1)}, bf16[128,256]{1,0:T(8,128)(2,1)S(1)}, u32[]{:S(2)}, u32[]{:S(2)}) %collective-permute-start.1) | collective-permute-done | bytes 65568 | tf_op jit(solution)/shard_map/ppermute | solution.py:578
  36.2 1.3 %remap.2 = (f32[8,16,256]{2,1,0:T(8,128)S(1)}, f32[4,16,128]{2,1,0:T(8,128)S(1)}, f32[4,16,128]{2,1,0:T(8,128)S(1)}, f32[8,16,256]{2,1,0:T(8,128)S(1)}) custom-call(s32[129]{0:T(256)S(1)} %pad_add_fusion.index_ref, bf16[128,256]{1,0:T(8,128)(2,1)S(1)} %collective-permute-done.1.far_i_ref, ...), custom_call_target="tpu_custom_call" | custom-call | tf_op jit(solution)/shard_map/remap/pallas_call | solution.py:262
  37.5 0.7 collective-permute-start.5
  38.2 4.0 %collective-permute-start.6 = (f32[4,16,128]{2,1,0:T(8,128)S(1)}, f32[4,16,128]{2,1,0:T(8,128)S(1)}, u32[]{:S(2)}, u32[]{:S(2)}) collective-permute-start(f32[4,16,128]{2,1,0:T(8,128)S(1)} %get-tuple-element.32), channel_id=1, source_target_pairs={{0,1},{1,0},{2,3},{3,2},{4,5},{5,4},{6,7},{7,6},{8,9},{9,8},{10,11... | collective-permute-start | bytes 98312 | tf_op jit(solution)/shard_map/ppermute | solution.py:578
  42.2 0.8 collective-permute-done.6.chip_ref
  43.1 0.6 pack_forcing.2
  43.7 5.5 %collective-permute-start.8 = (bf16[46,16,128]{2,1,0:T(8,128)(2,1)S(1)}, bf16[46,16,128]{2,1,0:T(8,128)(2,1)S(1)}, u32[]{:S(2)}, u32[]{:S(2)}) collective-permute-start(bf16[46,16,128]{2,1,0:T(8,128)(2,1)S(1)} %get-tuple-element.34), channel_id=1, source_target_pairs={{8,16},{16,8},{24,32},{32,24},{40,48},{48,40},{56,64},{64,56},{72,... | collective-permute-start | bytes 565256 | tf_op jit(solution)/shard_map/ppermute | solution.py:578
  49.2 1.9 %collective-permute-start.9 = (bf16[46,16,128]{2,1,0:T(8,128)(2,1)S(1)}, bf16[46,16,128]{2,1,0:T(8,128)(2,1)S(1)}, u32[]{:S(2)}, u32[]{:S(2)}) collective-permute-start(bf16[46,16,128]{2,1,0:T(8,128)(2,1)S(1)} %get-tuple-element.37), channel_id=1, source_target_pairs={{0,8},{8,0},{16,24},{24,16},{32,40},{40,32},{48,56},{56,48},{64,72... | collective-permute-start | bytes 565256 | tf_op jit(solution)/shard_map/ppermute | solution.py:578
  51.1 3.9 %collective-permute-start.10 = (bf16[20,16,128]{2,1,0:T(8,128)(2,1)S(1)}, bf16[20,16,128]{2,1,0:T(8,128)(2,1)S(1)}, u32[]{:S(2)}, u32[]{:S(2)}) collective-permute-start(bf16[20,16,128]{2,1,0:T(8,128)(2,1)S(1)} %get-tuple-element.33), channel_id=1, source_target_pairs={{16,32},{32,16},{24,40},{40,24},{48,64},{64,48},{56,72},{72,56},{8... | collective-permute-start | bytes 245768 | tf_op jit(solution)/shard_map/ppermute | solution.py:578
  55.0 2.7 %collective-permute-start.7 = (bf16[20,16,128]{2,1,0:T(8,128)(2,1)S(1)}, bf16[20,16,128]{2,1,0:T(8,128)(2,1)S(1)}, u32[]{:S(2)}, u32[]{:S(2)}) collective-permute-start(bf16[20,16,128]{2,1,0:T(8,128)(2,1)S(1)} %get-tuple-element.33), channel_id=1, source_target_pairs={{0,16},{16,0},{8,24},{24,8},{32,48},{48,32},{40,56},{56,40},{64,80... | collective-permute-start | bytes 245768 | tf_op jit(solution)/shard_map/ppermute | solution.py:578
  57.7 0.9 collective-permute-done.9.refs_6_.refs_9_
  58.7 3.8 %tracer_steps.2.refs_14_ = f32[5,16,256]{2,1,0:T(8,128)S(1)} custom-call(s32[9]{0:T(128)S(1)} %stack.31.place_ref.refs_0_, f32[10]{0:T(128)S(1)} %pad_maximum_fusion.config_ref.refs_1_, bf16[46,16,128]{2,1,0:T(8,128)(2,1)S(1)} %collective-permute-done.8.refs_2_.refs_5_, f32[8,16,256]{2,1,0:T(8,128)S(1)} %get-tuple-element.30.forcing_ref.refs_3_.refs_6_, ...), custom_call_target="tpu_custom_call" | custom-call | flops 10000000 | bytes 4000000 | tf_op jit(solution)/shard_map/tracer_steps/pallas_call | solution.py:404
  62.5 0.2 collective-permute-done.7.refs_4_
  62.6 2.6 %wave_steps.1 = (f32[8,16,256]{2,1,0:T(8,128)S(1)}, bf16[128,256]{1,0:T(8,128)(2,1)S(1)}) custom-call(s32[9]{0:T(128)S(1)} %stack.31.place_ref.refs_0_, f32[10]{0:T(128)S(1)} %pad_maximum_fusion.config_ref.refs_1_, f32[8,8]{1,0:T(8,128)S(1)} %bitcast.21, f32[8,8]{1,0:T(8,128)S(1)} %bitcast.23, bf16[20,16,128]{2,1,0:T(8,128)(2,1)S(1)} %collective-permute-done.7.refs_4_, ...), custom_call_target="tpu_custom_call" | custom-call | tf_op jit(solution)/shard_map/wave_steps/pallas_call | solution.py:561
  65.2 7.6 %collective-permute-start.11 = (bf16[128,256]{1,0:T(8,128)(2,1)S(1)}, bf16[128,256]{1,0:T(8,128)(2,1)S(1)}, u32[]{:S(2)}, u32[]{:S(2)}) collective-permute-start(bf16[128,256]{1,0:T(8,128)(2,1)S(1)} %get-tuple-element.39), channel_id=1, source_target_pairs={{0,256},{256,0},{1,257},{257,1},{2,258},{258,2},{3,259},{259,3},{4... | collective-permute-start | bytes 196616 | tf_op jit(solution)/shard_map/ppermute | solution.py:609
  72.8 2.5 %collective-permute-done.11.opposite_ref = bf16[128,256]{1,0:T(8,128)(2,1)S(1)} collective-permute-done((bf16[128,256]{1,0:T(8,128)(2,1)S(1)}, bf16[128,256]{1,0:T(8,128)(2,1)S(1)}, u32[]{:S(2)}, u32[]{:S(2)}) %collective-permute-start.11) | collective-permute-done | bytes 65568 | tf_op jit(solution)/shard_map/ppermute | solution.py:609
  75.4 6.4 %collective-permute-start.14 = (bf16[38,16,128]{2,1,0:T(8,128)(2,1)S(1)}, bf16[38,16,128]{2,1,0:T(8,128)(2,1)S(1)}, u32[]{:S(2)}, u32[]{:S(2)}) collective-permute-start(bf16[38,16,128]{2,1,0:T(8,128)(2,1)S(1)} %pack.3), channel_id=1, source_target_pairs={{8,16},{16,8},{24,32},{32,24},{40,48},{48,40},{56,64},{64,56},{72,... | collective-permute-start | bytes 466952 | tf_op jit(solution)/shard_map/ppermute | solution.py:578
  81.7 1.9 %collective-permute-start.13 = (bf16[38,16,128]{2,1,0:T(8,128)(2,1)S(1)}, bf16[38,16,128]{2,1,0:T(8,128)(2,1)S(1)}, u32[]{:S(2)}, u32[]{:S(2)}) collective-permute-start(bf16[38,16,128]{2,1,0:T(8,128)(2,1)S(1)} %pack.3), channel_id=1, source_target_pairs={{0,8},{8,0},{16,24},{24,16},{32,40},{40,32},{48,56},{56,48},{64,72... | collective-permute-start | bytes 466952 | tf_op jit(solution)/shard_map/ppermute | solution.py:578
  83.7 3.4 %collective-permute-start.15 = (bf16[128,256]{1,0:T(8,128)(2,1)S(1)}, bf16[128,256]{1,0:T(8,128)(2,1)S(1)}, u32[]{:S(2)}, u32[]{:S(2)}) collective-permute-start(bf16[128,256]{1,0:T(8,128)(2,1)S(1)} %collective-permute-done.11.opposite_ref), channel_id=1, source_target_pairs={{16,32},{32,16},{24,40},{40,24},{48,64},{64,48},{56,72},{72,56},{8... | collective-permute-start | bytes 196616 | tf_op jit(solution)/shard_map/ppermute | solution.py:578
  87.0 2.3 %collective-permute-start.12 = (bf16[128,256]{1,0:T(8,128)(2,1)S(1)}, bf16[128,256]{1,0:T(8,128)(2,1)S(1)}, u32[]{:S(2)}, u32[]{:S(2)}) collective-permute-start(bf16[128,256]{1,0:T(8,128)(2,1)S(1)} %collective-permute-done.11.opposite_ref), channel_id=1, source_target_pairs={{0,16},{16,0},{8,24},{24,8},{32,48},{48,32},{40,56},{56,40},{64,80... | collective-permute-start | bytes 196616 | tf_op jit(solution)/shard_map/ppermute | solution.py:578
  89.3 3.5 %collective-permute-done.15.far_c_ref = bf16[128,256]{1,0:T(8,128)(2,1)S(1)} collective-permute-done((bf16[128,256]{1,0:T(8,128)(2,1)S(1)}, bf16[128,256]{1,0:T(8,128)(2,1)S(1)}, u32[]{:S(2)}, u32[]{:S(2)}) %collective-permute-start.15) | collective-permute-done | bytes 65568 | tf_op jit(solution)/shard_map/ppermute | solution.py:578
  92.8 2.0 %collective-permute-done.12.far_i_ref = bf16[128,256]{1,0:T(8,128)(2,1)S(1)} collective-permute-done((bf16[128,256]{1,0:T(8,128)(2,1)S(1)}, bf16[128,256]{1,0:T(8,128)(2,1)S(1)}, u32[]{:S(2)}, u32[]{:S(2)}) %collective-permute-start.12) | collective-permute-done | bytes 65568 | tf_op jit(solution)/shard_map/ppermute | solution.py:578
  94.8 1.3 %remap.3 = (f32[8,16,256]{2,1,0:T(8,128)S(1)}, f32[4,16,128]{2,1,0:T(8,128)S(1)}, f32[4,16,128]{2,1,0:T(8,128)S(1)}, f32[8,16,256]{2,1,0:T(8,128)S(1)}) custom-call(s32[129]{0:T(256)S(1)} %pad_add_fusion.index_ref, bf16[128,256]{1,0:T(8,128)(2,1)S(1)} %collective-permute-done.12.far_i_ref, ...), custom_call_target="tpu_custom_call" | custom-call | tf_op jit(solution)/shard_map/remap/pallas_call | solution.py:262
  96.1 0.7 collective-permute-start.16
  96.8 5.1 %collective-permute-start.17 = (f32[4,16,128]{2,1,0:T(8,128)S(1)}, f32[4,16,128]{2,1,0:T(8,128)S(1)}, u32[]{:S(2)}, u32[]{:S(2)}) collective-permute-start(f32[4,16,128]{2,1,0:T(8,128)S(1)} %get-tuple-element.43), channel_id=1, source_target_pairs={{0,1},{1,0},{2,3},{3,2},{4,5},{5,4},{6,7},{7,6},{8,9},{9,8},{10,11... | collective-permute-start | bytes 98312 | tf_op jit(solution)/shard_map/ppermute | solution.py:578
  101.9 0.8 collective-permute-done.17.chip_ref
  102.7 0.6 pack_forcing.3
  103.3 6.2 %collective-permute-start.19 = (bf16[46,16,128]{2,1,0:T(8,128)(2,1)S(1)}, bf16[46,16,128]{2,1,0:T(8,128)(2,1)S(1)}, u32[]{:S(2)}, u32[]{:S(2)}) collective-permute-start(bf16[46,16,128]{2,1,0:T(8,128)(2,1)S(1)} %get-tuple-element.45), channel_id=1, source_target_pairs={{8,16},{16,8},{24,32},{32,24},{40,48},{48,40},{56,64},{64,56},{72,... | collective-permute-start | bytes 565256 | tf_op jit(solution)/shard_map/ppermute | solution.py:578
  109.5 1.9 %collective-permute-start.20 = (bf16[46,16,128]{2,1,0:T(8,128)(2,1)S(1)}, bf16[46,16,128]{2,1,0:T(8,128)(2,1)S(1)}, u32[]{:S(2)}, u32[]{:S(2)}) collective-permute-start(bf16[46,16,128]{2,1,0:T(8,128)(2,1)S(1)} %get-tuple-element.48), channel_id=1, source_target_pairs={{0,8},{8,0},{16,24},{24,16},{32,40},{40,32},{48,56},{56,48},{64,72... | collective-permute-start | bytes 565256 | tf_op jit(solution)/shard_map/ppermute | solution.py:578
  111.4 3.4 %collective-permute-start.21 = (bf16[20,16,128]{2,1,0:T(8,128)(2,1)S(1)}, bf16[20,16,128]{2,1,0:T(8,128)(2,1)S(1)}, u32[]{:S(2)}, u32[]{:S(2)}) collective-permute-start(bf16[20,16,128]{2,1,0:T(8,128)(2,1)S(1)} %get-tuple-element.44), channel_id=1, source_target_pairs={{16,32},{32,16},{24,40},{40,24},{48,64},{64,48},{56,72},{72,56},{8... | collective-permute-start | bytes 245768 | tf_op jit(solution)/shard_map/ppermute | solution.py:578
  114.8 1.9 %collective-permute-start.18 = (bf16[20,16,128]{2,1,0:T(8,128)(2,1)S(1)}, bf16[20,16,128]{2,1,0:T(8,128)(2,1)S(1)}, u32[]{:S(2)}, u32[]{:S(2)}) collective-permute-start(bf16[20,16,128]{2,1,0:T(8,128)(2,1)S(1)} %get-tuple-element.44), channel_id=1, source_target_pairs={{0,16},{16,0},{8,24},{24,8},{32,48},{48,32},{40,56},{56,40},{64,80... | collective-permute-start | bytes 245768 | tf_op jit(solution)/shard_map/ppermute | solution.py:578
  116.7 2.2 %collective-permute-done.20.refs_6_.refs_7_ = bf16[46,16,128]{2,1,0:T(8,128)(2,1)S(1)} collective-permute-done((bf16[46,16,128]{2,1,0:T(8,128)(2,1)S(1)}, bf16[46,16,128]{2,1,0:T(8,128)(2,1)S(1)}, u32[]{:S(2)}, u32[]{:S(2)}) %collective-permute-start.20) | collective-permute-done | bytes 188448 | tf_op jit(solution)/shard_map/ppermute | solution.py:578
  119.0 4.1 %tracer_steps.3 = (f32[5,16,256]{2,1,0:T(8,128)S(1)}, f32[8,16,256]{2,1,0:T(8,128)}) custom-call(s32[9]{0:T(128)S(1)} %stack.31.place_ref.refs_0_, f32[10]{0:T(128)S(1)} %pad_maximum_fusion.config_ref.refs_1_, bf16[46,16,128]{2,1,0:T(8,128)(2,1)S(1)} %collective-permute-done.19.refs_2_.refs_3_, ...), custom_call_target="tpu_custom_call" | custom-call | flops 10000000 | bytes 4000000 | tf_op jit(solution)/shard_map/tracer_steps/pallas_call | solution.py:404
  123.1 0.5 collective-permute-done.18.refs_2_
  123.6 3.0 %wave_steps_last.1 = f32[8,16,256]{2,1,0:T(8,128)} custom-call(s32[9]{0:T(128)S(1)} %stack.31.place_ref.refs_0_, f32[10]{0:T(128)S(1)} %pad_maximum_fusion.config_ref.refs_1_, bf16[20,16,128]{2,1,0:T(8,128)(2,1)S(1)} %collective-permute-done.18.refs_2_, bf16[46,16,128]{2,1,0:T(8,128)(2,1)S(1)} %collective-permute-done.19.refs_2_.refs_3_, ...), custom_call_target="tpu_custom_call" | custom-call | tf_op jit(solution)/shard_map/wave_steps_last/pallas_call | solution.py:561
  (35 shorter events, 0.6 us)
Async XLA Ops:
  3.2 14.3 %collective-permute-start = (bf16[128,256]{1,0:T(8,128)(2,1)}, bf16[128,256]{1,0:T(8,128)(2,1)S(1)}, u32[]{:S(2)}, u32[]{:S(2)}) collective-permute-start(bf16[128,256]{1,0:T(8,128)(2,1)} %get-tuple-element.27), channel_id=1, source_target_pairs={{0,256},{256,0},{1,257},{257,1},{2,258},{258,2},{3,259},{259,3},{4... | collective-permute-start | bytes 196616 | tf_op jit(solution)/shard_map/ppermute | solution.py:609
  14.2 0.7 copy-start.6
  14.2 3.3 %copy-start = (f32[8,16,256]{2,1,0:T(8,128)S(1)}, f32[8,16,256]{2,1,0:T(8,128)}, u32[]{:S(2)}) copy-start(f32[8,16,256]{2,1,0:T(8,128)} %get-tuple-element.28.fields_ref.refs_8_.refs_12_) | copy-start | bytes 393220
  15.0 0.7 copy-start.5
  16.1 0.7 copy-start.7
  16.1 0.7 copy-start.8
  17.5 15.4 %collective-permute-start.3 = (bf16[38,16,128]{2,1,0:T(8,128)(2,1)S(1)}, bf16[38,16,128]{2,1,0:T(8,128)(2,1)S(1)}, u32[]{:S(2)}, u32[]{:S(2)}) collective-permute-start(bf16[38,16,128]{2,1,0:T(8,128)(2,1)S(1)} %pack.2), channel_id=1, source_target_pairs={{8,16},{16,8},{24,32},{32,24},{40,48},{48,40},{56,64},{64,56},{72,... | collective-permute-start | bytes 466952 | tf_op jit(solution)/shard_map/ppermute | solution.py:578
  23.2 9.8 %collective-permute-start.2 = (bf16[38,16,128]{2,1,0:T(8,128)(2,1)S(1)}, bf16[38,16,128]{2,1,0:T(8,128)(2,1)S(1)}, u32[]{:S(2)}, u32[]{:S(2)}) collective-permute-start(bf16[38,16,128]{2,1,0:T(8,128)(2,1)S(1)} %pack.2), channel_id=1, source_target_pairs={{0,8},{8,0},{16,24},{24,16},{32,40},{40,32},{48,56},{56,48},{64,72... | collective-permute-start | bytes 466952 | tf_op jit(solution)/shard_map/ppermute | solution.py:578
  25.1 9.2 %collective-permute-start.4 = (bf16[128,256]{1,0:T(8,128)(2,1)S(1)}, bf16[128,256]{1,0:T(8,128)(2,1)S(1)}, u32[]{:S(2)}, u32[]{:S(2)}) collective-permute-start(bf16[128,256]{1,0:T(8,128)(2,1)S(1)} %collective-permute-done.opposite_ref), channel_id=1, source_target_pairs={{16,32},{32,16},{24,40},{40,24},{48,64},{64,48},{56,72},{72,56},{8... | collective-permute-start | bytes 196616 | tf_op jit(solution)/shard_map/ppermute | solution.py:578
  29.2 7.1 %collective-permute-start.1 = (bf16[128,256]{1,0:T(8,128)(2,1)S(1)}, bf16[128,256]{1,0:T(8,128)(2,1)S(1)}, u32[]{:S(2)}, u32[]{:S(2)}) collective-permute-start(bf16[128,256]{1,0:T(8,128)(2,1)S(1)} %collective-permute-done.opposite_ref), channel_id=1, source_target_pairs={{0,16},{16,0},{8,24},{24,8},{32,48},{48,32},{40,56},{56,40},{64,80... | collective-permute-start | bytes 196616 | tf_op jit(solution)/shard_map/ppermute | solution.py:578
  33.0 1.2 copy-start.1
  34.2 2.0 %copy-start.2 = (s32[16,256]{1,0:T(8,128)S(1)}, s32[16,256]{1,0:T(8,128)}, u32[]{:S(2)}) copy-start(s32[16,256]{1,0:T(8,128)} %get-tuple-element.29.land_ref.refs_16_) | copy-start | bytes 49156
  37.5 4.7 %collective-permute-start.5 = (f32[4,16,128]{2,1,0:T(8,128)S(1)}, f32[4,16,128]{2,1,0:T(8,128)S(1)}, u32[]{:S(2)}, u32[]{:S(2)}) collective-permute-start(f32[4,16,128]{2,1,0:T(8,128)S(1)} %get-tuple-element.31), channel_id=1, source_target_pairs={{1,2},{2,1},{3,4},{4,3},{5,6},{6,5},{9,10},{10,9},{11,12},{12,11},... | collective-permute-start | bytes 98312 | tf_op jit(solution)/shard_map/ppermute | solution.py:578
  38.2 4.9 %collective-permute-start.6 = (f32[4,16,128]{2,1,0:T(8,128)S(1)}, f32[4,16,128]{2,1,0:T(8,128)S(1)}, u32[]{:S(2)}, u32[]{:S(2)}) collective-permute-start(f32[4,16,128]{2,1,0:T(8,128)S(1)} %get-tuple-element.32), channel_id=1, source_target_pairs={{0,1},{1,0},{2,3},{3,2},{4,5},{5,4},{6,7},{7,6},{8,9},{9,8},{10,11... | collective-permute-start | bytes 98312 | tf_op jit(solution)/shard_map/ppermute | solution.py:578
  43.7 14.0 %collective-permute-start.8 = (bf16[46,16,128]{2,1,0:T(8,128)(2,1)S(1)}, bf16[46,16,128]{2,1,0:T(8,128)(2,1)S(1)}, u32[]{:S(2)}, u32[]{:S(2)}) collective-permute-start(bf16[46,16,128]{2,1,0:T(8,128)(2,1)S(1)} %get-tuple-element.34), channel_id=1, source_target_pairs={{8,16},{16,8},{24,32},{32,24},{40,48},{48,40},{56,64},{64,56},{72,... | collective-permute-start | bytes 565256 | tf_op jit(solution)/shard_map/ppermute | solution.py:578
  49.2 9.5 %collective-permute-start.9 = (bf16[46,16,128]{2,1,0:T(8,128)(2,1)S(1)}, bf16[46,16,128]{2,1,0:T(8,128)(2,1)S(1)}, u32[]{:S(2)}, u32[]{:S(2)}) collective-permute-start(bf16[46,16,128]{2,1,0:T(8,128)(2,1)S(1)} %get-tuple-element.37), channel_id=1, source_target_pairs={{0,8},{8,0},{16,24},{24,16},{32,40},{40,32},{48,56},{56,48},{64,72... | collective-permute-start | bytes 565256 | tf_op jit(solution)/shard_map/ppermute | solution.py:578
  51.1 11.3 %collective-permute-start.10 = (bf16[20,16,128]{2,1,0:T(8,128)(2,1)S(1)}, bf16[20,16,128]{2,1,0:T(8,128)(2,1)S(1)}, u32[]{:S(2)}, u32[]{:S(2)}) collective-permute-start(bf16[20,16,128]{2,1,0:T(8,128)(2,1)S(1)} %get-tuple-element.33), channel_id=1, source_target_pairs={{16,32},{32,16},{24,40},{40,24},{48,64},{64,48},{56,72},{72,56},{8... | collective-permute-start | bytes 245768 | tf_op jit(solution)/shard_map/ppermute | solution.py:578
  55.0 7.6 %collective-permute-start.7 = (bf16[20,16,128]{2,1,0:T(8,128)(2,1)S(1)}, bf16[20,16,128]{2,1,0:T(8,128)(2,1)S(1)}, u32[]{:S(2)}, u32[]{:S(2)}) collective-permute-start(bf16[20,16,128]{2,1,0:T(8,128)(2,1)S(1)} %get-tuple-element.33), channel_id=1, source_target_pairs={{0,16},{16,0},{8,24},{24,8},{32,48},{48,32},{40,56},{56,40},{64,80... | collective-permute-start | bytes 245768 | tf_op jit(solution)/shard_map/ppermute | solution.py:578
  58.7 4.0 %copy-start.3 = (f32[1,8,8]{2,1,0:T(8,128)S(1)}, f32[1,8,8]{2,1,0:T(8,128)}, u32[]{:S(2)}) copy-start(f32[1,8,8]{2,1,0:T(8,128)} %param.13) | copy-start | bytes 772
  58.7 4.0 %copy-start.4 = (f32[1,8,8]{2,1,0:T(8,128)S(1)}, f32[1,8,8]{2,1,0:T(8,128)}, u32[]{:S(2)}) copy-start(f32[1,8,8]{2,1,0:T(8,128)} %param.14) | copy-start | bytes 772
  65.2 10.1 %collective-permute-start.11 = (bf16[128,256]{1,0:T(8,128)(2,1)S(1)}, bf16[128,256]{1,0:T(8,128)(2,1)S(1)}, u32[]{:S(2)}, u32[]{:S(2)}) collective-permute-start(bf16[128,256]{1,0:T(8,128)(2,1)S(1)} %get-tuple-element.39), channel_id=1, source_target_pairs={{0,256},{256,0},{1,257},{257,1},{2,258},{258,2},{3,259},{259,3},{4... | collective-permute-start | bytes 196616 | tf_op jit(solution)/shard_map/ppermute | solution.py:609
  75.4 19.4 %collective-permute-start.14 = (bf16[38,16,128]{2,1,0:T(8,128)(2,1)S(1)}, bf16[38,16,128]{2,1,0:T(8,128)(2,1)S(1)}, u32[]{:S(2)}, u32[]{:S(2)}) collective-permute-start(bf16[38,16,128]{2,1,0:T(8,128)(2,1)S(1)} %pack.3), channel_id=1, source_target_pairs={{8,16},{16,8},{24,32},{32,24},{40,48},{48,40},{56,64},{64,56},{72,... | collective-permute-start | bytes 466952 | tf_op jit(solution)/shard_map/ppermute | solution.py:578
  81.7 13.1 %collective-permute-start.13 = (bf16[38,16,128]{2,1,0:T(8,128)(2,1)S(1)}, bf16[38,16,128]{2,1,0:T(8,128)(2,1)S(1)}, u32[]{:S(2)}, u32[]{:S(2)}) collective-permute-start(bf16[38,16,128]{2,1,0:T(8,128)(2,1)S(1)} %pack.3), channel_id=1, source_target_pairs={{0,8},{8,0},{16,24},{24,16},{32,40},{40,32},{48,56},{56,48},{64,72... | collective-permute-start | bytes 466952 | tf_op jit(solution)/shard_map/ppermute | solution.py:578
  83.7 9.2 %collective-permute-start.15 = (bf16[128,256]{1,0:T(8,128)(2,1)S(1)}, bf16[128,256]{1,0:T(8,128)(2,1)S(1)}, u32[]{:S(2)}, u32[]{:S(2)}) collective-permute-start(bf16[128,256]{1,0:T(8,128)(2,1)S(1)} %collective-permute-done.11.opposite_ref), channel_id=1, source_target_pairs={{16,32},{32,16},{24,40},{40,24},{48,64},{64,48},{56,72},{72,56},{8... | collective-permute-start | bytes 196616 | tf_op jit(solution)/shard_map/ppermute | solution.py:578
  87.0 7.8 %collective-permute-start.12 = (bf16[128,256]{1,0:T(8,128)(2,1)S(1)}, bf16[128,256]{1,0:T(8,128)(2,1)S(1)}, u32[]{:S(2)}, u32[]{:S(2)}) collective-permute-start(bf16[128,256]{1,0:T(8,128)(2,1)S(1)} %collective-permute-done.11.opposite_ref), channel_id=1, source_target_pairs={{0,16},{16,0},{8,24},{24,8},{32,48},{48,32},{40,56},{56,40},{64,80... | collective-permute-start | bytes 196616 | tf_op jit(solution)/shard_map/ppermute | solution.py:578
  96.1 5.8 %collective-permute-start.16 = (f32[4,16,128]{2,1,0:T(8,128)S(1)}, f32[4,16,128]{2,1,0:T(8,128)S(1)}, u32[]{:S(2)}, u32[]{:S(2)}) collective-permute-start(f32[4,16,128]{2,1,0:T(8,128)S(1)} %get-tuple-element.42), channel_id=1, source_target_pairs={{1,2},{2,1},{3,4},{4,3},{5,6},{6,5},{9,10},{10,9},{11,12},{12,11},... | collective-permute-start | bytes 98312 | tf_op jit(solution)/shard_map/ppermute | solution.py:578
  96.8 6.0 %collective-permute-start.17 = (f32[4,16,128]{2,1,0:T(8,128)S(1)}, f32[4,16,128]{2,1,0:T(8,128)S(1)}, u32[]{:S(2)}, u32[]{:S(2)}) collective-permute-start(f32[4,16,128]{2,1,0:T(8,128)S(1)} %get-tuple-element.43), channel_id=1, source_target_pairs={{0,1},{1,0},{2,3},{3,2},{4,5},{5,4},{6,7},{7,6},{8,9},{9,8},{10,11... | collective-permute-start | bytes 98312 | tf_op jit(solution)/shard_map/ppermute | solution.py:578
  103.3 13.4 %collective-permute-start.19 = (bf16[46,16,128]{2,1,0:T(8,128)(2,1)S(1)}, bf16[46,16,128]{2,1,0:T(8,128)(2,1)S(1)}, u32[]{:S(2)}, u32[]{:S(2)}) collective-permute-start(bf16[46,16,128]{2,1,0:T(8,128)(2,1)S(1)} %get-tuple-element.45), channel_id=1, source_target_pairs={{8,16},{16,8},{24,32},{32,24},{40,48},{48,40},{56,64},{64,56},{72,... | collective-permute-start | bytes 565256 | tf_op jit(solution)/shard_map/ppermute | solution.py:578
  109.5 9.5 %collective-permute-start.20 = (bf16[46,16,128]{2,1,0:T(8,128)(2,1)S(1)}, bf16[46,16,128]{2,1,0:T(8,128)(2,1)S(1)}, u32[]{:S(2)}, u32[]{:S(2)}) collective-permute-start(bf16[46,16,128]{2,1,0:T(8,128)(2,1)S(1)} %get-tuple-element.48), channel_id=1, source_target_pairs={{0,8},{8,0},{16,24},{24,16},{32,40},{40,32},{48,56},{56,48},{64,72... | collective-permute-start | bytes 565256 | tf_op jit(solution)/shard_map/ppermute | solution.py:578
  111.4 11.7 %collective-permute-start.21 = (bf16[20,16,128]{2,1,0:T(8,128)(2,1)S(1)}, bf16[20,16,128]{2,1,0:T(8,128)(2,1)S(1)}, u32[]{:S(2)}, u32[]{:S(2)}) collective-permute-start(bf16[20,16,128]{2,1,0:T(8,128)(2,1)S(1)} %get-tuple-element.44), channel_id=1, source_target_pairs={{16,32},{32,16},{24,40},{40,24},{48,64},{64,48},{56,72},{72,56},{8... | collective-permute-start | bytes 245768 | tf_op jit(solution)/shard_map/ppermute | solution.py:578
  114.8 8.8 %collective-permute-start.18 = (bf16[20,16,128]{2,1,0:T(8,128)(2,1)S(1)}, bf16[20,16,128]{2,1,0:T(8,128)(2,1)S(1)}, u32[]{:S(2)}, u32[]{:S(2)}) collective-permute-start(bf16[20,16,128]{2,1,0:T(8,128)(2,1)S(1)} %get-tuple-element.44), channel_id=1, source_target_pairs={{0,16},{16,0},{8,24},{24,8},{32,48},{48,32},{40,56},{56,40},{64,80... | collective-permute-start | bytes 245768 | tf_op jit(solution)/shard_map/ppermute | solution.py:578

commit v7 on v6

--- a/solution.py
+++ b/solution.py
@@ -33,7 +33,7 @@
 
 PAD = 8
 WAVE_SPEED = 8
-ROW0, COL0, ROW_END, COL_END, NEAR_C, NEAR_I, FAR_C, FAR_I, GY_ODD = range(9)
+ROW0, COL0, ROW_END, COL_END, AFTER_NEAR, AFTER_FAR, GY_ODD = range(10, 17)
 SMEM = pl.BlockSpec(memory_space=pltpu.SMEM)
 VMEM = pl.BlockSpec(memory_space=pltpu.VMEM)
 HBM = pl.BlockSpec(memory_space=pl.ANY)
@@ -50,6 +50,14 @@
     return jax.ShapeDtypeStruct(shape, dtype)
 
 
+def spread(config_ref, k, rows=8):
+    return jnp.broadcast_to(config_ref[:, k : k + 1], (rows, LANES))
+
+
+def chosen(flag, ones, others):
+    return [jnp.where(flag, one, other) for one, other in zip(ones, others)]
+
+
 def half_of(value, half):
     return value[:, half * LANES : (half + 1) * LANES]
 
@@ -57,12 +65,12 @@
 def write_export(fields, received, wet, smix_ref, imix_ref, turned, out_ref):
     scale = wet * jnp.sqrt(1.0 + fields[1] * fields[1] + fields[2] * fields[2])
     for c in range(FIELDS):
-        total = smix_ref[c, 0] * fields[0]
+        total = smix_ref[c : c + 1, 0:1] * fields[0]
         for k in range(1, FIELDS):
-            total = total + smix_ref[c, k] * fields[k]
-        other = imix_ref[c, 0] * received[0]
+            total = total + smix_ref[c : c + 1, k : k + 1] * fields[k]
+        other = imix_ref[c : c + 1, 0:1] * received[0]
         for k in range(1, FIELDS):
-            other = other + imix_ref[c, k] * received[k]
+            other = other + imix_ref[c : c + 1, k : k + 1] * received[k]
         value = scale * (total + other)
         for half in range(2):
             turned[half, pl.ds(c, ROWS, stride=FIELDS), :] = half_of(value, half)
@@ -109,7 +117,7 @@
         out_shape=(
             shaped((TURNED, COLS), bf16), shaped((FIELDS, ROWS, COLS)), shaped((ROWS, COLS), jnp.int32),
         ),
-        in_specs=[SMEM, SMEM, HBM, HBM, HBM],
+        in_specs=[VMEM, VMEM, HBM, HBM, HBM],
         out_specs=(VMEM,) * 3,
         scratch_shapes=[
             pltpu.VMEM((2, TURNED, LANES), f32),
@@ -136,32 +144,33 @@
             split_to(ref, wave_at + 2 * i + half, wave_low_at + 2 * i + half, fields_ref[i, :, cols])
 
 
-def pack_kernel(opposite_ref, fields_ref, index_ref, place_ref, config_ref, near_ref):
-    del index_ref, place_ref, config_ref
+def pack_kernel(opposite_ref, fields_ref, index_ref, config_ref, near_ref):
+    del index_ref, config_ref
     write_main(near_ref, 0, A_WAVE, A_WAVE + 6, fields_ref)
     for half in range(2):
         for i in range(TURNED // 16):
             near_ref[A_EXPORT + half * 8 + i] = opposite_ref[16 * i : 16 * i + 16, half * LANES : (half + 1) * LANES]
 
 
-def pack(opposite, fields, index, place, config):
+def pack(opposite, fields, index, config):
     return pl.pallas_call(
         pack_kernel,
         out_shape=shaped((A_PLANES, ROWS, LANES), bf16),
-        in_specs=[VMEM] * 2 + [HBM] * 3,
+        in_specs=[VMEM] * 2 + [HBM] * 2,
         out_specs=VMEM,
         compiler_params=params(),
         name="pack",
-    )(opposite, fields, index, place, config)
+    )(opposite, fields, index, config)
 
 
 def pack_forcing_kernel(
-    place_ref, forcing_ref, outer_ref, chip_ref, state_c_ref, state_i_ref,
+    config_ref, forcing_ref, outer_ref, chip_ref, state_c_ref, state_i_ref,
     out_c_ref, out_i_ref, far_ref, left_ref, right_ref,
 ):
-    odd = place_ref[GY_ODD] == 1
-    left_ref[...] = jnp.where(odd, chip_ref[...], outer_ref[...])
-    right_ref[...] = jnp.where(odd, outer_ref[...], chip_ref[...])
+    odd = spread(config_ref, GY_ODD, ROWS) > 0.5
+    for p in range(4):
+        left_ref[p] = jnp.where(odd, chip_ref[p], outer_ref[p])
+        right_ref[p] = jnp.where(odd, outer_ref[p], chip_ref[p])
     for ref, behind in ((out_c_ref, state_i_ref), (out_i_ref, state_c_ref)):
         write_main(ref, 0, B_WAVE + 2, B_WAVE + 10, forcing_ref)
         for k, strips in enumerate((left_ref, right_ref)):
@@ -177,16 +186,16 @@
         far_ref[C_STRIP_W + p] = out_c_ref[B_STRIP_W + p]
 
 
-def pack_forcing(place, forcing, outer, chip, state_c, state_i):
+def pack_forcing(config, forcing, outer, chip, state_c, state_i):
     payload, strips = shaped((B_PLANES, ROWS, LANES), bf16), shaped((4, ROWS, LANES))
     return pl.pallas_call(
         pack_forcing_kernel,
         out_shape=(payload, payload, shaped((C_PLANES, ROWS, LANES), bf16), strips, strips),
-        in_specs=[SMEM] + [VMEM] * 5,
+        in_specs=[VMEM] * 6,
         out_specs=(VMEM,) * 5,
         compiler_params=params(),
         name="pack_forcing",
-    )(place, forcing, outer, chip, state_c, state_i)
+    )(config, forcing, outer, chip, state_c, state_i)
 
 
 def stage_kernel(weight_ref, near_c_ref, near_i_ref, out_ref):
@@ -282,25 +291,24 @@
     return jnp.where(lane < STRIP, right, jnp.where(lane >= 96, left, 0.0))
 
 
-def place_field(dest, start, parts, strip_start=None):
+def place_field(dest, start, parts):
     for j, part in enumerate(parts):
-        at = strip_start if j == 2 and strip_start is not None else start
-        at = at if isinstance(at, int) else pl.multiple_of(at, 8)
-        dest[j, pl.ds(at, ROWS), :] = part
+        dest[j, start : start + ROWS, :] = part
 
 
 def joined(ref, at, low_at):
     return ref[at].astype(f32) + ref[low_at].astype(f32)
 
 
-def inside_tile(place_ref, first_row, count, j, shift=0):
+def inside_tile(config_ref, first_row, count, j, shift=0):
     shape = (count, LANES)
-    row = lax.broadcasted_iota(jnp.int32, shape, 0) + (place_ref[ROW0] + first_row)
+    row = (lax.broadcasted_iota(jnp.int32, shape, 0) + first_row).astype(f32) + spread(config_ref, ROW0, count)
     col = lax.broadcasted_iota(jnp.int32, shape, 1) + j * LANES
     if j == 2:
         col = jnp.where(col >= 3 * LANES - STRIP, col - 3 * LANES, col)
-    col = col + (place_ref[COL0] + shift)
-    ok = (row >= 0) & (row < place_ref[ROW_END]) & (col >= 0) & (col < place_ref[COL_END])
+    col = (col + shift).astype(f32) + spread(config_ref, COL0, count)
+    ok = (row >= 0.0) & (row < spread(config_ref, ROW_END, count))
+    ok = ok & (col >= 0.0) & (col < spread(config_ref, COL_END, count))
     return jnp.where(ok, 1.0, 0.0)
 
 
@@ -327,14 +335,17 @@
     return [ref[2 * i].astype(f32), ref[2 * i + 1].astype(f32), beside]
 
 
-def wave_parts(ref, at, low_at, strip_ref, strip_at, strip_low_at, i):
-    first, second = [joined(ref, at + 2 * i + half, low_at + 2 * i + half) for half in range(2)]
-    left, right = [joined(strip_ref, strip_at + k, strip_low_at + k) for k in range(2)]
-    return [first, second, sides(left, right, i + 1)]
+def wave_main(ref, at, low_at, i):
+    return [joined(ref, at + 2 * i + half, low_at + 2 * i + half) for half in range(2)]
+
+
+def wave_strip(ref, at, low_at, i):
+    left, right = [joined(ref, at + k, low_at + k) for k in range(2)]
+    return [sides(left, right, i + 1)]
 
 
 def tracer_kernel(
-    last, place_ref, config_ref, near_c_ref, forcing_ref, left_ref, right_ref, near_i_ref,
+    last, config_ref, near_c_ref, forcing_ref, left_ref, right_ref, near_i_ref,
     state_c_ref, fields_ref, state_i_ref, *refs
 ):
     if last:
@@ -342,21 +353,18 @@
         received_out[...] = received_ref[...]
     else:
         out_ref, state, forcing, coef = refs
-    pairs = (
-        ((place_ref[NEAR_C] - 1) * ROWS, near_c_ref, state_c_ref),
-        ((place_ref[NEAR_I] - 1) * ROWS, near_i_ref, state_i_ref),
-        (ROWS, None, None),
-    )
-    for start, near, main in pairs:
-        for i in range(TRACERS):
-            if near is None:
-                pushed = own_parts(forcing_ref, left_ref, right_ref, 0, WAVES + i)
-                parts = own_parts(fields_ref, left_ref, right_ref, 2, WAVES + i)
-            else:
-                pushed = tracer_parts(near, near, 10, B_WAVE, i)
-                parts = tracer_parts(main, near, B_STRIP_T, B_STRIP_W, i)
-            place_field(forcing.at[i], start, pushed)
-            place_field(state.at[0, i], start + PAD, parts)
+    after = spread(config_ref, AFTER_NEAR, ROWS) > 0.5
+    for i in range(TRACERS):
+        pushed, parts = [], []
+        for near, main in ((near_c_ref, state_c_ref), (near_i_ref, state_i_ref)):
+            pushed.append(tracer_parts(near, near, 10, B_WAVE, i))
+            parts.append(tracer_parts(main, near, B_STRIP_T, B_STRIP_W, i))
+        place_field(forcing.at[i], 0, chosen(after, pushed[1], pushed[0]))
+        place_field(forcing.at[i], ROWS, own_parts(forcing_ref, left_ref, right_ref, 0, WAVES + i))
+        place_field(forcing.at[i], 2 * ROWS, chosen(after, pushed[0], pushed[1]))
+        place_field(state.at[0, i], PAD, chosen(after, parts[1], parts[0]))
+        place_field(state.at[0, i], PAD + ROWS, own_parts(fields_ref, left_ref, right_ref, 2, WAVES + i))
+        place_field(state.at[0, i], PAD + 2 * ROWS, chosen(after, parts[0], parts[1]))
     height = 3 * ROWS
     for k in range(2):
         for i in range(TRACERS):
@@ -364,10 +372,10 @@
                 state[k, i, j, 0:PAD, :] = jnp.zeros((PAD, LANES), f32)
                 state[k, i, j, PAD + height : height + 2 * PAD, :] = jnp.zeros((PAD, LANES), f32)
     for j in range(3):
-        coef[j] = inside_tile(place_ref, -ROWS, height, j) * DIFFUSION
+        coef[j] = inside_tile(config_ref, -ROWS, height, j) * DIFFUSION
 
     lane = lax.broadcasted_iota(jnp.int32, (8, LANES), 1)
-    keep = [(1.0 - config_ref[WAVES + c]) - 4.0 * DIFFUSION for c in range(TRACERS)]
+    keep = [(1.0 - spread(config_ref, WAVES + c)) - 4.0 * DIFFUSION for c in range(TRACERS)]
 
     def step(source, dest, first, count):
         for t in range(first, first + count):
@@ -399,12 +407,12 @@
             out_ref[i, :, half * LANES : (half + 1) * LANES] = state[0, i, half, PAD + ROWS : PAD + 2 * ROWS, :]
 
 
-def tracer_steps(last, place, config, operands):
+def tracer_steps(last, config, operands):
     tracers, received = shaped((TRACERS, ROWS, COLS)), shaped((FIELDS, ROWS, COLS))
     return pl.pallas_call(
         lambda *refs: tracer_kernel(last, *refs),
         out_shape=(tracers, received) if last else tracers,
-        in_specs=[SMEM] * 2 + [VMEM] * len(operands),
+        in_specs=[VMEM] * (1 + len(operands)),
         out_specs=(VMEM, VMEM) if last else VMEM,
         scratch_shapes=[
             pltpu.VMEM((2, TRACERS, 3, 3 * ROWS + 2 * PAD, LANES), f32),
@@ -414,10 +422,10 @@
         compiler_params=params(),
         cost_estimate=pl.CostEstimate(flops=10_000_000, bytes_accessed=4_000_000, transcendentals=0),
         name="tracer_steps",
-    )(place, config, *operands)
-
-
-def wave_kernel(last, place_ref, config_ref, *refs):
+    )(config, *operands)
+
+
+def wave_kernel(last, config_ref, *refs):
     if not last:
         smix_ref, imix_ref, *refs = refs
     (far_i, near_c, forcing_ref, left_ref, right_ref, near_i, far_c,
@@ -429,37 +437,42 @@
     height = 5 * ROWS
     tiles = height // 8
 
-    row_of = {k: PAD + place_ref[k] * ROWS for k in (NEAR_C, NEAR_I, FAR_C, FAR_I)}
+    after = spread(config_ref, AFTER_NEAR, ROWS) > 0.5
+    after_far = spread(config_ref, AFTER_FAR, ROWS) > 0.5
     for i in range(WAVES):
         place_field(forcing.at[i], PAD + 2 * ROWS, own_parts(forcing_ref, left_ref, right_ref, 0, i))
         place_field(state.at[i], PAD + 2 * ROWS, own_parts(fields_ref, left_ref, right_ref, 2, i))
-        for near, main, at in ((near_c, state_c, row_of[NEAR_C]), (near_i, state_i, row_of[NEAR_I])):
-            pushed = wave_parts(near, B_WAVE + 2, B_WAVE + 10, near, B_WAVE, B_WAVE + 8, i)
-            place_field(forcing.at[i], at, pushed)
-            place_field(state.at[i], at, wave_parts(main, A_WAVE, A_WAVE + 6, near, B_STRIP_W, B_STRIP_W + 2, i))
-        for far, near, at, main_at in (
-            (far_c, near_c, row_of[FAR_C], 2 * row_of[NEAR_C] - (PAD + 2 * ROWS)),
-            (far_i, near_i, row_of[FAR_I], 2 * row_of[NEAR_I] - (PAD + 2 * ROWS)),
-        ):
-            place_field(forcing.at[i], at, wave_parts(far, 2, 10, far, 0, 8, i))
-            parts = wave_parts(near, B_BEHIND, B_BEHIND + 6, far, C_STRIP_W, C_STRIP_W + 2, i)
-            place_field(state.at[i], main_at, parts, at)
+        pushed, parts, behind = [], [], []
+        for near, main in ((near_c, state_c), (near_i, state_i)):
+            pushed.append(wave_main(near, B_WAVE + 2, B_WAVE + 10, i) + wave_strip(near, B_WAVE, B_WAVE + 8, i))
+            parts.append(wave_main(main, A_WAVE, A_WAVE + 6, i) + wave_strip(near, B_STRIP_W, B_STRIP_W + 2, i))
+            behind.append(wave_main(near, B_BEHIND, B_BEHIND + 6, i))
+        far_pushed = [wave_main(far, 2, 10, i) + wave_strip(far, 0, 8, i) for far in (far_c, far_i)]
+        far_strip = [wave_strip(far, C_STRIP_W, C_STRIP_W + 2, i) for far in (far_c, far_i)]
+        for k, slot in ((1, 0), (0, 4)):
+            near_slot = (slot + 2) // 2
+            place_field(forcing.at[i], PAD + near_slot * ROWS, chosen(after, pushed[k], pushed[1 - k]))
+            place_field(state.at[i], PAD + near_slot * ROWS, chosen(after, parts[k], parts[1 - k]))
+            place_field(forcing.at[i], PAD + slot * ROWS, chosen(after_far, far_pushed[k], far_pushed[1 - k]))
+            main = chosen(after, behind[k], behind[1 - k])
+            strip = chosen(after_far, far_strip[k], far_strip[1 - k])
+            place_field(state.at[i], PAD + slot * ROWS, main + strip)
         for j in range(3):
             for ref in (state, forcing):
                 ref[i, j, 0:PAD, :] = jnp.zeros((PAD, LANES), f32)
                 ref[i, j, PAD + height : height + 2 * PAD, :] = jnp.zeros((PAD, LANES), f32)
-    half_a = 0.5 * config_ref[WAVE_SPEED]
-    half_b = 0.5 * config_ref[WAVE_SPEED + 1]
+    half_a = 0.5 * config_ref[:, WAVE_SPEED : WAVE_SPEED + 1]
+    half_b = 0.5 * config_ref[:, WAVE_SPEED + 1 : WAVE_SPEED + 2]
     first_row = -2 * ROWS
     for j in range(3):
-        coef[0, j] = inside_tile(place_ref, first_row, height, j) * half_a
-        coef[1, j] = inside_tile(place_ref, first_row + 1, height, j) * half_b
-        coef[2, j] = inside_tile(place_ref, first_row - 1, height, j) * half_b
-        coef[3, j] = inside_tile(place_ref, first_row, height, j, 1) * half_b
-        coef[4, j] = inside_tile(place_ref, first_row, height, j, -1) * half_b
+        coef[0, j] = inside_tile(config_ref, first_row, height, j) * half_a
+        coef[1, j] = inside_tile(config_ref, first_row + 1, height, j) * half_b
+        coef[2, j] = inside_tile(config_ref, first_row - 1, height, j) * half_b
+        coef[3, j] = inside_tile(config_ref, first_row, height, j, 1) * half_b
+        coef[4, j] = inside_tile(config_ref, first_row, height, j, -1) * half_b
 
     lane = lax.broadcasted_iota(jnp.int32, (8, LANES), 1)
-    keep = [1.0 - config_ref[c] for c in range(WAVES)]
+    keep = [1.0 - spread(config_ref, c) for c in range(WAVES)]
 
     def load(ref, i, t, by=0):
         at = PAD + 8 * t + by
@@ -528,7 +541,7 @@
     power_u, total_u = decays(keep[1])
     power_v, total_v = decays(keep[2])
     for j in range(2):
-        inside = inside_tile(place_ref, 0, ROWS, j) * half_b
+        inside = inside_tile(config_ref, 0, ROWS, j) * half_b
         for t in own:
             at = PAD + 8 * t
             rows = slice(8 * (t - 4), 8 * (t - 4) + 8)
@@ -549,7 +562,7 @@
         write_export(fields, received, land_ref[...].astype(f32), smix_ref, imix_ref, turned, export_ref)
 
 
-def wave_steps(last, place, config, mixes, operands):
+def wave_steps(last, config, mixes, operands):
     state = shaped((FIELDS, ROWS, COLS))
     scratch = [
         pltpu.VMEM((WAVES, 3, 5 * ROWS + 2 * PAD, LANES), f32),
@@ -561,12 +574,12 @@
     return pl.pallas_call(
         lambda *refs: wave_kernel(last, *refs),
         out_shape=state if last else (state, shaped((TURNED, COLS), bf16)),
-        in_specs=[SMEM] * (2 + len(mixes)) + [VMEM] * len(operands),
+        in_specs=[VMEM] * (1 + len(mixes) + len(operands)),
         out_specs=VMEM if last else (VMEM,) * 2,
         scratch_shapes=scratch,
         compiler_params=params(),
         name="wave_steps_last" if last else "wave_steps",
-    )(place, config, *mixes, *operands)
+    )(config, *mixes, *operands)
 
 
 def exchanged(block, axis, distance, phase):
@@ -590,9 +603,9 @@
     side_far = 1 - 2 * ((gx // 2) % 2)
     place = jnp.stack([
         gx * ROWS, gy * COLS, lax.axis_size("gx") * ROWS, lax.axis_size("gy") * COLS,
-        2 - side_near, 2 + side_near, 2 - 2 * side_far, 2 + 2 * side_far, gy % 2,
-    ]).astype(jnp.int32)
-    config = jnp.concatenate([damping[0], wave_speed[0]])
+        gx % 2, (gx // 2) % 2, gy % 2,
+    ])
+    config = jnp.concatenate([damping[0], wave_speed[0], place.astype(f32)])[None]
     owner = remap_owner[0].reshape(-1)
     slot = remap_slot[0].reshape(-1)
     away = owner - gx
@@ -607,7 +620,7 @@
     for interval in range(ITERS):
         last = interval == ITERS - 1
         opposite = lax.ppermute(exported, "sec", [(0, 1), (1, 0)])
-        near = pack(opposite, fields, index, place, config)
+        near = pack(opposite, fields, index, config)
         state_c = exchanged(near, "gx", 1, 1)
         state_i = exchanged(near, "gx", 1, 0)
         export_c = exchanged(opposite, "gx", 2, 1)
@@ -619,7 +632,7 @@
         )
         outer = exchanged(to_outer, "gy", 1, 1)
         chip = exchanged(to_chip, "gy", 1, 0)
-        out_c, out_i, outer, left, right = pack_forcing(place, forcing, outer, chip, state_c, state_i)
+        out_c, out_i, outer, left, right = pack_forcing(config, forcing, outer, chip, state_c, state_i)
         near_c = exchanged(out_c, "gx", 1, 1)
         near_i = exchanged(out_i, "gx", 1, 0)
         far_c = exchanged(outer, "gx", 2, 1)
@@ -628,15 +641,15 @@
         state = (state_c, fields, state_i)
         operands = (near_c, *own, near_i, *state)
         if last:
-            tracers, received = tracer_steps(last, place, config, operands + (received,))
+            tracers, received = tracer_steps(last, config, operands + (received,))
         else:
-            tracers = tracer_steps(last, place, config, operands)
+            tracers = tracer_steps(last, config, operands)
         operands = (far_i, near_c, *own, near_i, far_c, *state, tracers)
         if last:
-            fields = wave_steps(last, place, config, (), operands)
+            fields = wave_steps(last, config, (), operands)
         else:
             operands += (received, land)
-            fields, exported = wave_steps(last, place, config, (smix, imix), operands)
+            fields, exported = wave_steps(last, config, (smix, imix), operands)
     return (fields[None], received[None])
 
 

time: 128 us -> 126 us (0.984)
  Pallas kernels: 19.8 us -> 17 us
where the time goes in v7:
time: 126 us; the launch traced here: 125 us
  starting transfers between devices  86.3 us (68%)
  Pallas kernels  17 us (13%)
  waiting for transfers between devices  17 us (13%)
  local copies, waits for them, and re-layouts  3.56 us (3%)
    ppermute x20, starting transfers between devices, exchanged(): return lax.ppermute(block, axis, route)  67.7 us
    ppermute x2, starting transfers between devices, local(): opposite = lax.ppermute(exported, 'sec', [(0, 1), (1, 0)])  18.6 us
    ppermute x20, waiting for transfers between devices, exchanged(): return lax.ppermute(block, axis, route)  13.7 us
    pallas_call x2, Pallas kernels, tracer_steps(): pl.pallas_call(lambda *refs: tracer_kernel(last, *refs), out_shape=(trace...  6.91 us
    pallas_call x2, Pallas kernels, wave_steps(): pl.pallas_call(lambda *refs: wave_kernel(last, *refs), out_shape=state if...  4.58 us
    ppermute x2, waiting for transfers between devices, local(): opposite = lax.ppermute(exported, 'sec', [(0, 1), (1, 0)])  3.27 us
    unnamed x19, local copies, waits for them, and re-layouts  3.07 us
    pallas_call x1, Pallas kernels, export(): pl.pallas_call(export_kernel, out_shape=(shaped((TURNED, COLS), bf16), sh...  2.64 us
  transfers between devices with their start and end apart: 22, of which 11 were waited for; matrix products, arithmetic and copies ran while one was open for 1% of the time, Pallas kernels for 6%

profile of v7, /device:TPU:6, one launch (start us, length us, event | category | flops | bytes accessed | tf_op | source)
XLA Modules:
  0.0 125.0 jit_solution(7818431979181197058)
XLA Ops:
  0.6 2.6 %export.1 = (bf16[128,256]{1,0:T(8,128)(2,1)}, f32[8,16,256]{2,1,0:T(8,128)}, s32[16,256]{1,0:T(8,128)}) custom-call(f32[8,8]{1,0:T(8,128)} %bitcast.20, f32[8,8]{1,0:T(8,128)} %bitcast.22, f32[8,16,256]{2,1,0:T(8,128)} %bitcast.25, f32[8,16,256]{2,1,0:T(8,128)} %bitcast.26, s32[16,256]{1,0:T(8,128)} %bitcast.27), custom_call_target="tpu_custom_call" | custom-call | tf_op jit(solution)/shard_map/export/pallas_call | solution.py:115
  3.3 10.9 %collective-permute-start = (bf16[128,256]{1,0:T(8,128)(2,1)}, bf16[128,256]{1,0:T(8,128)(2,1)S(1)}, u32[]{:S(2)}, u32[]{:S(2)}) collective-permute-start(bf16[128,256]{1,0:T(8,128)(2,1)} %get-tuple-element.27), channel_id=1, source_target_pairs={{0,256},{256,0},{1,257},{257,1},{2,258},{258,2},{3,259},{259,3},{4... | collective-permute-start | bytes 196616 | tf_op jit(solution)/shard_map/ppermute | solution.py:622
  14.4 0.5 copy-done.6
  14.9 0.1 copy.14
  15.0 0.1 sub.33
  15.2 0.5 copy-done.5
  15.7 0.1 copy.15
  15.8 0.1 reshape_squeeze.7
  16.0 0.6 copy-done.7
  16.7 0.8 collective-permute-done.opposite_ref
  17.6 5.6 %collective-permute-start.3 = (bf16[38,16,128]{2,1,0:T(8,128)(2,1)S(1)}, bf16[38,16,128]{2,1,0:T(8,128)(2,1)S(1)}, u32[]{:S(2)}, u32[]{:S(2)}) collective-permute-start(bf16[38,16,128]{2,1,0:T(8,128)(2,1)S(1)} %pack.2), channel_id=1, source_target_pairs={{8,16},{16,8},{24,32},{32,24},{40,48},{48,40},{56,64},{64,56},{72,... | collective-permute-start | bytes 466952 | tf_op jit(solution)/shard_map/ppermute | solution.py:591
  23.2 1.9 %collective-permute-start.2 = (bf16[38,16,128]{2,1,0:T(8,128)(2,1)S(1)}, bf16[38,16,128]{2,1,0:T(8,128)(2,1)S(1)}, u32[]{:S(2)}, u32[]{:S(2)}) collective-permute-start(bf16[38,16,128]{2,1,0:T(8,128)(2,1)S(1)} %pack.2), channel_id=1, source_target_pairs={{0,8},{8,0},{16,24},{24,16},{32,40},{40,32},{48,56},{56,48},{64,72... | collective-permute-start | bytes 466952 | tf_op jit(solution)/shard_map/ppermute | solution.py:591
  25.2 4.0 %collective-permute-start.4 = (bf16[128,256]{1,0:T(8,128)(2,1)S(1)}, bf16[128,256]{1,0:T(8,128)(2,1)S(1)}, u32[]{:S(2)}, u32[]{:S(2)}) collective-permute-start(bf16[128,256]{1,0:T(8,128)(2,1)S(1)} %collective-permute-done.opposite_ref), channel_id=1, source_target_pairs={{16,32},{32,16},{24,40},{40,24},{48,64},{64,48},{56,72},{72,56},{8... | collective-permute-start | bytes 196616 | tf_op jit(solution)/shard_map/ppermute | solution.py:591
  29.2 3.8 %collective-permute-start.1 = (bf16[128,256]{1,0:T(8,128)(2,1)S(1)}, bf16[128,256]{1,0:T(8,128)(2,1)S(1)}, u32[]{:S(2)}, u32[]{:S(2)}) collective-permute-start(bf16[128,256]{1,0:T(8,128)(2,1)S(1)} %collective-permute-done.opposite_ref), channel_id=1, source_target_pairs={{0,16},{16,0},{8,24},{24,8},{32,48},{48,32},{40,56},{56,40},{64,80... | collective-permute-start | bytes 196616 | tf_op jit(solution)/shard_map/ppermute | solution.py:591
  33.0 1.2 copy-done.1
  34.3 1.9 %collective-permute-done.1.far_i_ref = bf16[128,256]{1,0:T(8,128)(2,1)S(1)} collective-permute-done((bf16[128,256]{1,0:T(8,128)(2,1)S(1)}, bf16[128,256]{1,0:T(8,128)(2,1)S(1)}, u32[]{:S(2)}, u32[]{:S(2)}) %collective-permute-start.1) | collective-permute-done | bytes 65568 | tf_op jit(solution)/shard_map/ppermute | solution.py:591
  36.3 1.3 %remap.2 = (f32[8,16,256]{2,1,0:T(8,128)S(1)}, f32[4,16,128]{2,1,0:T(8,128)S(1)}, f32[4,16,128]{2,1,0:T(8,128)S(1)}, f32[8,16,256]{2,1,0:T(8,128)S(1)}) custom-call(s32[129]{0:T(256)S(1)} %pad_add_fusion.index_ref, bf16[128,256]{1,0:T(8,128)(2,1)S(1)} %collective-permute-done.1.far_i_ref, ...), custom_call_target="tpu_custom_call" | custom-call | tf_op jit(solution)/shard_map/remap/pallas_call | solution.py:271
  37.6 0.7 collective-permute-start.5
  38.2 3.9 %collective-permute-start.6 = (f32[4,16,128]{2,1,0:T(8,128)S(1)}, f32[4,16,128]{2,1,0:T(8,128)S(1)}, u32[]{:S(2)}, u32[]{:S(2)}) collective-permute-start(f32[4,16,128]{2,1,0:T(8,128)S(1)} %get-tuple-element.32), channel_id=1, source_target_pairs={{0,1},{1,0},{2,3},{3,2},{4,5},{5,4},{6,7},{7,6},{8,9},{9,8},{10,11... | collective-permute-start | bytes 98312 | tf_op jit(solution)/shard_map/ppermute | solution.py:591
  42.2 0.8 collective-permute-done.6.chip_ref
  43.1 5.5 %collective-permute-start.8 = (bf16[46,16,128]{2,1,0:T(8,128)(2,1)S(1)}, bf16[46,16,128]{2,1,0:T(8,128)(2,1)S(1)}, u32[]{:S(2)}, u32[]{:S(2)}) collective-permute-start(bf16[46,16,128]{2,1,0:T(8,128)(2,1)S(1)} %get-tuple-element.34), channel_id=1, source_target_pairs={{8,16},{16,8},{24,32},{32,24},{40,48},{48,40},{56,64},{64,56},{72,... | collective-permute-start | bytes 565256 | tf_op jit(solution)/shard_map/ppermute | solution.py:591
  48.6 1.9 %collective-permute-start.9 = (bf16[46,16,128]{2,1,0:T(8,128)(2,1)S(1)}, bf16[46,16,128]{2,1,0:T(8,128)(2,1)S(1)}, u32[]{:S(2)}, u32[]{:S(2)}) collective-permute-start(bf16[46,16,128]{2,1,0:T(8,128)(2,1)S(1)} %get-tuple-element.37), channel_id=1, source_target_pairs={{0,8},{8,0},{16,24},{24,16},{32,40},{40,32},{48,56},{56,48},{64,72... | collective-permute-start | bytes 565256 | tf_op jit(solution)/shard_map/ppermute | solution.py:591
  50.5 3.9 %collective-permute-start.10 = (bf16[20,16,128]{2,1,0:T(8,128)(2,1)S(1)}, bf16[20,16,128]{2,1,0:T(8,128)(2,1)S(1)}, u32[]{:S(2)}, u32[]{:S(2)}) collective-permute-start(bf16[20,16,128]{2,1,0:T(8,128)(2,1)S(1)} %get-tuple-element.33), channel_id=1, source_target_pairs={{16,32},{32,16},{24,40},{40,24},{48,64},{64,48},{56,72},{72,56},{8... | collective-permute-start | bytes 245768 | tf_op jit(solution)/shard_map/ppermute | solution.py:591
  54.4 2.7 %collective-permute-start.7 = (bf16[20,16,128]{2,1,0:T(8,128)(2,1)S(1)}, bf16[20,16,128]{2,1,0:T(8,128)(2,1)S(1)}, u32[]{:S(2)}, u32[]{:S(2)}) collective-permute-start(bf16[20,16,128]{2,1,0:T(8,128)(2,1)S(1)} %get-tuple-element.33), channel_id=1, source_target_pairs={{0,16},{16,0},{8,24},{24,8},{32,48},{48,32},{40,56},{56,40},{64,80... | collective-permute-start | bytes 245768 | tf_op jit(solution)/shard_map/ppermute | solution.py:591
  57.1 0.9 collective-permute-done.9.refs_5_.refs_8_
  58.1 3.3 %tracer_steps.2.refs_13_ = f32[5,16,256]{2,1,0:T(8,128)S(1)} custom-call(f32[1,17]{1,0:T(1,128)S(1)} %maximum_bitcast_fusion.config_ref.refs_0_, bf16[46,16,128]{2,1,0:T(8,128)(2,1)S(1)} %collective-permute-done.8.refs_1_.refs_4_, f32[8,16,256]{2,1,0:T(8,128)S(1)} %get-tuple-element.30.forcing_ref.refs_2_.refs_5_, ...), custom_call_target="tpu_custom_call" | custom-call | flops 10000000 | bytes 4000000 | tf_op jit(solution)/shard_map/tracer_steps/pallas_call | solution.py:412
  61.4 0.6 collective-permute-done.7.refs_3_
  62.1 2.1 %wave_steps.1 = (f32[8,16,256]{2,1,0:T(8,128)S(1)}, bf16[128,256]{1,0:T(8,128)(2,1)S(1)}) custom-call(f32[1,17]{1,0:T(1,128)S(1)} %maximum_bitcast_fusion.config_ref.refs_0_, f32[8,8]{1,0:T(8,128)S(1)} %bitcast.21, f32[8,8]{1,0:T(8,128)S(1)} %bitcast.23, bf16[20,16,128]{2,1,0:T(8,128)(2,1)S(1)} %collective-permute-done.7.refs_3_, ...), custom_call_target="tpu_custom_call" | custom-call | tf_op jit(solution)/shard_map/wave_steps/pallas_call | solution.py:574
  64.1 7.7 %collective-permute-start.11 = (bf16[128,256]{1,0:T(8,128)(2,1)S(1)}, bf16[128,256]{1,0:T(8,128)(2,1)S(1)}, u32[]{:S(2)}, u32[]{:S(2)}) collective-permute-start(bf16[128,256]{1,0:T(8,128)(2,1)S(1)} %get-tuple-element.39), channel_id=1, source_target_pairs={{0,256},{256,0},{1,257},{257,1},{2,258},{258,2},{3,259},{259,3},{4... | collective-permute-start | bytes 196616 | tf_op jit(solution)/shard_map/ppermute | solution.py:622
  71.9 2.5 %collective-permute-done.11.opposite_ref = bf16[128,256]{1,0:T(8,128)(2,1)S(1)} collective-permute-done((bf16[128,256]{1,0:T(8,128)(2,1)S(1)}, bf16[128,256]{1,0:T(8,128)(2,1)S(1)}, u32[]{:S(2)}, u32[]{:S(2)}) %collective-permute-start.11) | collective-permute-done | bytes 65568 | tf_op jit(solution)/shard_map/ppermute | solution.py:622
  74.3 6.5 %collective-permute-start.14 = (bf16[38,16,128]{2,1,0:T(8,128)(2,1)S(1)}, bf16[38,16,128]{2,1,0:T(8,128)(2,1)S(1)}, u32[]{:S(2)}, u32[]{:S(2)}) collective-permute-start(bf16[38,16,128]{2,1,0:T(8,128)(2,1)S(1)} %pack.3), channel_id=1, source_target_pairs={{8,16},{16,8},{24,32},{32,24},{40,48},{48,40},{56,64},{64,56},{72,... | collective-permute-start | bytes 466952 | tf_op jit(solution)/shard_map/ppermute | solution.py:591
  80.8 1.9 %collective-permute-start.13 = (bf16[38,16,128]{2,1,0:T(8,128)(2,1)S(1)}, bf16[38,16,128]{2,1,0:T(8,128)(2,1)S(1)}, u32[]{:S(2)}, u32[]{:S(2)}) collective-permute-start(bf16[38,16,128]{2,1,0:T(8,128)(2,1)S(1)} %pack.3), channel_id=1, source_target_pairs={{0,8},{8,0},{16,24},{24,16},{32,40},{40,32},{48,56},{56,48},{64,72... | collective-permute-start | bytes 466952 | tf_op jit(solution)/shard_map/ppermute | solution.py:591
  82.8 3.4 %collective-permute-start.15 = (bf16[128,256]{1,0:T(8,128)(2,1)S(1)}, bf16[128,256]{1,0:T(8,128)(2,1)S(1)}, u32[]{:S(2)}, u32[]{:S(2)}) collective-permute-start(bf16[128,256]{1,0:T(8,128)(2,1)S(1)} %collective-permute-done.11.opposite_ref), channel_id=1, source_target_pairs={{16,32},{32,16},{24,40},{40,24},{48,64},{64,48},{56,72},{72,56},{8... | collective-permute-start | bytes 196616 | tf_op jit(solution)/shard_map/ppermute | solution.py:591
  86.2 2.3 %collective-permute-start.12 = (bf16[128,256]{1,0:T(8,128)(2,1)S(1)}, bf16[128,256]{1,0:T(8,128)(2,1)S(1)}, u32[]{:S(2)}, u32[]{:S(2)}) collective-permute-start(bf16[128,256]{1,0:T(8,128)(2,1)S(1)} %collective-permute-done.11.opposite_ref), channel_id=1, source_target_pairs={{0,16},{16,0},{8,24},{24,8},{32,48},{48,32},{40,56},{56,40},{64,80... | collective-permute-start | bytes 196616 | tf_op jit(solution)/shard_map/ppermute | solution.py:591
  88.5 3.5 %collective-permute-done.15.far_c_ref = bf16[128,256]{1,0:T(8,128)(2,1)S(1)} collective-permute-done((bf16[128,256]{1,0:T(8,128)(2,1)S(1)}, bf16[128,256]{1,0:T(8,128)(2,1)S(1)}, u32[]{:S(2)}, u32[]{:S(2)}) %collective-permute-start.15) | collective-permute-done | bytes 65568 | tf_op jit(solution)/shard_map/ppermute | solution.py:591
  92.0 2.0 %collective-permute-done.12.far_i_ref = bf16[128,256]{1,0:T(8,128)(2,1)S(1)} collective-permute-done((bf16[128,256]{1,0:T(8,128)(2,1)S(1)}, bf16[128,256]{1,0:T(8,128)(2,1)S(1)}, u32[]{:S(2)}, u32[]{:S(2)}) %collective-permute-start.12) | collective-permute-done | bytes 65568 | tf_op jit(solution)/shard_map/ppermute | solution.py:591
  93.9 1.3 %remap.3 = (f32[8,16,256]{2,1,0:T(8,128)S(1)}, f32[4,16,128]{2,1,0:T(8,128)S(1)}, f32[4,16,128]{2,1,0:T(8,128)S(1)}, f32[8,16,256]{2,1,0:T(8,128)S(1)}) custom-call(s32[129]{0:T(256)S(1)} %pad_add_fusion.index_ref, bf16[128,256]{1,0:T(8,128)(2,1)S(1)} %collective-permute-done.12.far_i_ref, ...), custom_call_target="tpu_custom_call" | custom-call | tf_op jit(solution)/shard_map/remap/pallas_call | solution.py:271
  95.2 0.7 collective-permute-start.16
  95.9 5.7 %collective-permute-start.17 = (f32[4,16,128]{2,1,0:T(8,128)S(1)}, f32[4,16,128]{2,1,0:T(8,128)S(1)}, u32[]{:S(2)}, u32[]{:S(2)}) collective-permute-start(f32[4,16,128]{2,1,0:T(8,128)S(1)} %get-tuple-element.43), channel_id=1, source_target_pairs={{0,1},{1,0},{2,3},{3,2},{4,5},{5,4},{6,7},{7,6},{8,9},{9,8},{10,11... | collective-permute-start | bytes 98312 | tf_op jit(solution)/shard_map/ppermute | solution.py:591
  101.6 0.8 collective-permute-done.17.chip_ref
  102.5 5.5 %collective-permute-start.19 = (bf16[46,16,128]{2,1,0:T(8,128)(2,1)S(1)}, bf16[46,16,128]{2,1,0:T(8,128)(2,1)S(1)}, u32[]{:S(2)}, u32[]{:S(2)}) collective-permute-start(bf16[46,16,128]{2,1,0:T(8,128)(2,1)S(1)} %get-tuple-element.45), channel_id=1, source_target_pairs={{8,16},{16,8},{24,32},{32,24},{40,48},{48,40},{56,64},{64,56},{72,... | collective-permute-start | bytes 565256 | tf_op jit(solution)/shard_map/ppermute | solution.py:591
  108.0 1.9 %collective-permute-start.20 = (bf16[46,16,128]{2,1,0:T(8,128)(2,1)S(1)}, bf16[46,16,128]{2,1,0:T(8,128)(2,1)S(1)}, u32[]{:S(2)}, u32[]{:S(2)}) collective-permute-start(bf16[46,16,128]{2,1,0:T(8,128)(2,1)S(1)} %get-tuple-element.48), channel_id=1, source_target_pairs={{0,8},{8,0},{16,24},{24,16},{32,40},{40,32},{48,56},{56,48},{64,72... | collective-permute-start | bytes 565256 | tf_op jit(solution)/shard_map/ppermute | solution.py:591
  109.9 3.9 %collective-permute-start.21 = (bf16[20,16,128]{2,1,0:T(8,128)(2,1)S(1)}, bf16[20,16,128]{2,1,0:T(8,128)(2,1)S(1)}, u32[]{:S(2)}, u32[]{:S(2)}) collective-permute-start(bf16[20,16,128]{2,1,0:T(8,128)(2,1)S(1)} %get-tuple-element.44), channel_id=1, source_target_pairs={{16,32},{32,16},{24,40},{40,24},{48,64},{64,48},{56,72},{72,56},{8... | collective-permute-start | bytes 245768 | tf_op jit(solution)/shard_map/ppermute | solution.py:591
  113.9 1.9 %collective-permute-start.18 = (bf16[20,16,128]{2,1,0:T(8,128)(2,1)S(1)}, bf16[20,16,128]{2,1,0:T(8,128)(2,1)S(1)}, u32[]{:S(2)}, u32[]{:S(2)}) collective-permute-start(bf16[20,16,128]{2,1,0:T(8,128)(2,1)S(1)} %get-tuple-element.44), channel_id=1, source_target_pairs={{0,16},{16,0},{8,24},{24,8},{32,48},{48,32},{40,56},{56,40},{64,80... | collective-permute-start | bytes 245768 | tf_op jit(solution)/shard_map/ppermute | solution.py:591
  115.8 1.7 %collective-permute-done.20.refs_5_.refs_6_ = bf16[46,16,128]{2,1,0:T(8,128)(2,1)S(1)} collective-permute-done((bf16[46,16,128]{2,1,0:T(8,128)(2,1)S(1)}, bf16[46,16,128]{2,1,0:T(8,128)(2,1)S(1)}, u32[]{:S(2)}, u32[]{:S(2)}) %collective-permute-start.20) | collective-permute-done | bytes 188448 | tf_op jit(solution)/shard_map/ppermute | solution.py:591
  117.5 3.6 %tracer_steps.3 = (f32[5,16,256]{2,1,0:T(8,128)S(1)}, f32[8,16,256]{2,1,0:T(8,128)}) custom-call(f32[1,17]{1,0:T(1,128)S(1)} %maximum_bitcast_fusion.config_ref.refs_0_, bf16[46,16,128]{2,1,0:T(8,128)(2,1)S(1)} %collective-permute-done.19.refs_1_.refs_2_, f32[8,16,256]{2,1,0:T(8,128)S(1)} %get-tuple-element.41.forcing_ref.refs_2_.refs_3_, ...), custom_call_target="tpu_custom_call" | custom-call | flops 10000000 | bytes 4000000 | tf_op jit(solution)/shard_map/tracer_steps/pallas_call | solution.py:412
  121.1 1.4 %collective-permute-done.18.refs_1_ = bf16[20,16,128]{2,1,0:T(8,128)(2,1)S(1)} collective-permute-done((bf16[20,16,128]{2,1,0:T(8,128)(2,1)S(1)}, bf16[20,16,128]{2,1,0:T(8,128)(2,1)S(1)}, u32[]{:S(2)}, u32[]{:S(2)}) %collective-permute-start.18) | collective-permute-done | bytes 81952 | tf_op jit(solution)/shard_map/ppermute | solution.py:591
  122.5 2.5 %wave_steps_last.1 = f32[8,16,256]{2,1,0:T(8,128)} custom-call(f32[1,17]{1,0:T(1,128)S(1)} %maximum_bitcast_fusion.config_ref.refs_0_, bf16[20,16,128]{2,1,0:T(8,128)(2,1)S(1)} %collective-permute-done.18.refs_1_, bf16[46,16,128]{2,1,0:T(8,128)(2,1)S(1)} %collective-permute-done.19.refs_1_.refs_2_, ...), custom_call_target="tpu_custom_call" | custom-call | tf_op jit(solution)/shard_map/wave_steps_last/pallas_call | solution.py:574
  (36 shorter events, 0.6 us)
Async XLA Ops:
  3.3 14.3 %collective-permute-start = (bf16[128,256]{1,0:T(8,128)(2,1)}, bf16[128,256]{1,0:T(8,128)(2,1)S(1)}, u32[]{:S(2)}, u32[]{:S(2)}) collective-permute-start(bf16[128,256]{1,0:T(8,128)(2,1)} %get-tuple-element.27), channel_id=1, source_target_pairs={{0,256},{256,0},{1,257},{257,1},{2,258},{258,2},{3,259},{259,3},{4... | collective-permute-start | bytes 196616 | tf_op jit(solution)/shard_map/ppermute | solution.py:622
  14.2 0.7 copy-start.6
  14.2 3.3 %copy-start = (f32[8,16,256]{2,1,0:T(8,128)S(1)}, f32[8,16,256]{2,1,0:T(8,128)}, u32[]{:S(2)}) copy-start(f32[8,16,256]{2,1,0:T(8,128)} %get-tuple-element.28.fields_ref.refs_7_.refs_11_) | copy-start | bytes 393220
  15.0 0.7 copy-start.5
  16.0 0.7 copy-start.7
  16.0 0.7 copy-start.8
  17.6 15.4 %collective-permute-start.3 = (bf16[38,16,128]{2,1,0:T(8,128)(2,1)S(1)}, bf16[38,16,128]{2,1,0:T(8,128)(2,1)S(1)}, u32[]{:S(2)}, u32[]{:S(2)}) collective-permute-start(bf16[38,16,128]{2,1,0:T(8,128)(2,1)S(1)} %pack.2), channel_id=1, source_target_pairs={{8,16},{16,8},{24,32},{32,24},{40,48},{48,40},{56,64},{64,56},{72,... | collective-permute-start | bytes 466952 | tf_op jit(solution)/shard_map/ppermute | solution.py:591
  23.2 9.8 %collective-permute-start.2 = (bf16[38,16,128]{2,1,0:T(8,128)(2,1)S(1)}, bf16[38,16,128]{2,1,0:T(8,128)(2,1)S(1)}, u32[]{:S(2)}, u32[]{:S(2)}) collective-permute-start(bf16[38,16,128]{2,1,0:T(8,128)(2,1)S(1)} %pack.2), channel_id=1, source_target_pairs={{0,8},{8,0},{16,24},{24,16},{32,40},{40,32},{48,56},{56,48},{64,72... | collective-permute-start | bytes 466952 | tf_op jit(solution)/shard_map/ppermute | solution.py:591
  25.2 9.2 %collective-permute-start.4 = (bf16[128,256]{1,0:T(8,128)(2,1)S(1)}, bf16[128,256]{1,0:T(8,128)(2,1)S(1)}, u32[]{:S(2)}, u32[]{:S(2)}) collective-permute-start(bf16[128,256]{1,0:T(8,128)(2,1)S(1)} %collective-permute-done.opposite_ref), channel_id=1, source_target_pairs={{16,32},{32,16},{24,40},{40,24},{48,64},{64,48},{56,72},{72,56},{8... | collective-permute-start | bytes 196616 | tf_op jit(solution)/shard_map/ppermute | solution.py:591
  29.2 7.1 %collective-permute-start.1 = (bf16[128,256]{1,0:T(8,128)(2,1)S(1)}, bf16[128,256]{1,0:T(8,128)(2,1)S(1)}, u32[]{:S(2)}, u32[]{:S(2)}) collective-permute-start(bf16[128,256]{1,0:T(8,128)(2,1)S(1)} %collective-permute-done.opposite_ref), channel_id=1, source_target_pairs={{0,16},{16,0},{8,24},{24,8},{32,48},{48,32},{40,56},{56,40},{64,80... | collective-permute-start | bytes 196616 | tf_op jit(solution)/shard_map/ppermute | solution.py:591
  33.0 1.2 copy-start.1
  34.2 2.0 %copy-start.2 = (s32[16,256]{1,0:T(8,128)S(1)}, s32[16,256]{1,0:T(8,128)}, u32[]{:S(2)}) copy-start(s32[16,256]{1,0:T(8,128)} %get-tuple-element.29.land_ref.refs_15_) | copy-start | bytes 49156
  37.6 4.6 %collective-permute-start.5 = (f32[4,16,128]{2,1,0:T(8,128)S(1)}, f32[4,16,128]{2,1,0:T(8,128)S(1)}, u32[]{:S(2)}, u32[]{:S(2)}) collective-permute-start(f32[4,16,128]{2,1,0:T(8,128)S(1)} %get-tuple-element.31), channel_id=1, source_target_pairs={{1,2},{2,1},{3,4},{4,3},{5,6},{6,5},{9,10},{10,9},{11,12},{12,11},... | collective-permute-start | bytes 98312 | tf_op jit(solution)/shard_map/ppermute | solution.py:591
  38.2 4.8 %collective-permute-start.6 = (f32[4,16,128]{2,1,0:T(8,128)S(1)}, f32[4,16,128]{2,1,0:T(8,128)S(1)}, u32[]{:S(2)}, u32[]{:S(2)}) collective-permute-start(f32[4,16,128]{2,1,0:T(8,128)S(1)} %get-tuple-element.32), channel_id=1, source_target_pairs={{0,1},{1,0},{2,3},{3,2},{4,5},{5,4},{6,7},{7,6},{8,9},{9,8},{10,11... | collective-permute-start | bytes 98312 | tf_op jit(solution)/shard_map/ppermute | solution.py:591
  43.1 14.0 %collective-permute-start.8 = (bf16[46,16,128]{2,1,0:T(8,128)(2,1)S(1)}, bf16[46,16,128]{2,1,0:T(8,128)(2,1)S(1)}, u32[]{:S(2)}, u32[]{:S(2)}) collective-permute-start(bf16[46,16,128]{2,1,0:T(8,128)(2,1)S(1)} %get-tuple-element.34), channel_id=1, source_target_pairs={{8,16},{16,8},{24,32},{32,24},{40,48},{48,40},{56,64},{64,56},{72,... | collective-permute-start | bytes 565256 | tf_op jit(solution)/shard_map/ppermute | solution.py:591
  48.6 9.5 %collective-permute-start.9 = (bf16[46,16,128]{2,1,0:T(8,128)(2,1)S(1)}, bf16[46,16,128]{2,1,0:T(8,128)(2,1)S(1)}, u32[]{:S(2)}, u32[]{:S(2)}) collective-permute-start(bf16[46,16,128]{2,1,0:T(8,128)(2,1)S(1)} %get-tuple-element.37), channel_id=1, source_target_pairs={{0,8},{8,0},{16,24},{24,16},{32,40},{40,32},{48,56},{56,48},{64,72... | collective-permute-start | bytes 565256 | tf_op jit(solution)/shard_map/ppermute | solution.py:591
  50.5 10.9 %collective-permute-start.10 = (bf16[20,16,128]{2,1,0:T(8,128)(2,1)S(1)}, bf16[20,16,128]{2,1,0:T(8,128)(2,1)S(1)}, u32[]{:S(2)}, u32[]{:S(2)}) collective-permute-start(bf16[20,16,128]{2,1,0:T(8,128)(2,1)S(1)} %get-tuple-element.33), channel_id=1, source_target_pairs={{16,32},{32,16},{24,40},{40,24},{48,64},{64,48},{56,72},{72,56},{8... | collective-permute-start | bytes 245768 | tf_op jit(solution)/shard_map/ppermute | solution.py:591
  54.4 7.6 %collective-permute-start.7 = (bf16[20,16,128]{2,1,0:T(8,128)(2,1)S(1)}, bf16[20,16,128]{2,1,0:T(8,128)(2,1)S(1)}, u32[]{:S(2)}, u32[]{:S(2)}) collective-permute-start(bf16[20,16,128]{2,1,0:T(8,128)(2,1)S(1)} %get-tuple-element.33), channel_id=1, source_target_pairs={{0,16},{16,0},{8,24},{24,8},{32,48},{48,32},{40,56},{56,40},{64,80... | collective-permute-start | bytes 245768 | tf_op jit(solution)/shard_map/ppermute | solution.py:591
  58.1 4.0 %copy-start.3 = (f32[1,8,8]{2,1,0:T(8,128)S(1)}, f32[1,8,8]{2,1,0:T(8,128)}, u32[]{:S(2)}) copy-start(f32[1,8,8]{2,1,0:T(8,128)} %param.13) | copy-start | bytes 772
  58.1 4.0 %copy-start.4 = (f32[1,8,8]{2,1,0:T(8,128)S(1)}, f32[1,8,8]{2,1,0:T(8,128)}, u32[]{:S(2)}) copy-start(f32[1,8,8]{2,1,0:T(8,128)} %param.14) | copy-start | bytes 772
  64.1 10.2 %collective-permute-start.11 = (bf16[128,256]{1,0:T(8,128)(2,1)S(1)}, bf16[128,256]{1,0:T(8,128)(2,1)S(1)}, u32[]{:S(2)}, u32[]{:S(2)}) collective-permute-start(bf16[128,256]{1,0:T(8,128)(2,1)S(1)} %get-tuple-element.39), channel_id=1, source_target_pairs={{0,256},{256,0},{1,257},{257,1},{2,258},{258,2},{3,259},{259,3},{4... | collective-permute-start | bytes 196616 | tf_op jit(solution)/shard_map/ppermute | solution.py:622
  74.3 19.6 %collective-permute-start.14 = (bf16[38,16,128]{2,1,0:T(8,128)(2,1)S(1)}, bf16[38,16,128]{2,1,0:T(8,128)(2,1)S(1)}, u32[]{:S(2)}, u32[]{:S(2)}) collective-permute-start(bf16[38,16,128]{2,1,0:T(8,128)(2,1)S(1)} %pack.3), channel_id=1, source_target_pairs={{8,16},{16,8},{24,32},{32,24},{40,48},{48,40},{56,64},{64,56},{72,... | collective-permute-start | bytes 466952 | tf_op jit(solution)/shard_map/ppermute | solution.py:591
  80.8 13.1 %collective-permute-start.13 = (bf16[38,16,128]{2,1,0:T(8,128)(2,1)S(1)}, bf16[38,16,128]{2,1,0:T(8,128)(2,1)S(1)}, u32[]{:S(2)}, u32[]{:S(2)}) collective-permute-start(bf16[38,16,128]{2,1,0:T(8,128)(2,1)S(1)} %pack.3), channel_id=1, source_target_pairs={{0,8},{8,0},{16,24},{24,16},{32,40},{40,32},{48,56},{56,48},{64,72... | collective-permute-start | bytes 466952 | tf_op jit(solution)/shard_map/ppermute | solution.py:591
  82.8 9.2 %collective-permute-start.15 = (bf16[128,256]{1,0:T(8,128)(2,1)S(1)}, bf16[128,256]{1,0:T(8,128)(2,1)S(1)}, u32[]{:S(2)}, u32[]{:S(2)}) collective-permute-start(bf16[128,256]{1,0:T(8,128)(2,1)S(1)} %collective-permute-done.11.opposite_ref), channel_id=1, source_target_pairs={{16,32},{32,16},{24,40},{40,24},{48,64},{64,48},{56,72},{72,56},{8... | collective-permute-start | bytes 196616 | tf_op jit(solution)/shard_map/ppermute | solution.py:591
  86.2 7.8 %collective-permute-start.12 = (bf16[128,256]{1,0:T(8,128)(2,1)S(1)}, bf16[128,256]{1,0:T(8,128)(2,1)S(1)}, u32[]{:S(2)}, u32[]{:S(2)}) collective-permute-start(bf16[128,256]{1,0:T(8,128)(2,1)S(1)} %collective-permute-done.11.opposite_ref), channel_id=1, source_target_pairs={{0,16},{16,0},{8,24},{24,8},{32,48},{48,32},{40,56},{56,40},{64,80... | collective-permute-start | bytes 196616 | tf_op jit(solution)/shard_map/ppermute | solution.py:591
  95.2 6.4 %collective-permute-start.16 = (f32[4,16,128]{2,1,0:T(8,128)S(1)}, f32[4,16,128]{2,1,0:T(8,128)S(1)}, u32[]{:S(2)}, u32[]{:S(2)}) collective-permute-start(f32[4,16,128]{2,1,0:T(8,128)S(1)} %get-tuple-element.42), channel_id=1, source_target_pairs={{1,2},{2,1},{3,4},{4,3},{5,6},{6,5},{9,10},{10,9},{11,12},{12,11},... | collective-permute-start | bytes 98312 | tf_op jit(solution)/shard_map/ppermute | solution.py:591
  95.9 6.6 %collective-permute-start.17 = (f32[4,16,128]{2,1,0:T(8,128)S(1)}, f32[4,16,128]{2,1,0:T(8,128)S(1)}, u32[]{:S(2)}, u32[]{:S(2)}) collective-permute-start(f32[4,16,128]{2,1,0:T(8,128)S(1)} %get-tuple-element.43), channel_id=1, source_target_pairs={{0,1},{1,0},{2,3},{3,2},{4,5},{5,4},{6,7},{7,6},{8,9},{9,8},{10,11... | collective-permute-start | bytes 98312 | tf_op jit(solution)/shard_map/ppermute | solution.py:591
  102.5 13.3 %collective-permute-start.19 = (bf16[46,16,128]{2,1,0:T(8,128)(2,1)S(1)}, bf16[46,16,128]{2,1,0:T(8,128)(2,1)S(1)}, u32[]{:S(2)}, u32[]{:S(2)}) collective-permute-start(bf16[46,16,128]{2,1,0:T(8,128)(2,1)S(1)} %get-tuple-element.45), channel_id=1, source_target_pairs={{8,16},{16,8},{24,32},{32,24},{40,48},{48,40},{56,64},{64,56},{72,... | collective-permute-start | bytes 565256 | tf_op jit(solution)/shard_map/ppermute | solution.py:591
  108.0 9.5 %collective-permute-start.20 = (bf16[46,16,128]{2,1,0:T(8,128)(2,1)S(1)}, bf16[46,16,128]{2,1,0:T(8,128)(2,1)S(1)}, u32[]{:S(2)}, u32[]{:S(2)}) collective-permute-start(bf16[46,16,128]{2,1,0:T(8,128)(2,1)S(1)} %get-tuple-element.48), channel_id=1, source_target_pairs={{0,8},{8,0},{16,24},{24,16},{32,40},{40,32},{48,56},{56,48},{64,72... | collective-permute-start | bytes 565256 | tf_op jit(solution)/shard_map/ppermute | solution.py:591
  109.9 11.2 %collective-permute-start.21 = (bf16[20,16,128]{2,1,0:T(8,128)(2,1)S(1)}, bf16[20,16,128]{2,1,0:T(8,128)(2,1)S(1)}, u32[]{:S(2)}, u32[]{:S(2)}) collective-permute-start(bf16[20,16,128]{2,1,0:T(8,128)(2,1)S(1)} %get-tuple-element.44), channel_id=1, source_target_pairs={{16,32},{32,16},{24,40},{40,24},{48,64},{64,48},{56,72},{72,56},{8... | collective-permute-start | bytes 245768 | tf_op jit(solution)/shard_map/ppermute | solution.py:591
  113.9 8.6 %collective-permute-start.18 = (bf16[20,16,128]{2,1,0:T(8,128)(2,1)S(1)}, bf16[20,16,128]{2,1,0:T(8,128)(2,1)S(1)}, u32[]{:S(2)}, u32[]{:S(2)}) collective-permute-start(bf16[20,16,128]{2,1,0:T(8,128)(2,1)S(1)} %get-tuple-element.44), channel_id=1, source_target_pairs={{0,16},{16,0},{8,24},{24,8},{32,48},{48,32},{40,56},{56,40},{64,80... | collective-permute-start | bytes 245768 | tf_op jit(solution)/shard_map/ppermute | solution.py:591

commit v8 on v7

--- a/solution.py
+++ b/solution.py
@@ -27,9 +27,9 @@
 B_STRIP_T = 28
 B_STRIP_W = 30
 B_BEHIND = 34
-B_PLANES = 46
-C_STRIP_W = 16
-C_PLANES = 20
+B_PLANES = 40
+C_STRIP_W = 8
+C_PLANES = 10
 
 PAD = 8
 WAVE_SPEED = 8
@@ -94,35 +94,37 @@
 
 
 def export_kernel(
-    smix_ref, imix_ref, fields_ref, received_ref, land_ref,
-    out_ref, fields_out, land_out, turned, received_buf, sems,
+    smix_hbm, imix_hbm, fields_hbm, received_hbm, land_hbm, out_ref,
+    smix_ref, imix_ref, fields_ref, received_ref, land_ref, turned, sems,
 ):
-    copies = [
-        pltpu.make_async_copy(fields_ref, fields_out, sems.at[0]),
-        pltpu.make_async_copy(received_ref, received_buf, sems.at[1]),
-        pltpu.make_async_copy(land_ref, land_out, sems.at[2]),
-    ]
+    pairs = (
+        (fields_hbm, fields_ref), (received_hbm, received_ref), (land_hbm, land_ref),
+        (smix_hbm, smix_ref), (imix_hbm, imix_ref),
+    )
+    copies = [pltpu.make_async_copy(source, dest, sems.at[k]) for k, (source, dest) in enumerate(pairs)]
     for copy in copies:
         copy.start()
     for copy in copies:
         copy.wait()
-    fields = [fields_out[c] for c in range(FIELDS)]
-    received = [received_buf[c] for c in range(FIELDS)]
-    write_export(fields, received, land_out[...].astype(f32), smix_ref, imix_ref, turned, out_ref)
+    fields = [fields_ref[c] for c in range(FIELDS)]
+    received = [received_ref[c] for c in range(FIELDS)]
+    write_export(fields, received, land_ref[...].astype(f32), smix_ref, imix_ref, turned, out_ref)
 
 
 def export(fields, received, land, smix, imix):
     return pl.pallas_call(
         export_kernel,
-        out_shape=(
-            shaped((TURNED, COLS), bf16), shaped((FIELDS, ROWS, COLS)), shaped((ROWS, COLS), jnp.int32),
-        ),
-        in_specs=[VMEM, VMEM, HBM, HBM, HBM],
-        out_specs=(VMEM,) * 3,
+        out_shape=shaped((TURNED, COLS), bf16),
+        in_specs=[HBM] * 5,
+        out_specs=VMEM,
         scratch_shapes=[
+            pltpu.VMEM((FIELDS, FIELDS), f32),
+            pltpu.VMEM((FIELDS, FIELDS), f32),
+            pltpu.VMEM((FIELDS, ROWS, COLS), f32),
+            pltpu.VMEM((FIELDS, ROWS, COLS), f32),
+            pltpu.VMEM((ROWS, COLS), jnp.int32),
             pltpu.VMEM((2, TURNED, LANES), f32),
-            pltpu.VMEM((FIELDS, ROWS, COLS), f32),
-            pltpu.SemaphoreType.DMA((3,)),
+            pltpu.SemaphoreType.DMA((5,)),
         ],
         compiler_params=params(56),
         name="export",
@@ -178,11 +180,11 @@
             split_to(ref, B_WAVE + k, B_WAVE + 8 + k, strips[1])
             ref[B_STRIP_T + k] = strips[2].astype(bf16)
             split_to(ref, B_STRIP_W + k, B_STRIP_W + 2 + k, strips[3])
-        for p in range(12):
+        for p in range(6):
             ref[B_BEHIND + p] = behind[A_WAVE + p]
-    for p in range(16):
+    for p in range(8):
         far_ref[p] = out_c_ref[B_WAVE + p]
-    for p in range(4):
+    for p in range(2):
         far_ref[C_STRIP_W + p] = out_c_ref[B_STRIP_W + p]
 
 
@@ -335,12 +337,13 @@
     return [ref[2 * i].astype(f32), ref[2 * i + 1].astype(f32), beside]
 
 
-def wave_main(ref, at, low_at, i):
-    return [joined(ref, at + 2 * i + half, low_at + 2 * i + half) for half in range(2)]
-
-
-def wave_strip(ref, at, low_at, i):
-    left, right = [joined(ref, at + k, low_at + k) for k in range(2)]
+def wave_main(ref, at, i, low=None):
+    planes = [2 * i, 2 * i + 1]
+    return [ref[at + p].astype(f32) if low is None else joined(ref, at + p, at + low + p) for p in planes]
+
+
+def wave_strip(ref, at, i, low=None):
+    left, right = [ref[at + k].astype(f32) if low is None else joined(ref, at + k, at + low + k) for k in range(2)]
     return [sides(left, right, i + 1)]
 
 
@@ -444,11 +447,11 @@
         place_field(state.at[i], PAD + 2 * ROWS, own_parts(fields_ref, left_ref, right_ref, 2, i))
         pushed, parts, behind = [], [], []
         for near, main in ((near_c, state_c), (near_i, state_i)):
-            pushed.append(wave_main(near, B_WAVE + 2, B_WAVE + 10, i) + wave_strip(near, B_WAVE, B_WAVE + 8, i))
-            parts.append(wave_main(main, A_WAVE, A_WAVE + 6, i) + wave_strip(near, B_STRIP_W, B_STRIP_W + 2, i))
-            behind.append(wave_main(near, B_BEHIND, B_BEHIND + 6, i))
-        far_pushed = [wave_main(far, 2, 10, i) + wave_strip(far, 0, 8, i) for far in (far_c, far_i)]
-        far_strip = [wave_strip(far, C_STRIP_W, C_STRIP_W + 2, i) for far in (far_c, far_i)]
+            pushed.append(wave_main(near, B_WAVE + 2, i, 8) + wave_strip(near, B_WAVE, i, 8))
+            parts.append(wave_main(main, A_WAVE, i, 6) + wave_strip(near, B_STRIP_W, i, 2))
+            behind.append(wave_main(near, B_BEHIND, i))
+        far_pushed = [wave_main(far, 2, i) + wave_strip(far, 0, i) for far in (far_c, far_i)]
+        far_strip = [wave_strip(far, C_STRIP_W, i) for far in (far_c, far_i)]
         for k, slot in ((1, 0), (0, 4)):
             near_slot = (slot + 2) // 2
             place_field(forcing.at[i], PAD + near_slot * ROWS, chosen(after, pushed[k], pushed[1 - k]))
@@ -616,7 +619,8 @@
     index = jnp.concatenate([index, (gy % 2).astype(jnp.int32)[None]])
     weight = remap_weight[0].reshape(ROWS, COLS, 128)
 
-    exported, fields, land = export(section_state[0], prev_import[0], land_mask[0], smix, imix)
+    fields, land = section_state[0], land_mask[0]
+    exported = export(fields, prev_import[0], land, smix, imix)
     for interval in range(ITERS):
         last = interval == ITERS - 1
         opposite = lax.ppermute(exported, "sec", [(0, 1), (1, 0)])

time: 126 us -> 123 us (0.976)
  waiting for transfers between devices: 17 us -> 14.6 us
    ppermute x20, waiting for transfers between devices: 13.7 us -> 11.3 us  [exchanged(): return lax.ppermute(block, axis, route)]
  transfers between devices with their start and end apart: 22 -> 22, of which waited for: 11 -> 9; matrix products, arithmetic and copies ran while one was open for 1% -> 1% of each run, Pallas kernels for 6% -> 6%
where the time goes in v8:
time: 123 us; the launch traced here: 122 us
  starting transfers between devices  86.5 us (70%)
  Pallas kernels  16.2 us (13%)
  waiting for transfers between devices  14.6 us (12%)
  local copies, waits for them, and re-layouts  3.57 us (3%)
    ppermute x20, starting transfers between devices, exchanged(): return lax.ppermute(block, axis, route)  67.8 us
    ppermute x2, starting transfers between devices, local(): opposite = lax.ppermute(exported, 'sec', [(0, 1), (1, 0)])  18.6 us
    ppermute x20, waiting for transfers between devices, exchanged(): return lax.ppermute(block, axis, route)  11.3 us
    pallas_call x2, Pallas kernels, tracer_steps(): pl.pallas_call(lambda *refs: tracer_kernel(last, *refs), out_shape=(trace...  6.92 us
    pallas_call x2, Pallas kernels, wave_steps(): pl.pallas_call(lambda *refs: wave_kernel(last, *refs), out_shape=state if...  4.52 us
    ppermute x2, waiting for transfers between devices, local(): opposite = lax.ppermute(exported, 'sec', [(0, 1), (1, 0)])  3.29 us
    unnamed x19, local copies, waits for them, and re-layouts  3.08 us
    pallas_call x2, Pallas kernels, remap(): pl.pallas_call(remap_kernel, out_shape=(shaped((FIELDS, ROWS, COLS)), str...  2.56 us
  transfers between devices with their start and end apart: 22, of which 9 were waited for; matrix products, arithmetic and copies ran while one was open for 1% of the time, Pallas kernels for 6%

profile of v8, /device:TPU:6, one launch (start us, length us, event | category | flops | bytes accessed | tf_op | source)
XLA Modules:
  0.0 122.0 jit_solution(14760722042434308035)
XLA Ops:
  0.6 2.0 %export.1 = bf16[128,256]{1,0:T(8,128)(2,1)} custom-call(f32[8,8]{1,0:T(8,128)} %bitcast.29, f32[8,8]{1,0:T(8,128)} %bitcast.31, f32[8,16,256]{2,1,0:T(8,128)} %bitcast.19, f32[8,16,256]{2,1,0:T(8,128)} %bitcast.34, s32[16,256]{1,0:T(8,128)} %bitcast.25), custom_call_target="tpu_custom_call" | custom-call | tf_op jit(solution)/shard_map/export/pallas_call | solution.py:115
  2.6 10.9 %collective-permute-start = (bf16[128,256]{1,0:T(8,128)(2,1)}, bf16[128,256]{1,0:T(8,128)(2,1)S(1)}, u32[]{:S(2)}, u32[]{:S(2)}) collective-permute-start(bf16[128,256]{1,0:T(8,128)(2,1)} %export.1), channel_id=1, source_target_pairs={{0,256},{256,0},{1,257},{257,1},{2,258},{258,2},{3,259},{259,3},{4... | collective-permute-start | bytes 196616 | tf_op jit(solution)/shard_map/ppermute | solution.py:626
  13.6 0.1 stack.23
  13.7 0.5 copy-done.6
  14.2 0.1 copy.14
  14.3 0.1 sub.33
  14.5 0.5 copy-done.5
  15.0 0.1 copy.15
  15.1 0.1 reshape_squeeze.7
  15.3 0.6 copy-done.7
  16.1 0.8 collective-permute-done.opposite_ref
  16.9 5.6 %collective-permute-start.3 = (bf16[38,16,128]{2,1,0:T(8,128)(2,1)S(1)}, bf16[38,16,128]{2,1,0:T(8,128)(2,1)S(1)}, u32[]{:S(2)}, u32[]{:S(2)}) collective-permute-start(bf16[38,16,128]{2,1,0:T(8,128)(2,1)S(1)} %pack.2), channel_id=1, source_target_pairs={{8,16},{16,8},{24,32},{32,24},{40,48},{48,40},{56,64},{64,56},{72,... | collective-permute-start | bytes 466952 | tf_op jit(solution)/shard_map/ppermute | solution.py:594
  22.6 1.9 %collective-permute-start.2 = (bf16[38,16,128]{2,1,0:T(8,128)(2,1)S(1)}, bf16[38,16,128]{2,1,0:T(8,128)(2,1)S(1)}, u32[]{:S(2)}, u32[]{:S(2)}) collective-permute-start(bf16[38,16,128]{2,1,0:T(8,128)(2,1)S(1)} %pack.2), channel_id=1, source_target_pairs={{0,8},{8,0},{16,24},{24,16},{32,40},{40,32},{48,56},{56,48},{64,72... | collective-permute-start | bytes 466952 | tf_op jit(solution)/shard_map/ppermute | solution.py:594
  24.5 4.0 %collective-permute-start.4 = (bf16[128,256]{1,0:T(8,128)(2,1)S(1)}, bf16[128,256]{1,0:T(8,128)(2,1)S(1)}, u32[]{:S(2)}, u32[]{:S(2)}) collective-permute-start(bf16[128,256]{1,0:T(8,128)(2,1)S(1)} %collective-permute-done.opposite_ref), channel_id=1, source_target_pairs={{16,32},{32,16},{24,40},{40,24},{48,64},{64,48},{56,72},{72,56},{8... | collective-permute-start | bytes 196616 | tf_op jit(solution)/shard_map/ppermute | solution.py:594
  28.5 3.8 %collective-permute-start.1 = (bf16[128,256]{1,0:T(8,128)(2,1)S(1)}, bf16[128,256]{1,0:T(8,128)(2,1)S(1)}, u32[]{:S(2)}, u32[]{:S(2)}) collective-permute-start(bf16[128,256]{1,0:T(8,128)(2,1)S(1)} %collective-permute-done.opposite_ref), channel_id=1, source_target_pairs={{0,16},{16,0},{8,24},{24,8},{32,48},{48,32},{40,56},{56,40},{64,80... | collective-permute-start | bytes 196616 | tf_op jit(solution)/shard_map/ppermute | solution.py:594
  32.3 1.2 copy-done.1
  33.7 1.9 %collective-permute-done.1.far_i_ref = bf16[128,256]{1,0:T(8,128)(2,1)S(1)} collective-permute-done((bf16[128,256]{1,0:T(8,128)(2,1)S(1)}, bf16[128,256]{1,0:T(8,128)(2,1)S(1)}, u32[]{:S(2)}, u32[]{:S(2)}) %collective-permute-start.1) | collective-permute-done | bytes 65568 | tf_op jit(solution)/shard_map/ppermute | solution.py:594
  35.6 1.3 %remap.2 = (f32[8,16,256]{2,1,0:T(8,128)S(1)}, f32[4,16,128]{2,1,0:T(8,128)S(1)}, f32[4,16,128]{2,1,0:T(8,128)S(1)}, f32[8,16,256]{2,1,0:T(8,128)S(1)}) custom-call(s32[129]{0:T(256)S(1)} %pad_add_fusion.index_ref, bf16[128,256]{1,0:T(8,128)(2,1)S(1)} %collective-permute-done.1.far_i_ref, ...), custom_call_target="tpu_custom_call" | custom-call | tf_op jit(solution)/shard_map/remap/pallas_call | solution.py:273
  36.9 0.7 collective-permute-start.5
  37.5 3.9 %collective-permute-start.6 = (f32[4,16,128]{2,1,0:T(8,128)S(1)}, f32[4,16,128]{2,1,0:T(8,128)S(1)}, u32[]{:S(2)}, u32[]{:S(2)}) collective-permute-start(f32[4,16,128]{2,1,0:T(8,128)S(1)} %get-tuple-element.26), channel_id=1, source_target_pairs={{0,1},{1,0},{2,3},{3,2},{4,5},{5,4},{6,7},{7,6},{8,9},{9,8},{10,11... | collective-permute-start | bytes 98312 | tf_op jit(solution)/shard_map/ppermute | solution.py:594
  41.5 0.8 collective-permute-done.6.chip_ref
  42.3 0.1 pack_forcing.2
  42.4 5.5 %collective-permute-start.8 = (bf16[40,16,128]{2,1,0:T(8,128)(2,1)S(1)}, bf16[40,16,128]{2,1,0:T(8,128)(2,1)S(1)}, u32[]{:S(2)}, u32[]{:S(2)}) collective-permute-start(bf16[40,16,128]{2,1,0:T(8,128)(2,1)S(1)} %get-tuple-element.28), channel_id=1, source_target_pairs={{8,16},{16,8},{24,32},{32,24},{40,48},{48,40},{56,64},{64,56},{72,... | collective-permute-start | bytes 491528 | tf_op jit(solution)/shard_map/ppermute | solution.py:594
  47.9 1.9 %collective-permute-start.9 = (bf16[40,16,128]{2,1,0:T(8,128)(2,1)S(1)}, bf16[40,16,128]{2,1,0:T(8,128)(2,1)S(1)}, u32[]{:S(2)}, u32[]{:S(2)}) collective-permute-start(bf16[40,16,128]{2,1,0:T(8,128)(2,1)S(1)} %get-tuple-element.31), channel_id=1, source_target_pairs={{0,8},{8,0},{16,24},{24,16},{32,40},{40,32},{48,56},{56,48},{64,72... | collective-permute-start | bytes 491528 | tf_op jit(solution)/shard_map/ppermute | solution.py:594
  49.9 3.9 %collective-permute-start.10 = (bf16[10,16,128]{2,1,0:T(8,128)(2,1)S(1)}, bf16[10,16,128]{2,1,0:T(8,128)(2,1)S(1)}, u32[]{:S(2)}, u32[]{:S(2)}) collective-permute-start(bf16[10,16,128]{2,1,0:T(8,128)(2,1)S(1)} %get-tuple-element.27), channel_id=1, source_target_pairs={{16,32},{32,16},{24,40},{40,24},{48,64},{64,48},{56,72},{72,56},{8... | collective-permute-start | bytes 122888 | tf_op jit(solution)/shard_map/ppermute | solution.py:594
  53.8 2.7 %collective-permute-start.7 = (bf16[10,16,128]{2,1,0:T(8,128)(2,1)S(1)}, bf16[10,16,128]{2,1,0:T(8,128)(2,1)S(1)}, u32[]{:S(2)}, u32[]{:S(2)}) collective-permute-start(bf16[10,16,128]{2,1,0:T(8,128)(2,1)S(1)} %get-tuple-element.27), channel_id=1, source_target_pairs={{0,16},{16,0},{8,24},{24,8},{32,48},{48,32},{40,56},{56,40},{64,80... | collective-permute-start | bytes 122888 | tf_op jit(solution)/shard_map/ppermute | solution.py:594
  56.5 3.3 %tracer_steps.2.refs_13_ = f32[5,16,256]{2,1,0:T(8,128)S(1)} custom-call(f32[1,17]{1,0:T(1,128)S(1)} %maximum_bitcast_fusion.config_ref.refs_0_, bf16[40,16,128]{2,1,0:T(8,128)(2,1)S(1)} %collective-permute-done.8.refs_1_.refs_4_, f32[8,16,256]{2,1,0:T(8,128)S(1)} %get-tuple-element.24.forcing_ref.refs_2_.refs_5_, ...), custom_call_target="tpu_custom_call" | custom-call | flops 10000000 | bytes 4000000 | tf_op jit(solution)/shard_map/tracer_steps/pallas_call | solution.py:415
  59.8 1.1 collective-permute-done.7.refs_3_
  60.9 2.0 %wave_steps.1 = (f32[8,16,256]{2,1,0:T(8,128)S(1)}, bf16[128,256]{1,0:T(8,128)(2,1)S(1)}) custom-call(f32[1,17]{1,0:T(1,128)S(1)} %maximum_bitcast_fusion.config_ref.refs_0_, f32[8,8]{1,0:T(8,128)S(1)} %bitcast.30, f32[8,8]{1,0:T(8,128)S(1)} %bitcast.32, bf16[10,16,128]{2,1,0:T(8,128)(2,1)S(1)} %collective-permute-done.7.refs_3_, ...), custom_call_target="tpu_custom_call" | custom-call | tf_op jit(solution)/shard_map/wave_steps/pallas_call | solution.py:577
  62.9 7.7 %collective-permute-start.11 = (bf16[128,256]{1,0:T(8,128)(2,1)S(1)}, bf16[128,256]{1,0:T(8,128)(2,1)S(1)}, u32[]{:S(2)}, u32[]{:S(2)}) collective-permute-start(bf16[128,256]{1,0:T(8,128)(2,1)S(1)} %get-tuple-element.33), channel_id=1, source_target_pairs={{0,256},{256,0},{1,257},{257,1},{2,258},{258,2},{3,259},{259,3},{4... | collective-permute-start | bytes 196616 | tf_op jit(solution)/shard_map/ppermute | solution.py:626
  70.6 2.5 %collective-permute-done.11.opposite_ref = bf16[128,256]{1,0:T(8,128)(2,1)S(1)} collective-permute-done((bf16[128,256]{1,0:T(8,128)(2,1)S(1)}, bf16[128,256]{1,0:T(8,128)(2,1)S(1)}, u32[]{:S(2)}, u32[]{:S(2)}) %collective-permute-start.11) | collective-permute-done | bytes 65568 | tf_op jit(solution)/shard_map/ppermute | solution.py:626
  73.1 5.2 %collective-permute-start.14 = (bf16[38,16,128]{2,1,0:T(8,128)(2,1)S(1)}, bf16[38,16,128]{2,1,0:T(8,128)(2,1)S(1)}, u32[]{:S(2)}, u32[]{:S(2)}) collective-permute-start(bf16[38,16,128]{2,1,0:T(8,128)(2,1)S(1)} %pack.3), channel_id=1, source_target_pairs={{8,16},{16,8},{24,32},{32,24},{40,48},{48,40},{56,64},{64,56},{72,... | collective-permute-start | bytes 466952 | tf_op jit(solution)/shard_map/ppermute | solution.py:594
  78.3 1.9 %collective-permute-start.13 = (bf16[38,16,128]{2,1,0:T(8,128)(2,1)S(1)}, bf16[38,16,128]{2,1,0:T(8,128)(2,1)S(1)}, u32[]{:S(2)}, u32[]{:S(2)}) collective-permute-start(bf16[38,16,128]{2,1,0:T(8,128)(2,1)S(1)} %pack.3), channel_id=1, source_target_pairs={{0,8},{8,0},{16,24},{24,16},{32,40},{40,32},{48,56},{56,48},{64,72... | collective-permute-start | bytes 466952 | tf_op jit(solution)/shard_map/ppermute | solution.py:594
  80.2 4.2 %collective-permute-start.15 = (bf16[128,256]{1,0:T(8,128)(2,1)S(1)}, bf16[128,256]{1,0:T(8,128)(2,1)S(1)}, u32[]{:S(2)}, u32[]{:S(2)}) collective-permute-start(bf16[128,256]{1,0:T(8,128)(2,1)S(1)} %collective-permute-done.11.opposite_ref), channel_id=1, source_target_pairs={{16,32},{32,16},{24,40},{40,24},{48,64},{64,48},{56,72},{72,56},{8... | collective-permute-start | bytes 196616 | tf_op jit(solution)/shard_map/ppermute | solution.py:594
  84.5 2.4 %collective-permute-start.12 = (bf16[128,256]{1,0:T(8,128)(2,1)S(1)}, bf16[128,256]{1,0:T(8,128)(2,1)S(1)}, u32[]{:S(2)}, u32[]{:S(2)}) collective-permute-start(bf16[128,256]{1,0:T(8,128)(2,1)S(1)} %collective-permute-done.11.opposite_ref), channel_id=1, source_target_pairs={{0,16},{16,0},{8,24},{24,8},{32,48},{48,32},{40,56},{56,40},{64,80... | collective-permute-start | bytes 196616 | tf_op jit(solution)/shard_map/ppermute | solution.py:594
  86.9 2.5 %collective-permute-done.15.far_c_ref = bf16[128,256]{1,0:T(8,128)(2,1)S(1)} collective-permute-done((bf16[128,256]{1,0:T(8,128)(2,1)S(1)}, bf16[128,256]{1,0:T(8,128)(2,1)S(1)}, u32[]{:S(2)}, u32[]{:S(2)}) %collective-permute-start.15) | collective-permute-done | bytes 65568 | tf_op jit(solution)/shard_map/ppermute | solution.py:594
  89.4 2.8 %collective-permute-done.12.far_i_ref = bf16[128,256]{1,0:T(8,128)(2,1)S(1)} collective-permute-done((bf16[128,256]{1,0:T(8,128)(2,1)S(1)}, bf16[128,256]{1,0:T(8,128)(2,1)S(1)}, u32[]{:S(2)}, u32[]{:S(2)}) %collective-permute-start.12) | collective-permute-done | bytes 65568 | tf_op jit(solution)/shard_map/ppermute | solution.py:594
  92.2 1.3 %remap.3 = (f32[8,16,256]{2,1,0:T(8,128)S(1)}, f32[4,16,128]{2,1,0:T(8,128)S(1)}, f32[4,16,128]{2,1,0:T(8,128)S(1)}, f32[8,16,256]{2,1,0:T(8,128)S(1)}) custom-call(s32[129]{0:T(256)S(1)} %pad_add_fusion.index_ref, bf16[128,256]{1,0:T(8,128)(2,1)S(1)} %collective-permute-done.12.far_i_ref, ...), custom_call_target="tpu_custom_call" | custom-call | tf_op jit(solution)/shard_map/remap/pallas_call | solution.py:273
  93.5 0.7 collective-permute-start.16
  94.2 6.2 %collective-permute-start.17 = (f32[4,16,128]{2,1,0:T(8,128)S(1)}, f32[4,16,128]{2,1,0:T(8,128)S(1)}, u32[]{:S(2)}, u32[]{:S(2)}) collective-permute-start(f32[4,16,128]{2,1,0:T(8,128)S(1)} %get-tuple-element.37), channel_id=1, source_target_pairs={{0,1},{1,0},{2,3},{3,2},{4,5},{5,4},{6,7},{7,6},{8,9},{9,8},{10,11... | collective-permute-start | bytes 98312 | tf_op jit(solution)/shard_map/ppermute | solution.py:594
  100.4 0.8 collective-permute-done.17.chip_ref
  101.3 4.6 %collective-permute-start.19 = (bf16[40,16,128]{2,1,0:T(8,128)(2,1)S(1)}, bf16[40,16,128]{2,1,0:T(8,128)(2,1)S(1)}, u32[]{:S(2)}, u32[]{:S(2)}) collective-permute-start(bf16[40,16,128]{2,1,0:T(8,128)(2,1)S(1)} %get-tuple-element.39), channel_id=1, source_target_pairs={{8,16},{16,8},{24,32},{32,24},{40,48},{48,40},{56,64},{64,56},{72,... | collective-permute-start | bytes 491528 | tf_op jit(solution)/shard_map/ppermute | solution.py:594
  106.0 1.9 %collective-permute-start.20 = (bf16[40,16,128]{2,1,0:T(8,128)(2,1)S(1)}, bf16[40,16,128]{2,1,0:T(8,128)(2,1)S(1)}, u32[]{:S(2)}, u32[]{:S(2)}) collective-permute-start(bf16[40,16,128]{2,1,0:T(8,128)(2,1)S(1)} %get-tuple-element.42), channel_id=1, source_target_pairs={{0,8},{8,0},{16,24},{24,16},{32,40},{40,32},{48,56},{56,48},{64,72... | collective-permute-start | bytes 491528 | tf_op jit(solution)/shard_map/ppermute | solution.py:594
  107.9 4.8 %collective-permute-start.21 = (bf16[10,16,128]{2,1,0:T(8,128)(2,1)S(1)}, bf16[10,16,128]{2,1,0:T(8,128)(2,1)S(1)}, u32[]{:S(2)}, u32[]{:S(2)}) collective-permute-start(bf16[10,16,128]{2,1,0:T(8,128)(2,1)S(1)} %get-tuple-element.38), channel_id=1, source_target_pairs={{16,32},{32,16},{24,40},{40,24},{48,64},{64,48},{56,72},{72,56},{8... | collective-permute-start | bytes 122888 | tf_op jit(solution)/shard_map/ppermute | solution.py:594
  112.7 1.9 %collective-permute-start.18 = (bf16[10,16,128]{2,1,0:T(8,128)(2,1)S(1)}, bf16[10,16,128]{2,1,0:T(8,128)(2,1)S(1)}, u32[]{:S(2)}, u32[]{:S(2)}) collective-permute-start(bf16[10,16,128]{2,1,0:T(8,128)(2,1)S(1)} %get-tuple-element.38), channel_id=1, source_target_pairs={{0,16},{16,0},{8,24},{24,8},{32,48},{48,32},{40,56},{56,40},{64,80... | collective-permute-start | bytes 122888 | tf_op jit(solution)/shard_map/ppermute | solution.py:594
  114.6 3.6 %tracer_steps.3 = (f32[5,16,256]{2,1,0:T(8,128)S(1)}, f32[8,16,256]{2,1,0:T(8,128)}) custom-call(f32[1,17]{1,0:T(1,128)S(1)} %maximum_bitcast_fusion.config_ref.refs_0_, bf16[40,16,128]{2,1,0:T(8,128)(2,1)S(1)} %collective-permute-done.19.refs_1_.refs_2_, f32[8,16,256]{2,1,0:T(8,128)S(1)} %get-tuple-element.35.forcing_ref.refs_2_.refs_3_, ...), custom_call_target="tpu_custom_call" | custom-call | flops 10000000 | bytes 4000000 | tf_op jit(solution)/shard_map/tracer_steps/pallas_call | solution.py:415
  118.3 1.2 %collective-permute-done.18.refs_1_ = bf16[10,16,128]{2,1,0:T(8,128)(2,1)S(1)} collective-permute-done((bf16[10,16,128]{2,1,0:T(8,128)(2,1)S(1)}, bf16[10,16,128]{2,1,0:T(8,128)(2,1)S(1)}, u32[]{:S(2)}, u32[]{:S(2)}) %collective-permute-start.18) | collective-permute-done | bytes 40992 | tf_op jit(solution)/shard_map/ppermute | solution.py:594
  119.5 2.5 %wave_steps_last.1 = f32[8,16,256]{2,1,0:T(8,128)} custom-call(f32[1,17]{1,0:T(1,128)S(1)} %maximum_bitcast_fusion.config_ref.refs_0_, bf16[10,16,128]{2,1,0:T(8,128)(2,1)S(1)} %collective-permute-done.18.refs_1_, bf16[40,16,128]{2,1,0:T(8,128)(2,1)S(1)} %collective-permute-done.19.refs_1_.refs_2_, ...), custom_call_target="tpu_custom_call" | custom-call | tf_op jit(solution)/shard_map/wave_steps_last/pallas_call | solution.py:577
  (36 shorter events, 0.4 us)
Async XLA Ops:
  2.6 14.3 %collective-permute-start = (bf16[128,256]{1,0:T(8,128)(2,1)}, bf16[128,256]{1,0:T(8,128)(2,1)S(1)}, u32[]{:S(2)}, u32[]{:S(2)}) collective-permute-start(bf16[128,256]{1,0:T(8,128)(2,1)} %export.1), channel_id=1, source_target_pairs={{0,256},{256,0},{1,257},{257,1},{2,258},{258,2},{3,259},{259,3},{4... | collective-permute-start | bytes 196616 | tf_op jit(solution)/shard_map/ppermute | solution.py:626
  13.5 0.7 copy-start.6
  13.5 3.3 %copy-start = (f32[1,8,16,256]{3,2,1,0:T(8,128)S(1)}, f32[1,8,16,256]{3,2,1,0:T(8,128)}, u32[]{:S(2)}) copy-start(f32[1,8,16,256]{3,2,1,0:T(8,128)} %param.10) | copy-start | bytes 393220
  14.3 0.7 copy-start.5
  15.3 0.7 copy-start.7
  15.3 0.7 copy-start.8
  16.9 15.4 %collective-permute-start.3 = (bf16[38,16,128]{2,1,0:T(8,128)(2,1)S(1)}, bf16[38,16,128]{2,1,0:T(8,128)(2,1)S(1)}, u32[]{:S(2)}, u32[]{:S(2)}) collective-permute-start(bf16[38,16,128]{2,1,0:T(8,128)(2,1)S(1)} %pack.2), channel_id=1, source_target_pairs={{8,16},{16,8},{24,32},{32,24},{40,48},{48,40},{56,64},{64,56},{72,... | collective-permute-start | bytes 466952 | tf_op jit(solution)/shard_map/ppermute | solution.py:594
  22.6 9.8 %collective-permute-start.2 = (bf16[38,16,128]{2,1,0:T(8,128)(2,1)S(1)}, bf16[38,16,128]{2,1,0:T(8,128)(2,1)S(1)}, u32[]{:S(2)}, u32[]{:S(2)}) collective-permute-start(bf16[38,16,128]{2,1,0:T(8,128)(2,1)S(1)} %pack.2), channel_id=1, source_target_pairs={{0,8},{8,0},{16,24},{24,16},{32,40},{40,32},{48,56},{56,48},{64,72... | collective-permute-start | bytes 466952 | tf_op jit(solution)/shard_map/ppermute | solution.py:594
  24.5 9.2 %collective-permute-start.4 = (bf16[128,256]{1,0:T(8,128)(2,1)S(1)}, bf16[128,256]{1,0:T(8,128)(2,1)S(1)}, u32[]{:S(2)}, u32[]{:S(2)}) collective-permute-start(bf16[128,256]{1,0:T(8,128)(2,1)S(1)} %collective-permute-done.opposite_ref), channel_id=1, source_target_pairs={{16,32},{32,16},{24,40},{40,24},{48,64},{64,48},{56,72},{72,56},{8... | collective-permute-start | bytes 196616 | tf_op jit(solution)/shard_map/ppermute | solution.py:594
  28.5 7.1 %collective-permute-start.1 = (bf16[128,256]{1,0:T(8,128)(2,1)S(1)}, bf16[128,256]{1,0:T(8,128)(2,1)S(1)}, u32[]{:S(2)}, u32[]{:S(2)}) collective-permute-start(bf16[128,256]{1,0:T(8,128)(2,1)S(1)} %collective-permute-done.opposite_ref), channel_id=1, source_target_pairs={{0,16},{16,0},{8,24},{24,8},{32,48},{48,32},{40,56},{56,40},{64,80... | collective-permute-start | bytes 196616 | tf_op jit(solution)/shard_map/ppermute | solution.py:594
  32.3 1.2 %copy-start.1 = (bf16[1,16,4,64,128]{4,3,2,1,0:T(8,128)(2,1)S(1)}, bf16[1,16,4,64,128]{4,3,2,1,0:T(8,128)(2,1)}, u32[]{:S(2)}) copy-start(bf16[1,16,4,64,128]{4,3,2,1,0:T(8,128)(2,1)} %param.19) | copy-start | bytes 3145732
  33.6 2.0 %copy-start.2 = (s32[1,16,256]{2,1,0:T(8,128)S(1)}, s32[1,16,256]{2,1,0:T(8,128)}, u32[]{:S(2)}) copy-start(s32[1,16,256]{2,1,0:T(8,128)} %param.12) | copy-start | bytes 49156
  36.9 4.6 %collective-permute-start.5 = (f32[4,16,128]{2,1,0:T(8,128)S(1)}, f32[4,16,128]{2,1,0:T(8,128)S(1)}, u32[]{:S(2)}, u32[]{:S(2)}) collective-permute-start(f32[4,16,128]{2,1,0:T(8,128)S(1)} %get-tuple-element.25), channel_id=1, source_target_pairs={{1,2},{2,1},{3,4},{4,3},{5,6},{6,5},{9,10},{10,9},{11,12},{12,11},... | collective-permute-start | bytes 98312 | tf_op jit(solution)/shard_map/ppermute | solution.py:594
  37.5 4.8 %collective-permute-start.6 = (f32[4,16,128]{2,1,0:T(8,128)S(1)}, f32[4,16,128]{2,1,0:T(8,128)S(1)}, u32[]{:S(2)}, u32[]{:S(2)}) collective-permute-start(f32[4,16,128]{2,1,0:T(8,128)S(1)} %get-tuple-element.26), channel_id=1, source_target_pairs={{0,1},{1,0},{2,3},{3,2},{4,5},{5,4},{6,7},{7,6},{8,9},{9,8},{10,11... | collective-permute-start | bytes 98312 | tf_op jit(solution)/shard_map/ppermute | solution.py:594
  42.4 14.0 %collective-permute-start.8 = (bf16[40,16,128]{2,1,0:T(8,128)(2,1)S(1)}, bf16[40,16,128]{2,1,0:T(8,128)(2,1)S(1)}, u32[]{:S(2)}, u32[]{:S(2)}) collective-permute-start(bf16[40,16,128]{2,1,0:T(8,128)(2,1)S(1)} %get-tuple-element.28), channel_id=1, source_target_pairs={{8,16},{16,8},{24,32},{32,24},{40,48},{48,40},{56,64},{64,56},{72,... | collective-permute-start | bytes 491528 | tf_op jit(solution)/shard_map/ppermute | solution.py:594
  47.9 8.5 %collective-permute-start.9 = (bf16[40,16,128]{2,1,0:T(8,128)(2,1)S(1)}, bf16[40,16,128]{2,1,0:T(8,128)(2,1)S(1)}, u32[]{:S(2)}, u32[]{:S(2)}) collective-permute-start(bf16[40,16,128]{2,1,0:T(8,128)(2,1)S(1)} %get-tuple-element.31), channel_id=1, source_target_pairs={{0,8},{8,0},{16,24},{24,16},{32,40},{40,32},{48,56},{56,48},{64,72... | collective-permute-start | bytes 491528 | tf_op jit(solution)/shard_map/ppermute | solution.py:594
  49.9 9.9 %collective-permute-start.10 = (bf16[10,16,128]{2,1,0:T(8,128)(2,1)S(1)}, bf16[10,16,128]{2,1,0:T(8,128)(2,1)S(1)}, u32[]{:S(2)}, u32[]{:S(2)}) collective-permute-start(bf16[10,16,128]{2,1,0:T(8,128)(2,1)S(1)} %get-tuple-element.27), channel_id=1, source_target_pairs={{16,32},{32,16},{24,40},{40,24},{48,64},{64,48},{56,72},{72,56},{8... | collective-permute-start | bytes 122888 | tf_op jit(solution)/shard_map/ppermute | solution.py:594
  53.8 7.1 %collective-permute-start.7 = (bf16[10,16,128]{2,1,0:T(8,128)(2,1)S(1)}, bf16[10,16,128]{2,1,0:T(8,128)(2,1)S(1)}, u32[]{:S(2)}, u32[]{:S(2)}) collective-permute-start(bf16[10,16,128]{2,1,0:T(8,128)(2,1)S(1)} %get-tuple-element.27), channel_id=1, source_target_pairs={{0,16},{16,0},{8,24},{24,8},{32,48},{48,32},{40,56},{56,40},{64,80... | collective-permute-start | bytes 122888 | tf_op jit(solution)/shard_map/ppermute | solution.py:594
  56.5 4.4 %copy-start.3 = (f32[1,8,8]{2,1,0:T(8,128)S(1)}, f32[1,8,8]{2,1,0:T(8,128)}, u32[]{:S(2)}) copy-start(f32[1,8,8]{2,1,0:T(8,128)} %param.13) | copy-start | bytes 772
  56.5 4.4 %copy-start.4 = (f32[1,8,8]{2,1,0:T(8,128)S(1)}, f32[1,8,8]{2,1,0:T(8,128)}, u32[]{:S(2)}) copy-start(f32[1,8,8]{2,1,0:T(8,128)} %param.14) | copy-start | bytes 772
  62.9 10.2 %collective-permute-start.11 = (bf16[128,256]{1,0:T(8,128)(2,1)S(1)}, bf16[128,256]{1,0:T(8,128)(2,1)S(1)}, u32[]{:S(2)}, u32[]{:S(2)}) collective-permute-start(bf16[128,256]{1,0:T(8,128)(2,1)S(1)} %get-tuple-element.33), channel_id=1, source_target_pairs={{0,256},{256,0},{1,257},{257,1},{2,258},{258,2},{3,259},{259,3},{4... | collective-permute-start | bytes 196616 | tf_op jit(solution)/shard_map/ppermute | solution.py:626
  73.1 19.1 %collective-permute-start.14 = (bf16[38,16,128]{2,1,0:T(8,128)(2,1)S(1)}, bf16[38,16,128]{2,1,0:T(8,128)(2,1)S(1)}, u32[]{:S(2)}, u32[]{:S(2)}) collective-permute-start(bf16[38,16,128]{2,1,0:T(8,128)(2,1)S(1)} %pack.3), channel_id=1, source_target_pairs={{8,16},{16,8},{24,32},{32,24},{40,48},{48,40},{56,64},{64,56},{72,... | collective-permute-start | bytes 466952 | tf_op jit(solution)/shard_map/ppermute | solution.py:594
  78.3 13.9 %collective-permute-start.13 = (bf16[38,16,128]{2,1,0:T(8,128)(2,1)S(1)}, bf16[38,16,128]{2,1,0:T(8,128)(2,1)S(1)}, u32[]{:S(2)}, u32[]{:S(2)}) collective-permute-start(bf16[38,16,128]{2,1,0:T(8,128)(2,1)S(1)} %pack.3), channel_id=1, source_target_pairs={{0,8},{8,0},{16,24},{24,16},{32,40},{40,32},{48,56},{56,48},{64,72... | collective-permute-start | bytes 466952 | tf_op jit(solution)/shard_map/ppermute | solution.py:594
  80.2 9.2 %collective-permute-start.15 = (bf16[128,256]{1,0:T(8,128)(2,1)S(1)}, bf16[128,256]{1,0:T(8,128)(2,1)S(1)}, u32[]{:S(2)}, u32[]{:S(2)}) collective-permute-start(bf16[128,256]{1,0:T(8,128)(2,1)S(1)} %collective-permute-done.11.opposite_ref), channel_id=1, source_target_pairs={{16,32},{32,16},{24,40},{40,24},{48,64},{64,48},{56,72},{72,56},{8... | collective-permute-start | bytes 196616 | tf_op jit(solution)/shard_map/ppermute | solution.py:594
  84.5 7.8 %collective-permute-start.12 = (bf16[128,256]{1,0:T(8,128)(2,1)S(1)}, bf16[128,256]{1,0:T(8,128)(2,1)S(1)}, u32[]{:S(2)}, u32[]{:S(2)}) collective-permute-start(bf16[128,256]{1,0:T(8,128)(2,1)S(1)} %collective-permute-done.11.opposite_ref), channel_id=1, source_target_pairs={{0,16},{16,0},{8,24},{24,8},{32,48},{48,32},{40,56},{56,40},{64,80... | collective-permute-start | bytes 196616 | tf_op jit(solution)/shard_map/ppermute | solution.py:594
  93.5 6.9 %collective-permute-start.16 = (f32[4,16,128]{2,1,0:T(8,128)S(1)}, f32[4,16,128]{2,1,0:T(8,128)S(1)}, u32[]{:S(2)}, u32[]{:S(2)}) collective-permute-start(f32[4,16,128]{2,1,0:T(8,128)S(1)} %get-tuple-element.36), channel_id=1, source_target_pairs={{1,2},{2,1},{3,4},{4,3},{5,6},{6,5},{9,10},{10,9},{11,12},{12,11},... | collective-permute-start | bytes 98312 | tf_op jit(solution)/shard_map/ppermute | solution.py:594
  94.2 7.0 %collective-permute-start.17 = (f32[4,16,128]{2,1,0:T(8,128)S(1)}, f32[4,16,128]{2,1,0:T(8,128)S(1)}, u32[]{:S(2)}, u32[]{:S(2)}) collective-permute-start(f32[4,16,128]{2,1,0:T(8,128)S(1)} %get-tuple-element.37), channel_id=1, source_target_pairs={{0,1},{1,0},{2,3},{3,2},{4,5},{5,4},{6,7},{7,6},{8,9},{9,8},{10,11... | collective-permute-start | bytes 98312 | tf_op jit(solution)/shard_map/ppermute | solution.py:594
  101.3 13.3 %collective-permute-start.19 = (bf16[40,16,128]{2,1,0:T(8,128)(2,1)S(1)}, bf16[40,16,128]{2,1,0:T(8,128)(2,1)S(1)}, u32[]{:S(2)}, u32[]{:S(2)}) collective-permute-start(bf16[40,16,128]{2,1,0:T(8,128)(2,1)S(1)} %get-tuple-element.39), channel_id=1, source_target_pairs={{8,16},{16,8},{24,32},{32,24},{40,48},{48,40},{56,64},{64,56},{72,... | collective-permute-start | bytes 491528 | tf_op jit(solution)/shard_map/ppermute | solution.py:594
  106.0 8.7 %collective-permute-start.20 = (bf16[40,16,128]{2,1,0:T(8,128)(2,1)S(1)}, bf16[40,16,128]{2,1,0:T(8,128)(2,1)S(1)}, u32[]{:S(2)}, u32[]{:S(2)}) collective-permute-start(bf16[40,16,128]{2,1,0:T(8,128)(2,1)S(1)} %get-tuple-element.42), channel_id=1, source_target_pairs={{0,8},{8,0},{16,24},{24,16},{32,40},{40,32},{48,56},{56,48},{64,72... | collective-permute-start | bytes 491528 | tf_op jit(solution)/shard_map/ppermute | solution.py:594
  107.9 10.4 %collective-permute-start.21 = (bf16[10,16,128]{2,1,0:T(8,128)(2,1)S(1)}, bf16[10,16,128]{2,1,0:T(8,128)(2,1)S(1)}, u32[]{:S(2)}, u32[]{:S(2)}) collective-permute-start(bf16[10,16,128]{2,1,0:T(8,128)(2,1)S(1)} %get-tuple-element.38), channel_id=1, source_target_pairs={{16,32},{32,16},{24,40},{40,24},{48,64},{64,48},{56,72},{72,56},{8... | collective-permute-start | bytes 122888 | tf_op jit(solution)/shard_map/ppermute | solution.py:594
  112.7 6.8 %collective-permute-start.18 = (bf16[10,16,128]{2,1,0:T(8,128)(2,1)S(1)}, bf16[10,16,128]{2,1,0:T(8,128)(2,1)S(1)}, u32[]{:S(2)}, u32[]{:S(2)}) collective-permute-start(bf16[10,16,128]{2,1,0:T(8,128)(2,1)S(1)} %get-tuple-element.38), channel_id=1, source_target_pairs={{0,16},{16,0},{8,24},{24,8},{32,48},{48,32},{40,56},{56,40},{64,80... | collective-permute-start | bytes 122888 | tf_op jit(solution)/shard_map/ppermute | solution.py:594

commit v9 on v8

--- a/solution.py
+++ b/solution.py
@@ -146,23 +146,23 @@
             split_to(ref, wave_at + 2 * i + half, wave_low_at + 2 * i + half, fields_ref[i, :, cols])
 
 
-def pack_kernel(opposite_ref, fields_ref, index_ref, config_ref, near_ref):
-    del index_ref, config_ref
+def pack_kernel(opposite_ref, fields_ref, index_ref, config_ref, mixes_ref, near_ref):
+    del index_ref, config_ref, mixes_ref
     write_main(near_ref, 0, A_WAVE, A_WAVE + 6, fields_ref)
     for half in range(2):
         for i in range(TURNED // 16):
             near_ref[A_EXPORT + half * 8 + i] = opposite_ref[16 * i : 16 * i + 16, half * LANES : (half + 1) * LANES]
 
 
-def pack(opposite, fields, index, config):
+def pack(opposite, fields, index, config, mixes):
     return pl.pallas_call(
         pack_kernel,
         out_shape=shaped((A_PLANES, ROWS, LANES), bf16),
-        in_specs=[VMEM] * 2 + [HBM] * 2,
+        in_specs=[VMEM] * 2 + [HBM] * 3,
         out_specs=VMEM,
         compiler_params=params(),
         name="pack",
-    )(opposite, fields, index, config)
+    )(opposite, fields, index, config, mixes)
 
 
 def pack_forcing_kernel(
@@ -217,9 +217,11 @@
 
 
 def remap_kernel(
-    index_ref, far_i_ref, near_i_ref, opposite_ref, near_c_ref, far_c_ref, weight_ref, land_ref, fields_ref,
-    forcing_ref, chip_ref, outer_ref, import_ref, table, turned,
+    index_hbm, far_c_ref, near_c_ref, opposite_ref, near_i_ref, far_i_ref, weight_ref, land_ref, fields_ref,
+    forcing_ref, chip_ref, outer_ref, import_ref, table, turned, index_ref, sem,
 ):
+    copy = pltpu.make_async_copy(index_hbm, index_ref, sem)
+    copy.start()
     half_count = 5 * ROWS * 2
     windows = [far_c_ref, near_c_ref, opposite_ref, near_i_ref, far_i_ref]
     for w, ref in enumerate(windows):
@@ -238,6 +240,7 @@
     lane8 = lax.broadcasted_iota(jnp.int32, (8, LANES), 1)
     low_half = lane8 < 64
     ones = jnp.ones((8, LANES), f32)
+    copy.wait()
     for x in range(ROWS):
         pieces = []
         for seg in range(4):
@@ -273,11 +276,13 @@
     return pl.pallas_call(
         remap_kernel,
         out_shape=(shaped((FIELDS, ROWS, COLS)), strips, strips, shaped((FIELDS, ROWS, COLS))),
-        in_specs=[SMEM] + [VMEM] * 8,
+        in_specs=[HBM] + [VMEM] * 8,
         out_specs=(VMEM,) * 4,
         scratch_shapes=[
             pltpu.VMEM((2 * 5 * ROWS * 2, FIELDS, LANES), f32),
             pltpu.VMEM((2, TURNED, LANES), f32),
+            pltpu.SMEM((2 * TURNED,), jnp.int32),
+            pltpu.SemaphoreType.DMA,
         ],
         compiler_params=params(),
         name="remap",
@@ -352,10 +357,9 @@
     state_c_ref, fields_ref, state_i_ref, *refs
 ):
     if last:
-        received_ref, out_ref, received_out, state, forcing, coef = refs
+        received_ref, received_out, *refs = refs
         received_out[...] = received_ref[...]
-    else:
-        out_ref, state, forcing, coef = refs
+    out_ref, wave_state, wave_forcing, wave_coef, state, forcing, coef = refs
     after = spread(config_ref, AFTER_NEAR, ROWS) > 0.5
     for i in range(TRACERS):
         pushed, parts = [], []
@@ -368,6 +372,25 @@
         place_field(state.at[0, i], PAD, chosen(after, parts[1], parts[0]))
         place_field(state.at[0, i], PAD + ROWS, own_parts(fields_ref, left_ref, right_ref, 2, WAVES + i))
         place_field(state.at[0, i], PAD + 2 * ROWS, chosen(after, parts[0], parts[1]))
+    for i in range(WAVES):
+        pushed, parts = [], []
+        for near, main in ((near_c_ref, state_c_ref), (near_i_ref, state_i_ref)):
+            pushed.append(wave_main(near, B_WAVE + 2, i, 8) + wave_strip(near, B_WAVE, i, 8))
+            parts.append(wave_main(main, A_WAVE, i, 6) + wave_strip(near, B_STRIP_W, i, 2))
+        place_field(wave_forcing.at[i], ROWS, own_parts(forcing_ref, left_ref, right_ref, 0, i))
+        place_field(wave_state.at[i], ROWS, own_parts(fields_ref, left_ref, right_ref, 2, i))
+        for k, slot in ((1, 0), (0, 2)):
+            place_field(wave_forcing.at[i], slot * ROWS, chosen(after, pushed[k], pushed[1 - k]))
+            place_field(wave_state.at[i], slot * ROWS, chosen(after, parts[k], parts[1 - k]))
+    half_a = 0.5 * config_ref[:, WAVE_SPEED : WAVE_SPEED + 1]
+    half_b = 0.5 * config_ref[:, WAVE_SPEED + 1 : WAVE_SPEED + 2]
+    first_row, rows = -2 * ROWS, 5 * ROWS
+    for j in range(3):
+        wave_coef[0, j] = inside_tile(config_ref, first_row, rows, j) * half_a
+        wave_coef[1, j] = inside_tile(config_ref, first_row + 1, rows, j) * half_b
+        wave_coef[2, j] = inside_tile(config_ref, first_row - 1, rows, j) * half_b
+        wave_coef[3, j] = inside_tile(config_ref, first_row, rows, j, 1) * half_b
+        wave_coef[4, j] = inside_tile(config_ref, first_row, rows, j, -1) * half_b
     height = 3 * ROWS
     for k in range(2):
         for i in range(TRACERS):
@@ -411,12 +434,15 @@
 
 
 def tracer_steps(last, config, operands):
-    tracers, received = shaped((TRACERS, ROWS, COLS)), shaped((FIELDS, ROWS, COLS))
+    inner = shaped((WAVES, 3, 3 * ROWS, LANES))
+    outs = [shaped((TRACERS, ROWS, COLS)), inner, inner, shaped((5, 3, 5 * ROWS, LANES))]
+    if last:
+        outs = [shaped((FIELDS, ROWS, COLS))] + outs
     return pl.pallas_call(
         lambda *refs: tracer_kernel(last, *refs),
-        out_shape=(tracers, received) if last else tracers,
+        out_shape=tuple(outs),
         in_specs=[VMEM] * (1 + len(operands)),
-        out_specs=(VMEM, VMEM) if last else VMEM,
+        out_specs=(VMEM,) * len(outs),
         scratch_shapes=[
             pltpu.VMEM((2, TRACERS, 3, 3 * ROWS + 2 * PAD, LANES), f32),
             pltpu.VMEM((TRACERS, 3, 3 * ROWS, LANES), f32),
@@ -430,49 +456,33 @@
 
 def wave_kernel(last, config_ref, *refs):
     if not last:
-        smix_ref, imix_ref, *refs = refs
-    (far_i, near_c, forcing_ref, left_ref, right_ref, near_i, far_c,
-     state_c, fields_ref, state_i, tracers_ref, *refs) = refs
+        mixes_ref, *refs = refs
+        smix_ref, imix_ref = mixes_ref.at[pl.ds(0, FIELDS)], mixes_ref.at[pl.ds(FIELDS, FIELDS)]
+    far_i, near_c, near_i, far_c, tracers_ref, inner_state, inner_forcing, coef, *refs = refs
     if last:
-        out_ref, state, forcing, coef = refs
+        out_ref, state, forcing, push = refs
     else:
-        received_ref, land_ref, out_ref, export_ref, state, forcing, coef, turned = refs
+        received_ref, land_ref, out_ref, export_ref, state, forcing, push, turned = refs
     height = 5 * ROWS
     tiles = height // 8
 
     after = spread(config_ref, AFTER_NEAR, ROWS) > 0.5
     after_far = spread(config_ref, AFTER_FAR, ROWS) > 0.5
     for i in range(WAVES):
-        place_field(forcing.at[i], PAD + 2 * ROWS, own_parts(forcing_ref, left_ref, right_ref, 0, i))
-        place_field(state.at[i], PAD + 2 * ROWS, own_parts(fields_ref, left_ref, right_ref, 2, i))
-        pushed, parts, behind = [], [], []
-        for near, main in ((near_c, state_c), (near_i, state_i)):
-            pushed.append(wave_main(near, B_WAVE + 2, i, 8) + wave_strip(near, B_WAVE, i, 8))
-            parts.append(wave_main(main, A_WAVE, i, 6) + wave_strip(near, B_STRIP_W, i, 2))
-            behind.append(wave_main(near, B_BEHIND, i))
+        for j in range(3):
+            for ref, inner in ((state, inner_state), (forcing, inner_forcing)):
+                ref[i, j, PAD + ROWS : PAD + 4 * ROWS, :] = inner[i, j]
+                ref[i, j, 0:PAD, :] = jnp.zeros((PAD, LANES), f32)
+                ref[i, j, PAD + height : height + 2 * PAD, :] = jnp.zeros((PAD, LANES), f32)
+        behind = [wave_main(near, B_BEHIND, i) for near in (near_c, near_i)]
         far_pushed = [wave_main(far, 2, i) + wave_strip(far, 0, i) for far in (far_c, far_i)]
         far_strip = [wave_strip(far, C_STRIP_W, i) for far in (far_c, far_i)]
         for k, slot in ((1, 0), (0, 4)):
-            near_slot = (slot + 2) // 2
-            place_field(forcing.at[i], PAD + near_slot * ROWS, chosen(after, pushed[k], pushed[1 - k]))
-            place_field(state.at[i], PAD + near_slot * ROWS, chosen(after, parts[k], parts[1 - k]))
             place_field(forcing.at[i], PAD + slot * ROWS, chosen(after_far, far_pushed[k], far_pushed[1 - k]))
             main = chosen(after, behind[k], behind[1 - k])
             strip = chosen(after_far, far_strip[k], far_strip[1 - k])
             place_field(state.at[i], PAD + slot * ROWS, main + strip)
-        for j in range(3):
-            for ref in (state, forcing):
-                ref[i, j, 0:PAD, :] = jnp.zeros((PAD, LANES), f32)
-                ref[i, j, PAD + height : height + 2 * PAD, :] = jnp.zeros((PAD, LANES), f32)
-    half_a = 0.5 * config_ref[:, WAVE_SPEED : WAVE_SPEED + 1]
     half_b = 0.5 * config_ref[:, WAVE_SPEED + 1 : WAVE_SPEED + 2]
-    first_row = -2 * ROWS
-    for j in range(3):
-        coef[0, j] = inside_tile(config_ref, first_row, height, j) * half_a
-        coef[1, j] = inside_tile(config_ref, first_row + 1, height, j) * half_b
-        coef[2, j] = inside_tile(config_ref, first_row - 1, height, j) * half_b
-        coef[3, j] = inside_tile(config_ref, first_row, height, j, 1) * half_b
-        coef[4, j] = inside_tile(config_ref, first_row, height, j, -1) * half_b
 
     lane = lax.broadcasted_iota(jnp.int32, (8, LANES), 1)
     keep = [1.0 - spread(config_ref, c) for c in range(WAVES)]
@@ -496,8 +506,8 @@
         at = PAD + 8 * t
         push_u, push_v = along(forcing, 1, t), across(load(forcing, 2, t))
         for j in range(3):
-            coef[5, j, 8 * t : 8 * t + 8, :] = push_u[j]
-            coef[6, j, 8 * t : 8 * t + 8, :] = push_v[j]
+            push[0, j, 8 * t : 8 * t + 8, :] = push_u[j]
+            push[1, j, 8 * t : 8 * t + 8, :] = push_v[j]
     own = (4, 5)
     sum_u = {t: [jnp.zeros((8, LANES), f32)] * 2 for t in (3, 4, 5, 6)}
     sum_v = {t: [jnp.zeros((8, LANES), f32)] * 3 for t in own}
@@ -507,9 +517,9 @@
         span = range(first, tiles - first)
         for t in span:
             here = slice(8 * t, 8 * t + 8)
-            push = load(forcing, 0, t)
+            lift = load(forcing, 0, t)
             for j in range(3):
-                h[t][j] = (keep[0] * h[t][j] + push[j]) - coef[0, j, here, :] * (du[t][j] + dv[t][j])
+                h[t][j] = (keep[0] * h[t][j] + lift[j]) - coef[0, j, here, :] * (du[t][j] + dv[t][j])
                 if not final:
                     state[0, j, PAD + 8 * t : PAD + 8 * t + 8, :] = h[t][j]
         for t in sum_u:
@@ -524,10 +534,10 @@
             up, down = load(state, 0, t, 2), load(state, 0, t, -2)
             for j in range(3):
                 mid = h[t][j]
-                du[t][j] = (keep[1] * du[t][j] + coef[5, j, here, :]) - (
+                du[t][j] = (keep[1] * du[t][j] + push[0, j, here, :]) - (
                     coef[1, j, here, :] * (up[j] - mid) - coef[2, j, here, :] * (mid - down[j])
                 )
-                dv[t][j] = (keep[2] * dv[t][j] + coef[6, j, here, :]) - (
+                dv[t][j] = (keep[2] * dv[t][j] + push[1, j, here, :]) - (
                     coef[3, j, here, :] * (east[j] - mid) - coef[4, j, here, :] * (mid - west[j])
                 )
 
@@ -570,7 +580,7 @@
     scratch = [
         pltpu.VMEM((WAVES, 3, 5 * ROWS + 2 * PAD, LANES), f32),
         pltpu.VMEM((WAVES, 3, 5 * ROWS + 2 * PAD, LANES), f32),
-        pltpu.VMEM((7, 3, 5 * ROWS, LANES), f32),
+        pltpu.VMEM((2, 3, 5 * ROWS, LANES), f32),
     ]
     if not last:
         scratch.append(pltpu.VMEM((2, TURNED, LANES), f32))
@@ -616,15 +626,16 @@
     entry = (window * ROWS + slot // 4) * 2 + (slot % 4) // 2
     second = lax.iota(jnp.int32, owner.shape[0]) % 2
     index = entry + ((slot % 2) ^ second) * (5 * ROWS * 2)
-    index = jnp.concatenate([index, (gy % 2).astype(jnp.int32)[None]])
+    index = jnp.concatenate([index, jnp.full((TURNED,), gy % 2, jnp.int32)])
     weight = remap_weight[0].reshape(ROWS, COLS, 128)
+    mixes = jnp.concatenate([smix, imix], axis=0)
 
     fields, land = section_state[0], land_mask[0]
     exported = export(fields, prev_import[0], land, smix, imix)
     for interval in range(ITERS):
         last = interval == ITERS - 1
         opposite = lax.ppermute(exported, "sec", [(0, 1), (1, 0)])
-        near = pack(opposite, fields, index, config)
+        near = pack(opposite, fields, index, config, mixes)
         state_c = exchanged(near, "gx", 1, 1)
         state_i = exchanged(near, "gx", 1, 0)
         export_c = exchanged(opposite, "gx", 2, 1)
@@ -632,7 +643,7 @@
         if interval == 0:
             weight = stage(weight, state_c, state_i)
         forcing, to_chip, to_outer, received = remap(
-            index, (export_i, state_i, opposite, state_c, export_c), weight, land, fields
+            index, (export_c, state_c, opposite, state_i, export_i), weight, land, fields
         )
         outer = exchanged(to_outer, "gy", 1, 1)
         chip = exchanged(to_chip, "gy", 1, 0)
@@ -645,15 +656,15 @@
         state = (state_c, fields, state_i)
         operands = (near_c, *own, near_i, *state)
         if last:
-            tracers, received = tracer_steps(last, config, operands + (received,))
+            received, *prepared = tracer_steps(last, config, operands + (received,))
         else:
-            tracers = tracer_steps(last, config, operands)
-        operands = (far_i, near_c, *own, near_i, far_c, *state, tracers)
+            prepared = tracer_steps(last, config, operands)
+        operands = (far_i, near_c, near_i, far_c, *prepared)
         if last:
             fields = wave_steps(last, config, (), operands)
         else:
             operands += (received, land)
-            fields, exported = wave_steps(last, config, (smix, imix), operands)
+            fields, exported = wave_steps(last, config, (mixes,), operands)
     return (fields[None], received[None])
 
 

time: 123 us -> 123 us (level)
  waiting for transfers between devices: 14.6 us -> 13 us
    ppermute x20, waiting for transfers between devices: 11.3 us -> 9.79 us  [exchanged(): return lax.ppermute(block, axis, route)]
  transfers between devices with their start and end apart: 22 -> 22, of which waited for: 9 -> 10; matrix products, arithmetic and copies ran while one was open for 1% -> 1% of each run, Pallas kernels for 6% -> 6%
where the time goes in v9:
time: 123 us; the launch traced here: 122 us
  starting transfers between devices  87.3 us (71%)
  Pallas kernels  16.4 us (13%)
  waiting for transfers between devices  13 us (11%)
  local copies, waits for them, and re-layouts  3.69 us (3%)
    ppermute x20, starting transfers between devices, exchanged(): return lax.ppermute(block, axis, route)  68.8 us
    ppermute x2, starting transfers between devices, local(): opposite = lax.ppermute(exported, 'sec', [(0, 1), (1, 0)])  18.5 us
    ppermute x20, waiting for transfers between devices, exchanged(): return lax.ppermute(block, axis, route)  9.79 us
    pallas_call x2, Pallas kernels, tracer_steps(): pl.pallas_call(lambda *refs: tracer_kernel(last, *refs), out_shape=tuple(...  7.39 us
    pallas_call x2, Pallas kernels, wave_steps(): pl.pallas_call(lambda *refs: wave_kernel(last, *refs), out_shape=state if...  4.46 us
    ppermute x2, waiting for transfers between devices, local(): opposite = lax.ppermute(exported, 'sec', [(0, 1), (1, 0)])  3.21 us
    unnamed x19, local copies, waits for them, and re-layouts  3.19 us
  transfers between devices with their start and end apart: 22, of which 10 were waited for; matrix products, arithmetic and copies ran while one was open for 1% of the time, Pallas kernels for 6%

profile of v9, /device:TPU:6, one launch (start us, length us, event | category | flops | bytes accessed | tf_op | source)
XLA Modules:
  0.0 121.6 jit_solution(7221785341741936513)
XLA Ops:
  0.6 2.0 %export.1 = bf16[128,256]{1,0:T(8,128)(2,1)} custom-call(f32[8,8]{1,0:T(8,128)} %bitcast.32, f32[8,8]{1,0:T(8,128)} %bitcast.30, f32[8,16,256]{2,1,0:T(8,128)} %bitcast.19, f32[8,16,256]{2,1,0:T(8,128)} %bitcast.29, s32[16,256]{1,0:T(8,128)} %bitcast.24), custom_call_target="tpu_custom_call" | custom-call | tf_op jit(solution)/shard_map/export/pallas_call | solution.py:115
  2.6 10.9 %collective-permute-start = (bf16[128,256]{1,0:T(8,128)(2,1)}, bf16[128,256]{1,0:T(8,128)(2,1)S(1)}, u32[]{:S(2)}, u32[]{:S(2)}) collective-permute-start(bf16[128,256]{1,0:T(8,128)(2,1)} %export.1), channel_id=1, source_target_pairs={{0,256},{256,0},{1,257},{257,1},{2,258},{258,2},{3,259},{259,3},{4... | collective-permute-start | bytes 196616 | tf_op jit(solution)/shard_map/ppermute | solution.py:637
  13.6 0.6 copy-done.3
  14.2 0.1 copy.14
  14.4 0.1 sub.33
  14.5 0.5 copy-done.5
  15.0 0.1 copy.15
  15.2 0.1 reshape_squeeze.7
  15.4 0.1 stack.23
  15.5 0.6 copy-done.7
  16.2 0.7 collective-permute-done.opposite_ref
  16.9 5.6 %collective-permute-start.2 = (bf16[38,16,128]{2,1,0:T(8,128)(2,1)S(1)}, bf16[38,16,128]{2,1,0:T(8,128)(2,1)S(1)}, u32[]{:S(2)}, u32[]{:S(2)}) collective-permute-start(bf16[38,16,128]{2,1,0:T(8,128)(2,1)S(1)} %pack.2), channel_id=1, source_target_pairs={{8,16},{16,8},{24,32},{32,24},{40,48},{48,40},{56,64},{64,56},{72,... | collective-permute-start | bytes 466952 | tf_op jit(solution)/shard_map/ppermute | solution.py:604
  22.6 1.9 %collective-permute-start.3 = (bf16[38,16,128]{2,1,0:T(8,128)(2,1)S(1)}, bf16[38,16,128]{2,1,0:T(8,128)(2,1)S(1)}, u32[]{:S(2)}, u32[]{:S(2)}) collective-permute-start(bf16[38,16,128]{2,1,0:T(8,128)(2,1)S(1)} %pack.2), channel_id=1, source_target_pairs={{0,8},{8,0},{16,24},{24,16},{32,40},{40,32},{48,56},{56,48},{64,72... | collective-permute-start | bytes 466952 | tf_op jit(solution)/shard_map/ppermute | solution.py:604
  24.5 4.0 %collective-permute-start.1 = (bf16[128,256]{1,0:T(8,128)(2,1)S(1)}, bf16[128,256]{1,0:T(8,128)(2,1)S(1)}, u32[]{:S(2)}, u32[]{:S(2)}) collective-permute-start(bf16[128,256]{1,0:T(8,128)(2,1)S(1)} %collective-permute-done.opposite_ref), channel_id=1, source_target_pairs={{16,32},{32,16},{24,40},{40,24},{48,64},{64,48},{56,72},{72,56},{8... | collective-permute-start | bytes 196616 | tf_op jit(solution)/shard_map/ppermute | solution.py:604
  28.5 3.8 %collective-permute-start.4 = (bf16[128,256]{1,0:T(8,128)(2,1)S(1)}, bf16[128,256]{1,0:T(8,128)(2,1)S(1)}, u32[]{:S(2)}, u32[]{:S(2)}) collective-permute-start(bf16[128,256]{1,0:T(8,128)(2,1)S(1)} %collective-permute-done.opposite_ref), channel_id=1, source_target_pairs={{0,16},{16,0},{8,24},{24,8},{32,48},{48,32},{40,56},{56,40},{64,80... | collective-permute-start | bytes 196616 | tf_op jit(solution)/shard_map/ppermute | solution.py:604
  32.3 1.2 %copy-done.1 = bf16[1,16,4,64,128]{4,3,2,1,0:T(8,128)(2,1)S(1)} copy-done((bf16[1,16,4,64,128]{4,3,2,1,0:T(8,128)(2,1)S(1)}, bf16[1,16,4,64,128]{4,3,2,1,0:T(8,128)(2,1)}, u32[]{:S(2)}) %copy-start.1) | copy-done | bytes 1048600
  33.7 1.9 %collective-permute-done.4.far_i_ref = bf16[128,256]{1,0:T(8,128)(2,1)S(1)} collective-permute-done((bf16[128,256]{1,0:T(8,128)(2,1)S(1)}, bf16[128,256]{1,0:T(8,128)(2,1)S(1)}, u32[]{:S(2)}, u32[]{:S(2)}) %collective-permute-start.4) | collective-permute-done | bytes 65568 | tf_op jit(solution)/shard_map/ppermute | solution.py:604
  35.6 1.2 remap.2
  36.8 0.7 collective-permute-start.5
  37.4 4.1 %collective-permute-start.6 = (f32[4,16,128]{2,1,0:T(8,128)S(1)}, f32[4,16,128]{2,1,0:T(8,128)S(1)}, u32[]{:S(2)}, u32[]{:S(2)}) collective-permute-start(f32[4,16,128]{2,1,0:T(8,128)S(1)} %get-tuple-element.33), channel_id=1, source_target_pairs={{0,1},{1,0},{2,3},{3,2},{4,5},{5,4},{6,7},{7,6},{8,9},{9,8},{10,11... | collective-permute-start | bytes 98312 | tf_op jit(solution)/shard_map/ppermute | solution.py:604
  41.5 0.8 collective-permute-done.6.chip_ref
  42.4 5.5 %collective-permute-start.8 = (bf16[40,16,128]{2,1,0:T(8,128)(2,1)S(1)}, bf16[40,16,128]{2,1,0:T(8,128)(2,1)S(1)}, u32[]{:S(2)}, u32[]{:S(2)}) collective-permute-start(bf16[40,16,128]{2,1,0:T(8,128)(2,1)S(1)} %get-tuple-element.35), channel_id=1, source_target_pairs={{8,16},{16,8},{24,32},{32,24},{40,48},{48,40},{56,64},{64,56},{72,... | collective-permute-start | bytes 491528 | tf_op jit(solution)/shard_map/ppermute | solution.py:604
  47.9 1.9 %collective-permute-start.9 = (bf16[40,16,128]{2,1,0:T(8,128)(2,1)S(1)}, bf16[40,16,128]{2,1,0:T(8,128)(2,1)S(1)}, u32[]{:S(2)}, u32[]{:S(2)}) collective-permute-start(bf16[40,16,128]{2,1,0:T(8,128)(2,1)S(1)} %get-tuple-element.36), channel_id=1, source_target_pairs={{0,8},{8,0},{16,24},{24,16},{32,40},{40,32},{48,56},{56,48},{64,72... | collective-permute-start | bytes 491528 | tf_op jit(solution)/shard_map/ppermute | solution.py:604
  49.9 3.9 %collective-permute-start.10 = (bf16[10,16,128]{2,1,0:T(8,128)(2,1)S(1)}, bf16[10,16,128]{2,1,0:T(8,128)(2,1)S(1)}, u32[]{:S(2)}, u32[]{:S(2)}) collective-permute-start(bf16[10,16,128]{2,1,0:T(8,128)(2,1)S(1)} %get-tuple-element.34), channel_id=1, source_target_pairs={{16,32},{32,16},{24,40},{40,24},{48,64},{64,48},{56,72},{72,56},{8... | collective-permute-start | bytes 122888 | tf_op jit(solution)/shard_map/ppermute | solution.py:604
  53.8 2.7 %collective-permute-start.7 = (bf16[10,16,128]{2,1,0:T(8,128)(2,1)S(1)}, bf16[10,16,128]{2,1,0:T(8,128)(2,1)S(1)}, u32[]{:S(2)}, u32[]{:S(2)}) collective-permute-start(bf16[10,16,128]{2,1,0:T(8,128)(2,1)S(1)} %get-tuple-element.34), channel_id=1, source_target_pairs={{0,16},{16,0},{8,24},{24,8},{32,48},{48,32},{40,56},{56,40},{64,80... | collective-permute-start | bytes 122888 | tf_op jit(solution)/shard_map/ppermute | solution.py:604
  56.5 3.5 %tracer_steps.2 = (f32[5,16,256]{2,1,0:T(8,128)S(1)}, f32[3,3,48,128]{3,2,1,0:T(8,128)S(1)}, f32[3,3,48,128]{3,2,1,0:T(8,128)S(1)}, f32[5,3,80,128]{3,2,1,0:T(8,128)S(1)}) custom-call(f32[1,17]{1,0:T(1,128)S(1)} %maximum_bitcast_fusion.config_ref.refs_0_, bf16[40,16,128]{2,1,0:T(8,128)(2,1)S(1)} %collective-permute-done.8.refs_1_.refs_3_, ...), custom_call_target="tpu_custom_call" | custom-call | flops 10000000 | bytes 4000000 | tf_op jit(solution)/shard_map/tracer_steps/pallas_call | solution.py:441
  60.0 0.9 collective-permute-done.7.refs_2_
  60.9 2.0 %wave_steps.1 = (f32[8,16,256]{2,1,0:T(8,128)S(1)}, bf16[128,256]{1,0:T(8,128)(2,1)S(1)}) custom-call(f32[1,17]{1,0:T(1,128)S(1)} %maximum_bitcast_fusion.config_ref.refs_0_, f32[16,8]{1,0:T(8,128)S(1)} %pad_maximum_fusion.mixes_ref.refs_1_, bf16[10,16,128]{2,1,0:T(8,128)(2,1)S(1)} %collective-permute-done.7.refs_2_, ...), custom_call_target="tpu_custom_call" | custom-call | tf_op jit(solution)/shard_map/wave_steps/pallas_call | solution.py:587
  62.9 7.6 %collective-permute-start.11 = (bf16[128,256]{1,0:T(8,128)(2,1)S(1)}, bf16[128,256]{1,0:T(8,128)(2,1)S(1)}, u32[]{:S(2)}, u32[]{:S(2)}) collective-permute-start(bf16[128,256]{1,0:T(8,128)(2,1)S(1)} %get-tuple-element.44), channel_id=1, source_target_pairs={{0,256},{256,0},{1,257},{257,1},{2,258},{258,2},{3,259},{259,3},{4... | collective-permute-start | bytes 196616 | tf_op jit(solution)/shard_map/ppermute | solution.py:637
  70.5 2.5 %collective-permute-done.11.opposite_ref = bf16[128,256]{1,0:T(8,128)(2,1)S(1)} collective-permute-done((bf16[128,256]{1,0:T(8,128)(2,1)S(1)}, bf16[128,256]{1,0:T(8,128)(2,1)S(1)}, u32[]{:S(2)}, u32[]{:S(2)}) %collective-permute-start.11) | collective-permute-done | bytes 65568 | tf_op jit(solution)/shard_map/ppermute | solution.py:637
  73.0 5.2 %collective-permute-start.13 = (bf16[38,16,128]{2,1,0:T(8,128)(2,1)S(1)}, bf16[38,16,128]{2,1,0:T(8,128)(2,1)S(1)}, u32[]{:S(2)}, u32[]{:S(2)}) collective-permute-start(bf16[38,16,128]{2,1,0:T(8,128)(2,1)S(1)} %pack.3), channel_id=1, source_target_pairs={{8,16},{16,8},{24,32},{32,24},{40,48},{48,40},{56,64},{64,56},{72,... | collective-permute-start | bytes 466952 | tf_op jit(solution)/shard_map/ppermute | solution.py:604
  78.2 1.9 %collective-permute-start.14 = (bf16[38,16,128]{2,1,0:T(8,128)(2,1)S(1)}, bf16[38,16,128]{2,1,0:T(8,128)(2,1)S(1)}, u32[]{:S(2)}, u32[]{:S(2)}) collective-permute-start(bf16[38,16,128]{2,1,0:T(8,128)(2,1)S(1)} %pack.3), channel_id=1, source_target_pairs={{0,8},{8,0},{16,24},{24,16},{32,40},{40,32},{48,56},{56,48},{64,72... | collective-permute-start | bytes 466952 | tf_op jit(solution)/shard_map/ppermute | solution.py:604
  80.1 4.2 %collective-permute-start.12 = (bf16[128,256]{1,0:T(8,128)(2,1)S(1)}, bf16[128,256]{1,0:T(8,128)(2,1)S(1)}, u32[]{:S(2)}, u32[]{:S(2)}) collective-permute-start(bf16[128,256]{1,0:T(8,128)(2,1)S(1)} %collective-permute-done.11.opposite_ref), channel_id=1, source_target_pairs={{16,32},{32,16},{24,40},{40,24},{48,64},{64,48},{56,72},{72,56},{8... | collective-permute-start | bytes 196616 | tf_op jit(solution)/shard_map/ppermute | solution.py:604
  84.4 2.6 %collective-permute-start.15 = (bf16[128,256]{1,0:T(8,128)(2,1)S(1)}, bf16[128,256]{1,0:T(8,128)(2,1)S(1)}, u32[]{:S(2)}, u32[]{:S(2)}) collective-permute-start(bf16[128,256]{1,0:T(8,128)(2,1)S(1)} %collective-permute-done.11.opposite_ref), channel_id=1, source_target_pairs={{0,16},{16,0},{8,24},{24,8},{32,48},{48,32},{40,56},{56,40},{64,80... | collective-permute-start | bytes 196616 | tf_op jit(solution)/shard_map/ppermute | solution.py:604
  87.0 2.4 %collective-permute-done.12.far_c_ref = bf16[128,256]{1,0:T(8,128)(2,1)S(1)} collective-permute-done((bf16[128,256]{1,0:T(8,128)(2,1)S(1)}, bf16[128,256]{1,0:T(8,128)(2,1)S(1)}, u32[]{:S(2)}, u32[]{:S(2)}) %collective-permute-start.12) | collective-permute-done | bytes 65568 | tf_op jit(solution)/shard_map/ppermute | solution.py:604
  89.4 2.0 %collective-permute-done.15.far_i_ref = bf16[128,256]{1,0:T(8,128)(2,1)S(1)} collective-permute-done((bf16[128,256]{1,0:T(8,128)(2,1)S(1)}, bf16[128,256]{1,0:T(8,128)(2,1)S(1)}, u32[]{:S(2)}, u32[]{:S(2)}) %collective-permute-start.15) | collective-permute-done | bytes 65568 | tf_op jit(solution)/shard_map/ppermute | solution.py:604
  91.4 1.2 remap.3
  92.6 0.7 collective-permute-start.16
  93.3 6.3 %collective-permute-start.17 = (f32[4,16,128]{2,1,0:T(8,128)S(1)}, f32[4,16,128]{2,1,0:T(8,128)S(1)}, u32[]{:S(2)}, u32[]{:S(2)}) collective-permute-start(f32[4,16,128]{2,1,0:T(8,128)S(1)} %get-tuple-element.48), channel_id=1, source_target_pairs={{0,1},{1,0},{2,3},{3,2},{4,5},{5,4},{6,7},{7,6},{8,9},{9,8},{10,11... | collective-permute-start | bytes 98312 | tf_op jit(solution)/shard_map/ppermute | solution.py:604
  99.6 0.8 collective-permute-done.17.chip_ref
  100.5 5.3 %collective-permute-start.19 = (bf16[40,16,128]{2,1,0:T(8,128)(2,1)S(1)}, bf16[40,16,128]{2,1,0:T(8,128)(2,1)S(1)}, u32[]{:S(2)}, u32[]{:S(2)}) collective-permute-start(bf16[40,16,128]{2,1,0:T(8,128)(2,1)S(1)} %get-tuple-element.50), channel_id=1, source_target_pairs={{8,16},{16,8},{24,32},{32,24},{40,48},{48,40},{56,64},{64,56},{72,... | collective-permute-start | bytes 491528 | tf_op jit(solution)/shard_map/ppermute | solution.py:604
  105.8 1.9 %collective-permute-start.20 = (bf16[40,16,128]{2,1,0:T(8,128)(2,1)S(1)}, bf16[40,16,128]{2,1,0:T(8,128)(2,1)S(1)}, u32[]{:S(2)}, u32[]{:S(2)}) collective-permute-start(bf16[40,16,128]{2,1,0:T(8,128)(2,1)S(1)} %get-tuple-element.51), channel_id=1, source_target_pairs={{0,8},{8,0},{16,24},{24,16},{32,40},{40,32},{48,56},{56,48},{64,72... | collective-permute-start | bytes 491528 | tf_op jit(solution)/shard_map/ppermute | solution.py:604
  107.7 2.4 %collective-permute-start.18 = (bf16[10,16,128]{2,1,0:T(8,128)(2,1)S(1)}, bf16[10,16,128]{2,1,0:T(8,128)(2,1)S(1)}, u32[]{:S(2)}, u32[]{:S(2)}) collective-permute-start(bf16[10,16,128]{2,1,0:T(8,128)(2,1)S(1)} %get-tuple-element.49), channel_id=1, source_target_pairs={{0,16},{16,0},{8,24},{24,8},{32,48},{48,32},{40,56},{56,40},{64,80... | collective-permute-start | bytes 122888 | tf_op jit(solution)/shard_map/ppermute | solution.py:604
  110.2 4.2 %collective-permute-start.21 = (bf16[10,16,128]{2,1,0:T(8,128)(2,1)S(1)}, bf16[10,16,128]{2,1,0:T(8,128)(2,1)S(1)}, u32[]{:S(2)}, u32[]{:S(2)}) collective-permute-start(bf16[10,16,128]{2,1,0:T(8,128)(2,1)S(1)} %get-tuple-element.49), channel_id=1, source_target_pairs={{16,32},{32,16},{24,40},{40,24},{48,64},{64,48},{56,72},{72,56},{8... | collective-permute-start | bytes 122888 | tf_op jit(solution)/shard_map/ppermute | solution.py:604
  114.4 0.3 collective-permute-done.20.refs_5_.refs_3_
  114.7 3.9 %tracer_steps.3 = (f32[8,16,256]{2,1,0:T(8,128)}, f32[5,16,256]{2,1,0:T(8,128)S(1)}, f32[3,3,48,128]{3,2,1,0:T(8,128)S(1)}, f32[3,3,48,128]{3,2,1,0:T(8,128)S(1)}, f32[5,3,80,128]{3,2,1,0:T(8,128)S(1)}) custom-call(f32[1,17]{1,0:T(1,128)S(1)} %maximum_bitcast_fusion.config_ref.refs_0_, bf16[40,16,128]{2,1,0:T(8,128)(2,1)S(1)} %collective-permute-done.19.refs_1_.refs_2_, ...), custom_call_target="tpu_custom_call" | custom-call | flops 10000000 | bytes 4000000 | tf_op jit(solution)/shard_map/tracer_steps/pallas_call | solution.py:441
  118.6 0.5 collective-permute-done.21.refs_4_
  119.1 2.5 %wave_steps_last.1 = f32[8,16,256]{2,1,0:T(8,128)} custom-call(f32[1,17]{1,0:T(1,128)S(1)} %maximum_bitcast_fusion.config_ref.refs_0_, bf16[10,16,128]{2,1,0:T(8,128)(2,1)S(1)} %collective-permute-done.18.refs_1_, bf16[40,16,128]{2,1,0:T(8,128)(2,1)S(1)} %collective-permute-done.19.refs_1_.refs_2_, ...), custom_call_target="tpu_custom_call" | custom-call | tf_op jit(solution)/shard_map/wave_steps_last/pallas_call | solution.py:587
  (37 shorter events, 0.5 us)
Async XLA Ops:
  2.6 14.3 %collective-permute-start = (bf16[128,256]{1,0:T(8,128)(2,1)}, bf16[128,256]{1,0:T(8,128)(2,1)S(1)}, u32[]{:S(2)}, u32[]{:S(2)}) collective-permute-start(bf16[128,256]{1,0:T(8,128)(2,1)} %export.1), channel_id=1, source_target_pairs={{0,256},{256,0},{1,257},{257,1},{2,258},{258,2},{3,259},{259,3},{4... | collective-permute-start | bytes 196616 | tf_op jit(solution)/shard_map/ppermute | solution.py:637
  13.5 0.7 copy-start.3
  13.5 0.7 copy-start.4
  13.6 0.7 copy-start.6
  13.6 3.3 %copy-start = (f32[1,8,16,256]{3,2,1,0:T(8,128)S(1)}, f32[1,8,16,256]{3,2,1,0:T(8,128)}, u32[]{:S(2)}) copy-start(f32[1,8,16,256]{3,2,1,0:T(8,128)} %param.10) | copy-start | bytes 393220
  14.4 0.7 copy-start.5
  15.5 0.7 copy-start.7
  15.5 0.7 copy-start.8
  16.9 15.4 %collective-permute-start.2 = (bf16[38,16,128]{2,1,0:T(8,128)(2,1)S(1)}, bf16[38,16,128]{2,1,0:T(8,128)(2,1)S(1)}, u32[]{:S(2)}, u32[]{:S(2)}) collective-permute-start(bf16[38,16,128]{2,1,0:T(8,128)(2,1)S(1)} %pack.2), channel_id=1, source_target_pairs={{8,16},{16,8},{24,32},{32,24},{40,48},{48,40},{56,64},{64,56},{72,... | collective-permute-start | bytes 466952 | tf_op jit(solution)/shard_map/ppermute | solution.py:604
  22.6 9.8 %collective-permute-start.3 = (bf16[38,16,128]{2,1,0:T(8,128)(2,1)S(1)}, bf16[38,16,128]{2,1,0:T(8,128)(2,1)S(1)}, u32[]{:S(2)}, u32[]{:S(2)}) collective-permute-start(bf16[38,16,128]{2,1,0:T(8,128)(2,1)S(1)} %pack.2), channel_id=1, source_target_pairs={{0,8},{8,0},{16,24},{24,16},{32,40},{40,32},{48,56},{56,48},{64,72... | collective-permute-start | bytes 466952 | tf_op jit(solution)/shard_map/ppermute | solution.py:604
  24.5 9.2 %collective-permute-start.1 = (bf16[128,256]{1,0:T(8,128)(2,1)S(1)}, bf16[128,256]{1,0:T(8,128)(2,1)S(1)}, u32[]{:S(2)}, u32[]{:S(2)}) collective-permute-start(bf16[128,256]{1,0:T(8,128)(2,1)S(1)} %collective-permute-done.opposite_ref), channel_id=1, source_target_pairs={{16,32},{32,16},{24,40},{40,24},{48,64},{64,48},{56,72},{72,56},{8... | collective-permute-start | bytes 196616 | tf_op jit(solution)/shard_map/ppermute | solution.py:604
  28.5 7.1 %collective-permute-start.4 = (bf16[128,256]{1,0:T(8,128)(2,1)S(1)}, bf16[128,256]{1,0:T(8,128)(2,1)S(1)}, u32[]{:S(2)}, u32[]{:S(2)}) collective-permute-start(bf16[128,256]{1,0:T(8,128)(2,1)S(1)} %collective-permute-done.opposite_ref), channel_id=1, source_target_pairs={{0,16},{16,0},{8,24},{24,8},{32,48},{48,32},{40,56},{56,40},{64,80... | collective-permute-start | bytes 196616 | tf_op jit(solution)/shard_map/ppermute | solution.py:604
  32.3 1.2 %copy-start.1 = (bf16[1,16,4,64,128]{4,3,2,1,0:T(8,128)(2,1)S(1)}, bf16[1,16,4,64,128]{4,3,2,1,0:T(8,128)(2,1)}, u32[]{:S(2)}) copy-start(bf16[1,16,4,64,128]{4,3,2,1,0:T(8,128)(2,1)} %param.19) | copy-start | bytes 3145732
  33.6 2.0 %copy-start.2 = (s32[1,16,256]{2,1,0:T(8,128)S(1)}, s32[1,16,256]{2,1,0:T(8,128)}, u32[]{:S(2)}) copy-start(s32[1,16,256]{2,1,0:T(8,128)} %param.12) | copy-start | bytes 49156
  36.8 4.8 %collective-permute-start.5 = (f32[4,16,128]{2,1,0:T(8,128)S(1)}, f32[4,16,128]{2,1,0:T(8,128)S(1)}, u32[]{:S(2)}, u32[]{:S(2)}) collective-permute-start(f32[4,16,128]{2,1,0:T(8,128)S(1)} %get-tuple-element.32), channel_id=1, source_target_pairs={{1,2},{2,1},{3,4},{4,3},{5,6},{6,5},{9,10},{10,9},{11,12},{12,11},... | collective-permute-start | bytes 98312 | tf_op jit(solution)/shard_map/ppermute | solution.py:604
  37.4 4.9 %collective-permute-start.6 = (f32[4,16,128]{2,1,0:T(8,128)S(1)}, f32[4,16,128]{2,1,0:T(8,128)S(1)}, u32[]{:S(2)}, u32[]{:S(2)}) collective-permute-start(f32[4,16,128]{2,1,0:T(8,128)S(1)} %get-tuple-element.33), channel_id=1, source_target_pairs={{0,1},{1,0},{2,3},{3,2},{4,5},{5,4},{6,7},{7,6},{8,9},{9,8},{10,11... | collective-permute-start | bytes 98312 | tf_op jit(solution)/shard_map/ppermute | solution.py:604
  42.4 14.0 %collective-permute-start.8 = (bf16[40,16,128]{2,1,0:T(8,128)(2,1)S(1)}, bf16[40,16,128]{2,1,0:T(8,128)(2,1)S(1)}, u32[]{:S(2)}, u32[]{:S(2)}) collective-permute-start(bf16[40,16,128]{2,1,0:T(8,128)(2,1)S(1)} %get-tuple-element.35), channel_id=1, source_target_pairs={{8,16},{16,8},{24,32},{32,24},{40,48},{48,40},{56,64},{64,56},{72,... | collective-permute-start | bytes 491528 | tf_op jit(solution)/shard_map/ppermute | solution.py:604
  47.9 8.5 %collective-permute-start.9 = (bf16[40,16,128]{2,1,0:T(8,128)(2,1)S(1)}, bf16[40,16,128]{2,1,0:T(8,128)(2,1)S(1)}, u32[]{:S(2)}, u32[]{:S(2)}) collective-permute-start(bf16[40,16,128]{2,1,0:T(8,128)(2,1)S(1)} %get-tuple-element.36), channel_id=1, source_target_pairs={{0,8},{8,0},{16,24},{24,16},{32,40},{40,32},{48,56},{56,48},{64,72... | collective-permute-start | bytes 491528 | tf_op jit(solution)/shard_map/ppermute | solution.py:604
  49.9 10.1 %collective-permute-start.10 = (bf16[10,16,128]{2,1,0:T(8,128)(2,1)S(1)}, bf16[10,16,128]{2,1,0:T(8,128)(2,1)S(1)}, u32[]{:S(2)}, u32[]{:S(2)}) collective-permute-start(bf16[10,16,128]{2,1,0:T(8,128)(2,1)S(1)} %get-tuple-element.34), channel_id=1, source_target_pairs={{16,32},{32,16},{24,40},{40,24},{48,64},{64,48},{56,72},{72,56},{8... | collective-permute-start | bytes 122888 | tf_op jit(solution)/shard_map/ppermute | solution.py:604
  53.8 7.1 %collective-permute-start.7 = (bf16[10,16,128]{2,1,0:T(8,128)(2,1)S(1)}, bf16[10,16,128]{2,1,0:T(8,128)(2,1)S(1)}, u32[]{:S(2)}, u32[]{:S(2)}) collective-permute-start(bf16[10,16,128]{2,1,0:T(8,128)(2,1)S(1)} %get-tuple-element.34), channel_id=1, source_target_pairs={{0,16},{16,0},{8,24},{24,8},{32,48},{48,32},{40,56},{56,40},{64,80... | collective-permute-start | bytes 122888 | tf_op jit(solution)/shard_map/ppermute | solution.py:604
  62.9 10.1 %collective-permute-start.11 = (bf16[128,256]{1,0:T(8,128)(2,1)S(1)}, bf16[128,256]{1,0:T(8,128)(2,1)S(1)}, u32[]{:S(2)}, u32[]{:S(2)}) collective-permute-start(bf16[128,256]{1,0:T(8,128)(2,1)S(1)} %get-tuple-element.44), channel_id=1, source_target_pairs={{0,256},{256,0},{1,257},{257,1},{2,258},{258,2},{3,259},{259,3},{4... | collective-permute-start | bytes 196616 | tf_op jit(solution)/shard_map/ppermute | solution.py:637
  73.0 18.4 %collective-permute-start.13 = (bf16[38,16,128]{2,1,0:T(8,128)(2,1)S(1)}, bf16[38,16,128]{2,1,0:T(8,128)(2,1)S(1)}, u32[]{:S(2)}, u32[]{:S(2)}) collective-permute-start(bf16[38,16,128]{2,1,0:T(8,128)(2,1)S(1)} %pack.3), channel_id=1, source_target_pairs={{8,16},{16,8},{24,32},{32,24},{40,48},{48,40},{56,64},{64,56},{72,... | collective-permute-start | bytes 466952 | tf_op jit(solution)/shard_map/ppermute | solution.py:604
  78.2 13.2 %collective-permute-start.14 = (bf16[38,16,128]{2,1,0:T(8,128)(2,1)S(1)}, bf16[38,16,128]{2,1,0:T(8,128)(2,1)S(1)}, u32[]{:S(2)}, u32[]{:S(2)}) collective-permute-start(bf16[38,16,128]{2,1,0:T(8,128)(2,1)S(1)} %pack.3), channel_id=1, source_target_pairs={{0,8},{8,0},{16,24},{24,16},{32,40},{40,32},{48,56},{56,48},{64,72... | collective-permute-start | bytes 466952 | tf_op jit(solution)/shard_map/ppermute | solution.py:604
  80.1 9.3 %collective-permute-start.12 = (bf16[128,256]{1,0:T(8,128)(2,1)S(1)}, bf16[128,256]{1,0:T(8,128)(2,1)S(1)}, u32[]{:S(2)}, u32[]{:S(2)}) collective-permute-start(bf16[128,256]{1,0:T(8,128)(2,1)S(1)} %collective-permute-done.11.opposite_ref), channel_id=1, source_target_pairs={{16,32},{32,16},{24,40},{40,24},{48,64},{64,48},{56,72},{72,56},{8... | collective-permute-start | bytes 196616 | tf_op jit(solution)/shard_map/ppermute | solution.py:604
  84.4 7.1 %collective-permute-start.15 = (bf16[128,256]{1,0:T(8,128)(2,1)S(1)}, bf16[128,256]{1,0:T(8,128)(2,1)S(1)}, u32[]{:S(2)}, u32[]{:S(2)}) collective-permute-start(bf16[128,256]{1,0:T(8,128)(2,1)S(1)} %collective-permute-done.11.opposite_ref), channel_id=1, source_target_pairs={{0,16},{16,0},{8,24},{24,8},{32,48},{48,32},{40,56},{56,40},{64,80... | collective-permute-start | bytes 196616 | tf_op jit(solution)/shard_map/ppermute | solution.py:604
  92.6 6.9 %collective-permute-start.16 = (f32[4,16,128]{2,1,0:T(8,128)S(1)}, f32[4,16,128]{2,1,0:T(8,128)S(1)}, u32[]{:S(2)}, u32[]{:S(2)}) collective-permute-start(f32[4,16,128]{2,1,0:T(8,128)S(1)} %get-tuple-element.47), channel_id=1, source_target_pairs={{1,2},{2,1},{3,4},{4,3},{5,6},{6,5},{9,10},{10,9},{11,12},{12,11},... | collective-permute-start | bytes 98312 | tf_op jit(solution)/shard_map/ppermute | solution.py:604
  93.3 7.1 %collective-permute-start.17 = (f32[4,16,128]{2,1,0:T(8,128)S(1)}, f32[4,16,128]{2,1,0:T(8,128)S(1)}, u32[]{:S(2)}, u32[]{:S(2)}) collective-permute-start(f32[4,16,128]{2,1,0:T(8,128)S(1)} %get-tuple-element.48), channel_id=1, source_target_pairs={{0,1},{1,0},{2,3},{3,2},{4,5},{5,4},{6,7},{7,6},{8,9},{9,8},{10,11... | collective-permute-start | bytes 98312 | tf_op jit(solution)/shard_map/ppermute | solution.py:604
  100.5 13.9 %collective-permute-start.19 = (bf16[40,16,128]{2,1,0:T(8,128)(2,1)S(1)}, bf16[40,16,128]{2,1,0:T(8,128)(2,1)S(1)}, u32[]{:S(2)}, u32[]{:S(2)}) collective-permute-start(bf16[40,16,128]{2,1,0:T(8,128)(2,1)S(1)} %get-tuple-element.50), channel_id=1, source_target_pairs={{8,16},{16,8},{24,32},{32,24},{40,48},{48,40},{56,64},{64,56},{72,... | collective-permute-start | bytes 491528 | tf_op jit(solution)/shard_map/ppermute | solution.py:604
  105.8 8.9 %collective-permute-start.20 = (bf16[40,16,128]{2,1,0:T(8,128)(2,1)S(1)}, bf16[40,16,128]{2,1,0:T(8,128)(2,1)S(1)}, u32[]{:S(2)}, u32[]{:S(2)}) collective-permute-start(bf16[40,16,128]{2,1,0:T(8,128)(2,1)S(1)} %get-tuple-element.51), channel_id=1, source_target_pairs={{0,8},{8,0},{16,24},{24,16},{32,40},{40,32},{48,56},{56,48},{64,72... | collective-permute-start | bytes 491528 | tf_op jit(solution)/shard_map/ppermute | solution.py:604
  107.7 10.8 %collective-permute-start.18 = (bf16[10,16,128]{2,1,0:T(8,128)(2,1)S(1)}, bf16[10,16,128]{2,1,0:T(8,128)(2,1)S(1)}, u32[]{:S(2)}, u32[]{:S(2)}) collective-permute-start(bf16[10,16,128]{2,1,0:T(8,128)(2,1)S(1)} %get-tuple-element.49), channel_id=1, source_target_pairs={{0,16},{16,0},{8,24},{24,8},{32,48},{48,32},{40,56},{56,40},{64,80... | collective-permute-start | bytes 122888 | tf_op jit(solution)/shard_map/ppermute | solution.py:604
  110.2 8.9 %collective-permute-start.21 = (bf16[10,16,128]{2,1,0:T(8,128)(2,1)S(1)}, bf16[10,16,128]{2,1,0:T(8,128)(2,1)S(1)}, u32[]{:S(2)}, u32[]{:S(2)}) collective-permute-start(bf16[10,16,128]{2,1,0:T(8,128)(2,1)S(1)} %get-tuple-element.49), channel_id=1, source_target_pairs={{16,32},{32,16},{24,40},{40,24},{48,64},{64,48},{56,72},{72,56},{8... | collective-permute-start | bytes 122888 | tf_op jit(solution)/shard_map/ppermute | solution.py:604

commit v10 on v9

--- a/solution.py
+++ b/solution.py
@@ -458,7 +458,8 @@
     if not last:
         mixes_ref, *refs = refs
         smix_ref, imix_ref = mixes_ref.at[pl.ds(0, FIELDS)], mixes_ref.at[pl.ds(FIELDS, FIELDS)]
-    far_i, near_c, near_i, far_c, tracers_ref, inner_state, inner_forcing, coef, *refs = refs
+    first, near_c, near_i, second, tracers_ref, inner_state, inner_forcing, coef, *refs = refs
+    far_c, far_i = (first, second) if last else (second, first)
     if last:
         out_ref, state, forcing, push = refs
     else:
@@ -659,7 +660,8 @@
             received, *prepared = tracer_steps(last, config, operands + (received,))
         else:
             prepared = tracer_steps(last, config, operands)
-        operands = (far_i, near_c, near_i, far_c, *prepared)
+        operands = (far_c, near_c, near_i, far_i) if last else (far_i, near_c, near_i, far_c)
+        operands += tuple(prepared)
         if last:
             fields = wave_steps(last, config, (), operands)
         else:

time: 123 us -> 122 us (level)
  no operation moved by 1% of the time
where the time goes in v10:
time: 122 us; the launch traced here: 121 us
  starting transfers between devices  86.7 us (71%)
  Pallas kernels  16.4 us (13%)
  waiting for transfers between devices  13.1 us (11%)
  local copies, waits for them, and re-layouts  3.69 us (3%)
    ppermute x20, starting transfers between devices, exchanged(): return lax.ppermute(block, axis, route)  68.2 us
    ppermute x2, starting transfers between devices, local(): opposite = lax.ppermute(exported, 'sec', [(0, 1), (1, 0)])  18.5 us
    ppermute x20, waiting for transfers between devices, exchanged(): return lax.ppermute(block, axis, route)  9.94 us
    pallas_call x2, Pallas kernels, tracer_steps(): pl.pallas_call(lambda *refs: tracer_kernel(last, *refs), out_shape=tuple(...  7.39 us
    pallas_call x2, Pallas kernels, wave_steps(): pl.pallas_call(lambda *refs: wave_kernel(last, *refs), out_shape=state if...  4.47 us
    ppermute x2, waiting for transfers between devices, local(): opposite = lax.ppermute(exported, 'sec', [(0, 1), (1, 0)])  3.21 us
    unnamed x19, local copies, waits for them, and re-layouts  3.19 us
  transfers between devices with their start and end apart: 22, of which 10 were waited for; matrix products, arithmetic and copies ran while one was open for 1% of the time, Pallas kernels for 6%

profile of v10, /device:TPU:6, one launch (start us, length us, event | category | flops | bytes accessed | tf_op | source)
XLA Modules:
  0.0 121.1 jit_solution(7562942015884203807)
XLA Ops:
  0.6 2.0 %export.1 = bf16[128,256]{1,0:T(8,128)(2,1)} custom-call(f32[8,8]{1,0:T(8,128)} %bitcast.32, f32[8,8]{1,0:T(8,128)} %bitcast.30, f32[8,16,256]{2,1,0:T(8,128)} %bitcast.19, f32[8,16,256]{2,1,0:T(8,128)} %bitcast.29, s32[16,256]{1,0:T(8,128)} %bitcast.24), custom_call_target="tpu_custom_call" | custom-call | tf_op jit(solution)/shard_map/export/pallas_call | solution.py:115
  2.6 10.9 %collective-permute-start = (bf16[128,256]{1,0:T(8,128)(2,1)}, bf16[128,256]{1,0:T(8,128)(2,1)S(1)}, u32[]{:S(2)}, u32[]{:S(2)}) collective-permute-start(bf16[128,256]{1,0:T(8,128)(2,1)} %export.1), channel_id=1, source_target_pairs={{0,256},{256,0},{1,257},{257,1},{2,258},{258,2},{3,259},{259,3},{4... | collective-permute-start | bytes 196616 | tf_op jit(solution)/shard_map/ppermute | solution.py:638
  13.6 0.6 copy-done.3
  14.2 0.1 copy.14
  14.4 0.1 sub.33
  14.5 0.5 copy-done.5
  15.0 0.1 copy.15
  15.2 0.1 reshape_squeeze.7
  15.4 0.1 stack.23
  15.5 0.6 copy-done.7
  16.2 0.7 collective-permute-done.opposite_ref
  16.9 5.6 %collective-permute-start.2 = (bf16[38,16,128]{2,1,0:T(8,128)(2,1)S(1)}, bf16[38,16,128]{2,1,0:T(8,128)(2,1)S(1)}, u32[]{:S(2)}, u32[]{:S(2)}) collective-permute-start(bf16[38,16,128]{2,1,0:T(8,128)(2,1)S(1)} %pack.2), channel_id=1, source_target_pairs={{8,16},{16,8},{24,32},{32,24},{40,48},{48,40},{56,64},{64,56},{72,... | collective-permute-start | bytes 466952 | tf_op jit(solution)/shard_map/ppermute | solution.py:605
  22.6 1.9 %collective-permute-start.3 = (bf16[38,16,128]{2,1,0:T(8,128)(2,1)S(1)}, bf16[38,16,128]{2,1,0:T(8,128)(2,1)S(1)}, u32[]{:S(2)}, u32[]{:S(2)}) collective-permute-start(bf16[38,16,128]{2,1,0:T(8,128)(2,1)S(1)} %pack.2), channel_id=1, source_target_pairs={{0,8},{8,0},{16,24},{24,16},{32,40},{40,32},{48,56},{56,48},{64,72... | collective-permute-start | bytes 466952 | tf_op jit(solution)/shard_map/ppermute | solution.py:605
  24.5 4.0 %collective-permute-start.1 = (bf16[128,256]{1,0:T(8,128)(2,1)S(1)}, bf16[128,256]{1,0:T(8,128)(2,1)S(1)}, u32[]{:S(2)}, u32[]{:S(2)}) collective-permute-start(bf16[128,256]{1,0:T(8,128)(2,1)S(1)} %collective-permute-done.opposite_ref), channel_id=1, source_target_pairs={{16,32},{32,16},{24,40},{40,24},{48,64},{64,48},{56,72},{72,56},{8... | collective-permute-start | bytes 196616 | tf_op jit(solution)/shard_map/ppermute | solution.py:605
  28.5 3.8 %collective-permute-start.4 = (bf16[128,256]{1,0:T(8,128)(2,1)S(1)}, bf16[128,256]{1,0:T(8,128)(2,1)S(1)}, u32[]{:S(2)}, u32[]{:S(2)}) collective-permute-start(bf16[128,256]{1,0:T(8,128)(2,1)S(1)} %collective-permute-done.opposite_ref), channel_id=1, source_target_pairs={{0,16},{16,0},{8,24},{24,8},{32,48},{48,32},{40,56},{56,40},{64,80... | collective-permute-start | bytes 196616 | tf_op jit(solution)/shard_map/ppermute | solution.py:605
  32.3 1.2 %copy-done.1 = bf16[1,16,4,64,128]{4,3,2,1,0:T(8,128)(2,1)S(1)} copy-done((bf16[1,16,4,64,128]{4,3,2,1,0:T(8,128)(2,1)S(1)}, bf16[1,16,4,64,128]{4,3,2,1,0:T(8,128)(2,1)}, u32[]{:S(2)}) %copy-start.1) | copy-done | bytes 1048600
  33.7 1.9 %collective-permute-done.4.far_i_ref = bf16[128,256]{1,0:T(8,128)(2,1)S(1)} collective-permute-done((bf16[128,256]{1,0:T(8,128)(2,1)S(1)}, bf16[128,256]{1,0:T(8,128)(2,1)S(1)}, u32[]{:S(2)}, u32[]{:S(2)}) %collective-permute-start.4) | collective-permute-done | bytes 65568 | tf_op jit(solution)/shard_map/ppermute | solution.py:605
  35.6 1.1 remap.2
  36.7 0.7 collective-permute-start.5
  37.4 4.1 %collective-permute-start.6 = (f32[4,16,128]{2,1,0:T(8,128)S(1)}, f32[4,16,128]{2,1,0:T(8,128)S(1)}, u32[]{:S(2)}, u32[]{:S(2)}) collective-permute-start(f32[4,16,128]{2,1,0:T(8,128)S(1)} %get-tuple-element.33), channel_id=1, source_target_pairs={{0,1},{1,0},{2,3},{3,2},{4,5},{5,4},{6,7},{7,6},{8,9},{9,8},{10,11... | collective-permute-start | bytes 98312 | tf_op jit(solution)/shard_map/ppermute | solution.py:605
  41.5 0.8 collective-permute-done.6.chip_ref
  42.4 5.5 %collective-permute-start.8 = (bf16[40,16,128]{2,1,0:T(8,128)(2,1)S(1)}, bf16[40,16,128]{2,1,0:T(8,128)(2,1)S(1)}, u32[]{:S(2)}, u32[]{:S(2)}) collective-permute-start(bf16[40,16,128]{2,1,0:T(8,128)(2,1)S(1)} %get-tuple-element.35), channel_id=1, source_target_pairs={{8,16},{16,8},{24,32},{32,24},{40,48},{48,40},{56,64},{64,56},{72,... | collective-permute-start | bytes 491528 | tf_op jit(solution)/shard_map/ppermute | solution.py:605
  47.9 1.9 %collective-permute-start.9 = (bf16[40,16,128]{2,1,0:T(8,128)(2,1)S(1)}, bf16[40,16,128]{2,1,0:T(8,128)(2,1)S(1)}, u32[]{:S(2)}, u32[]{:S(2)}) collective-permute-start(bf16[40,16,128]{2,1,0:T(8,128)(2,1)S(1)} %get-tuple-element.36), channel_id=1, source_target_pairs={{0,8},{8,0},{16,24},{24,16},{32,40},{40,32},{48,56},{56,48},{64,72... | collective-permute-start | bytes 491528 | tf_op jit(solution)/shard_map/ppermute | solution.py:605
  49.9 3.9 %collective-permute-start.10 = (bf16[10,16,128]{2,1,0:T(8,128)(2,1)S(1)}, bf16[10,16,128]{2,1,0:T(8,128)(2,1)S(1)}, u32[]{:S(2)}, u32[]{:S(2)}) collective-permute-start(bf16[10,16,128]{2,1,0:T(8,128)(2,1)S(1)} %get-tuple-element.34), channel_id=1, source_target_pairs={{16,32},{32,16},{24,40},{40,24},{48,64},{64,48},{56,72},{72,56},{8... | collective-permute-start | bytes 122888 | tf_op jit(solution)/shard_map/ppermute | solution.py:605
  53.8 2.7 %collective-permute-start.7 = (bf16[10,16,128]{2,1,0:T(8,128)(2,1)S(1)}, bf16[10,16,128]{2,1,0:T(8,128)(2,1)S(1)}, u32[]{:S(2)}, u32[]{:S(2)}) collective-permute-start(bf16[10,16,128]{2,1,0:T(8,128)(2,1)S(1)} %get-tuple-element.34), channel_id=1, source_target_pairs={{0,16},{16,0},{8,24},{24,8},{32,48},{48,32},{40,56},{56,40},{64,80... | collective-permute-start | bytes 122888 | tf_op jit(solution)/shard_map/ppermute | solution.py:605
  56.5 3.5 %tracer_steps.2 = (f32[5,16,256]{2,1,0:T(8,128)S(1)}, f32[3,3,48,128]{3,2,1,0:T(8,128)S(1)}, f32[3,3,48,128]{3,2,1,0:T(8,128)S(1)}, f32[5,3,80,128]{3,2,1,0:T(8,128)S(1)}) custom-call(f32[1,17]{1,0:T(1,128)S(1)} %maximum_bitcast_fusion.config_ref.refs_0_, bf16[40,16,128]{2,1,0:T(8,128)(2,1)S(1)} %collective-permute-done.8.refs_1_.refs_3_, ...), custom_call_target="tpu_custom_call" | custom-call | flops 10000000 | bytes 4000000 | tf_op jit(solution)/shard_map/tracer_steps/pallas_call | solution.py:441
  60.0 0.9 collective-permute-done.7.refs_2_
  60.9 2.0 %wave_steps.1 = (f32[8,16,256]{2,1,0:T(8,128)S(1)}, bf16[128,256]{1,0:T(8,128)(2,1)S(1)}) custom-call(f32[1,17]{1,0:T(1,128)S(1)} %maximum_bitcast_fusion.config_ref.refs_0_, f32[16,8]{1,0:T(8,128)S(1)} %pad_maximum_fusion.mixes_ref.refs_1_, bf16[10,16,128]{2,1,0:T(8,128)(2,1)S(1)} %collective-permute-done.7.refs_2_, ...), custom_call_target="tpu_custom_call" | custom-call | tf_op jit(solution)/shard_map/wave_steps/pallas_call | solution.py:588
  62.9 7.6 %collective-permute-start.11 = (bf16[128,256]{1,0:T(8,128)(2,1)S(1)}, bf16[128,256]{1,0:T(8,128)(2,1)S(1)}, u32[]{:S(2)}, u32[]{:S(2)}) collective-permute-start(bf16[128,256]{1,0:T(8,128)(2,1)S(1)} %get-tuple-element.44), channel_id=1, source_target_pairs={{0,256},{256,0},{1,257},{257,1},{2,258},{258,2},{3,259},{259,3},{4... | collective-permute-start | bytes 196616 | tf_op jit(solution)/shard_map/ppermute | solution.py:638
  70.5 2.5 %collective-permute-done.11.opposite_ref = bf16[128,256]{1,0:T(8,128)(2,1)S(1)} collective-permute-done((bf16[128,256]{1,0:T(8,128)(2,1)S(1)}, bf16[128,256]{1,0:T(8,128)(2,1)S(1)}, u32[]{:S(2)}, u32[]{:S(2)}) %collective-permute-start.11) | collective-permute-done | bytes 65568 | tf_op jit(solution)/shard_map/ppermute | solution.py:638
  73.0 5.2 %collective-permute-start.13 = (bf16[38,16,128]{2,1,0:T(8,128)(2,1)S(1)}, bf16[38,16,128]{2,1,0:T(8,128)(2,1)S(1)}, u32[]{:S(2)}, u32[]{:S(2)}) collective-permute-start(bf16[38,16,128]{2,1,0:T(8,128)(2,1)S(1)} %pack.3), channel_id=1, source_target_pairs={{8,16},{16,8},{24,32},{32,24},{40,48},{48,40},{56,64},{64,56},{72,... | collective-permute-start | bytes 466952 | tf_op jit(solution)/shard_map/ppermute | solution.py:605
  78.2 1.9 %collective-permute-start.14 = (bf16[38,16,128]{2,1,0:T(8,128)(2,1)S(1)}, bf16[38,16,128]{2,1,0:T(8,128)(2,1)S(1)}, u32[]{:S(2)}, u32[]{:S(2)}) collective-permute-start(bf16[38,16,128]{2,1,0:T(8,128)(2,1)S(1)} %pack.3), channel_id=1, source_target_pairs={{0,8},{8,0},{16,24},{24,16},{32,40},{40,32},{48,56},{56,48},{64,72... | collective-permute-start | bytes 466952 | tf_op jit(solution)/shard_map/ppermute | solution.py:605
  80.1 4.2 %collective-permute-start.12 = (bf16[128,256]{1,0:T(8,128)(2,1)S(1)}, bf16[128,256]{1,0:T(8,128)(2,1)S(1)}, u32[]{:S(2)}, u32[]{:S(2)}) collective-permute-start(bf16[128,256]{1,0:T(8,128)(2,1)S(1)} %collective-permute-done.11.opposite_ref), channel_id=1, source_target_pairs={{16,32},{32,16},{24,40},{40,24},{48,64},{64,48},{56,72},{72,56},{8... | collective-permute-start | bytes 196616 | tf_op jit(solution)/shard_map/ppermute | solution.py:605
  84.4 2.6 %collective-permute-start.15 = (bf16[128,256]{1,0:T(8,128)(2,1)S(1)}, bf16[128,256]{1,0:T(8,128)(2,1)S(1)}, u32[]{:S(2)}, u32[]{:S(2)}) collective-permute-start(bf16[128,256]{1,0:T(8,128)(2,1)S(1)} %collective-permute-done.11.opposite_ref), channel_id=1, source_target_pairs={{0,16},{16,0},{8,24},{24,8},{32,48},{48,32},{40,56},{56,40},{64,80... | collective-permute-start | bytes 196616 | tf_op jit(solution)/shard_map/ppermute | solution.py:605
  87.0 2.4 %collective-permute-done.12.far_c_ref = bf16[128,256]{1,0:T(8,128)(2,1)S(1)} collective-permute-done((bf16[128,256]{1,0:T(8,128)(2,1)S(1)}, bf16[128,256]{1,0:T(8,128)(2,1)S(1)}, u32[]{:S(2)}, u32[]{:S(2)}) %collective-permute-start.12) | collective-permute-done | bytes 65568 | tf_op jit(solution)/shard_map/ppermute | solution.py:605
  89.4 2.0 %collective-permute-done.15.far_i_ref = bf16[128,256]{1,0:T(8,128)(2,1)S(1)} collective-permute-done((bf16[128,256]{1,0:T(8,128)(2,1)S(1)}, bf16[128,256]{1,0:T(8,128)(2,1)S(1)}, u32[]{:S(2)}, u32[]{:S(2)}) %collective-permute-start.15) | collective-permute-done | bytes 65568 | tf_op jit(solution)/shard_map/ppermute | solution.py:605
  91.4 1.1 remap.3
  92.6 0.7 collective-permute-start.16
  93.3 6.3 %collective-permute-start.17 = (f32[4,16,128]{2,1,0:T(8,128)S(1)}, f32[4,16,128]{2,1,0:T(8,128)S(1)}, u32[]{:S(2)}, u32[]{:S(2)}) collective-permute-start(f32[4,16,128]{2,1,0:T(8,128)S(1)} %get-tuple-element.48), channel_id=1, source_target_pairs={{0,1},{1,0},{2,3},{3,2},{4,5},{5,4},{6,7},{7,6},{8,9},{9,8},{10,11... | collective-permute-start | bytes 98312 | tf_op jit(solution)/shard_map/ppermute | solution.py:605
  99.6 0.8 collective-permute-done.17.chip_ref
  100.5 5.3 %collective-permute-start.19 = (bf16[40,16,128]{2,1,0:T(8,128)(2,1)S(1)}, bf16[40,16,128]{2,1,0:T(8,128)(2,1)S(1)}, u32[]{:S(2)}, u32[]{:S(2)}) collective-permute-start(bf16[40,16,128]{2,1,0:T(8,128)(2,1)S(1)} %get-tuple-element.50), channel_id=1, source_target_pairs={{8,16},{16,8},{24,32},{32,24},{40,48},{48,40},{56,64},{64,56},{72,... | collective-permute-start | bytes 491528 | tf_op jit(solution)/shard_map/ppermute | solution.py:605
  105.8 1.9 %collective-permute-start.20 = (bf16[40,16,128]{2,1,0:T(8,128)(2,1)S(1)}, bf16[40,16,128]{2,1,0:T(8,128)(2,1)S(1)}, u32[]{:S(2)}, u32[]{:S(2)}) collective-permute-start(bf16[40,16,128]{2,1,0:T(8,128)(2,1)S(1)} %get-tuple-element.51), channel_id=1, source_target_pairs={{0,8},{8,0},{16,24},{24,16},{32,40},{40,32},{48,56},{56,48},{64,72... | collective-permute-start | bytes 491528 | tf_op jit(solution)/shard_map/ppermute | solution.py:605
  107.7 4.1 %collective-permute-start.18 = (bf16[10,16,128]{2,1,0:T(8,128)(2,1)S(1)}, bf16[10,16,128]{2,1,0:T(8,128)(2,1)S(1)}, u32[]{:S(2)}, u32[]{:S(2)}) collective-permute-start(bf16[10,16,128]{2,1,0:T(8,128)(2,1)S(1)} %get-tuple-element.49), channel_id=1, source_target_pairs={{16,32},{32,16},{24,40},{40,24},{48,64},{64,48},{56,72},{72,56},{8... | collective-permute-start | bytes 122888 | tf_op jit(solution)/shard_map/ppermute | solution.py:605
  111.8 1.9 %collective-permute-start.21 = (bf16[10,16,128]{2,1,0:T(8,128)(2,1)S(1)}, bf16[10,16,128]{2,1,0:T(8,128)(2,1)S(1)}, u32[]{:S(2)}, u32[]{:S(2)}) collective-permute-start(bf16[10,16,128]{2,1,0:T(8,128)(2,1)S(1)} %get-tuple-element.49), channel_id=1, source_target_pairs={{0,16},{16,0},{8,24},{24,8},{32,48},{48,32},{40,56},{56,40},{64,80... | collective-permute-start | bytes 122888 | tf_op jit(solution)/shard_map/ppermute | solution.py:605
  113.8 0.6 collective-permute-done.20.refs_5_.refs_3_
  114.3 3.9 %tracer_steps.3 = (f32[8,16,256]{2,1,0:T(8,128)}, f32[5,16,256]{2,1,0:T(8,128)S(1)}, f32[3,3,48,128]{3,2,1,0:T(8,128)S(1)}, f32[3,3,48,128]{3,2,1,0:T(8,128)S(1)}, f32[5,3,80,128]{3,2,1,0:T(8,128)S(1)}) custom-call(f32[1,17]{1,0:T(1,128)S(1)} %maximum_bitcast_fusion.config_ref.refs_0_, bf16[40,16,128]{2,1,0:T(8,128)(2,1)S(1)} %collective-permute-done.19.refs_1_.refs_2_, ...), custom_call_target="tpu_custom_call" | custom-call | flops 10000000 | bytes 4000000 | tf_op jit(solution)/shard_map/tracer_steps/pallas_call | solution.py:441
  118.2 0.4 collective-permute-done.21.refs_4_
  118.6 2.5 %wave_steps_last.1 = f32[8,16,256]{2,1,0:T(8,128)} custom-call(f32[1,17]{1,0:T(1,128)S(1)} %maximum_bitcast_fusion.config_ref.refs_0_, bf16[10,16,128]{2,1,0:T(8,128)(2,1)S(1)} %collective-permute-done.18.refs_1_, bf16[40,16,128]{2,1,0:T(8,128)(2,1)S(1)} %collective-permute-done.19.refs_1_.refs_2_, ...), custom_call_target="tpu_custom_call" | custom-call | tf_op jit(solution)/shard_map/wave_steps_last/pallas_call | solution.py:588
  (37 shorter events, 0.5 us)
Async XLA Ops:
  2.6 14.3 %collective-permute-start = (bf16[128,256]{1,0:T(8,128)(2,1)}, bf16[128,256]{1,0:T(8,128)(2,1)S(1)}, u32[]{:S(2)}, u32[]{:S(2)}) collective-permute-start(bf16[128,256]{1,0:T(8,128)(2,1)} %export.1), channel_id=1, source_target_pairs={{0,256},{256,0},{1,257},{257,1},{2,258},{258,2},{3,259},{259,3},{4... | collective-permute-start | bytes 196616 | tf_op jit(solution)/shard_map/ppermute | solution.py:638
  13.5 0.7 copy-start.3
  13.5 0.7 copy-start.4
  13.6 0.7 copy-start.6
  13.6 3.3 %copy-start = (f32[1,8,16,256]{3,2,1,0:T(8,128)S(1)}, f32[1,8,16,256]{3,2,1,0:T(8,128)}, u32[]{:S(2)}) copy-start(f32[1,8,16,256]{3,2,1,0:T(8,128)} %param.10) | copy-start | bytes 393220
  14.4 0.7 copy-start.5
  15.5 0.7 copy-start.7
  15.5 0.7 copy-start.8
  16.9 15.4 %collective-permute-start.2 = (bf16[38,16,128]{2,1,0:T(8,128)(2,1)S(1)}, bf16[38,16,128]{2,1,0:T(8,128)(2,1)S(1)}, u32[]{:S(2)}, u32[]{:S(2)}) collective-permute-start(bf16[38,16,128]{2,1,0:T(8,128)(2,1)S(1)} %pack.2), channel_id=1, source_target_pairs={{8,16},{16,8},{24,32},{32,24},{40,48},{48,40},{56,64},{64,56},{72,... | collective-permute-start | bytes 466952 | tf_op jit(solution)/shard_map/ppermute | solution.py:605
  22.6 9.8 %collective-permute-start.3 = (bf16[38,16,128]{2,1,0:T(8,128)(2,1)S(1)}, bf16[38,16,128]{2,1,0:T(8,128)(2,1)S(1)}, u32[]{:S(2)}, u32[]{:S(2)}) collective-permute-start(bf16[38,16,128]{2,1,0:T(8,128)(2,1)S(1)} %pack.2), channel_id=1, source_target_pairs={{0,8},{8,0},{16,24},{24,16},{32,40},{40,32},{48,56},{56,48},{64,72... | collective-permute-start | bytes 466952 | tf_op jit(solution)/shard_map/ppermute | solution.py:605
  24.5 9.2 %collective-permute-start.1 = (bf16[128,256]{1,0:T(8,128)(2,1)S(1)}, bf16[128,256]{1,0:T(8,128)(2,1)S(1)}, u32[]{:S(2)}, u32[]{:S(2)}) collective-permute-start(bf16[128,256]{1,0:T(8,128)(2,1)S(1)} %collective-permute-done.opposite_ref), channel_id=1, source_target_pairs={{16,32},{32,16},{24,40},{40,24},{48,64},{64,48},{56,72},{72,56},{8... | collective-permute-start | bytes 196616 | tf_op jit(solution)/shard_map/ppermute | solution.py:605
  28.5 7.1 %collective-permute-start.4 = (bf16[128,256]{1,0:T(8,128)(2,1)S(1)}, bf16[128,256]{1,0:T(8,128)(2,1)S(1)}, u32[]{:S(2)}, u32[]{:S(2)}) collective-permute-start(bf16[128,256]{1,0:T(8,128)(2,1)S(1)} %collective-permute-done.opposite_ref), channel_id=1, source_target_pairs={{0,16},{16,0},{8,24},{24,8},{32,48},{48,32},{40,56},{56,40},{64,80... | collective-permute-start | bytes 196616 | tf_op jit(solution)/shard_map/ppermute | solution.py:605
  32.3 1.2 %copy-start.1 = (bf16[1,16,4,64,128]{4,3,2,1,0:T(8,128)(2,1)S(1)}, bf16[1,16,4,64,128]{4,3,2,1,0:T(8,128)(2,1)}, u32[]{:S(2)}) copy-start(bf16[1,16,4,64,128]{4,3,2,1,0:T(8,128)(2,1)} %param.19) | copy-start | bytes 3145732
  33.6 2.0 %copy-start.2 = (s32[1,16,256]{2,1,0:T(8,128)S(1)}, s32[1,16,256]{2,1,0:T(8,128)}, u32[]{:S(2)}) copy-start(s32[1,16,256]{2,1,0:T(8,128)} %param.12) | copy-start | bytes 49156
  36.7 4.8 %collective-permute-start.5 = (f32[4,16,128]{2,1,0:T(8,128)S(1)}, f32[4,16,128]{2,1,0:T(8,128)S(1)}, u32[]{:S(2)}, u32[]{:S(2)}) collective-permute-start(f32[4,16,128]{2,1,0:T(8,128)S(1)} %get-tuple-element.32), channel_id=1, source_target_pairs={{1,2},{2,1},{3,4},{4,3},{5,6},{6,5},{9,10},{10,9},{11,12},{12,11},... | collective-permute-start | bytes 98312 | tf_op jit(solution)/shard_map/ppermute | solution.py:605
  37.4 4.9 %collective-permute-start.6 = (f32[4,16,128]{2,1,0:T(8,128)S(1)}, f32[4,16,128]{2,1,0:T(8,128)S(1)}, u32[]{:S(2)}, u32[]{:S(2)}) collective-permute-start(f32[4,16,128]{2,1,0:T(8,128)S(1)} %get-tuple-element.33), channel_id=1, source_target_pairs={{0,1},{1,0},{2,3},{3,2},{4,5},{5,4},{6,7},{7,6},{8,9},{9,8},{10,11... | collective-permute-start | bytes 98312 | tf_op jit(solution)/shard_map/ppermute | solution.py:605
  42.4 14.0 %collective-permute-start.8 = (bf16[40,16,128]{2,1,0:T(8,128)(2,1)S(1)}, bf16[40,16,128]{2,1,0:T(8,128)(2,1)S(1)}, u32[]{:S(2)}, u32[]{:S(2)}) collective-permute-start(bf16[40,16,128]{2,1,0:T(8,128)(2,1)S(1)} %get-tuple-element.35), channel_id=1, source_target_pairs={{8,16},{16,8},{24,32},{32,24},{40,48},{48,40},{56,64},{64,56},{72,... | collective-permute-start | bytes 491528 | tf_op jit(solution)/shard_map/ppermute | solution.py:605
  47.9 8.5 %collective-permute-start.9 = (bf16[40,16,128]{2,1,0:T(8,128)(2,1)S(1)}, bf16[40,16,128]{2,1,0:T(8,128)(2,1)S(1)}, u32[]{:S(2)}, u32[]{:S(2)}) collective-permute-start(bf16[40,16,128]{2,1,0:T(8,128)(2,1)S(1)} %get-tuple-element.36), channel_id=1, source_target_pairs={{0,8},{8,0},{16,24},{24,16},{32,40},{40,32},{48,56},{56,48},{64,72... | collective-permute-start | bytes 491528 | tf_op jit(solution)/shard_map/ppermute | solution.py:605
  49.9 10.1 %collective-permute-start.10 = (bf16[10,16,128]{2,1,0:T(8,128)(2,1)S(1)}, bf16[10,16,128]{2,1,0:T(8,128)(2,1)S(1)}, u32[]{:S(2)}, u32[]{:S(2)}) collective-permute-start(bf16[10,16,128]{2,1,0:T(8,128)(2,1)S(1)} %get-tuple-element.34), channel_id=1, source_target_pairs={{16,32},{32,16},{24,40},{40,24},{48,64},{64,48},{56,72},{72,56},{8... | collective-permute-start | bytes 122888 | tf_op jit(solution)/shard_map/ppermute | solution.py:605
  53.8 7.1 %collective-permute-start.7 = (bf16[10,16,128]{2,1,0:T(8,128)(2,1)S(1)}, bf16[10,16,128]{2,1,0:T(8,128)(2,1)S(1)}, u32[]{:S(2)}, u32[]{:S(2)}) collective-permute-start(bf16[10,16,128]{2,1,0:T(8,128)(2,1)S(1)} %get-tuple-element.34), channel_id=1, source_target_pairs={{0,16},{16,0},{8,24},{24,8},{32,48},{48,32},{40,56},{56,40},{64,80... | collective-permute-start | bytes 122888 | tf_op jit(solution)/shard_map/ppermute | solution.py:605
  62.9 10.1 %collective-permute-start.11 = (bf16[128,256]{1,0:T(8,128)(2,1)S(1)}, bf16[128,256]{1,0:T(8,128)(2,1)S(1)}, u32[]{:S(2)}, u32[]{:S(2)}) collective-permute-start(bf16[128,256]{1,0:T(8,128)(2,1)S(1)} %get-tuple-element.44), channel_id=1, source_target_pairs={{0,256},{256,0},{1,257},{257,1},{2,258},{258,2},{3,259},{259,3},{4... | collective-permute-start | bytes 196616 | tf_op jit(solution)/shard_map/ppermute | solution.py:638
  73.0 18.4 %collective-permute-start.13 = (bf16[38,16,128]{2,1,0:T(8,128)(2,1)S(1)}, bf16[38,16,128]{2,1,0:T(8,128)(2,1)S(1)}, u32[]{:S(2)}, u32[]{:S(2)}) collective-permute-start(bf16[38,16,128]{2,1,0:T(8,128)(2,1)S(1)} %pack.3), channel_id=1, source_target_pairs={{8,16},{16,8},{24,32},{32,24},{40,48},{48,40},{56,64},{64,56},{72,... | collective-permute-start | bytes 466952 | tf_op jit(solution)/shard_map/ppermute | solution.py:605
  78.2 13.2 %collective-permute-start.14 = (bf16[38,16,128]{2,1,0:T(8,128)(2,1)S(1)}, bf16[38,16,128]{2,1,0:T(8,128)(2,1)S(1)}, u32[]{:S(2)}, u32[]{:S(2)}) collective-permute-start(bf16[38,16,128]{2,1,0:T(8,128)(2,1)S(1)} %pack.3), channel_id=1, source_target_pairs={{0,8},{8,0},{16,24},{24,16},{32,40},{40,32},{48,56},{56,48},{64,72... | collective-permute-start | bytes 466952 | tf_op jit(solution)/shard_map/ppermute | solution.py:605
  80.1 9.3 %collective-permute-start.12 = (bf16[128,256]{1,0:T(8,128)(2,1)S(1)}, bf16[128,256]{1,0:T(8,128)(2,1)S(1)}, u32[]{:S(2)}, u32[]{:S(2)}) collective-permute-start(bf16[128,256]{1,0:T(8,128)(2,1)S(1)} %collective-permute-done.11.opposite_ref), channel_id=1, source_target_pairs={{16,32},{32,16},{24,40},{40,24},{48,64},{64,48},{56,72},{72,56},{8... | collective-permute-start | bytes 196616 | tf_op jit(solution)/shard_map/ppermute | solution.py:605
  84.4 7.1 %collective-permute-start.15 = (bf16[128,256]{1,0:T(8,128)(2,1)S(1)}, bf16[128,256]{1,0:T(8,128)(2,1)S(1)}, u32[]{:S(2)}, u32[]{:S(2)}) collective-permute-start(bf16[128,256]{1,0:T(8,128)(2,1)S(1)} %collective-permute-done.11.opposite_ref), channel_id=1, source_target_pairs={{0,16},{16,0},{8,24},{24,8},{32,48},{48,32},{40,56},{56,40},{64,80... | collective-permute-start | bytes 196616 | tf_op jit(solution)/shard_map/ppermute | solution.py:605
  92.6 7.0 %collective-permute-start.16 = (f32[4,16,128]{2,1,0:T(8,128)S(1)}, f32[4,16,128]{2,1,0:T(8,128)S(1)}, u32[]{:S(2)}, u32[]{:S(2)}) collective-permute-start(f32[4,16,128]{2,1,0:T(8,128)S(1)} %get-tuple-element.47), channel_id=1, source_target_pairs={{1,2},{2,1},{3,4},{4,3},{5,6},{6,5},{9,10},{10,9},{11,12},{12,11},... | collective-permute-start | bytes 98312 | tf_op jit(solution)/shard_map/ppermute | solution.py:605
  93.3 7.1 %collective-permute-start.17 = (f32[4,16,128]{2,1,0:T(8,128)S(1)}, f32[4,16,128]{2,1,0:T(8,128)S(1)}, u32[]{:S(2)}, u32[]{:S(2)}) collective-permute-start(f32[4,16,128]{2,1,0:T(8,128)S(1)} %get-tuple-element.48), channel_id=1, source_target_pairs={{0,1},{1,0},{2,3},{3,2},{4,5},{5,4},{6,7},{7,6},{8,9},{9,8},{10,11... | collective-permute-start | bytes 98312 | tf_op jit(solution)/shard_map/ppermute | solution.py:605
  100.5 13.3 %collective-permute-start.19 = (bf16[40,16,128]{2,1,0:T(8,128)(2,1)S(1)}, bf16[40,16,128]{2,1,0:T(8,128)(2,1)S(1)}, u32[]{:S(2)}, u32[]{:S(2)}) collective-permute-start(bf16[40,16,128]{2,1,0:T(8,128)(2,1)S(1)} %get-tuple-element.50), channel_id=1, source_target_pairs={{8,16},{16,8},{24,32},{32,24},{40,48},{48,40},{56,64},{64,56},{72,... | collective-permute-start | bytes 491528 | tf_op jit(solution)/shard_map/ppermute | solution.py:605
  105.8 8.5 %collective-permute-start.20 = (bf16[40,16,128]{2,1,0:T(8,128)(2,1)S(1)}, bf16[40,16,128]{2,1,0:T(8,128)(2,1)S(1)}, u32[]{:S(2)}, u32[]{:S(2)}) collective-permute-start(bf16[40,16,128]{2,1,0:T(8,128)(2,1)S(1)} %get-tuple-element.51), channel_id=1, source_target_pairs={{0,8},{8,0},{16,24},{24,16},{32,40},{40,32},{48,56},{56,48},{64,72... | collective-permute-start | bytes 491528 | tf_op jit(solution)/shard_map/ppermute | solution.py:605
  107.7 10.4 %collective-permute-start.18 = (bf16[10,16,128]{2,1,0:T(8,128)(2,1)S(1)}, bf16[10,16,128]{2,1,0:T(8,128)(2,1)S(1)}, u32[]{:S(2)}, u32[]{:S(2)}) collective-permute-start(bf16[10,16,128]{2,1,0:T(8,128)(2,1)S(1)} %get-tuple-element.49), channel_id=1, source_target_pairs={{16,32},{32,16},{24,40},{40,24},{48,64},{64,48},{56,72},{72,56},{8... | collective-permute-start | bytes 122888 | tf_op jit(solution)/shard_map/ppermute | solution.py:605
  111.8 6.8 %collective-permute-start.21 = (bf16[10,16,128]{2,1,0:T(8,128)(2,1)S(1)}, bf16[10,16,128]{2,1,0:T(8,128)(2,1)S(1)}, u32[]{:S(2)}, u32[]{:S(2)}) collective-permute-start(bf16[10,16,128]{2,1,0:T(8,128)(2,1)S(1)} %get-tuple-element.49), channel_id=1, source_target_pairs={{0,16},{16,0},{8,24},{24,8},{32,48},{48,32},{40,56},{56,40},{64,80... | collective-permute-start | bytes 122888 | tf_op jit(solution)/shard_map/ppermute | solution.py:605

commit v11 on v10

--- a/solution.py
+++ b/solution.py
@@ -24,10 +24,10 @@
 A_EXPORT = 22
 A_PLANES = 38
 B_WAVE = 12
-B_STRIP_T = 28
-B_STRIP_W = 30
-B_BEHIND = 34
-B_PLANES = 40
+B_STRIP_T = 20
+B_STRIP_W = 22
+B_BEHIND = 26
+B_PLANES = 32
 C_STRIP_W = 8
 C_PLANES = 10
 
@@ -137,18 +137,22 @@
     ref[low_at] = (value - high.astype(f32)).astype(bf16)
 
 
-def write_main(ref, tracer_at, wave_at, wave_low_at, fields_ref):
+def write_main(ref, tracer_at, wave_at, fields_ref, low=None):
     for half in range(2):
         cols = slice(half * LANES, (half + 1) * LANES)
         for i in range(TRACERS):
             ref[tracer_at + 2 * i + half] = fields_ref[WAVES + i, :, cols].astype(bf16)
         for i in range(WAVES):
-            split_to(ref, wave_at + 2 * i + half, wave_low_at + 2 * i + half, fields_ref[i, :, cols])
+            at = wave_at + 2 * i + half
+            if low is None:
+                ref[at] = fields_ref[i, :, cols].astype(bf16)
+            else:
+                split_to(ref, at, at + low, fields_ref[i, :, cols])
 
 
 def pack_kernel(opposite_ref, fields_ref, index_ref, config_ref, mixes_ref, near_ref):
     del index_ref, config_ref, mixes_ref
-    write_main(near_ref, 0, A_WAVE, A_WAVE + 6, fields_ref)
+    write_main(near_ref, 0, A_WAVE, fields_ref, 6)
     for half in range(2):
         for i in range(TURNED // 16):
             near_ref[A_EXPORT + half * 8 + i] = opposite_ref[16 * i : 16 * i + 16, half * LANES : (half + 1) * LANES]
@@ -174,10 +178,10 @@
         left_ref[p] = jnp.where(odd, chip_ref[p], outer_ref[p])
         right_ref[p] = jnp.where(odd, outer_ref[p], chip_ref[p])
     for ref, behind in ((out_c_ref, state_i_ref), (out_i_ref, state_c_ref)):
-        write_main(ref, 0, B_WAVE + 2, B_WAVE + 10, forcing_ref)
+        write_main(ref, 0, B_WAVE + 2, forcing_ref)
         for k, strips in enumerate((left_ref, right_ref)):
             ref[10 + k] = strips[0].astype(bf16)
-            split_to(ref, B_WAVE + k, B_WAVE + 8 + k, strips[1])
+            ref[B_WAVE + k] = strips[1].astype(bf16)
             ref[B_STRIP_T + k] = strips[2].astype(bf16)
             split_to(ref, B_STRIP_W + k, B_STRIP_W + 2 + k, strips[3])
         for p in range(6):
@@ -375,7 +379,7 @@
     for i in range(WAVES):
         pushed, parts = [], []
         for near, main in ((near_c_ref, state_c_ref), (near_i_ref, state_i_ref)):
-            pushed.append(wave_main(near, B_WAVE + 2, i, 8) + wave_strip(near, B_WAVE, i, 8))
+            pushed.append(wave_main(near, B_WAVE + 2, i) + wave_strip(near, B_WAVE, i))
             parts.append(wave_main(main, A_WAVE, i, 6) + wave_strip(near, B_STRIP_W, i, 2))
         place_field(wave_forcing.at[i], ROWS, own_parts(forcing_ref, left_ref, right_ref, 0, i))
         place_field(wave_state.at[i], ROWS, own_parts(fields_ref, left_ref, right_ref, 2, i))

time: 122 us -> 122 us (level)
  transfers between devices with their start and end apart: 22 -> 22, of which waited for: 10 -> 9; matrix products, arithmetic and copies ran while one was open for 1% -> 1% of each run, Pallas kernels for 6% -> 6%
where the time goes in v11:
time: 122 us; the launch traced here: 121 us
  starting transfers between devices  86.7 us (71%)
  Pallas kernels  16.3 us (13%)
  waiting for transfers between devices  13.2 us (11%)
  local copies, waits for them, and re-layouts  3.69 us (3%)
    ppermute x20, starting transfers between devices, exchanged(): return lax.ppermute(block, axis, route)  68.2 us
    ppermute x2, starting transfers between devices, local(): opposite = lax.ppermute(exported, 'sec', [(0, 1), (1, 0)])  18.5 us
    ppermute x20, waiting for transfers between devices, exchanged(): return lax.ppermute(block, axis, route)  9.96 us
    pallas_call x2, Pallas kernels, tracer_steps(): pl.pallas_call(lambda *refs: tracer_kernel(last, *refs), out_shape=tuple(...  7.37 us
    pallas_call x2, Pallas kernels, wave_steps(): pl.pallas_call(lambda *refs: wave_kernel(last, *refs), out_shape=state if...  4.45 us
    ppermute x2, waiting for transfers between devices, local(): opposite = lax.ppermute(exported, 'sec', [(0, 1), (1, 0)])  3.21 us
    unnamed x19, local copies, waits for them, and re-layouts  3.19 us
  transfers between devices with their start and end apart: 22, of which 9 were waited for; matrix products, arithmetic and copies ran while one was open for 1% of the time, Pallas kernels for 6%

profile of v11, /device:TPU:6, one launch (start us, length us, event | category | flops | bytes accessed | tf_op | source)
XLA Modules:
  0.0 121.1 jit_solution(8313417088313055805)
XLA Ops:
  0.6 2.0 %export.1 = bf16[128,256]{1,0:T(8,128)(2,1)} custom-call(f32[8,8]{1,0:T(8,128)} %bitcast.32, f32[8,8]{1,0:T(8,128)} %bitcast.30, f32[8,16,256]{2,1,0:T(8,128)} %bitcast.19, f32[8,16,256]{2,1,0:T(8,128)} %bitcast.29, s32[16,256]{1,0:T(8,128)} %bitcast.24), custom_call_target="tpu_custom_call" | custom-call | tf_op jit(solution)/shard_map/export/pallas_call | solution.py:115
  2.6 10.9 %collective-permute-start = (bf16[128,256]{1,0:T(8,128)(2,1)}, bf16[128,256]{1,0:T(8,128)(2,1)S(1)}, u32[]{:S(2)}, u32[]{:S(2)}) collective-permute-start(bf16[128,256]{1,0:T(8,128)(2,1)} %export.1), channel_id=1, source_target_pairs={{0,256},{256,0},{1,257},{257,1},{2,258},{258,2},{3,259},{259,3},{4... | collective-permute-start | bytes 196616 | tf_op jit(solution)/shard_map/ppermute | solution.py:642
  13.6 0.6 copy-done.3
  14.2 0.1 copy.14
  14.4 0.1 sub.33
  14.5 0.5 copy-done.5
  15.0 0.1 copy.15
  15.2 0.1 reshape_squeeze.7
  15.4 0.1 stack.23
  15.5 0.6 copy-done.7
  16.2 0.7 collective-permute-done.opposite_ref
  16.9 5.6 %collective-permute-start.2 = (bf16[38,16,128]{2,1,0:T(8,128)(2,1)S(1)}, bf16[38,16,128]{2,1,0:T(8,128)(2,1)S(1)}, u32[]{:S(2)}, u32[]{:S(2)}) collective-permute-start(bf16[38,16,128]{2,1,0:T(8,128)(2,1)S(1)} %pack.2), channel_id=1, source_target_pairs={{8,16},{16,8},{24,32},{32,24},{40,48},{48,40},{56,64},{64,56},{72,... | collective-permute-start | bytes 466952 | tf_op jit(solution)/shard_map/ppermute | solution.py:609
  22.6 1.9 %collective-permute-start.3 = (bf16[38,16,128]{2,1,0:T(8,128)(2,1)S(1)}, bf16[38,16,128]{2,1,0:T(8,128)(2,1)S(1)}, u32[]{:S(2)}, u32[]{:S(2)}) collective-permute-start(bf16[38,16,128]{2,1,0:T(8,128)(2,1)S(1)} %pack.2), channel_id=1, source_target_pairs={{0,8},{8,0},{16,24},{24,16},{32,40},{40,32},{48,56},{56,48},{64,72... | collective-permute-start | bytes 466952 | tf_op jit(solution)/shard_map/ppermute | solution.py:609
  24.5 4.0 %collective-permute-start.1 = (bf16[128,256]{1,0:T(8,128)(2,1)S(1)}, bf16[128,256]{1,0:T(8,128)(2,1)S(1)}, u32[]{:S(2)}, u32[]{:S(2)}) collective-permute-start(bf16[128,256]{1,0:T(8,128)(2,1)S(1)} %collective-permute-done.opposite_ref), channel_id=1, source_target_pairs={{16,32},{32,16},{24,40},{40,24},{48,64},{64,48},{56,72},{72,56},{8... | collective-permute-start | bytes 196616 | tf_op jit(solution)/shard_map/ppermute | solution.py:609
  28.5 3.8 %collective-permute-start.4 = (bf16[128,256]{1,0:T(8,128)(2,1)S(1)}, bf16[128,256]{1,0:T(8,128)(2,1)S(1)}, u32[]{:S(2)}, u32[]{:S(2)}) collective-permute-start(bf16[128,256]{1,0:T(8,128)(2,1)S(1)} %collective-permute-done.opposite_ref), channel_id=1, source_target_pairs={{0,16},{16,0},{8,24},{24,8},{32,48},{48,32},{40,56},{56,40},{64,80... | collective-permute-start | bytes 196616 | tf_op jit(solution)/shard_map/ppermute | solution.py:609
  32.3 1.2 %copy-done.1 = bf16[1,16,4,64,128]{4,3,2,1,0:T(8,128)(2,1)S(1)} copy-done((bf16[1,16,4,64,128]{4,3,2,1,0:T(8,128)(2,1)S(1)}, bf16[1,16,4,64,128]{4,3,2,1,0:T(8,128)(2,1)}, u32[]{:S(2)}) %copy-start.1) | copy-done | bytes 1048600
  33.7 1.9 %collective-permute-done.4.far_i_ref = bf16[128,256]{1,0:T(8,128)(2,1)S(1)} collective-permute-done((bf16[128,256]{1,0:T(8,128)(2,1)S(1)}, bf16[128,256]{1,0:T(8,128)(2,1)S(1)}, u32[]{:S(2)}, u32[]{:S(2)}) %collective-permute-start.4) | collective-permute-done | bytes 65568 | tf_op jit(solution)/shard_map/ppermute | solution.py:609
  35.6 1.1 remap.2
  36.7 0.7 collective-permute-start.5
  37.4 4.1 %collective-permute-start.6 = (f32[4,16,128]{2,1,0:T(8,128)S(1)}, f32[4,16,128]{2,1,0:T(8,128)S(1)}, u32[]{:S(2)}, u32[]{:S(2)}) collective-permute-start(f32[4,16,128]{2,1,0:T(8,128)S(1)} %get-tuple-element.33), channel_id=1, source_target_pairs={{0,1},{1,0},{2,3},{3,2},{4,5},{5,4},{6,7},{7,6},{8,9},{9,8},{10,11... | collective-permute-start | bytes 98312 | tf_op jit(solution)/shard_map/ppermute | solution.py:609
  41.5 0.8 collective-permute-done.6.chip_ref
  42.4 5.5 %collective-permute-start.8 = (bf16[32,16,128]{2,1,0:T(8,128)(2,1)S(1)}, bf16[32,16,128]{2,1,0:T(8,128)(2,1)S(1)}, u32[]{:S(2)}, u32[]{:S(2)}) collective-permute-start(bf16[32,16,128]{2,1,0:T(8,128)(2,1)S(1)} %get-tuple-element.35), channel_id=1, source_target_pairs={{8,16},{16,8},{24,32},{32,24},{40,48},{48,40},{56,64},{64,56},{72,... | collective-permute-start | bytes 393224 | tf_op jit(solution)/shard_map/ppermute | solution.py:609
  47.9 1.9 %collective-permute-start.9 = (bf16[32,16,128]{2,1,0:T(8,128)(2,1)S(1)}, bf16[32,16,128]{2,1,0:T(8,128)(2,1)S(1)}, u32[]{:S(2)}, u32[]{:S(2)}) collective-permute-start(bf16[32,16,128]{2,1,0:T(8,128)(2,1)S(1)} %get-tuple-element.36), channel_id=1, source_target_pairs={{0,8},{8,0},{16,24},{24,16},{32,40},{40,32},{48,56},{56,48},{64,72... | collective-permute-start | bytes 393224 | tf_op jit(solution)/shard_map/ppermute | solution.py:609
  49.9 3.9 %collective-permute-start.10 = (bf16[10,16,128]{2,1,0:T(8,128)(2,1)S(1)}, bf16[10,16,128]{2,1,0:T(8,128)(2,1)S(1)}, u32[]{:S(2)}, u32[]{:S(2)}) collective-permute-start(bf16[10,16,128]{2,1,0:T(8,128)(2,1)S(1)} %get-tuple-element.34), channel_id=1, source_target_pairs={{16,32},{32,16},{24,40},{40,24},{48,64},{64,48},{56,72},{72,56},{8... | collective-permute-start | bytes 122888 | tf_op jit(solution)/shard_map/ppermute | solution.py:609
  53.8 2.7 %collective-permute-start.7 = (bf16[10,16,128]{2,1,0:T(8,128)(2,1)S(1)}, bf16[10,16,128]{2,1,0:T(8,128)(2,1)S(1)}, u32[]{:S(2)}, u32[]{:S(2)}) collective-permute-start(bf16[10,16,128]{2,1,0:T(8,128)(2,1)S(1)} %get-tuple-element.34), channel_id=1, source_target_pairs={{0,16},{16,0},{8,24},{24,8},{32,48},{48,32},{40,56},{56,40},{64,80... | collective-permute-start | bytes 122888 | tf_op jit(solution)/shard_map/ppermute | solution.py:609
  56.5 3.5 %tracer_steps.2 = (f32[5,16,256]{2,1,0:T(8,128)S(1)}, f32[3,3,48,128]{3,2,1,0:T(8,128)S(1)}, f32[3,3,48,128]{3,2,1,0:T(8,128)S(1)}, f32[5,3,80,128]{3,2,1,0:T(8,128)S(1)}) custom-call(f32[1,17]{1,0:T(1,128)S(1)} %maximum_bitcast_fusion.config_ref.refs_0_, bf16[32,16,128]{2,1,0:T(8,128)(2,1)S(1)} %collective-permute-done.8.refs_1_.refs_3_, ...), custom_call_target="tpu_custom_call" | custom-call | flops 10000000 | bytes 4000000 | tf_op jit(solution)/shard_map/tracer_steps/pallas_call | solution.py:445
  60.0 0.9 collective-permute-done.7.refs_2_
  60.9 2.0 %wave_steps.1 = (f32[8,16,256]{2,1,0:T(8,128)S(1)}, bf16[128,256]{1,0:T(8,128)(2,1)S(1)}) custom-call(f32[1,17]{1,0:T(1,128)S(1)} %maximum_bitcast_fusion.config_ref.refs_0_, f32[16,8]{1,0:T(8,128)S(1)} %pad_maximum_fusion.mixes_ref.refs_1_, bf16[10,16,128]{2,1,0:T(8,128)(2,1)S(1)} %collective-permute-done.7.refs_2_, ...), custom_call_target="tpu_custom_call" | custom-call | tf_op jit(solution)/shard_map/wave_steps/pallas_call | solution.py:592
  62.9 7.6 %collective-permute-start.11 = (bf16[128,256]{1,0:T(8,128)(2,1)S(1)}, bf16[128,256]{1,0:T(8,128)(2,1)S(1)}, u32[]{:S(2)}, u32[]{:S(2)}) collective-permute-start(bf16[128,256]{1,0:T(8,128)(2,1)S(1)} %get-tuple-element.44), channel_id=1, source_target_pairs={{0,256},{256,0},{1,257},{257,1},{2,258},{258,2},{3,259},{259,3},{4... | collective-permute-start | bytes 196616 | tf_op jit(solution)/shard_map/ppermute | solution.py:642
  70.5 2.5 %collective-permute-done.11.opposite_ref = bf16[128,256]{1,0:T(8,128)(2,1)S(1)} collective-permute-done((bf16[128,256]{1,0:T(8,128)(2,1)S(1)}, bf16[128,256]{1,0:T(8,128)(2,1)S(1)}, u32[]{:S(2)}, u32[]{:S(2)}) %collective-permute-start.11) | collective-permute-done | bytes 65568 | tf_op jit(solution)/shard_map/ppermute | solution.py:642
  73.0 5.2 %collective-permute-start.13 = (bf16[38,16,128]{2,1,0:T(8,128)(2,1)S(1)}, bf16[38,16,128]{2,1,0:T(8,128)(2,1)S(1)}, u32[]{:S(2)}, u32[]{:S(2)}) collective-permute-start(bf16[38,16,128]{2,1,0:T(8,128)(2,1)S(1)} %pack.3), channel_id=1, source_target_pairs={{8,16},{16,8},{24,32},{32,24},{40,48},{48,40},{56,64},{64,56},{72,... | collective-permute-start | bytes 466952 | tf_op jit(solution)/shard_map/ppermute | solution.py:609
  78.2 1.9 %collective-permute-start.14 = (bf16[38,16,128]{2,1,0:T(8,128)(2,1)S(1)}, bf16[38,16,128]{2,1,0:T(8,128)(2,1)S(1)}, u32[]{:S(2)}, u32[]{:S(2)}) collective-permute-start(bf16[38,16,128]{2,1,0:T(8,128)(2,1)S(1)} %pack.3), channel_id=1, source_target_pairs={{0,8},{8,0},{16,24},{24,16},{32,40},{40,32},{48,56},{56,48},{64,72... | collective-permute-start | bytes 466952 | tf_op jit(solution)/shard_map/ppermute | solution.py:609
  80.1 4.2 %collective-permute-start.12 = (bf16[128,256]{1,0:T(8,128)(2,1)S(1)}, bf16[128,256]{1,0:T(8,128)(2,1)S(1)}, u32[]{:S(2)}, u32[]{:S(2)}) collective-permute-start(bf16[128,256]{1,0:T(8,128)(2,1)S(1)} %collective-permute-done.11.opposite_ref), channel_id=1, source_target_pairs={{16,32},{32,16},{24,40},{40,24},{48,64},{64,48},{56,72},{72,56},{8... | collective-permute-start | bytes 196616 | tf_op jit(solution)/shard_map/ppermute | solution.py:609
  84.4 2.6 %collective-permute-start.15 = (bf16[128,256]{1,0:T(8,128)(2,1)S(1)}, bf16[128,256]{1,0:T(8,128)(2,1)S(1)}, u32[]{:S(2)}, u32[]{:S(2)}) collective-permute-start(bf16[128,256]{1,0:T(8,128)(2,1)S(1)} %collective-permute-done.11.opposite_ref), channel_id=1, source_target_pairs={{0,16},{16,0},{8,24},{24,8},{32,48},{48,32},{40,56},{56,40},{64,80... | collective-permute-start | bytes 196616 | tf_op jit(solution)/shard_map/ppermute | solution.py:609
  87.0 2.4 %collective-permute-done.12.far_c_ref = bf16[128,256]{1,0:T(8,128)(2,1)S(1)} collective-permute-done((bf16[128,256]{1,0:T(8,128)(2,1)S(1)}, bf16[128,256]{1,0:T(8,128)(2,1)S(1)}, u32[]{:S(2)}, u32[]{:S(2)}) %collective-permute-start.12) | collective-permute-done | bytes 65568 | tf_op jit(solution)/shard_map/ppermute | solution.py:609
  89.4 2.0 %collective-permute-done.15.far_i_ref = bf16[128,256]{1,0:T(8,128)(2,1)S(1)} collective-permute-done((bf16[128,256]{1,0:T(8,128)(2,1)S(1)}, bf16[128,256]{1,0:T(8,128)(2,1)S(1)}, u32[]{:S(2)}, u32[]{:S(2)}) %collective-permute-start.15) | collective-permute-done | bytes 65568 | tf_op jit(solution)/shard_map/ppermute | solution.py:609
  91.4 1.1 remap.3
  92.6 0.7 collective-permute-start.16
  93.3 6.3 %collective-permute-start.17 = (f32[4,16,128]{2,1,0:T(8,128)S(1)}, f32[4,16,128]{2,1,0:T(8,128)S(1)}, u32[]{:S(2)}, u32[]{:S(2)}) collective-permute-start(f32[4,16,128]{2,1,0:T(8,128)S(1)} %get-tuple-element.48), channel_id=1, source_target_pairs={{0,1},{1,0},{2,3},{3,2},{4,5},{5,4},{6,7},{7,6},{8,9},{9,8},{10,11... | collective-permute-start | bytes 98312 | tf_op jit(solution)/shard_map/ppermute | solution.py:609
  99.6 0.8 collective-permute-done.17.chip_ref
  100.4 0.1 pack_forcing.3
  100.5 5.3 %collective-permute-start.19 = (bf16[32,16,128]{2,1,0:T(8,128)(2,1)S(1)}, bf16[32,16,128]{2,1,0:T(8,128)(2,1)S(1)}, u32[]{:S(2)}, u32[]{:S(2)}) collective-permute-start(bf16[32,16,128]{2,1,0:T(8,128)(2,1)S(1)} %get-tuple-element.50), channel_id=1, source_target_pairs={{8,16},{16,8},{24,32},{32,24},{40,48},{48,40},{56,64},{64,56},{72,... | collective-permute-start | bytes 393224 | tf_op jit(solution)/shard_map/ppermute | solution.py:609
  105.8 1.9 %collective-permute-start.20 = (bf16[32,16,128]{2,1,0:T(8,128)(2,1)S(1)}, bf16[32,16,128]{2,1,0:T(8,128)(2,1)S(1)}, u32[]{:S(2)}, u32[]{:S(2)}) collective-permute-start(bf16[32,16,128]{2,1,0:T(8,128)(2,1)S(1)} %get-tuple-element.51), channel_id=1, source_target_pairs={{0,8},{8,0},{16,24},{24,16},{32,40},{40,32},{48,56},{56,48},{64,72... | collective-permute-start | bytes 393224 | tf_op jit(solution)/shard_map/ppermute | solution.py:609
  107.7 4.1 %collective-permute-start.18 = (bf16[10,16,128]{2,1,0:T(8,128)(2,1)S(1)}, bf16[10,16,128]{2,1,0:T(8,128)(2,1)S(1)}, u32[]{:S(2)}, u32[]{:S(2)}) collective-permute-start(bf16[10,16,128]{2,1,0:T(8,128)(2,1)S(1)} %get-tuple-element.49), channel_id=1, source_target_pairs={{16,32},{32,16},{24,40},{40,24},{48,64},{64,48},{56,72},{72,56},{8... | collective-permute-start | bytes 122888 | tf_op jit(solution)/shard_map/ppermute | solution.py:609
  111.8 1.9 %collective-permute-start.21 = (bf16[10,16,128]{2,1,0:T(8,128)(2,1)S(1)}, bf16[10,16,128]{2,1,0:T(8,128)(2,1)S(1)}, u32[]{:S(2)}, u32[]{:S(2)}) collective-permute-start(bf16[10,16,128]{2,1,0:T(8,128)(2,1)S(1)} %get-tuple-element.49), channel_id=1, source_target_pairs={{0,16},{16,0},{8,24},{24,8},{32,48},{48,32},{40,56},{56,40},{64,80... | collective-permute-start | bytes 122888 | tf_op jit(solution)/shard_map/ppermute | solution.py:609
  113.8 3.9 %tracer_steps.3 = (f32[8,16,256]{2,1,0:T(8,128)}, f32[5,16,256]{2,1,0:T(8,128)S(1)}, f32[3,3,48,128]{3,2,1,0:T(8,128)S(1)}, f32[3,3,48,128]{3,2,1,0:T(8,128)S(1)}, f32[5,3,80,128]{3,2,1,0:T(8,128)S(1)}) custom-call(f32[1,17]{1,0:T(1,128)S(1)} %maximum_bitcast_fusion.config_ref.refs_0_, bf16[32,16,128]{2,1,0:T(8,128)(2,1)S(1)} %collective-permute-done.19.refs_1_.refs_2_, ...), custom_call_target="tpu_custom_call" | custom-call | flops 10000000 | bytes 4000000 | tf_op jit(solution)/shard_map/tracer_steps/pallas_call | solution.py:445
  117.6 1.0 collective-permute-done.21.refs_4_
  118.6 2.5 %wave_steps_last.1 = f32[8,16,256]{2,1,0:T(8,128)} custom-call(f32[1,17]{1,0:T(1,128)S(1)} %maximum_bitcast_fusion.config_ref.refs_0_, bf16[10,16,128]{2,1,0:T(8,128)(2,1)S(1)} %collective-permute-done.18.refs_1_, bf16[32,16,128]{2,1,0:T(8,128)(2,1)S(1)} %collective-permute-done.19.refs_1_.refs_2_, ...), custom_call_target="tpu_custom_call" | custom-call | tf_op jit(solution)/shard_map/wave_steps_last/pallas_call | solution.py:592
  (37 shorter events, 0.4 us)
Async XLA Ops:
  2.6 14.3 %collective-permute-start = (bf16[128,256]{1,0:T(8,128)(2,1)}, bf16[128,256]{1,0:T(8,128)(2,1)S(1)}, u32[]{:S(2)}, u32[]{:S(2)}) collective-permute-start(bf16[128,256]{1,0:T(8,128)(2,1)} %export.1), channel_id=1, source_target_pairs={{0,256},{256,0},{1,257},{257,1},{2,258},{258,2},{3,259},{259,3},{4... | collective-permute-start | bytes 196616 | tf_op jit(solution)/shard_map/ppermute | solution.py:642
  13.5 0.7 copy-start.3
  13.5 0.7 copy-start.4
  13.6 0.7 copy-start.6
  13.6 3.3 %copy-start = (f32[1,8,16,256]{3,2,1,0:T(8,128)S(1)}, f32[1,8,16,256]{3,2,1,0:T(8,128)}, u32[]{:S(2)}) copy-start(f32[1,8,16,256]{3,2,1,0:T(8,128)} %param.10) | copy-start | bytes 393220
  14.4 0.7 copy-start.5
  15.5 0.7 copy-start.7
  15.5 0.7 copy-start.8
  16.9 15.4 %collective-permute-start.2 = (bf16[38,16,128]{2,1,0:T(8,128)(2,1)S(1)}, bf16[38,16,128]{2,1,0:T(8,128)(2,1)S(1)}, u32[]{:S(2)}, u32[]{:S(2)}) collective-permute-start(bf16[38,16,128]{2,1,0:T(8,128)(2,1)S(1)} %pack.2), channel_id=1, source_target_pairs={{8,16},{16,8},{24,32},{32,24},{40,48},{48,40},{56,64},{64,56},{72,... | collective-permute-start | bytes 466952 | tf_op jit(solution)/shard_map/ppermute | solution.py:609
  22.6 9.8 %collective-permute-start.3 = (bf16[38,16,128]{2,1,0:T(8,128)(2,1)S(1)}, bf16[38,16,128]{2,1,0:T(8,128)(2,1)S(1)}, u32[]{:S(2)}, u32[]{:S(2)}) collective-permute-start(bf16[38,16,128]{2,1,0:T(8,128)(2,1)S(1)} %pack.2), channel_id=1, source_target_pairs={{0,8},{8,0},{16,24},{24,16},{32,40},{40,32},{48,56},{56,48},{64,72... | collective-permute-start | bytes 466952 | tf_op jit(solution)/shard_map/ppermute | solution.py:609
  24.5 9.2 %collective-permute-start.1 = (bf16[128,256]{1,0:T(8,128)(2,1)S(1)}, bf16[128,256]{1,0:T(8,128)(2,1)S(1)}, u32[]{:S(2)}, u32[]{:S(2)}) collective-permute-start(bf16[128,256]{1,0:T(8,128)(2,1)S(1)} %collective-permute-done.opposite_ref), channel_id=1, source_target_pairs={{16,32},{32,16},{24,40},{40,24},{48,64},{64,48},{56,72},{72,56},{8... | collective-permute-start | bytes 196616 | tf_op jit(solution)/shard_map/ppermute | solution.py:609
  28.5 7.1 %collective-permute-start.4 = (bf16[128,256]{1,0:T(8,128)(2,1)S(1)}, bf16[128,256]{1,0:T(8,128)(2,1)S(1)}, u32[]{:S(2)}, u32[]{:S(2)}) collective-permute-start(bf16[128,256]{1,0:T(8,128)(2,1)S(1)} %collective-permute-done.opposite_ref), channel_id=1, source_target_pairs={{0,16},{16,0},{8,24},{24,8},{32,48},{48,32},{40,56},{56,40},{64,80... | collective-permute-start | bytes 196616 | tf_op jit(solution)/shard_map/ppermute | solution.py:609
  32.3 1.2 %copy-start.1 = (bf16[1,16,4,64,128]{4,3,2,1,0:T(8,128)(2,1)S(1)}, bf16[1,16,4,64,128]{4,3,2,1,0:T(8,128)(2,1)}, u32[]{:S(2)}) copy-start(bf16[1,16,4,64,128]{4,3,2,1,0:T(8,128)(2,1)} %param.19) | copy-start | bytes 3145732
  33.6 2.0 %copy-start.2 = (s32[1,16,256]{2,1,0:T(8,128)S(1)}, s32[1,16,256]{2,1,0:T(8,128)}, u32[]{:S(2)}) copy-start(s32[1,16,256]{2,1,0:T(8,128)} %param.12) | copy-start | bytes 49156
  36.7 4.8 %collective-permute-start.5 = (f32[4,16,128]{2,1,0:T(8,128)S(1)}, f32[4,16,128]{2,1,0:T(8,128)S(1)}, u32[]{:S(2)}, u32[]{:S(2)}) collective-permute-start(f32[4,16,128]{2,1,0:T(8,128)S(1)} %get-tuple-element.32), channel_id=1, source_target_pairs={{1,2},{2,1},{3,4},{4,3},{5,6},{6,5},{9,10},{10,9},{11,12},{12,11},... | collective-permute-start | bytes 98312 | tf_op jit(solution)/shard_map/ppermute | solution.py:609
  37.4 4.9 %collective-permute-start.6 = (f32[4,16,128]{2,1,0:T(8,128)S(1)}, f32[4,16,128]{2,1,0:T(8,128)S(1)}, u32[]{:S(2)}, u32[]{:S(2)}) collective-permute-start(f32[4,16,128]{2,1,0:T(8,128)S(1)} %get-tuple-element.33), channel_id=1, source_target_pairs={{0,1},{1,0},{2,3},{3,2},{4,5},{5,4},{6,7},{7,6},{8,9},{9,8},{10,11... | collective-permute-start | bytes 98312 | tf_op jit(solution)/shard_map/ppermute | solution.py:609
  42.4 14.0 %collective-permute-start.8 = (bf16[32,16,128]{2,1,0:T(8,128)(2,1)S(1)}, bf16[32,16,128]{2,1,0:T(8,128)(2,1)S(1)}, u32[]{:S(2)}, u32[]{:S(2)}) collective-permute-start(bf16[32,16,128]{2,1,0:T(8,128)(2,1)S(1)} %get-tuple-element.35), channel_id=1, source_target_pairs={{8,16},{16,8},{24,32},{32,24},{40,48},{48,40},{56,64},{64,56},{72,... | collective-permute-start | bytes 393224 | tf_op jit(solution)/shard_map/ppermute | solution.py:609
  47.9 8.5 %collective-permute-start.9 = (bf16[32,16,128]{2,1,0:T(8,128)(2,1)S(1)}, bf16[32,16,128]{2,1,0:T(8,128)(2,1)S(1)}, u32[]{:S(2)}, u32[]{:S(2)}) collective-permute-start(bf16[32,16,128]{2,1,0:T(8,128)(2,1)S(1)} %get-tuple-element.36), channel_id=1, source_target_pairs={{0,8},{8,0},{16,24},{24,16},{32,40},{40,32},{48,56},{56,48},{64,72... | collective-permute-start | bytes 393224 | tf_op jit(solution)/shard_map/ppermute | solution.py:609
  49.9 10.1 %collective-permute-start.10 = (bf16[10,16,128]{2,1,0:T(8,128)(2,1)S(1)}, bf16[10,16,128]{2,1,0:T(8,128)(2,1)S(1)}, u32[]{:S(2)}, u32[]{:S(2)}) collective-permute-start(bf16[10,16,128]{2,1,0:T(8,128)(2,1)S(1)} %get-tuple-element.34), channel_id=1, source_target_pairs={{16,32},{32,16},{24,40},{40,24},{48,64},{64,48},{56,72},{72,56},{8... | collective-permute-start | bytes 122888 | tf_op jit(solution)/shard_map/ppermute | solution.py:609
  53.8 7.1 %collective-permute-start.7 = (bf16[10,16,128]{2,1,0:T(8,128)(2,1)S(1)}, bf16[10,16,128]{2,1,0:T(8,128)(2,1)S(1)}, u32[]{:S(2)}, u32[]{:S(2)}) collective-permute-start(bf16[10,16,128]{2,1,0:T(8,128)(2,1)S(1)} %get-tuple-element.34), channel_id=1, source_target_pairs={{0,16},{16,0},{8,24},{24,8},{32,48},{48,32},{40,56},{56,40},{64,80... | collective-permute-start | bytes 122888 | tf_op jit(solution)/shard_map/ppermute | solution.py:609
  62.9 10.1 %collective-permute-start.11 = (bf16[128,256]{1,0:T(8,128)(2,1)S(1)}, bf16[128,256]{1,0:T(8,128)(2,1)S(1)}, u32[]{:S(2)}, u32[]{:S(2)}) collective-permute-start(bf16[128,256]{1,0:T(8,128)(2,1)S(1)} %get-tuple-element.44), channel_id=1, source_target_pairs={{0,256},{256,0},{1,257},{257,1},{2,258},{258,2},{3,259},{259,3},{4... | collective-permute-start | bytes 196616 | tf_op jit(solution)/shard_map/ppermute | solution.py:642
  73.0 18.4 %collective-permute-start.13 = (bf16[38,16,128]{2,1,0:T(8,128)(2,1)S(1)}, bf16[38,16,128]{2,1,0:T(8,128)(2,1)S(1)}, u32[]{:S(2)}, u32[]{:S(2)}) collective-permute-start(bf16[38,16,128]{2,1,0:T(8,128)(2,1)S(1)} %pack.3), channel_id=1, source_target_pairs={{8,16},{16,8},{24,32},{32,24},{40,48},{48,40},{56,64},{64,56},{72,... | collective-permute-start | bytes 466952 | tf_op jit(solution)/shard_map/ppermute | solution.py:609
  78.2 13.2 %collective-permute-start.14 = (bf16[38,16,128]{2,1,0:T(8,128)(2,1)S(1)}, bf16[38,16,128]{2,1,0:T(8,128)(2,1)S(1)}, u32[]{:S(2)}, u32[]{:S(2)}) collective-permute-start(bf16[38,16,128]{2,1,0:T(8,128)(2,1)S(1)} %pack.3), channel_id=1, source_target_pairs={{0,8},{8,0},{16,24},{24,16},{32,40},{40,32},{48,56},{56,48},{64,72... | collective-permute-start | bytes 466952 | tf_op jit(solution)/shard_map/ppermute | solution.py:609
  80.1 9.3 %collective-permute-start.12 = (bf16[128,256]{1,0:T(8,128)(2,1)S(1)}, bf16[128,256]{1,0:T(8,128)(2,1)S(1)}, u32[]{:S(2)}, u32[]{:S(2)}) collective-permute-start(bf16[128,256]{1,0:T(8,128)(2,1)S(1)} %collective-permute-done.11.opposite_ref), channel_id=1, source_target_pairs={{16,32},{32,16},{24,40},{40,24},{48,64},{64,48},{56,72},{72,56},{8... | collective-permute-start | bytes 196616 | tf_op jit(solution)/shard_map/ppermute | solution.py:609
  84.4 7.1 %collective-permute-start.15 = (bf16[128,256]{1,0:T(8,128)(2,1)S(1)}, bf16[128,256]{1,0:T(8,128)(2,1)S(1)}, u32[]{:S(2)}, u32[]{:S(2)}) collective-permute-start(bf16[128,256]{1,0:T(8,128)(2,1)S(1)} %collective-permute-done.11.opposite_ref), channel_id=1, source_target_pairs={{0,16},{16,0},{8,24},{24,8},{32,48},{48,32},{40,56},{56,40},{64,80... | collective-permute-start | bytes 196616 | tf_op jit(solution)/shard_map/ppermute | solution.py:609
  92.6 7.0 %collective-permute-start.16 = (f32[4,16,128]{2,1,0:T(8,128)S(1)}, f32[4,16,128]{2,1,0:T(8,128)S(1)}, u32[]{:S(2)}, u32[]{:S(2)}) collective-permute-start(f32[4,16,128]{2,1,0:T(8,128)S(1)} %get-tuple-element.47), channel_id=1, source_target_pairs={{1,2},{2,1},{3,4},{4,3},{5,6},{6,5},{9,10},{10,9},{11,12},{12,11},... | collective-permute-start | bytes 98312 | tf_op jit(solution)/shard_map/ppermute | solution.py:609
  93.3 7.1 %collective-permute-start.17 = (f32[4,16,128]{2,1,0:T(8,128)S(1)}, f32[4,16,128]{2,1,0:T(8,128)S(1)}, u32[]{:S(2)}, u32[]{:S(2)}) collective-permute-start(f32[4,16,128]{2,1,0:T(8,128)S(1)} %get-tuple-element.48), channel_id=1, source_target_pairs={{0,1},{1,0},{2,3},{3,2},{4,5},{5,4},{6,7},{7,6},{8,9},{9,8},{10,11... | collective-permute-start | bytes 98312 | tf_op jit(solution)/shard_map/ppermute | solution.py:609
  100.5 13.3 %collective-permute-start.19 = (bf16[32,16,128]{2,1,0:T(8,128)(2,1)S(1)}, bf16[32,16,128]{2,1,0:T(8,128)(2,1)S(1)}, u32[]{:S(2)}, u32[]{:S(2)}) collective-permute-start(bf16[32,16,128]{2,1,0:T(8,128)(2,1)S(1)} %get-tuple-element.50), channel_id=1, source_target_pairs={{8,16},{16,8},{24,32},{32,24},{40,48},{48,40},{56,64},{64,56},{72,... | collective-permute-start | bytes 393224 | tf_op jit(solution)/shard_map/ppermute | solution.py:609
  105.8 8.0 %collective-permute-start.20 = (bf16[32,16,128]{2,1,0:T(8,128)(2,1)S(1)}, bf16[32,16,128]{2,1,0:T(8,128)(2,1)S(1)}, u32[]{:S(2)}, u32[]{:S(2)}) collective-permute-start(bf16[32,16,128]{2,1,0:T(8,128)(2,1)S(1)} %get-tuple-element.51), channel_id=1, source_target_pairs={{0,8},{8,0},{16,24},{24,16},{32,40},{40,32},{48,56},{56,48},{64,72... | collective-permute-start | bytes 393224 | tf_op jit(solution)/shard_map/ppermute | solution.py:609
  107.7 9.9 %collective-permute-start.18 = (bf16[10,16,128]{2,1,0:T(8,128)(2,1)S(1)}, bf16[10,16,128]{2,1,0:T(8,128)(2,1)S(1)}, u32[]{:S(2)}, u32[]{:S(2)}) collective-permute-start(bf16[10,16,128]{2,1,0:T(8,128)(2,1)S(1)} %get-tuple-element.49), channel_id=1, source_target_pairs={{16,32},{32,16},{24,40},{40,24},{48,64},{64,48},{56,72},{72,56},{8... | collective-permute-start | bytes 122888 | tf_op jit(solution)/shard_map/ppermute | solution.py:609
  111.8 6.8 %collective-permute-start.21 = (bf16[10,16,128]{2,1,0:T(8,128)(2,1)S(1)}, bf16[10,16,128]{2,1,0:T(8,128)(2,1)S(1)}, u32[]{:S(2)}, u32[]{:S(2)}) collective-permute-start(bf16[10,16,128]{2,1,0:T(8,128)(2,1)S(1)} %get-tuple-element.49), channel_id=1, source_target_pairs={{0,16},{16,0},{8,24},{24,8},{32,48},{48,32},{40,56},{56,40},{64,80... | collective-permute-start | bytes 122888 | tf_op jit(solution)/shard_map/ppermute | solution.py:609
